TPU v7x, 32 devices: a whole 2x2x4 slice. The times are simulated.
32 devices in a mesh: snap: 2 (over x), inner: 16 (over z, y, core).
Axes of the slice: x: 2, y: 2, z: 4, core: 2. Of those that a mesh axis runs over, the one named last changes fastest.
Arguments:
- vertices: float32 [16384, 256], P(('snap', 'inner')), parts along dimension 0, may hold values from -0.75 to 0.75
- vertex_moments: float32 [16384, 256], P(('snap', 'inner')), parts along dimension 0, may hold values from 0.1 to 2
- contexts: float32 [32768, 256], P(('snap', 'inner')), parts along dimension 0, may hold values from -0.75 to 0.75
- context_moments: float32 [32768, 256], P(('snap', 'inner')), parts along dimension 0, may hold values from 0.1 to 2
- edge_counts: int32 [3, 512, 32768], P(None, None, ('snap', 'inner')), parts along dimension 2, may hold values from 0 to 4
- negative_weights: int32 [3, 32768], P(None, ('snap', 'inner')), parts along dimension 1, may hold values from 1 to 6
Outputs:
- vertex_out: float32 [16384, 256], P(('snap', 'inner')), parts along dimension 0
- vertex_moments_out: float32 [16384, 256], P(('snap', 'inner')), parts along dimension 0
- context_out: float32 [32768, 256], P(('snap', 'inner')), parts along dimension 0
- context_moments_out: float32 [32768, 256], P(('snap', 'inner')), parts along dimension 0
There are 2 independent parts, one for each index of `snap`. A program takes and returns all parts, laid end to end along the dimension named above; each array names one. Nothing has to cross between parts.
All inputs are finite; a program needn't handle non-finite values.
Results may differ from a plain program's by a relative error of at most 0.0001.
Values sent between devices are 32-bit elements; how exact they have to be, the bound alone decides.
No kernel may reach another device: no remote copies, remote signals or barrier semaphores. Data moves between devices by JAX's collectives and lax.ppermute only.
A program may use at most 64 MiB of HBM per device.

v0:
```python
import jax
import jax.numpy as jnp
from jax import lax
from jax.sharding import PartitionSpec as P


def from_behind(value, axis, steps):
    count = lax.axis_size(axis)
    pairs = [(source, (source + steps) % count) for source in range(count)]
    return lax.ppermute(value, axis, pairs)


def local_step(ublk, gblk, cblk, hblk, counts, negs):
    scores = jnp.dot(ublk, cblk.T, precision=lax.Precision.HIGHEST)
    ecount = counts.astype(jnp.float32)
    resid = (ecount + negs.astype(jnp.float32)[None, :]) * jax.nn.sigmoid(scores) - ecount
    grad_u = jnp.dot(resid, cblk, precision=lax.Precision.HIGHEST)
    grad_c = jnp.dot(resid.T, ublk, precision=lax.Precision.HIGHEST)
    gblk = gblk + grad_u * grad_u
    ublk = ublk - 0.05 * grad_u / jnp.sqrt(gblk)
    hblk = hblk + grad_c * grad_c
    cblk = cblk - 0.05 * grad_c / jnp.sqrt(hblk)
    return (ublk, gblk, cblk, hblk)


def per_device(vertices, vertex_moments, contexts, context_moments, edge_counts, negative_weights):
    ublk = vertices
    gblk = vertex_moments
    cblk = contexts
    hblk = context_moments
    nsteps = edge_counts.shape[0]
    for step in range(nsteps):
        ublk, gblk, cblk, hblk = local_step(
            ublk, gblk, cblk, hblk, edge_counts[step], negative_weights[step]
        )
        if step + 1 < nsteps:
            ublk = from_behind(ublk, "inner", 1)
            gblk = from_behind(gblk, "inner", 1)
    homed = from_behind(jnp.stack([ublk, gblk]), "inner", 1 - nsteps)
    return (homed[0], homed[1], cblk, hblk)


def solution(mesh):
    return jax.shard_map(
        per_device,
        mesh=mesh,
        in_specs=(
            P(("snap", "inner"), None),
            P(("snap", "inner"), None),
            P(("snap", "inner"), None),
            P(("snap", "inner"), None),
            P(None, None, ("snap", "inner")),
            P(None, ("snap", "inner")),
        ),
        out_specs=(
            P(("snap", "inner"), None),
            P(("snap", "inner"), None),
            P(("snap", "inner"), None),
            P(("snap", "inner"), None),
        ),
        check_vma=False,
    )
```

profile of v0, /device:TPU:0, one launch (start us, length us, event | category | flops | bytes accessed | tf_op | source)
XLA Modules:
  0.0 68.6 jit_solution(9668787253701556961)
XLA Ops:
  0.6 0.8 %slice_convert_fusion = (f32[1,1024]{1,0:T(1,128)S(1)}, f32[1,1024]{1,0:T(1,128)S(1)}, f32[1,1024]{1,0:T(1,128)S(1)}) fusion(s32[3,1024]{1,0:T(4,128)} %param.11), kind=kLoop, calls=%fused_computation.25 | loop fusion | flops 3072 | bytes 24576 | tf_op jit(solution)/shard_map/convert_element_type | solution.py:16
  1.5 0.0 slice-start
  1.5 0.0 copy-start
  1.5 0.0 copy-start.2
  1.5 0.0 copy-start.3
  1.5 0.0 slice-start.1
  1.5 4.6 %bitcast_subtract_fusion.2 = f32[512,1024]{1,0:T(8,128)S(1)} fusion(s32[3,512,1024]{2,1,0:T(8,128)} %param.10, f32[512,256]{1,0:T(8,128)} %param.6, f32[1024,256]{1,0:T(8,128)} %param.8, f32[1024]{0:T(1024)S(1)} %bitcast.50), kind=kOutput, calls=%fused_computation.6 | convolution fusion | flops 1614282752 | bytes 5771264 | tf_op jit(solution)/shard_map/dot_general | solution.py:14
  6.2 0.0 copy-done
  6.2 0.0 copy-done.2
  6.2 0.0 copy-done.3
  6.2 1.9 %multiply_subtract_fusion.4 = (f32[512,256]{1,0:T(8,128)S(1)}, f32[512,256]{1,0:T(8,128)S(1)}) fusion(f32[512,256]{1,0:T(8,128)S(1)} %copy-done.2, f32[512,256]{1,0:T(8,128)S(1)} %copy-done.3, f32[512,1024]{1,0:T(8,128)S(1)} %bitcast_subtract_fusion.2, f32[1024,256]{1,0:T(8,128)S(1)} %copy-done), kind=kOutput, calls=%fused_computation.22 | convolution fusion | flops 1611268096 | bytes 5242880 | tf_op jit(solution)/shard_map/dot_general | solution.py:17
  8.1 0.0 copy-start.1
  8.1 0.5 collective-permute-start
  8.6 2.6 %collective-permute-start.1 = (f32[512,256]{1,0:T(8,128)S(1)}, f32[512,256]{1,0:T(8,128)S(1)}, u32[]{:S(2)}, u32[]{:S(2)}) collective-permute-start(f32[512,256]{1,0:T(8,128)S(1)} %get-tuple-element.9), channel_id=1, source_target_pairs={{0,1},{1,2},{2,3},{3,4},{4,5},{5,6},{6,7},{7,8},{8,9},{9,10},{10,1... | collective-permute-start | bytes 1572872 | tf_op jit(solution)/shard_map/ppermute | solution.py:10
  11.2 3.5 %fusion.5 = f32[1024,256]{1,0:T(8,128)S(1)} fusion(f32[512,1024]{1,0:T(8,128)S(1)} %bitcast_subtract_fusion.2, f32[512,256]{1,0:T(8,128)S(1)} %copy-done.2), kind=kOutput, calls=%fused_computation.29 | convolution fusion | flops 1610612736 | bytes 3670016 | tf_op jit(solution)/shard_map/dot_general | solution.py:18
  14.7 5.7 %collective-permute-done = f32[512,256]{1,0:T(8,128)S(1)} collective-permute-done((f32[512,256]{1,0:T(8,128)S(1)}, f32[512,256]{1,0:T(8,128)S(1)}, u32[]{:S(2)}, u32[]{:S(2)}) %collective-permute-start) | collective-permute-done | bytes 524320 | tf_op jit(solution)/shard_map/ppermute | solution.py:10
  20.4 0.0 slice-done
  20.4 0.0 slice-done.1
  20.4 0.0 copy-done.1
  20.5 2.6 %bitcast_subtract_fusion.1 = f32[512,1024]{1,0:T(8,128)S(1)} fusion(s32[3,512,1024]{2,1,0:T(8,128)S(1)} %bitcast.52, f32[512,256]{1,0:T(8,128)S(1)} %collective-permute-done, f32[1024]{0:T(1024)S(1)} %bitcast.49, f32[1024,256]{1,0:T(8,128)S(1)} %copy-done, f32[1024,256]{1,0:T(8,128)S(1)} %fusion.5, f32[1024,256]{1,0:T(8,128)S(1)} %copy-done.1), kind=kOutput, calls=%fused_computation.3 | convolution fusion | flops 1615593472 | bytes 7868416 | tf_op jit(solution)/shard_map/dot_general | solution.py:14
  23.0 3.0 %collective-permute-done.1 = f32[512,256]{1,0:T(8,128)S(1)} collective-permute-done((f32[512,256]{1,0:T(8,128)S(1)}, f32[512,256]{1,0:T(8,128)S(1)}, u32[]{:S(2)}, u32[]{:S(2)}) %collective-permute-start.1) | collective-permute-done | bytes 524320 | tf_op jit(solution)/shard_map/ppermute | solution.py:10
  26.1 2.0 %multiply_subtract_fusion.3 = (f32[512,256]{1,0:T(8,128)S(1)}, f32[512,256]{1,0:T(8,128)S(1)}) fusion(f32[512,256]{1,0:T(8,128)S(1)} %collective-permute-done, f32[512,256]{1,0:T(8,128)S(1)} %collective-permute-done.1, f32[512,1024]{1,0:T(8,128)S(1)} %bitcast_subtract_fusion.1, f32[1024,256]{1,0:T(8,128)S(1)} %copy-done, f32[1024,256]{1,0:T(8,128)S(1)} %fusion.5, ...), kind=kOutput, calls=%fused_computation.20 | convolution fusion | flops 1612578816 | bytes 7340032 | tf_op jit(solution)/shard_map/dot_general | solution.py:17
  28.1 0.1 collective-permute-start.2
  28.1 0.3 collective-permute-start.3
  28.4 3.8 %multiply_subtract_fusion.1 = (f32[1024,256]{1,0:T(8,128)S(1)}, f32[1024,256]{1,0:T(8,128)S(1)}) fusion(f32[1024,256]{1,0:T(8,128)S(1)} %copy-done.1, f32[1024,256]{1,0:T(8,128)S(1)} %fusion.5, f32[1024,256]{1,0:T(8,128)S(1)} %copy-done, f32[512,1024]{1,0:T(8,128)S(1)} %bitcast_subtract_fusion.1, f32[512,256]{1,0:T(8,128)S(1)} %collective-permute-done), kind=kOutput, calls=%fused_computation.12 | convolution fusion | flops 1613234176 | bytes 7864320 | tf_op jit(solution)/shard_map/dot_general | solution.py:18
  32.2 7.2 %collective-permute-done.2 = f32[512,256]{1,0:T(8,128)S(1)} collective-permute-done((f32[512,256]{1,0:T(8,128)S(1)}, f32[512,256]{1,0:T(8,128)S(1)}, u32[]{:S(2)}, u32[]{:S(2)}) %collective-permute-start.2) | collective-permute-done | bytes 524320 | tf_op jit(solution)/shard_map/ppermute | solution.py:10
  39.4 2.4 %bitcast_subtract_fusion = f32[512,1024]{1,0:T(8,128)S(1)} fusion(s32[3,512,1024]{2,1,0:T(8,128)S(1)} %bitcast.52, f32[512,256]{1,0:T(8,128)S(1)} %collective-permute-done.2, f32[1024,256]{1,0:T(8,128)S(1)} %get-tuple-element.17, f32[1024]{0:T(1024)S(1)} %bitcast.48), kind=kOutput, calls=%fused_computation | convolution fusion | flops 1614282752 | bytes 5771264 | tf_op jit(solution)/shard_map/dot_general | solution.py:14
  41.8 1.8 %fusion.6 = f32[512,256]{1,0:T(8,128)S(1)} fusion(f32[512,1024]{1,0:T(8,128)S(1)} %bitcast_subtract_fusion, f32[1024,256]{1,0:T(8,128)S(1)} %get-tuple-element.17), kind=kOutput, calls=%fused_computation.30 | convolution fusion | flops 1610612736 | bytes 3670016 | tf_op jit(solution)/shard_map/dot_general | solution.py:17
  43.7 1.5 %collective-permute-done.3 = f32[512,256]{1,0:T(8,128)S(1)} collective-permute-done((f32[512,256]{1,0:T(8,128)S(1)}, f32[512,256]{1,0:T(8,128)S(1)}, u32[]{:S(2)}, u32[]{:S(2)}) %collective-permute-start.3) | collective-permute-done | bytes 524320 | tf_op jit(solution)/shard_map/ppermute | solution.py:10
  45.1 0.1 subtract_bitcast_fusion
  45.3 0.1 pad_maximum_fusion
  45.3 0.1 collective-permute-start.4
  45.4 5.0 %multiply_subtract_fusion = (f32[1024,256]{1,0:T(8,128)}, f32[1024,256]{1,0:T(8,128)}) fusion(f32[1024,256]{1,0:T(8,128)S(1)} %get-tuple-element.17, f32[1024,256]{1,0:T(8,128)S(1)} %get-tuple-element.18, f32[1024,256]{1,0:T(8,128)S(1)} %copy-done.1, f32[1024,256]{1,0:T(8,128)S(1)} %fusion.5, f32[512,1024]{1,0:T(8,128)S(1)} %bitcast_subtract_fusion, ...), kind=kOutput, calls=%fused_computation.10 | convolution fusion | flops 1612972032 | bytes 8912896 | tf_op jit(solution)/shard_map/dot_general | solution.py:18
  50.4 17.1 %collective-permute-done.4 = f32[2,512,256]{2,1,0:T(8,128)S(1)} collective-permute-done((f32[2,512,256]{2,1,0:T(8,128)S(1)}, f32[2,512,256]{2,1,0:T(8,128)S(1)}, u32[]{:S(2)}, u32[]{:S(2)}) %collective-permute-start.4) | collective-permute-done | bytes 1048608 | tf_op jit(solution)/shard_map/ppermute | solution.py:10
  67.5 1.0 %slice_bitcast_fusion = (f32[512,256]{1,0:T(8,128)}, f32[512,256]{1,0:T(8,128)}) fusion(f32[2,512,256]{2,1,0:T(8,128)S(1)} %collective-permute-done.4), kind=kLoop, calls=%fused_computation.16 | loop fusion | bytes 2097152 | tf_op jit(solution)/shard_map/squeeze | solution.py:40
  (1 shorter events, 0.0 us)
Async XLA Ops:
  1.5 19.0 %slice-start = ((s8[6291456]{0:T(1024)(128)(4,1)}), s8[4194304]{0:T(1024)(128)(4,1)S(1)}, s32[]{:S(2)}) async-start(s8[6291456]{0:T(1024)(128)(4,1)} %bitcast.51), calls=%async_computation | async-start | bytes 8388608
  1.5 4.7 %copy-start = (f32[1024,256]{1,0:T(8,128)S(1)}, f32[1024,256]{1,0:T(8,128)}, u32[]{:S(2)}) copy-start(f32[1024,256]{1,0:T(8,128)} %param.8) | copy-start | bytes 3145732
  1.5 4.7 %copy-start.2 = (f32[512,256]{1,0:T(8,128)S(1)}, f32[512,256]{1,0:T(8,128)}, u32[]{:S(2)}) copy-start(f32[512,256]{1,0:T(8,128)} %param.6) | copy-start | bytes 1572868
  1.5 4.7 %copy-start.3 = (f32[512,256]{1,0:T(8,128)S(1)}, f32[512,256]{1,0:T(8,128)}, u32[]{:S(2)}) copy-start(f32[512,256]{1,0:T(8,128)} %param.7) | copy-start | bytes 1572868
  1.5 18.9 %slice-start.1 = ((s8[6291456]{0:T(1024)(128)(4,1)}), s8[2097152]{0:T(1024)(128)(4,1)S(1)}, s32[]{:S(2)}) async-start(s8[6291456]{0:T(1024)(128)(4,1)} %bitcast.51), calls=%async_computation.1 | async-start | bytes 4194304
  8.1 12.4 %copy-start.1 = (f32[1024,256]{1,0:T(8,128)S(1)}, f32[1024,256]{1,0:T(8,128)}, u32[]{:S(2)}) copy-start(f32[1024,256]{1,0:T(8,128)} %param.9) | copy-start | bytes 3145732
  8.1 12.4 %collective-permute-start = (f32[512,256]{1,0:T(8,128)S(1)}, f32[512,256]{1,0:T(8,128)S(1)}, u32[]{:S(2)}, u32[]{:S(2)}) collective-permute-start(f32[512,256]{1,0:T(8,128)S(1)} %get-tuple-element.8), channel_id=1, source_target_pairs={{0,1},{1,2},{2,3},{3,4},{4,5},{5,6},{6,7},{7,8},{8,9},{9,10},{10,1... | collective-permute-start | bytes 1572872 | tf_op jit(solution)/shard_map/ppermute | solution.py:10
  8.6 17.5 %collective-permute-start.1 = (f32[512,256]{1,0:T(8,128)S(1)}, f32[512,256]{1,0:T(8,128)S(1)}, u32[]{:S(2)}, u32[]{:S(2)}) collective-permute-start(f32[512,256]{1,0:T(8,128)S(1)} %get-tuple-element.9), channel_id=1, source_target_pairs={{0,1},{1,2},{2,3},{3,4},{4,5},{5,6},{6,7},{7,8},{8,9},{9,10},{10,1... | collective-permute-start | bytes 1572872 | tf_op jit(solution)/shard_map/ppermute | solution.py:10
  28.1 11.4 %collective-permute-start.2 = (f32[512,256]{1,0:T(8,128)S(1)}, f32[512,256]{1,0:T(8,128)S(1)}, u32[]{:S(2)}, u32[]{:S(2)}) collective-permute-start(f32[512,256]{1,0:T(8,128)S(1)} %get-tuple-element.6), channel_id=1, source_target_pairs={{0,1},{1,2},{2,3},{3,4},{4,5},{5,6},{6,7},{7,8},{8,9},{9,10},{10,1... | collective-permute-start | bytes 1572872 | tf_op jit(solution)/shard_map/ppermute | solution.py:10
  28.1 17.0 %collective-permute-start.3 = (f32[512,256]{1,0:T(8,128)S(1)}, f32[512,256]{1,0:T(8,128)S(1)}, u32[]{:S(2)}, u32[]{:S(2)}) collective-permute-start(f32[512,256]{1,0:T(8,128)S(1)} %get-tuple-element.7), channel_id=1, source_target_pairs={{0,1},{1,2},{2,3},{3,4},{4,5},{5,6},{6,7},{7,8},{8,9},{9,10},{10,1... | collective-permute-start | bytes 1572872 | tf_op jit(solution)/shard_map/ppermute | solution.py:10
  45.3 22.2 %collective-permute-start.4 = (f32[2,512,256]{2,1,0:T(8,128)S(1)}, f32[2,512,256]{2,1,0:T(8,128)S(1)}, u32[]{:S(2)}, u32[]{:S(2)}) collective-permute-start(f32[2,512,256]{2,1,0:T(8,128)S(1)} %pad_maximum_fusion), channel_id=1, source_target_pairs={{0,14},{1,15},{2,0},{3,1},{4,2},{5,3},{6,4},{7,5},{8,6},{9,7},{10,... | collective-permute-start | bytes 3145736 | tf_op jit(solution)/shard_map/ppermute | solution.py:10
where the time goes:
time: 68.8 us; the launch traced here: 68.6 us
  waiting for transfers between devices  34.5 us (50%)
  matrix products  27.6 us (40%)
  starting transfers between devices  3.53 us (5%)
  local copies, waits for them, and re-layouts  1.07 us (2%)
  other arithmetic  1.03 us (1%)
  between operations  0.81 us (1%)
    ppermute x5, waiting for transfers between devices, from_behind(): return lax.ppermute(value, axis, pairs)  34.5 us
    dot_general x3, matrix products, local_step(): grad_c = jnp.dot(resid.T, ublk, precision=lax.Precision.HIGHEST)  12.3 us
    dot_general x3, matrix products, local_step(): scores = jnp.dot(ublk, cblk.T, precision=lax.Precision.HIGHEST)  9.61 us
    dot_general x3, matrix products, local_step(): grad_u = jnp.dot(resid, cblk, precision=lax.Precision.HIGHEST)  5.68 us
    ppermute x5, starting transfers between devices, from_behind(): return lax.ppermute(value, axis, pairs)  3.53 us
  transfers between devices with their start and end apart: 5, of which 5 were waited for; matrix products, arithmetic and copies ran while one was open for 28% of the time, Pallas kernels for 0%

commit v1 on v0

v1 whole, which is shorter than its diff:
```python
import jax
import jax.numpy as jnp
from jax import lax
from jax.experimental import pallas as pl
from jax.experimental.pallas import tpu as pltpu
from jax.sharding import PartitionSpec as P

F32 = jnp.float32
BF16 = jnp.bfloat16
RATE = 0.05
VMEM = pl.BlockSpec(memory_space=pltpu.VMEM)
HBM = pl.BlockSpec(memory_space=pltpu.HBM)
ANY = pl.BlockSpec(memory_space=pl.ANY)


def split(x):
    high = x.astype(BF16)
    return high, (x - high.astype(F32)).astype(BF16)


def product(a, b, dim_a, dim_b):
    def one(x, y):
        return lax.dot_general(
            x, y, (((dim_a,), (dim_b,)), ((), ())), preferred_element_type=F32
        )

    return one(a[0], b[0]) + (one(a[1], b[0]) + one(a[0], b[1]))


def block_of(size, most):
    return most if size % most == 0 else size


def is_odd():
    return lax.rem(lax.axis_index("inner"), 2) == 1


def adagrad(value, moment, grad):
    moment = moment + grad * grad
    return value - RATE * grad * lax.rsqrt(moment), moment


def vertex_pass(u, c, e, w, r_high, r_low, emit):
    cs = split(c[...])
    wf = w.astype(F32)
    rows = block_of(u.shape[0], 256)
    for i in range(u.shape[0] // rows):
        at = pl.ds(i * rows, rows)
        half_scores = product(split(0.5 * u[at, :]), cs, 1, 1)
        ef = e(i, rows).astype(F32)
        resid = split((ef + wf) * jnp.tanh(half_scores) + (wf - ef))
        r_high[at, :] = resid[0]
        r_low[at, :] = resid[1]
        emit(at, 0.5 * product(resid, cs, 1, 0))


def context_pass(u, c, h, r_high, r_low, c_out, h_out):
    us = split(0.5 * u[...])
    rows = block_of(c.shape[0], 256)
    for j in range(c.shape[0] // rows):
        at = pl.ds(j * rows, rows)
        grad = product((r_high[:, at], r_low[:, at]), us, 0, 0)
        c_out[at, :], h_out[at, :] = adagrad(c[at, :], h[at, :], grad)


def call(body, in_specs, outs, scratch, args, name):
    return pl.pallas_call(
        body,
        out_shape=outs,
        in_specs=in_specs,
        out_specs=[VMEM] * len(outs),
        scratch_shapes=scratch,
        compiler_params=pltpu.CompilerParams(vmem_limit_bytes=24 << 20),
        name=name,
    )(*args)


def load(pairs, sems):
    copies = [pltpu.make_async_copy(a, b, sems.at[i]) for i, (a, b) in enumerate(pairs)]
    for copy in copies:
        copy.start()
    return copies


def first_odd(u, g, c, e, w, s1, r_high, r_low, ub, gb, cb, eb, sems):
    nrows = ub.shape[0]
    rows = block_of(nrows, 256)
    count = nrows // rows

    @pl.when(is_odd())
    def _():
        copies = load(
            [(u, ub), (c, cb)]
            + [(e.at[0, pl.ds(i * rows, rows)], eb.at[pl.ds(i * rows, rows)]) for i in range(count)]
            + [(g, gb)],
            sems,
        )
        copies[0].wait()
        copies[1].wait()

        def edges(i, rows):
            copies[2 + i].wait()
            if i == count - 1:
                copies[-1].wait()
            return eb[pl.ds(i * rows, rows), :]

        grads = []
        vertex_pass(ub, cb, edges, w[0:1, :], r_high, r_low, lambda at, grad: grads.append((at, grad)))
        for at, grad in grads:
            s1[0, at, :], s1[1, at, :] = adagrad(ub[at, :], gb[at, :], grad)


def first_rest(u, g, c, h, e, w, r_high_in, r_low_in, s1, c_out, h_out, ub, gb, cb, hb, eb, r_high, r_low, sems):
    odd = is_odd()
    load_context = [(u, ub), (c, cb), (h, hb)]

    @pl.when(odd)
    def _():
        for copy in load(load_context, sems):
            copy.wait()
        context_pass(ub, cb, hb, r_high_in, r_low_in, c_out, h_out)

    @pl.when(jnp.logical_not(odd))
    def _():
        for copy in load(load_context + [(g, gb), (e.at[0], eb)], sems):
            copy.wait()

        def emit(at, grad):
            s1[0, at, :], s1[1, at, :] = adagrad(ub[at, :], gb[at, :], grad)

        vertex_pass(ub, cb, lambda i, rows: eb[pl.ds(i * rows, rows), :], w[0:1, :], r_high, r_low, emit)
        context_pass(ub, cb, hb, r_high, r_low, c_out, h_out)


def second_odd(s1, c, h, e, w, u2, s2, c_out, h_out, r_high, r_low):
    @pl.when(is_odd())
    def _():
        def emit(at, grad):
            value, moment = adagrad(s1[0, at, :], s1[1, at, :], grad)
            u2[at, :] = value
            s2[0, at, :] = value
            s2[1, at, :] = moment

        vertex_pass(s1.at[0], c, lambda i, rows: e[pl.ds(i * rows, rows), :], w[1:2, :], r_high, r_low, emit)
        context_pass(s1.at[0], c, h, r_high, r_low, c_out, h_out)


def second_even(s1, c, h, e, w, after, g1, u2, c_out, h_out, r_high, r_low):
    @pl.when(jnp.logical_not(is_odd()))
    def _():
        def emit(at, grad):
            g1[at, :] = grad
            u2[at, :] = adagrad(s1[0, at, :], s1[1, at, :], grad)[0]

        vertex_pass(s1.at[0], c, lambda i, rows: e[pl.ds(i * rows, rows), :], w[1:2, :], r_high, r_low, emit)
        context_pass(s1.at[0], c, h, r_high, r_low, c_out, h_out)


def third(odd, u, c, e, w, after, g2, r_high, r_low):
    @pl.when(is_odd() == odd)
    def _():
        def emit(at, grad):
            g2[at, :] = grad

        vertex_pass(u, c, lambda i, rows: e[pl.ds(i * rows, rows), :], w[2:3, :], r_high, r_low, emit)


def third_odd(*refs):
    third(True, *refs)


def third_even(*refs):
    third(False, *refs)


def third_context(u_odd, c_odd, h_odd, rh_odd, rl_odd, u_even, c_even, h_even, rh_even, rl_even, c_out, h_out):
    odd = is_odd()

    @pl.when(odd)
    def _():
        context_pass(u_odd, c_odd, h_odd, rh_odd, rl_odd, c_out, h_out)

    @pl.when(jnp.logical_not(odd))
    def _():
        context_pass(u_even, c_even, h_even, rh_even, rl_even, c_out, h_out)


def last(s1, g1, g2_odd, s2, g2_even, u_out, g_out):
    odd = is_odd()

    @pl.when(odd)
    def _():
        value, moment = adagrad(s1[0], s1[1], g1[...])
        u_out[...], g_out[...] = adagrad(value, moment, g2_odd[...])

    @pl.when(jnp.logical_not(odd))
    def _():
        u_out[...], g_out[...] = adagrad(s2[0], s2[1], g2_even[...])


def per_device(vertices, vertex_moments, contexts, context_moments, edge_counts, negative_weights):
    nrows, width = vertices.shape
    ncols = contexts.shape[0]
    count = lax.axis_size("inner")
    assert count % 2 == 0 and edge_counts.shape[0] == 3

    ring = [(i, (i + 1) % count) for i in range(count)]
    unring = [(b, a) for a, b in ring]
    swap = [(i, i ^ 1) for i in range(count)]
    home_odd = [(i, (i - 2) % count if i % 2 else i) for i in range(count)]
    home_even = [(i, i if i % 2 else (i - 2) % count) for i in range(count)]

    def move(value, pairs):
        return lax.ppermute(value, "inner", pairs)

    def f32(*shape):
        return jax.ShapeDtypeStruct(shape, F32)

    block = f32(nrows, width)
    pair = f32(2, nrows, width)
    ctx = f32(ncols, width)
    half = jax.ShapeDtypeStruct((nrows, ncols), BF16)
    half_buf = pltpu.VMEM((nrows, ncols), BF16)
    vert_buf = pltpu.VMEM((nrows, width), F32)
    ctx_buf = pltpu.VMEM((ncols, width), F32)
    edge_buf = pltpu.VMEM((nrows, ncols), jnp.int32)
    sems = pltpu.SemaphoreType.DMA((3 + max(2, nrows // block_of(nrows, 256)),))

    s1o, rh0, rl0 = call(
        first_odd, [HBM] * 4 + [VMEM], [pair, half, half],
        [vert_buf, vert_buf, ctx_buf, edge_buf, sems],
        (vertices, vertex_moments, contexts, edge_counts, negative_weights), "first_odd",
    )
    s1x = move(s1o, ring)
    s1, c1, h1 = call(
        first_rest, [HBM] * 5 + [VMEM] * 3, [pair, ctx, ctx],
        [vert_buf, vert_buf, ctx_buf, ctx_buf, edge_buf, half_buf, half_buf, sems],
        (vertices, vertex_moments, contexts, context_moments, edge_counts, negative_weights, rh0, rl0), "first_rest",
    )
    s1i = move(s1, swap)
    u2e, s2e, c2o, h2o = call(
        second_odd, [VMEM] * 5, [block, pair, ctx, ctx], [half_buf, half_buf],
        (s1i, c1, h1, edge_counts[1], negative_weights), "second_odd",
    )
    u2x = move(u2e, ring)
    s2h = move(s2e, swap)
    g1, u2b, c2e, h2e = call(
        second_even, [VMEM] * 5 + [ANY], [block, block, ctx, ctx], [half_buf, half_buf],
        (s1x, c1, h1, edge_counts[1], negative_weights, u2e), "second_even",
    )
    g1x = move(g1, unring)
    u2i = move(u2b, swap)
    g2o, rho, rlo = call(
        third_odd, [VMEM] * 4 + [ANY], [block, half, half], [],
        (u2i, c2o, edge_counts[2], negative_weights, u2b), "third_odd",
    )
    g2xo = move(g2o, home_odd)
    g2e, rhe, rle = call(
        third_even, [VMEM] * 4 + [ANY], [block, half, half], [],
        (u2x, c2e, edge_counts[2], negative_weights, g2o), "third_even",
    )
    g2xe = move(g2e, home_even)
    c3, h3 = call(
        third_context, [VMEM] * 10, [ctx, ctx], [],
        (u2i, c2o, h2o, rho, rlo, u2x, c2e, h2e, rhe, rle), "third_context",
    )
    u3, g3 = call(last, [VMEM] * 5, [block, block], [], (s1o, g1x, g2xo, s2h, g2xe), "last")
    return u3, g3, c3, h3


def solution(mesh):
    split_rows = P(("snap", "inner"), None)
    return jax.shard_map(
        per_device,
        mesh=mesh,
        in_specs=(
            split_rows,
            split_rows,
            split_rows,
            split_rows,
            P(None, None, ("snap", "inner")),
            P(None, ("snap", "inner")),
        ),
        out_specs=(split_rows,) * 4,
        check_vma=False,
    )
```

time: 68.8 us -> 63.6 us (0.924)
  matrix products: 27.6 us -> 0 us
  Pallas kernels: 0 us -> 12.3 us
  local copies, waits for them, and re-layouts: 1.07 us -> 8.28 us
  starting transfers between devices: 3.53 us -> 8.19 us
  other arithmetic: 1.03 us -> 0 us
  waiting for transfers between devices: 34.5 us -> 33.7 us
    dot_general x9 -> x0, matrix products: 27.6 us -> none  [the longest x3 12.3 us: local_step(): grad_c = jnp.dot(resid.T, ublk, precision=lax.Precision.HIGHEST)]
    pallas_call x0 -> x8, Pallas kernels: none -> 12.3 us  [call(): pl.pallas_call(body, out_shape=outs, in_specs=in_specs, out_specs=[VMEM]...]
    unnamed x12, local copies, waits for them, and re-layouts: 0.04 us -> 7.97 us
    ppermute x5 -> x8, starting transfers between devices: 3.53 us -> 8.19 us  [move(): return lax.ppermute(value, 'inner', pairs)]
    convert_element_type x1 -> x0, other arithmetic: 0.84 us -> none  [local_step(): negs.astype(jnp.float32)[None, :]]
    ppermute x5 -> x8, waiting for transfers between devices: 34.5 us -> 33.7 us  [move(): return lax.ppermute(value, 'inner', pairs)]
    squeeze x1, local copies, waits for them, and re-layouts: 1.03 us -> 0.31 us  [per_device(): edge_counts[2]]
  transfers between devices with their start and end apart: 5 -> 8, of which waited for: 5 -> 4; matrix products, arithmetic and copies ran while one was open for 28% -> 0% of each run, Pallas kernels for 0% -> 8%
where the time goes in v1:
time: 63.6 us; the launch traced here: 63.2 us
  waiting for transfers between devices  33.7 us (53%)
  Pallas kernels  12.3 us (19%)
  local copies, waits for them, and re-layouts  8.28 us (13%)
  starting transfers between devices  8.19 us (13%)
  between operations  0.72 us (1%)
    ppermute x8, waiting for transfers between devices, move(): return lax.ppermute(value, 'inner', pairs)  33.7 us
    pallas_call x8, Pallas kernels, call(): pl.pallas_call(body, out_shape=outs, in_specs=in_specs, out_specs=[VMEM]...  12.3 us
    ppermute x8, starting transfers between devices, move(): return lax.ppermute(value, 'inner', pairs)  8.19 us
    unnamed x12, local copies, waits for them, and re-layouts  7.97 us
  transfers between devices with their start and end apart: 8, of which 4 were waited for; matrix products, arithmetic and copies ran while one was open for 0% of the time, Pallas kernels for 8%

profile of v1, /device:TPU:0, one launch (start us, length us, event | category | flops | bytes accessed | tf_op | source)
XLA Modules:
  0.0 63.2 jit_solution(1121196992682939727)
XLA Ops:
  0.6 0.0 copy-start
  0.6 2.8 %copy-done = s32[3,512,1024]{2,1,0:T(8,128)S(1)} copy-done((s32[3,512,1024]{2,1,0:T(8,128)S(1)}, s32[3,512,1024]{2,1,0:T(8,128)}, u32[]{:S(2)}) %copy-start) | copy-done | bytes 6291480
  3.4 0.0 copy-start.1
  3.4 1.2 %copy-done.1 = f32[1024,256]{1,0:T(8,128)S(1)} copy-done((f32[1024,256]{1,0:T(8,128)S(1)}, f32[1024,256]{1,0:T(8,128)}, u32[]{:S(2)}) %copy-start.1) | copy-done | bytes 1048600
  4.6 0.0 copy-start.2
  4.6 1.0 %copy-done.2 = f32[512,256]{1,0:T(8,128)S(1)} copy-done((f32[512,256]{1,0:T(8,128)S(1)}, f32[512,256]{1,0:T(8,128)}, u32[]{:S(2)}) %copy-start.2) | copy-done | bytes 524312
  5.7 0.0 copy-start.3
  5.7 1.0 %copy-done.3 = f32[512,256]{1,0:T(8,128)S(1)} copy-done((f32[512,256]{1,0:T(8,128)S(1)}, f32[512,256]{1,0:T(8,128)}, u32[]{:S(2)}) %copy-start.3) | copy-done | bytes 524312
  6.7 0.0 copy-start.5
  6.7 0.7 %copy-done.5 = s32[3,1024]{1,0:T(4,128)S(1)} copy-done((s32[3,1024]{1,0:T(4,128)S(1)}, s32[3,1024]{1,0:T(4,128)}, u32[]{:S(2)}) %copy-start.5) | copy-done | bytes 12312
  7.4 0.0 copy-start.4
  7.5 1.2 %copy-done.4 = f32[1024,256]{1,0:T(8,128)S(1)} copy-done((f32[1024,256]{1,0:T(8,128)S(1)}, f32[1024,256]{1,0:T(8,128)}, u32[]{:S(2)}) %copy-start.4) | copy-done | bytes 1048600
  8.7 3.2 %first_rest.1 = (f32[2,512,256]{2,1,0:T(8,128)S(1)}, f32[1024,256]{1,0:T(8,128)S(1)}, f32[1024,256]{1,0:T(8,128)S(1)}) custom-call(f32[512,256]{1,0:T(8,128)S(1)} %copy-done.2, f32[512,256]{1,0:T(8,128)S(1)} %copy-done.3, f32[1024,256]{1,0:T(8,128)S(1)} %copy-done.1, f32[1024,256]{1,0:T(8,128)S(1)} %copy-done.4, s32[3,512,1024]{2,1,0:T(8,128)S(1)} %copy-done, ...), custom_call_target="tpu_custom_call" | custom-call | tf_op jit(solution)/shard_map/first_rest/pallas_call | solution.py:67
  11.9 0.9 %collective-permute-start.1 = (f32[2,512,256]{2,1,0:T(8,128)S(1)}, f32[2,512,256]{2,1,0:T(8,128)S(1)}, u32[]{:S(2)}, u32[]{:S(2)}) collective-permute-start(f32[2,512,256]{2,1,0:T(8,128)S(1)} %get-tuple-element.33), channel_id=1, source_target_pairs={{0,1},{1,0},{2,3},{3,2},{4,5},{5,4},{6,7},{7,6},{8,9},{9,8},{10,11... | collective-permute-start | bytes 3145736 | tf_op jit(solution)/shard_map/ppermute | solution.py:214
  12.8 0.1 collective-permute-start
  12.9 0.3 slice_bitcast_fusion
  13.2 1.9 %collective-permute-done.1.s1 = f32[2,512,256]{2,1,0:T(8,128)S(1)} collective-permute-done((f32[2,512,256]{2,1,0:T(8,128)S(1)}, f32[2,512,256]{2,1,0:T(8,128)S(1)}, u32[]{:S(2)}, u32[]{:S(2)}) %collective-permute-start.1) | collective-permute-done | bytes 1048608 | tf_op jit(solution)/shard_map/ppermute | solution.py:214
  15.1 15.4 %collective-permute-done.s1 = f32[2,512,256]{2,1,0:T(8,128)S(1)} collective-permute-done((f32[2,512,256]{2,1,0:T(8,128)S(1)}, f32[2,512,256]{2,1,0:T(8,128)S(1)}, u32[]{:S(2)}, u32[]{:S(2)}) %collective-permute-start) | collective-permute-done | bytes 1048608 | tf_op jit(solution)/shard_map/ppermute | solution.py:214
  30.5 2.8 %second_even.1 = (f32[512,256]{1,0:T(8,128)S(1)}, f32[512,256]{1,0:T(8,128)S(1)}, f32[1024,256]{1,0:T(8,128)S(1)}, f32[1024,256]{1,0:T(8,128)S(1)}) custom-call(f32[2,512,256]{2,1,0:T(8,128)S(1)} %collective-permute-done.s1, f32[1024,256]{1,0:T(8,128)S(1)} %get-tuple-element.31.c, f32[1024,256]{1,0:T(8,128)S(1)} %get-tuple-element.32.h, ...), custom_call_target="tpu_custom_call" | custom-call | tf_op jit(solution)/shard_map/second_even/pallas_call | solution.py:67
  33.4 0.1 collective-permute-start.3
  33.4 0.5 collective-permute-start.6
  33.9 0.0 collective-permute-start.5
  33.9 4.0 %collective-permute-start.2 = (f32[512,256]{1,0:T(8,128)S(1)}, f32[512,256]{1,0:T(8,128)S(1)}, u32[]{:S(2)}, u32[]{:S(2)}) collective-permute-start(f32[512,256]{1,0:T(8,128)S(1)} %get-tuple-element.35), channel_id=1, source_target_pairs={{1,0},{2,1},{3,2},{4,3},{5,4},{6,5},{7,6},{8,7},{9,8},{10,9},{11,1... | collective-permute-start | bytes 1572872 | tf_op jit(solution)/shard_map/ppermute | solution.py:214
  37.9 0.0 collective-permute-done.3.refs_0_.u_odd
  37.9 7.0 %collective-permute-done.6.refs_0_.u_even = f32[512,256]{1,0:T(8,128)S(1)} collective-permute-done((f32[512,256]{1,0:T(8,128)S(1)}, f32[512,256]{1,0:T(8,128)S(1)}, u32[]{:S(2)}, u32[]{:S(2)}) %collective-permute-start.6) | collective-permute-done | bytes 524320 | tf_op jit(solution)/shard_map/ppermute | solution.py:214
  44.9 2.6 %third_even.1 = (f32[512,256]{1,0:T(8,128)S(1)}, bf16[512,1024]{1,0:T(8,128)(2,1)S(1)}, bf16[512,1024]{1,0:T(8,128)(2,1)S(1)}) custom-call(f32[512,256]{1,0:T(8,128)S(1)} %collective-permute-done.6.refs_0_.u_even, f32[1024,256]{1,0:T(8,128)S(1)} %get-tuple-element.40.refs_1_.c_even, s32[512,1024]{1,0:T(8,128)S(1)} %get-tuple-element.52.refs_2_, ...), custom_call_target="tpu_custom_call" | custom-call | tf_op jit(solution)/shard_map/third_even/pallas_call | solution.py:67
  47.5 1.9 %collective-permute-start.7 = (f32[512,256]{1,0:T(8,128)S(1)}, f32[512,256]{1,0:T(8,128)S(1)}, u32[]{:S(2)}, u32[]{:S(2)}) collective-permute-start(f32[512,256]{1,0:T(8,128)S(1)} %get-tuple-element.41), channel_id=1, source_target_pairs={{0,14},{1,1},{2,0},{3,3},{4,2},{5,5},{6,4},{7,7},{8,6},{9,9},{10,8... | collective-permute-start | bytes 1572872 | tf_op jit(solution)/shard_map/ppermute | solution.py:214
  49.4 0.7 %collective-permute-start.4 = (f32[512,256]{1,0:T(8,128)S(1)}, f32[512,256]{1,0:T(8,128)S(1)}, u32[]{:S(2)}, u32[]{:S(2)}) collective-permute-start(f32[512,256]{1,0:T(8,128)S(1)} %get-tuple-element.38.refs_4_), channel_id=1, source_target_pairs={{0,0},{1,15},{2,2},{3,1},{4,4},{5,3},{6,6},{7,5},{8,8},{9,7},{10,1... | collective-permute-start | bytes 1572872 | tf_op jit(solution)/shard_map/ppermute | solution.py:214
  50.1 2.5 %third_context.1 = (f32[1024,256]{1,0:T(8,128)}, f32[1024,256]{1,0:T(8,128)}) custom-call(f32[512,256]{1,0:T(8,128)S(1)} %collective-permute-done.3.refs_0_.u_odd, f32[1024,256]{1,0:T(8,128)S(1)} %get-tuple-element.37.refs_1_.c_odd, f32[1024,256]{1,0:T(8,128)S(1)} %get-tuple-element.44.h_odd, bf16[512,1024]{1,0:T(8,128)(2,1)S(1)} %get-tuple-element.45.rh_odd, ...), custom_call_target="tpu_custom_call" | custom-call | tf_op jit(solution)/shard_map/third_context/pallas_call | solution.py:67
  52.7 0.0 collective-permute-done.2.g1
  52.7 0.0 collective-permute-done.5.s2
  52.7 9.4 %collective-permute-done.7.g2_even = f32[512,256]{1,0:T(8,128)S(1)} collective-permute-done((f32[512,256]{1,0:T(8,128)S(1)}, f32[512,256]{1,0:T(8,128)S(1)}, u32[]{:S(2)}, u32[]{:S(2)}) %collective-permute-start.7) | collective-permute-done | bytes 524320 | tf_op jit(solution)/shard_map/ppermute | solution.py:214
  62.1 0.0 collective-permute-done.4.g2_odd
  62.1 1.1 %last.1 = (f32[512,256]{1,0:T(8,128)}, f32[512,256]{1,0:T(8,128)}) custom-call(f32[2,512,256]{2,1,0:T(8,128)S(1)} %get-tuple-element.28.s1, f32[512,256]{1,0:T(8,128)S(1)} %collective-permute-done.2.g1, f32[512,256]{1,0:T(8,128)S(1)} %collective-permute-done.4.g2_odd, f32[2,512,256]{2,1,0:T(8,128)S(1)} %collective-permute-done.5.s2, ...), custom_call_target="tpu_custom_call" | custom-call | tf_op jit(solution)/shard_map/last/pallas_call | solution.py:67
  (3 shorter events, 0.0 us)
Async XLA Ops:
  0.6 2.8 %copy-start = (s32[3,512,1024]{2,1,0:T(8,128)S(1)}, s32[3,512,1024]{2,1,0:T(8,128)}, u32[]{:S(2)}) copy-start(s32[3,512,1024]{2,1,0:T(8,128)} %e.3) | copy-start | bytes 18874372
  3.4 1.2 %copy-start.1 = (f32[1024,256]{1,0:T(8,128)S(1)}, f32[1024,256]{1,0:T(8,128)}, u32[]{:S(2)}) copy-start(f32[1024,256]{1,0:T(8,128)} %c.3) | copy-start | bytes 3145732
  4.6 1.0 %copy-start.2 = (f32[512,256]{1,0:T(8,128)S(1)}, f32[512,256]{1,0:T(8,128)}, u32[]{:S(2)}) copy-start(f32[512,256]{1,0:T(8,128)} %u.3) | copy-start | bytes 1572868
  5.7 1.0 %copy-start.3 = (f32[512,256]{1,0:T(8,128)S(1)}, f32[512,256]{1,0:T(8,128)}, u32[]{:S(2)}) copy-start(f32[512,256]{1,0:T(8,128)} %g.3) | copy-start | bytes 1572868
  6.7 0.7 %copy-start.5 = (s32[3,1024]{1,0:T(4,128)S(1)}, s32[3,1024]{1,0:T(4,128)}, u32[]{:S(2)}) copy-start(s32[3,1024]{1,0:T(4,128)} %refs_3_.3) | copy-start | bytes 36868
  7.4 1.2 %copy-start.4 = (f32[1024,256]{1,0:T(8,128)S(1)}, f32[1024,256]{1,0:T(8,128)}, u32[]{:S(2)}) copy-start(f32[1024,256]{1,0:T(8,128)} %h.1) | copy-start | bytes 3145732
  11.9 3.2 %collective-permute-start.1 = (f32[2,512,256]{2,1,0:T(8,128)S(1)}, f32[2,512,256]{2,1,0:T(8,128)S(1)}, u32[]{:S(2)}, u32[]{:S(2)}) collective-permute-start(f32[2,512,256]{2,1,0:T(8,128)S(1)} %get-tuple-element.33), channel_id=1, source_target_pairs={{0,1},{1,0},{2,3},{3,2},{4,5},{5,4},{6,7},{7,6},{8,9},{9,8},{10,11... | collective-permute-start | bytes 3145736 | tf_op jit(solution)/shard_map/ppermute | solution.py:214
  12.8 17.7 %collective-permute-start = (f32[2,512,256]{2,1,0:T(8,128)S(1)}, f32[2,512,256]{2,1,0:T(8,128)S(1)}, u32[]{:S(2)}, u32[]{:S(2)}) collective-permute-start(f32[2,512,256]{2,1,0:T(8,128)S(1)} %get-tuple-element.28.s1), channel_id=1, source_target_pairs={{0,1},{1,2},{2,3},{3,4},{4,5},{5,6},{6,7},{7,8},{8,9},{9,10},{10,1... | collective-permute-start | bytes 3145736 | tf_op jit(solution)/shard_map/ppermute | solution.py:214
  33.4 4.6 %collective-permute-start.3 = (f32[512,256]{1,0:T(8,128)S(1)}, f32[512,256]{1,0:T(8,128)S(1)}, u32[]{:S(2)}, u32[]{:S(2)}) collective-permute-start(f32[512,256]{1,0:T(8,128)S(1)} %get-tuple-element.36.refs_4_), channel_id=1, source_target_pairs={{0,1},{1,0},{2,3},{3,2},{4,5},{5,4},{6,7},{7,6},{8,9},{9,8},{10,11... | collective-permute-start | bytes 1572872 | tf_op jit(solution)/shard_map/ppermute | solution.py:214
  33.4 11.5 %collective-permute-start.6 = (f32[512,256]{1,0:T(8,128)S(1)}, f32[512,256]{1,0:T(8,128)S(1)}, u32[]{:S(2)}, u32[]{:S(2)}) collective-permute-start(f32[512,256]{1,0:T(8,128)S(1)} %get-tuple-element.34.after), channel_id=1, source_target_pairs={{0,1},{1,2},{2,3},{3,4},{4,5},{5,6},{6,7},{7,8},{8,9},{9,10},{10,1... | collective-permute-start | bytes 1572872 | tf_op jit(solution)/shard_map/ppermute | solution.py:214
  33.9 18.7 %collective-permute-start.5 = (f32[2,512,256]{2,1,0:T(8,128)S(1)}, f32[2,512,256]{2,1,0:T(8,128)S(1)}, u32[]{:S(2)}, u32[]{:S(2)}) collective-permute-start(f32[2,512,256]{2,1,0:T(8,128)S(1)} %get-tuple-element.39), channel_id=1, source_target_pairs={{0,1},{1,0},{2,3},{3,2},{4,5},{5,4},{6,7},{7,6},{8,9},{9,8},{10,11... | collective-permute-start | bytes 3145736 | tf_op jit(solution)/shard_map/ppermute | solution.py:214
  33.9 18.7 %collective-permute-start.2 = (f32[512,256]{1,0:T(8,128)S(1)}, f32[512,256]{1,0:T(8,128)S(1)}, u32[]{:S(2)}, u32[]{:S(2)}) collective-permute-start(f32[512,256]{1,0:T(8,128)S(1)} %get-tuple-element.35), channel_id=1, source_target_pairs={{1,0},{2,1},{3,2},{4,3},{5,4},{6,5},{7,6},{8,7},{9,8},{10,9},{11,1... | collective-permute-start | bytes 1572872 | tf_op jit(solution)/shard_map/ppermute | solution.py:214
  47.5 14.6 %collective-permute-start.7 = (f32[512,256]{1,0:T(8,128)S(1)}, f32[512,256]{1,0:T(8,128)S(1)}, u32[]{:S(2)}, u32[]{:S(2)}) collective-permute-start(f32[512,256]{1,0:T(8,128)S(1)} %get-tuple-element.41), channel_id=1, source_target_pairs={{0,14},{1,1},{2,0},{3,3},{4,2},{5,5},{6,4},{7,7},{8,6},{9,9},{10,8... | collective-permute-start | bytes 1572872 | tf_op jit(solution)/shard_map/ppermute | solution.py:214
  49.4 12.7 %collective-permute-start.4 = (f32[512,256]{1,0:T(8,128)S(1)}, f32[512,256]{1,0:T(8,128)S(1)}, u32[]{:S(2)}, u32[]{:S(2)}) collective-permute-start(f32[512,256]{1,0:T(8,128)S(1)} %get-tuple-element.38.refs_4_), channel_id=1, source_target_pairs={{0,0},{1,15},{2,2},{3,1},{4,4},{5,3},{6,6},{7,5},{8,8},{9,7},{10,1... | collective-permute-start | bytes 1572872 | tf_op jit(solution)/shard_map/ppermute | solution.py:214

commit v2 on v1

--- a/solution.py
+++ b/solution.py
@@ -63,14 +63,15 @@
         c_out[at, :], h_out[at, :] = adagrad(c[at, :], h[at, :], grad)
 
 
-def call(body, in_specs, outs, scratch, args, name):
+def call(body, in_specs, outs, scratch, args, name, room=24):
     return pl.pallas_call(
         body,
         out_shape=outs,
         in_specs=in_specs,
         out_specs=[VMEM] * len(outs),
         scratch_shapes=scratch,
-        compiler_params=pltpu.CompilerParams(vmem_limit_bytes=24 << 20),
+        compiler_params=pltpu.CompilerParams(vmem_limit_bytes=room << 20),
+        cost_estimate=pl.CostEstimate(flops=1024, bytes_accessed=1024, transcendentals=0),
         name=name,
     )(*args)
 
@@ -110,7 +111,7 @@
             s1[0, at, :], s1[1, at, :] = adagrad(ub[at, :], gb[at, :], grad)
 
 
-def first_rest(u, g, c, h, e, w, r_high_in, r_low_in, s1, c_out, h_out, ub, gb, cb, hb, eb, r_high, r_low, sems):
+def first_rest(u, g, c, h, e, w, r_high_in, r_low_in, su, sg, c_out, h_out, ub, gb, cb, hb, eb, r_high, r_low, sems):
     odd = is_odd()
     load_context = [(u, ub), (c, cb), (h, hb)]
 
@@ -126,33 +127,35 @@
             copy.wait()
 
         def emit(at, grad):
-            s1[0, at, :], s1[1, at, :] = adagrad(ub[at, :], gb[at, :], grad)
+            su[at, :], sg[at, :] = adagrad(ub[at, :], gb[at, :], grad)
 
         vertex_pass(ub, cb, lambda i, rows: eb[pl.ds(i * rows, rows), :], w[0:1, :], r_high, r_low, emit)
         context_pass(ub, cb, hb, r_high, r_low, c_out, h_out)
 
 
-def second_odd(s1, c, h, e, w, u2, s2, c_out, h_out, r_high, r_low):
+def second_odd(su, sg, c, h, e, w, u2, s2, c_out, h_out, r_high, r_low):
     @pl.when(is_odd())
     def _():
         def emit(at, grad):
-            value, moment = adagrad(s1[0, at, :], s1[1, at, :], grad)
+            value, moment = adagrad(su[at, :], sg[at, :], grad)
             u2[at, :] = value
             s2[0, at, :] = value
             s2[1, at, :] = moment
 
+        vertex_pass(su, c, lambda i, rows: e[pl.ds(i * rows, rows), :], w[1:2, :], r_high, r_low, emit)
+        context_pass(su, c, h, r_high, r_low, c_out, h_out)
+
+
+def second_even(s1, c, h, e, w, after, g1, u2_top, u2_end, c_out, h_out, r_high, r_low):
+    @pl.when(jnp.logical_not(is_odd()))
+    def _():
+        def emit(at, grad):
+            g1[at, :] = grad
+
         vertex_pass(s1.at[0], c, lambda i, rows: e[pl.ds(i * rows, rows), :], w[1:2, :], r_high, r_low, emit)
-        context_pass(s1.at[0], c, h, r_high, r_low, c_out, h_out)
-
-
-def second_even(s1, c, h, e, w, after, g1, u2, c_out, h_out, r_high, r_low):
-    @pl.when(jnp.logical_not(is_odd()))
-    def _():
-        def emit(at, grad):
-            g1[at, :] = grad
-            u2[at, :] = adagrad(s1[0, at, :], s1[1, at, :], grad)[0]
-
-        vertex_pass(s1.at[0], c, lambda i, rows: e[pl.ds(i * rows, rows), :], w[1:2, :], r_high, r_low, emit)
+        middle = u2_top.shape[0]
+        for u2, at in ((u2_top, pl.ds(0, middle)), (u2_end, pl.ds(middle, middle))):
+            u2[...] = adagrad(s1[0, at, :], s1[1, at, :], g1[at, :])[0]
         context_pass(s1.at[0], c, h, r_high, r_low, c_out, h_out)
 
 
@@ -165,8 +168,11 @@
         vertex_pass(u, c, lambda i, rows: e[pl.ds(i * rows, rows), :], w[2:3, :], r_high, r_low, emit)
 
 
-def third_odd(*refs):
-    third(True, *refs)
+def third_odd(u_top, u_end, c, e, w, after, u, *refs):
+    middle = u_top.shape[0]
+    u[:middle, :] = u_top[...]
+    u[middle:, :] = u_end[...]
+    third(True, u, c, e, w, after, *refs)
 
 
 def third_even(*refs):
@@ -226,33 +232,39 @@
     edge_buf = pltpu.VMEM((nrows, ncols), jnp.int32)
     sems = pltpu.SemaphoreType.DMA((3 + max(2, nrows // block_of(nrows, 256)),))
 
+    hbm = [
+        pltpu.with_memory_space_constraint(x, pltpu.HBM)
+        for x in (vertices, vertex_moments, contexts, context_moments, edge_counts)
+    ]
     s1o, rh0, rl0 = call(
         first_odd, [HBM] * 4 + [VMEM], [pair, half, half],
         [vert_buf, vert_buf, ctx_buf, edge_buf, sems],
-        (vertices, vertex_moments, contexts, edge_counts, negative_weights), "first_odd",
+        (*hbm[:3], hbm[4], negative_weights), "first_odd",
     )
     s1x = move(s1o, ring)
-    s1, c1, h1 = call(
-        first_rest, [HBM] * 5 + [VMEM] * 3, [pair, ctx, ctx],
+    su, sg, c1, h1 = call(
+        first_rest, [HBM] * 5 + [VMEM] * 3, [block, block, ctx, ctx],
         [vert_buf, vert_buf, ctx_buf, ctx_buf, edge_buf, half_buf, half_buf, sems],
-        (vertices, vertex_moments, contexts, context_moments, edge_counts, negative_weights, rh0, rl0), "first_rest",
-    )
-    s1i = move(s1, swap)
+        (*hbm, negative_weights, rh0, rl0), "first_rest",
+    )
+    sui = move(su, swap)
+    sgi = move(sg, swap)
     u2e, s2e, c2o, h2o = call(
-        second_odd, [VMEM] * 5, [block, pair, ctx, ctx], [half_buf, half_buf],
-        (s1i, c1, h1, edge_counts[1], negative_weights), "second_odd",
+        second_odd, [VMEM] * 6, [block, pair, ctx, ctx], [half_buf, half_buf],
+        (sui, sgi, c1, h1, edge_counts[1], negative_weights), "second_odd",
     )
     u2x = move(u2e, ring)
     s2h = move(s2e, swap)
-    g1, u2b, c2e, h2e = call(
-        second_even, [VMEM] * 5 + [ANY], [block, block, ctx, ctx], [half_buf, half_buf],
+    g1, u2t, u2d, c2e, h2e = call(
+        second_even, [VMEM] * 5 + [ANY], [block, f32(nrows // 2, width), f32(nrows // 2, width), ctx, ctx], [half_buf, half_buf],
         (s1x, c1, h1, edge_counts[1], negative_weights, u2e), "second_even",
     )
     g1x = move(g1, unring)
-    u2i = move(u2b, swap)
-    g2o, rho, rlo = call(
-        third_odd, [VMEM] * 4 + [ANY], [block, half, half], [],
-        (u2i, c2o, edge_counts[2], negative_weights, u2b), "third_odd",
+    u2ti = move(u2t, swap)
+    u2di = move(u2d, swap)
+    u2i, g2o, rho, rlo = call(
+        third_odd, [VMEM] * 5 + [ANY], [block, block, half, half], [],
+        (u2ti, u2di, c2o, edge_counts[2], negative_weights, u2t), "third_odd",
     )
     g2xo = move(g2o, home_odd)
     g2e, rhe, rle = call(

time: 63.6 us -> 49.2 us (0.77)
  waiting for transfers between devices: 33.7 us -> 20.1 us
  local copies, waits for them, and re-layouts: 8.28 us -> 1.04 us
  starting transfers between devices: 8.19 us -> 12.5 us
  Pallas kernels: 12.3 us -> 14.6 us
    ppermute x8 -> x10, waiting for transfers between devices: 33.7 us -> 20.1 us  [move(): return lax.ppermute(value, 'inner', pairs)]
    unnamed x12 -> x8, local copies, waits for them, and re-layouts: 7.97 us -> 0.73 us
    ppermute x8 -> x10, starting transfers between devices: 8.19 us -> 12.5 us  [move(): return lax.ppermute(value, 'inner', pairs)]
    pallas_call x8, Pallas kernels: 12.3 us -> 14.6 us  [call(): pl.pallas_call(body, out_shape=outs, in_specs=in_specs, out_specs=[VMEM]...]
  transfers between devices with their start and end apart: 8 -> 10, of which waited for: 4 -> 7; matrix products, arithmetic and copies ran while one was open for 0% -> 1% of each run, Pallas kernels for 8% -> 28%
where the time goes in v2:
time: 49.2 us; the launch traced here: 49 us
  waiting for transfers between devices  20.1 us (41%)
  Pallas kernels  14.6 us (30%)
  starting transfers between devices  12.5 us (25%)
  local copies, waits for them, and re-layouts  1.04 us (2%)
  between operations  0.74 us (2%)
    ppermute x10, waiting for transfers between devices, move(): return lax.ppermute(value, 'inner', pairs)  20.1 us
    pallas_call x8, Pallas kernels, call(): pl.pallas_call(body, out_shape=outs, in_specs=in_specs, out_specs=[VMEM]...  14.6 us
    ppermute x10, starting transfers between devices, move(): return lax.ppermute(value, 'inner', pairs)  12.5 us
  transfers between devices with their start and end apart: 10, of which 7 were waited for; matrix products, arithmetic and copies ran while one was open for 1% of the time, Pallas kernels for 28%

profile of v2, /device:TPU:0, one launch (start us, length us, event | category | flops | bytes accessed | tf_op | source)
XLA Modules:
  0.0 49.0 jit_solution(5959651164317550047)
XLA Ops:
  0.6 0.0 copy-start
  0.6 0.7 %copy-done = s32[3,1024]{1,0:T(4,128)S(1)} copy-done((s32[3,1024]{1,0:T(4,128)S(1)}, s32[3,1024]{1,0:T(4,128)}, u32[]{:S(2)}) %copy-start) | copy-done | bytes 12312
  1.4 5.0 %collective-permute-start = (f32[2,512,256]{2,1,0:T(8,128)S(1)}, f32[2,512,256]{2,1,0:T(8,128)S(1)}, u32[]{:S(2)}, u32[]{:S(2)}) collective-permute-start(f32[2,512,256]{2,1,0:T(8,128)S(1)} %get-tuple-element.31.s1), channel_id=1, source_target_pairs={{0,1},{1,2},{2,3},{3,4},{4,5},{5,6},{6,7},{7,8},{8,9},{9,10},{10,1... | collective-permute-start | bytes 3145736 | tf_op jit(solution)/shard_map/ppermute | solution.py:220
  6.4 0.0 slice-start
  6.4 0.0 slice-start.1
  6.4 5.5 %first_rest.1 = (f32[512,256]{1,0:T(8,128)S(1)}, f32[512,256]{1,0:T(8,128)S(1)}, f32[1024,256]{1,0:T(8,128)S(1)}, f32[1024,256]{1,0:T(8,128)S(1)}) custom-call(f32[512,256]{1,0:T(8,128)} %u.3, f32[512,256]{1,0:T(8,128)} %g.3, f32[1024,256]{1,0:T(8,128)} %c.3, f32[1024,256]{1,0:T(8,128)} %h.1, s32[3,512,1024]{2,1,0:T(8,128)} %e.3, s32[3,1024]{1,0:T(4,128)S(1)} %copy-done, ...), custom_call_target="tpu_custom_call" | custom-call | flops 1024 | bytes 1024 | tf_op jit(solution)/shard_map/first_rest/pallas_call | solution.py:67
  11.9 0.1 collective-permute-start.1
  12.0 0.0 copy-start.1
  12.0 0.5 collective-permute-start.2
  12.5 0.0 slice-done
  12.5 0.0 slice-done.1
  12.5 0.3 slice_bitcast_fusion
  12.8 1.1 %collective-permute-done.1.su = f32[512,256]{1,0:T(8,128)S(1)} collective-permute-done((f32[512,256]{1,0:T(8,128)S(1)}, f32[512,256]{1,0:T(8,128)S(1)}, u32[]{:S(2)}, u32[]{:S(2)}) %collective-permute-start.1) | collective-permute-done | bytes 524320 | tf_op jit(solution)/shard_map/ppermute | solution.py:220
  13.9 0.7 %collective-permute-done.2.sg = f32[512,256]{1,0:T(8,128)S(1)} collective-permute-done((f32[512,256]{1,0:T(8,128)S(1)}, f32[512,256]{1,0:T(8,128)S(1)}, u32[]{:S(2)}, u32[]{:S(2)}) %collective-permute-start.2) | collective-permute-done | bytes 524320 | tf_op jit(solution)/shard_map/ppermute | solution.py:220
  14.6 0.0 copy-done.1
  14.6 3.0 %collective-permute-start.8 = (f32[512,256]{1,0:T(8,128)S(1)}, f32[512,256]{1,0:T(8,128)S(1)}, u32[]{:S(2)}, u32[]{:S(2)}) collective-permute-start(f32[512,256]{1,0:T(8,128)S(1)} %get-tuple-element.38.after), channel_id=1, source_target_pairs={{0,1},{1,2},{2,3},{3,4},{4,5},{5,6},{6,7},{7,8},{8,9},{9,10},{10,1... | collective-permute-start | bytes 1572872 | tf_op jit(solution)/shard_map/ppermute | solution.py:220
  17.6 0.1 collective-permute-start.7
  17.7 6.1 %collective-permute-done.s1 = f32[2,512,256]{2,1,0:T(8,128)S(1)} collective-permute-done((f32[2,512,256]{2,1,0:T(8,128)S(1)}, f32[2,512,256]{2,1,0:T(8,128)S(1)}, u32[]{:S(2)}, u32[]{:S(2)}) %collective-permute-start) | collective-permute-done | bytes 1048608 | tf_op jit(solution)/shard_map/ppermute | solution.py:220
  23.8 2.8 %second_even.1 = (f32[512,256]{1,0:T(8,128)S(1)}, f32[256,256]{1,0:T(8,128)S(1)}, f32[256,256]{1,0:T(8,128)S(1)}, f32[1024,256]{1,0:T(8,128)S(1)}, f32[1024,256]{1,0:T(8,128)S(1)}) custom-call(f32[2,512,256]{2,1,0:T(8,128)S(1)} %collective-permute-done.s1, f32[1024,256]{1,0:T(8,128)S(1)} %get-tuple-element.34.c, f32[1024,256]{1,0:T(8,128)S(1)} %get-tuple-element.35.h, ...), custom_call_target="tpu_custom_call" | custom-call | flops 1024 | bytes 1024 | tf_op jit(solution)/shard_map/second_even/pallas_call | solution.py:67
  26.7 0.1 collective-permute-start.5
  26.7 0.5 %collective-permute-start.4 = (f32[256,256]{1,0:T(8,128)S(1)}, f32[256,256]{1,0:T(8,128)S(1)}, u32[]{:S(2)}, u32[]{:S(2)}) collective-permute-start(f32[256,256]{1,0:T(8,128)S(1)} %get-tuple-element.40.after), channel_id=1, source_target_pairs={{0,1},{1,0},{2,3},{3,2},{4,5},{5,4},{6,7},{7,6},{8,9},{9,8},{10,11... | collective-permute-start | bytes 786440 | tf_op jit(solution)/shard_map/ppermute | solution.py:220
  27.2 0.2 collective-permute-start.3
  27.4 0.8 %collective-permute-done.5.u_end = f32[256,256]{1,0:T(8,128)S(1)} collective-permute-done((f32[256,256]{1,0:T(8,128)S(1)}, f32[256,256]{1,0:T(8,128)S(1)}, u32[]{:S(2)}, u32[]{:S(2)}) %collective-permute-start.5) | collective-permute-done | bytes 262176 | tf_op jit(solution)/shard_map/ppermute | solution.py:220
  28.3 0.4 collective-permute-done.4.u_top
  28.7 0.8 %collective-permute-done.8.refs_0_.u_even = f32[512,256]{1,0:T(8,128)S(1)} collective-permute-done((f32[512,256]{1,0:T(8,128)S(1)}, f32[512,256]{1,0:T(8,128)S(1)}, u32[]{:S(2)}, u32[]{:S(2)}) %collective-permute-start.8) | collective-permute-done | bytes 524320 | tf_op jit(solution)/shard_map/ppermute | solution.py:220
  29.5 2.6 %third_even.1 = (f32[512,256]{1,0:T(8,128)S(1)}, bf16[512,1024]{1,0:T(8,128)(2,1)S(1)}, bf16[512,1024]{1,0:T(8,128)(2,1)S(1)}) custom-call(f32[512,256]{1,0:T(8,128)S(1)} %collective-permute-done.8.refs_0_.u_even, f32[1024,256]{1,0:T(8,128)S(1)} %get-tuple-element.45.refs_1_.c_even, s32[512,1024]{1,0:T(8,128)S(1)} %get-tuple-element.58.e.refs_2_, ...), custom_call_target="tpu_custom_call" | custom-call | flops 1024 | bytes 1024 | tf_op jit(solution)/shard_map/third_even/pallas_call | solution.py:67
  32.1 2.4 %collective-permute-start.9 = (f32[512,256]{1,0:T(8,128)S(1)}, f32[512,256]{1,0:T(8,128)S(1)}, u32[]{:S(2)}, u32[]{:S(2)}) collective-permute-start(f32[512,256]{1,0:T(8,128)S(1)} %get-tuple-element.46), channel_id=1, source_target_pairs={{0,14},{1,1},{2,0},{3,3},{4,2},{5,5},{6,4},{7,7},{8,6},{9,9},{10,8... | collective-permute-start | bytes 1572872 | tf_op jit(solution)/shard_map/ppermute | solution.py:220
  34.5 0.7 %collective-permute-start.6 = (f32[512,256]{1,0:T(8,128)S(1)}, f32[512,256]{1,0:T(8,128)S(1)}, u32[]{:S(2)}, u32[]{:S(2)}) collective-permute-start(f32[512,256]{1,0:T(8,128)S(1)} %get-tuple-element.43.refs_4_), channel_id=1, source_target_pairs={{0,0},{1,15},{2,2},{3,1},{4,4},{5,3},{6,6},{7,5},{8,8},{9,7},{10,1... | collective-permute-start | bytes 1572872 | tf_op jit(solution)/shard_map/ppermute | solution.py:220
  35.2 2.5 %third_context.1 = (f32[1024,256]{1,0:T(8,128)}, f32[1024,256]{1,0:T(8,128)}) custom-call(f32[512,256]{1,0:T(8,128)S(1)} %get-tuple-element.49.u_odd, f32[1024,256]{1,0:T(8,128)S(1)} %get-tuple-element.42.c.c_odd, f32[1024,256]{1,0:T(8,128)S(1)} %get-tuple-element.50.h_odd, bf16[512,1024]{1,0:T(8,128)(2,1)S(1)} %get-tuple-element.51.rh_odd, ...), custom_call_target="tpu_custom_call" | custom-call | flops 1024 | bytes 1024 | tf_op jit(solution)/shard_map/third_context/pallas_call | solution.py:67
  37.8 0.0 collective-permute-done.3.g1
  37.8 0.0 collective-permute-done.7.s2
  37.8 10.1 %collective-permute-done.9.g2_even = f32[512,256]{1,0:T(8,128)S(1)} collective-permute-done((f32[512,256]{1,0:T(8,128)S(1)}, f32[512,256]{1,0:T(8,128)S(1)}, u32[]{:S(2)}, u32[]{:S(2)}) %collective-permute-start.9) | collective-permute-done | bytes 524320 | tf_op jit(solution)/shard_map/ppermute | solution.py:220
  47.9 0.0 collective-permute-done.6.g2_odd
  47.9 1.1 %last.1 = (f32[512,256]{1,0:T(8,128)}, f32[512,256]{1,0:T(8,128)}) custom-call(f32[2,512,256]{2,1,0:T(8,128)S(1)} %get-tuple-element.31.s1, f32[512,256]{1,0:T(8,128)S(1)} %collective-permute-done.3.g1, f32[512,256]{1,0:T(8,128)S(1)} %collective-permute-done.6.g2_odd, f32[2,512,256]{2,1,0:T(8,128)S(1)} %collective-permute-done.7.s2, ...), custom_call_target="tpu_custom_call" | custom-call | flops 1024 | bytes 1024 | tf_op jit(solution)/shard_map/last/pallas_call | solution.py:67
  (4 shorter events, 0.1 us)
Async XLA Ops:
  0.6 0.7 %copy-start = (s32[3,1024]{1,0:T(4,128)S(1)}, s32[3,1024]{1,0:T(4,128)}, u32[]{:S(2)}) copy-start(s32[3,1024]{1,0:T(4,128)} %refs_3_.1) | copy-start | bytes 36868
  1.4 22.4 %collective-permute-start = (f32[2,512,256]{2,1,0:T(8,128)S(1)}, f32[2,512,256]{2,1,0:T(8,128)S(1)}, u32[]{:S(2)}, u32[]{:S(2)}) collective-permute-start(f32[2,512,256]{2,1,0:T(8,128)S(1)} %get-tuple-element.31.s1), channel_id=1, source_target_pairs={{0,1},{1,2},{2,3},{3,4},{4,5},{5,6},{6,7},{7,8},{8,9},{9,10},{10,1... | collective-permute-start | bytes 3145736 | tf_op jit(solution)/shard_map/ppermute | solution.py:220
  6.4 6.1 %slice-start = ((s8[6291456]{0:T(1024)(128)(4,1)}), s8[4194304]{0:T(1024)(128)(4,1)S(1)}, s32[]{:S(2)}) async-start(s8[6291456]{0:T(1024)(128)(4,1)} %bitcast.4), calls=%async_computation | async-start | bytes 8388608
  6.4 6.1 %slice-start.1 = ((s8[6291456]{0:T(1024)(128)(4,1)}), s8[2097152]{0:T(1024)(128)(4,1)S(1)}, s32[]{:S(2)}) async-start(s8[6291456]{0:T(1024)(128)(4,1)} %bitcast.4), calls=%async_computation.1 | async-start | bytes 4194304
  11.9 2.0 %collective-permute-start.1 = (f32[512,256]{1,0:T(8,128)S(1)}, f32[512,256]{1,0:T(8,128)S(1)}, u32[]{:S(2)}, u32[]{:S(2)}) collective-permute-start(f32[512,256]{1,0:T(8,128)S(1)} %get-tuple-element.36), channel_id=1, source_target_pairs={{0,1},{1,0},{2,3},{3,2},{4,5},{5,4},{6,7},{7,6},{8,9},{9,8},{10,11... | collective-permute-start | bytes 1572872 | tf_op jit(solution)/shard_map/ppermute | solution.py:220
  12.0 2.6 %copy-start.1 = (s32[3,1024]{1,0:T(4,128)S(1)}, s32[3,1024]{1,0:T(4,128)}, u32[]{:S(2)}) copy-start(s32[3,1024]{1,0:T(4,128)} %refs_3_.1) | copy-start | bytes 36868
  12.0 2.6 %collective-permute-start.2 = (f32[512,256]{1,0:T(8,128)S(1)}, f32[512,256]{1,0:T(8,128)S(1)}, u32[]{:S(2)}, u32[]{:S(2)}) collective-permute-start(f32[512,256]{1,0:T(8,128)S(1)} %get-tuple-element.37), channel_id=1, source_target_pairs={{0,1},{1,0},{2,3},{3,2},{4,5},{5,4},{6,7},{7,6},{8,9},{9,8},{10,11... | collective-permute-start | bytes 1572872 | tf_op jit(solution)/shard_map/ppermute | solution.py:220
  14.6 14.9 %collective-permute-start.8 = (f32[512,256]{1,0:T(8,128)S(1)}, f32[512,256]{1,0:T(8,128)S(1)}, u32[]{:S(2)}, u32[]{:S(2)}) collective-permute-start(f32[512,256]{1,0:T(8,128)S(1)} %get-tuple-element.38.after), channel_id=1, source_target_pairs={{0,1},{1,2},{2,3},{3,4},{4,5},{5,6},{6,7},{7,8},{8,9},{9,10},{10,1... | collective-permute-start | bytes 1572872 | tf_op jit(solution)/shard_map/ppermute | solution.py:220
  17.6 20.1 %collective-permute-start.7 = (f32[2,512,256]{2,1,0:T(8,128)S(1)}, f32[2,512,256]{2,1,0:T(8,128)S(1)}, u32[]{:S(2)}, u32[]{:S(2)}) collective-permute-start(f32[2,512,256]{2,1,0:T(8,128)S(1)} %get-tuple-element.44), channel_id=1, source_target_pairs={{0,1},{1,0},{2,3},{3,2},{4,5},{5,4},{6,7},{7,6},{8,9},{9,8},{10,11... | collective-permute-start | bytes 3145736 | tf_op jit(solution)/shard_map/ppermute | solution.py:220
  26.7 1.6 %collective-permute-start.5 = (f32[256,256]{1,0:T(8,128)S(1)}, f32[256,256]{1,0:T(8,128)S(1)}, u32[]{:S(2)}, u32[]{:S(2)}) collective-permute-start(f32[256,256]{1,0:T(8,128)S(1)} %get-tuple-element.41), channel_id=1, source_target_pairs={{0,1},{1,0},{2,3},{3,2},{4,5},{5,4},{6,7},{7,6},{8,9},{9,8},{10,11... | collective-permute-start | bytes 786440 | tf_op jit(solution)/shard_map/ppermute | solution.py:220
  26.7 1.9 %collective-permute-start.4 = (f32[256,256]{1,0:T(8,128)S(1)}, f32[256,256]{1,0:T(8,128)S(1)}, u32[]{:S(2)}, u32[]{:S(2)}) collective-permute-start(f32[256,256]{1,0:T(8,128)S(1)} %get-tuple-element.40.after), channel_id=1, source_target_pairs={{0,1},{1,0},{2,3},{3,2},{4,5},{5,4},{6,7},{7,6},{8,9},{9,8},{10,11... | collective-permute-start | bytes 786440 | tf_op jit(solution)/shard_map/ppermute | solution.py:220
  27.2 10.5 %collective-permute-start.3 = (f32[512,256]{1,0:T(8,128)S(1)}, f32[512,256]{1,0:T(8,128)S(1)}, u32[]{:S(2)}, u32[]{:S(2)}) collective-permute-start(f32[512,256]{1,0:T(8,128)S(1)} %get-tuple-element.39), channel_id=1, source_target_pairs={{1,0},{2,1},{3,2},{4,3},{5,4},{6,5},{7,6},{8,7},{9,8},{10,9},{11,1... | collective-permute-start | bytes 1572872 | tf_op jit(solution)/shard_map/ppermute | solution.py:220
  32.1 15.8 %collective-permute-start.9 = (f32[512,256]{1,0:T(8,128)S(1)}, f32[512,256]{1,0:T(8,128)S(1)}, u32[]{:S(2)}, u32[]{:S(2)}) collective-permute-start(f32[512,256]{1,0:T(8,128)S(1)} %get-tuple-element.46), channel_id=1, source_target_pairs={{0,14},{1,1},{2,0},{3,3},{4,2},{5,5},{6,4},{7,7},{8,6},{9,9},{10,8... | collective-permute-start | bytes 1572872 | tf_op jit(solution)/shard_map/ppermute | solution.py:220
  34.5 13.4 %collective-permute-start.6 = (f32[512,256]{1,0:T(8,128)S(1)}, f32[512,256]{1,0:T(8,128)S(1)}, u32[]{:S(2)}, u32[]{:S(2)}) collective-permute-start(f32[512,256]{1,0:T(8,128)S(1)} %get-tuple-element.43.refs_4_), channel_id=1, source_target_pairs={{0,0},{1,15},{2,2},{3,1},{4,4},{5,3},{6,6},{7,5},{8,8},{9,7},{10,1... | collective-permute-start | bytes 1572872 | tf_op jit(solution)/shard_map/ppermute | solution.py:220

commit v3 on v2

v3 whole, which is shorter than its diff:
```python
import jax
import jax.numpy as jnp
from jax import lax
from jax.experimental import pallas as pl
from jax.experimental.pallas import tpu as pltpu
from jax.sharding import PartitionSpec as P

F32 = jnp.float32
BF16 = jnp.bfloat16
RATE = 0.05
VMEM = pl.BlockSpec(memory_space=pltpu.VMEM)
HBM = pl.BlockSpec(memory_space=pltpu.HBM)
ANY = pl.BlockSpec(memory_space=pl.ANY)


def split(x):
    high = x.astype(BF16)
    return high, (x - high.astype(F32)).astype(BF16)


def product(a, b, dim_a, dim_b):
    def one(x, y):
        return lax.dot_general(
            x, y, (((dim_a,), (dim_b,)), ((), ())), preferred_element_type=F32
        )

    return one(a[0], b[0]) + (one(a[1], b[0]) + one(a[0], b[1]))


def block_of(size, most):
    return most if size % most == 0 else size


def is_odd():
    return lax.rem(lax.axis_index("inner"), 2) == 1


def adagrad(value, moment, grad):
    moment = moment + grad * grad
    return value - RATE * grad * lax.rsqrt(moment), moment


def vertex_pass(u, c, e, w, r_high, r_low, ready=None):
    us = split(0.5 * u[...])
    wf = w.astype(F32)
    cols = block_of(c.shape[0], 256)
    count = c.shape[0] // cols
    parts = []

    def scores(j):
        if ready is not None:
            ready(j)
        parts.append(split(c[pl.ds(j * cols, cols), :]))
        return product(us, parts[j], 1, 1)

    grad = None
    half_scores = scores(0)
    for j in range(count):
        at = pl.ds(j * cols, cols)
        later = scores(j + 1) if j + 1 < count else None
        ef = e[:, at].astype(F32)
        wj = wf[:, j * cols : (j + 1) * cols]
        resid = split((ef + wj) * jnp.tanh(half_scores) + (wj - ef))
        r_high[:, at] = resid[0]
        r_low[:, at] = resid[1]
        term = product(resid, parts[j], 1, 0)
        grad = term if grad is None else grad + term
        half_scores = later
    return 0.5 * grad


def context_pass(u, c, h, r_high, r_low, c_out, h_out):
    us = split(0.5 * u[...])
    rows = block_of(c.shape[0], 256)
    for j in range(c.shape[0] // rows):
        at = pl.ds(j * rows, rows)
        grad = product((r_high[:, at], r_low[:, at]), us, 0, 0)
        c_out[at, :], h_out[at, :] = adagrad(c[at, :], h[at, :], grad)


def call(body, in_specs, outs, scratch, args, name, room=24):
    return pl.pallas_call(
        body,
        out_shape=outs,
        in_specs=in_specs,
        out_specs=[VMEM] * len(outs),
        scratch_shapes=scratch,
        compiler_params=pltpu.CompilerParams(vmem_limit_bytes=room << 20),
        cost_estimate=pl.CostEstimate(flops=1024, bytes_accessed=1024, transcendentals=0),
        name=name,
    )(*args)


def load(pairs, sems, first=0):
    copies = [pltpu.make_async_copy(a, b, sems.at[first + i]) for i, (a, b) in enumerate(pairs)]
    for copy in copies:
        copy.start()
    return copies


def load_chunks(u, c, e, w, ub, cb, eb, wb, more, sems):
    cols = block_of(cb.shape[0], 256)
    count = cb.shape[0] // cols
    chunks = []
    for j in range(count):
        at = pl.ds(j * cols, cols)
        chunks += [(c.at[at], cb.at[at]), (e.at[0, :, at], eb.at[:, at])]
    copies = load([(w, wb), (u, ub)] + chunks[:4], sems)
    copies[0].wait()
    copies += load(chunks[4:] + more, sems, len(copies))
    copies[1].wait()

    def ready(j):
        copies[2 + 2 * j].wait()
        copies[3 + 2 * j].wait()

    return ready, copies[2 + 2 * count :]


def first_odd(u, g, c, e, w, s1, r_high, r_low, ub, gb, cb, eb, wb, sems):
    @pl.when(is_odd())
    def _():
        ready, more = load_chunks(u, c, e, w, ub, cb, eb, wb, [(g, gb)], sems)
        grad = vertex_pass(ub, cb, eb, wb[0:1, :], r_high, r_low, ready)
        more[0].wait()
        s1[0], s1[1] = adagrad(ub[...], gb[...], grad)


def first_rest(
    u, g, c, h, e, w, r_high_in, r_low_in, u1, g1, c_out, h_out,
    ub, gb, cb, hb, eb, wb, r_high, r_low, sems,
):
    odd = is_odd()

    @pl.when(odd)
    def _():
        for copy in load([(u, ub), (c, cb), (h, hb)], sems):
            copy.wait()
        context_pass(ub, cb, hb, r_high_in, r_low_in, c_out, h_out)

    @pl.when(jnp.logical_not(odd))
    def _():
        ready, more = load_chunks(u, c, e, w, ub, cb, eb, wb, [(g, gb), (h, hb)], sems)
        grad = vertex_pass(ub, cb, eb, wb[0:1, :], r_high, r_low, ready)
        more[0].wait()
        u1[...], g1[...] = adagrad(ub[...], gb[...], grad)
        more[1].wait()
        context_pass(ub, cb, hb, r_high, r_low, c_out, h_out)


def second_odd(u1, g1, c, h, e, w, u2, s2, c_out, h_out, r_high, r_low):
    @pl.when(is_odd())
    def _():
        grad = vertex_pass(u1, c, e.at[1], w[1:2, :], r_high, r_low)
        value, moment = adagrad(u1[...], g1[...], grad)
        u2[...] = value
        s2[0], s2[1] = value, moment
        context_pass(u1, c, h, r_high, r_low, c_out, h_out)


def second_even(s1, c, h, e, w, after, grad_out, u2_top, u2_end, c_out, h_out, r_high, r_low):
    @pl.when(jnp.logical_not(is_odd()))
    def _():
        grad = vertex_pass(s1.at[0], c, e.at[1], w[1:2, :], r_high, r_low)
        grad_out[...] = grad
        value = adagrad(s1[0], s1[1], grad)[0]
        middle = u2_top.shape[0]
        u2_top[...], u2_end[...] = value[:middle], value[middle:]
        context_pass(s1.at[0], c, h, r_high, r_low, c_out, h_out)


def third(odd, u, c, e, w, after, g2, r_high, r_low):
    @pl.when(is_odd() == odd)
    def _():
        g2[...] = vertex_pass(u, c, e.at[2], w[2:3, :], r_high, r_low)


def third_odd(u_top, u_end, c, e, w, after, u, *refs):
    middle = u_top.shape[0]
    u[:middle, :] = u_top[...]
    u[middle:, :] = u_end[...]
    third(True, u, c, e, w, after, *refs)


def third_even(*refs):
    third(False, *refs)


def third_context(u_odd, c_odd, h_odd, rh_odd, rl_odd, u_even, c_even, h_even, rh_even, rl_even, c_out, h_out):
    odd = is_odd()

    @pl.when(odd)
    def _():
        context_pass(u_odd, c_odd, h_odd, rh_odd, rl_odd, c_out, h_out)

    @pl.when(jnp.logical_not(odd))
    def _():
        context_pass(u_even, c_even, h_even, rh_even, rl_even, c_out, h_out)


def last(s1, g1, g2_odd, s2, g2_even, u_out, g_out):
    odd = is_odd()

    @pl.when(odd)
    def _():
        value, moment = adagrad(s1[0], s1[1], g1[...])
        u_out[...], g_out[...] = adagrad(value, moment, g2_odd[...])

    @pl.when(jnp.logical_not(odd))
    def _():
        u_out[...], g_out[...] = adagrad(s2[0], s2[1], g2_even[...])


def per_device(vertices, vertex_moments, contexts, context_moments, edge_counts, negative_weights):
    nrows, width = vertices.shape
    ncols = contexts.shape[0]
    count = lax.axis_size("inner")
    assert count % 2 == 0 and edge_counts.shape[0] == 3

    ring = [(i, (i + 1) % count) for i in range(count)]
    unring = [(b, a) for a, b in ring]
    swap = [(i, i ^ 1) for i in range(count)]
    home_odd = [(i, (i - 2) % count if i % 2 else i) for i in range(count)]
    home_even = [(i, i if i % 2 else (i - 2) % count) for i in range(count)]

    def move(value, pairs):
        return lax.ppermute(value, "inner", pairs)

    def f32(*shape):
        return jax.ShapeDtypeStruct(shape, F32)

    block = f32(nrows, width)
    part = f32(nrows // 2, width)
    pair = f32(2, nrows, width)
    ctx = f32(ncols, width)
    half = jax.ShapeDtypeStruct((nrows, ncols), BF16)
    half_buf = pltpu.VMEM((nrows, ncols), BF16)
    vert_buf = pltpu.VMEM((nrows, width), F32)
    ctx_buf = pltpu.VMEM((ncols, width), F32)
    edge_buf = pltpu.VMEM((nrows, ncols), jnp.int32)
    weight_buf = pltpu.VMEM(negative_weights.shape, jnp.int32)
    sems = pltpu.SemaphoreType.DMA((4 + 2 * (ncols // block_of(ncols, 256)),))
    hbm = [
        pltpu.with_memory_space_constraint(x, pltpu.HBM)
        for x in (vertices, vertex_moments, contexts, context_moments, edge_counts, negative_weights)
    ]

    s1o, rh0, rl0 = call(
        first_odd, [HBM] * 5, [pair, half, half],
        [vert_buf, vert_buf, ctx_buf, edge_buf, weight_buf, sems],
        (*hbm[:3], *hbm[4:]), "first_odd",
    )
    s1x = move(s1o, ring)
    *s1, c1, h1 = call(
        first_rest, [HBM] * 6 + [VMEM] * 2, [block, block, ctx, ctx],
        [vert_buf, vert_buf, ctx_buf, ctx_buf, edge_buf, weight_buf, half_buf, half_buf, sems],
        (*hbm, rh0, rl0), "first_rest",
    )
    s1i = [move(x, swap) for x in s1]
    u2e, s2e, c2o, h2o = call(
        second_odd, [VMEM] * 6, [block, pair, ctx, ctx], [half_buf, half_buf],
        (*s1i, c1, h1, edge_counts, negative_weights), "second_odd",
    )
    u2x = move(u2e, ring)
    s2h = move(s2e, swap)
    g1, u2t, u2d, c2e, h2e = call(
        second_even, [VMEM] * 5 + [ANY], [block, part, part, ctx, ctx], [half_buf, half_buf],
        (s1x, c1, h1, edge_counts, negative_weights, u2e), "second_even",
    )
    g1x = move(g1, unring)
    u2ti = move(u2t, swap)
    u2di = move(u2d, swap)
    u2i, g2o, rho, rlo = call(
        third_odd, [VMEM] * 5 + [ANY], [block, block, half, half], [],
        (u2ti, u2di, c2o, edge_counts, negative_weights, u2t), "third_odd",
    )
    g2xo = move(g2o, home_odd)
    g2e, rhe, rle = call(
        third_even, [VMEM] * 4 + [ANY], [block, half, half], [],
        (u2x, c2e, edge_counts, negative_weights, g2o), "third_even",
    )
    g2xe = move(g2e, home_even)
    c3, h3 = call(
        third_context, [VMEM] * 10, [ctx, ctx], [],
        (u2i, c2o, h2o, rho, rlo, u2x, c2e, h2e, rhe, rle), "third_context",
    )
    u3, g3 = call(last, [VMEM] * 5, [block, block], [], (s1o, g1x, g2xo, s2h, g2xe), "last")
    return u3, g3, c3, h3


def solution(mesh):
    split_rows = P(("snap", "inner"), None)
    return jax.shard_map(
        per_device,
        mesh=mesh,
        in_specs=(
            split_rows,
            split_rows,
            split_rows,
            split_rows,
            P(None, None, ("snap", "inner")),
            P(None, ("snap", "inner")),
        ),
        out_specs=(split_rows,) * 4,
        check_vma=False,
    )
```

time: 49.2 us -> 47.7 us (0.970)
  local copies, waits for them, and re-layouts: 1.04 us -> 0.02 us
    unnamed x8 -> x6, local copies, waits for them, and re-layouts: 0.73 us -> 0.02 us
  transfers between devices with their start and end apart: 10 -> 10, of which waited for: 7 -> 7; matrix products, arithmetic and copies ran while one was open for 1% -> 0% of each run, Pallas kernels for 28% -> 28%
where the time goes in v3:
time: 47.7 us; the launch traced here: 47.5 us
  waiting for transfers between devices  19.8 us (42%)
  Pallas kernels  14.7 us (31%)
  starting transfers between devices  12.2 us (26%)
  between operations  0.75 us (2%)
    ppermute x10, waiting for transfers between devices, move(): return lax.ppermute(value, 'inner', pairs)  19.8 us
    pallas_call x8, Pallas kernels, call(): pl.pallas_call(body, out_shape=outs, in_specs=in_specs, out_specs=[VMEM]...  14.7 us
    ppermute x10, starting transfers between devices, move(): return lax.ppermute(value, 'inner', pairs)  12.2 us
  transfers between devices with their start and end apart: 10, of which 7 were waited for; matrix products, arithmetic and copies ran while one was open for 0% of the time, Pallas kernels for 28%

profile of v3, /device:TPU:0, one launch (start us, length us, event | category | flops | bytes accessed | tf_op | source)
XLA Modules:
  0.0 47.5 jit_solution(4416112569495622261)
XLA Ops:
  0.6 0.1 first_odd.1
  0.8 0.0 slice-start
  0.8 0.0 copy-start
  0.8 4.7 %collective-permute-start = (f32[2,512,256]{2,1,0:T(8,128)S(1)}, f32[2,512,256]{2,1,0:T(8,128)S(1)}, u32[]{:S(2)}, u32[]{:S(2)}) collective-permute-start(f32[2,512,256]{2,1,0:T(8,128)S(1)} %get-tuple-element.31.s1), channel_id=1, source_target_pairs={{0,1},{1,2},{2,3},{3,4},{4,5},{5,6},{6,7},{7,8},{8,9},{9,10},{10,1... | collective-permute-start | bytes 3145736 | tf_op jit(solution)/shard_map/ppermute | solution.py:227
  5.5 0.0 slice-start.1
  5.5 5.9 %first_rest.1 = (f32[512,256]{1,0:T(8,128)S(1)}, f32[512,256]{1,0:T(8,128)S(1)}, f32[1024,256]{1,0:T(8,128)S(1)}, f32[1024,256]{1,0:T(8,128)S(1)}) custom-call(f32[512,256]{1,0:T(8,128)} %u.3, f32[512,256]{1,0:T(8,128)} %g.3, f32[1024,256]{1,0:T(8,128)} %c.3, f32[1024,256]{1,0:T(8,128)} %h.1, s32[3,512,1024]{2,1,0:T(8,128)} %refs_2_.1, s32[3,1024]{1,0:T(4,128)} %refs_3_.1, ...), custom_call_target="tpu_custom_call" | custom-call | flops 1024 | bytes 1024 | tf_op jit(solution)/shard_map/first_rest/pallas_call | solution.py:82
  11.5 0.1 collective-permute-start.1
  11.5 0.5 %collective-permute-start.2 = (f32[512,256]{1,0:T(8,128)S(1)}, f32[512,256]{1,0:T(8,128)S(1)}, u32[]{:S(2)}, u32[]{:S(2)}) collective-permute-start(f32[512,256]{1,0:T(8,128)S(1)} %get-tuple-element.37), channel_id=1, source_target_pairs={{0,1},{1,0},{2,3},{3,2},{4,5},{5,4},{6,7},{7,6},{8,9},{9,8},{10,11... | collective-permute-start | bytes 1572872 | tf_op jit(solution)/shard_map/ppermute | solution.py:227
  12.0 1.4 %collective-permute-done.1.u1 = f32[512,256]{1,0:T(8,128)S(1)} collective-permute-done((f32[512,256]{1,0:T(8,128)S(1)}, f32[512,256]{1,0:T(8,128)S(1)}, u32[]{:S(2)}, u32[]{:S(2)}) %collective-permute-start.1) | collective-permute-done | bytes 524320 | tf_op jit(solution)/shard_map/ppermute | solution.py:227
  13.4 0.7 %collective-permute-done.2.g1 = f32[512,256]{1,0:T(8,128)S(1)} collective-permute-done((f32[512,256]{1,0:T(8,128)S(1)}, f32[512,256]{1,0:T(8,128)S(1)}, u32[]{:S(2)}, u32[]{:S(2)}) %collective-permute-start.2) | collective-permute-done | bytes 524320 | tf_op jit(solution)/shard_map/ppermute | solution.py:227
  14.2 0.0 slice-done
  14.2 0.0 copy-done
  14.2 0.0 slice-done.1
  14.2 2.9 %collective-permute-start.8 = (f32[512,256]{1,0:T(8,128)S(1)}, f32[512,256]{1,0:T(8,128)S(1)}, u32[]{:S(2)}, u32[]{:S(2)}) collective-permute-start(f32[512,256]{1,0:T(8,128)S(1)} %get-tuple-element.38.after), channel_id=1, source_target_pairs={{0,1},{1,2},{2,3},{3,4},{4,5},{5,6},{6,7},{7,8},{8,9},{9,10},{10,1... | collective-permute-start | bytes 1572872 | tf_op jit(solution)/shard_map/ppermute | solution.py:227
  17.1 0.1 collective-permute-start.7
  17.2 5.8 %collective-permute-done.s1 = f32[2,512,256]{2,1,0:T(8,128)S(1)} collective-permute-done((f32[2,512,256]{2,1,0:T(8,128)S(1)}, f32[2,512,256]{2,1,0:T(8,128)S(1)}, u32[]{:S(2)}, u32[]{:S(2)}) %collective-permute-start) | collective-permute-done | bytes 1048608 | tf_op jit(solution)/shard_map/ppermute | solution.py:227
  23.0 2.7 %second_even.1 = (f32[512,256]{1,0:T(8,128)S(1)}, f32[256,256]{1,0:T(8,128)S(1)}, f32[256,256]{1,0:T(8,128)S(1)}, f32[1024,256]{1,0:T(8,128)S(1)}, f32[1024,256]{1,0:T(8,128)S(1)}) custom-call(f32[2,512,256]{2,1,0:T(8,128)S(1)} %collective-permute-done.s1, f32[1024,256]{1,0:T(8,128)S(1)} %get-tuple-element.34.c, f32[1024,256]{1,0:T(8,128)S(1)} %get-tuple-element.35.h, ...), custom_call_target="tpu_custom_call" | custom-call | flops 1024 | bytes 1024 | tf_op jit(solution)/shard_map/second_even/pallas_call | solution.py:82
  25.8 0.1 collective-permute-start.4
  25.8 0.5 %collective-permute-start.5 = (f32[256,256]{1,0:T(8,128)S(1)}, f32[256,256]{1,0:T(8,128)S(1)}, u32[]{:S(2)}, u32[]{:S(2)}) collective-permute-start(f32[256,256]{1,0:T(8,128)S(1)} %get-tuple-element.41), channel_id=1, source_target_pairs={{0,1},{1,0},{2,3},{3,2},{4,5},{5,4},{6,7},{7,6},{8,9},{9,8},{10,11... | collective-permute-start | bytes 786440 | tf_op jit(solution)/shard_map/ppermute | solution.py:227
  26.3 0.2 collective-permute-start.3
  26.5 0.8 %collective-permute-done.4.u_top = f32[256,256]{1,0:T(8,128)S(1)} collective-permute-done((f32[256,256]{1,0:T(8,128)S(1)}, f32[256,256]{1,0:T(8,128)S(1)}, u32[]{:S(2)}, u32[]{:S(2)}) %collective-permute-start.4) | collective-permute-done | bytes 262176 | tf_op jit(solution)/shard_map/ppermute | solution.py:227
  27.4 0.4 collective-permute-done.5.u_end
  27.8 0.7 %collective-permute-start.6 = (f32[512,256]{1,0:T(8,128)S(1)}, f32[512,256]{1,0:T(8,128)S(1)}, u32[]{:S(2)}, u32[]{:S(2)}) collective-permute-start(f32[512,256]{1,0:T(8,128)S(1)} %get-tuple-element.43.refs_4_), channel_id=1, source_target_pairs={{0,0},{1,15},{2,2},{3,1},{4,4},{5,3},{6,6},{7,5},{8,8},{9,7},{10,1... | collective-permute-start | bytes 1572872 | tf_op jit(solution)/shard_map/ppermute | solution.py:227
  28.5 0.5 %collective-permute-done.8.refs_0_.u_even = f32[512,256]{1,0:T(8,128)S(1)} collective-permute-done((f32[512,256]{1,0:T(8,128)S(1)}, f32[512,256]{1,0:T(8,128)S(1)}, u32[]{:S(2)}, u32[]{:S(2)}) %collective-permute-start.8) | collective-permute-done | bytes 524320 | tf_op jit(solution)/shard_map/ppermute | solution.py:227
  29.0 2.3 %third_even.1 = (f32[512,256]{1,0:T(8,128)S(1)}, bf16[512,1024]{1,0:T(8,128)(2,1)S(1)}, bf16[512,1024]{1,0:T(8,128)(2,1)S(1)}) custom-call(f32[512,256]{1,0:T(8,128)S(1)} %collective-permute-done.8.refs_0_.u_even, f32[1024,256]{1,0:T(8,128)S(1)} %get-tuple-element.45.refs_1_.c_even, s32[3,512,1024]{2,1,0:T(8,128)S(1)} %bitcast.1, s32[3,1024]{1,0:T(4,128)S(1)} %copy-done, ...), custom_call_target="tpu_custom_call" | custom-call | flops 1024 | bytes 1024 | tf_op jit(solution)/shard_map/third_even/pallas_call | solution.py:82
  31.3 2.4 %collective-permute-start.9 = (f32[512,256]{1,0:T(8,128)S(1)}, f32[512,256]{1,0:T(8,128)S(1)}, u32[]{:S(2)}, u32[]{:S(2)}) collective-permute-start(f32[512,256]{1,0:T(8,128)S(1)} %get-tuple-element.46), channel_id=1, source_target_pairs={{0,14},{1,1},{2,0},{3,3},{4,2},{5,5},{6,4},{7,7},{8,6},{9,9},{10,8... | collective-permute-start | bytes 1572872 | tf_op jit(solution)/shard_map/ppermute | solution.py:227
  33.7 2.5 %third_context.1 = (f32[1024,256]{1,0:T(8,128)}, f32[1024,256]{1,0:T(8,128)}) custom-call(f32[512,256]{1,0:T(8,128)S(1)} %get-tuple-element.49.u_odd, f32[1024,256]{1,0:T(8,128)S(1)} %get-tuple-element.42.c.c_odd, f32[1024,256]{1,0:T(8,128)S(1)} %get-tuple-element.50.h_odd, bf16[512,1024]{1,0:T(8,128)(2,1)S(1)} %get-tuple-element.51.rh_odd, ...), custom_call_target="tpu_custom_call" | custom-call | flops 1024 | bytes 1024 | tf_op jit(solution)/shard_map/third_context/pallas_call | solution.py:82
  36.3 0.0 collective-permute-done.3.g1
  36.3 0.0 collective-permute-done.7.s2
  36.3 0.0 collective-permute-done.6.g2_odd
  36.3 10.2 %collective-permute-done.9.g2_even = f32[512,256]{1,0:T(8,128)S(1)} collective-permute-done((f32[512,256]{1,0:T(8,128)S(1)}, f32[512,256]{1,0:T(8,128)S(1)}, u32[]{:S(2)}, u32[]{:S(2)}) %collective-permute-start.9) | collective-permute-done | bytes 524320 | tf_op jit(solution)/shard_map/ppermute | solution.py:227
  46.4 1.1 %last.1 = (f32[512,256]{1,0:T(8,128)}, f32[512,256]{1,0:T(8,128)}) custom-call(f32[2,512,256]{2,1,0:T(8,128)S(1)} %get-tuple-element.31.s1, f32[512,256]{1,0:T(8,128)S(1)} %collective-permute-done.3.g1, f32[512,256]{1,0:T(8,128)S(1)} %collective-permute-done.6.g2_odd, f32[2,512,256]{2,1,0:T(8,128)S(1)} %collective-permute-done.7.s2, ...), custom_call_target="tpu_custom_call" | custom-call | flops 1024 | bytes 1024 | tf_op jit(solution)/shard_map/last/pallas_call | solution.py:82
  (3 shorter events, 0.1 us)
Async XLA Ops:
  0.8 13.4 %slice-start = ((s8[6291456]{0:T(1024)(128)(4,1)}), s8[4194304]{0:T(1024)(128)(4,1)S(1)}, s32[]{:S(2)}) async-start(s8[6291456]{0:T(1024)(128)(4,1)} %bitcast), calls=%async_computation | async-start | bytes 8388608
  0.8 13.4 %copy-start = (s32[3,1024]{1,0:T(4,128)S(1)}, s32[3,1024]{1,0:T(4,128)}, u32[]{:S(2)}) copy-start(s32[3,1024]{1,0:T(4,128)} %refs_3_.1) | copy-start | bytes 36868
  0.8 22.2 %collective-permute-start = (f32[2,512,256]{2,1,0:T(8,128)S(1)}, f32[2,512,256]{2,1,0:T(8,128)S(1)}, u32[]{:S(2)}, u32[]{:S(2)}) collective-permute-start(f32[2,512,256]{2,1,0:T(8,128)S(1)} %get-tuple-element.31.s1), channel_id=1, source_target_pairs={{0,1},{1,2},{2,3},{3,4},{4,5},{5,6},{6,7},{7,8},{8,9},{9,10},{10,1... | collective-permute-start | bytes 3145736 | tf_op jit(solution)/shard_map/ppermute | solution.py:227
  5.5 8.7 %slice-start.1 = ((s8[6291456]{0:T(1024)(128)(4,1)}), s8[2097152]{0:T(1024)(128)(4,1)S(1)}, s32[]{:S(2)}) async-start(s8[6291456]{0:T(1024)(128)(4,1)} %bitcast), calls=%async_computation.1 | async-start | bytes 4194304
  11.5 2.0 %collective-permute-start.1 = (f32[512,256]{1,0:T(8,128)S(1)}, f32[512,256]{1,0:T(8,128)S(1)}, u32[]{:S(2)}, u32[]{:S(2)}) collective-permute-start(f32[512,256]{1,0:T(8,128)S(1)} %get-tuple-element.36), channel_id=1, source_target_pairs={{0,1},{1,0},{2,3},{3,2},{4,5},{5,4},{6,7},{7,6},{8,9},{9,8},{10,11... | collective-permute-start | bytes 1572872 | tf_op jit(solution)/shard_map/ppermute | solution.py:227
  11.5 2.6 %collective-permute-start.2 = (f32[512,256]{1,0:T(8,128)S(1)}, f32[512,256]{1,0:T(8,128)S(1)}, u32[]{:S(2)}, u32[]{:S(2)}) collective-permute-start(f32[512,256]{1,0:T(8,128)S(1)} %get-tuple-element.37), channel_id=1, source_target_pairs={{0,1},{1,0},{2,3},{3,2},{4,5},{5,4},{6,7},{7,6},{8,9},{9,8},{10,11... | collective-permute-start | bytes 1572872 | tf_op jit(solution)/shard_map/ppermute | solution.py:227
  14.2 14.8 %collective-permute-start.8 = (f32[512,256]{1,0:T(8,128)S(1)}, f32[512,256]{1,0:T(8,128)S(1)}, u32[]{:S(2)}, u32[]{:S(2)}) collective-permute-start(f32[512,256]{1,0:T(8,128)S(1)} %get-tuple-element.38.after), channel_id=1, source_target_pairs={{0,1},{1,2},{2,3},{3,4},{4,5},{5,6},{6,7},{7,8},{8,9},{9,10},{10,1... | collective-permute-start | bytes 1572872 | tf_op jit(solution)/shard_map/ppermute | solution.py:227
  17.1 19.1 %collective-permute-start.7 = (f32[2,512,256]{2,1,0:T(8,128)S(1)}, f32[2,512,256]{2,1,0:T(8,128)S(1)}, u32[]{:S(2)}, u32[]{:S(2)}) collective-permute-start(f32[2,512,256]{2,1,0:T(8,128)S(1)} %get-tuple-element.44), channel_id=1, source_target_pairs={{0,1},{1,0},{2,3},{3,2},{4,5},{5,4},{6,7},{7,6},{8,9},{9,8},{10,11... | collective-permute-start | bytes 3145736 | tf_op jit(solution)/shard_map/ppermute | solution.py:227
  25.8 1.6 %collective-permute-start.4 = (f32[256,256]{1,0:T(8,128)S(1)}, f32[256,256]{1,0:T(8,128)S(1)}, u32[]{:S(2)}, u32[]{:S(2)}) collective-permute-start(f32[256,256]{1,0:T(8,128)S(1)} %get-tuple-element.40.after), channel_id=1, source_target_pairs={{0,1},{1,0},{2,3},{3,2},{4,5},{5,4},{6,7},{7,6},{8,9},{9,8},{10,11... | collective-permute-start | bytes 786440 | tf_op jit(solution)/shard_map/ppermute | solution.py:227
  25.8 1.9 %collective-permute-start.5 = (f32[256,256]{1,0:T(8,128)S(1)}, f32[256,256]{1,0:T(8,128)S(1)}, u32[]{:S(2)}, u32[]{:S(2)}) collective-permute-start(f32[256,256]{1,0:T(8,128)S(1)} %get-tuple-element.41), channel_id=1, source_target_pairs={{0,1},{1,0},{2,3},{3,2},{4,5},{5,4},{6,7},{7,6},{8,9},{9,8},{10,11... | collective-permute-start | bytes 786440 | tf_op jit(solution)/shard_map/ppermute | solution.py:227
  26.3 9.9 %collective-permute-start.3 = (f32[512,256]{1,0:T(8,128)S(1)}, f32[512,256]{1,0:T(8,128)S(1)}, u32[]{:S(2)}, u32[]{:S(2)}) collective-permute-start(f32[512,256]{1,0:T(8,128)S(1)} %get-tuple-element.39), channel_id=1, source_target_pairs={{1,0},{2,1},{3,2},{4,3},{5,4},{6,5},{7,6},{8,7},{9,8},{10,9},{11,1... | collective-permute-start | bytes 1572872 | tf_op jit(solution)/shard_map/ppermute | solution.py:227
  27.8 8.5 %collective-permute-start.6 = (f32[512,256]{1,0:T(8,128)S(1)}, f32[512,256]{1,0:T(8,128)S(1)}, u32[]{:S(2)}, u32[]{:S(2)}) collective-permute-start(f32[512,256]{1,0:T(8,128)S(1)} %get-tuple-element.43.refs_4_), channel_id=1, source_target_pairs={{0,0},{1,15},{2,2},{3,1},{4,4},{5,3},{6,6},{7,5},{8,8},{9,7},{10,1... | collective-permute-start | bytes 1572872 | tf_op jit(solution)/shard_map/ppermute | solution.py:227
  31.3 15.1 %collective-permute-start.9 = (f32[512,256]{1,0:T(8,128)S(1)}, f32[512,256]{1,0:T(8,128)S(1)}, u32[]{:S(2)}, u32[]{:S(2)}) collective-permute-start(f32[512,256]{1,0:T(8,128)S(1)} %get-tuple-element.46), channel_id=1, source_target_pairs={{0,14},{1,1},{2,0},{3,3},{4,2},{5,5},{6,4},{7,7},{8,6},{9,9},{10,8... | collective-permute-start | bytes 1572872 | tf_op jit(solution)/shard_map/ppermute | solution.py:227

commit v4 on v3

--- a/solution.py
+++ b/solution.py
@@ -8,6 +8,7 @@
 F32 = jnp.float32
 BF16 = jnp.bfloat16
 RATE = 0.05
+EARLY = 3
 VMEM = pl.BlockSpec(memory_space=pltpu.VMEM)
 HBM = pl.BlockSpec(memory_space=pltpu.HBM)
 ANY = pl.BlockSpec(memory_space=pl.ANY)
@@ -69,12 +70,12 @@
     return 0.5 * grad
 
 
-def context_pass(u, c, h, r_high, r_low, c_out, h_out):
-    us = split(0.5 * u[...])
+def context_pass(parts, c, h, c_out, h_out):
+    us = [split(0.5 * u[...]) for u, _, _ in parts]
     rows = block_of(c.shape[0], 256)
     for j in range(c.shape[0] // rows):
         at = pl.ds(j * rows, rows)
-        grad = product((r_high[:, at], r_low[:, at]), us, 0, 0)
+        grad = sum(product((high[:, at], low[:, at]), u, 0, 0) for u, (_, high, low) in zip(us, parts))
         c_out[at, :], h_out[at, :] = adagrad(c[at, :], h[at, :], grad)
 
 
@@ -98,75 +99,126 @@
     return copies
 
 
-def load_chunks(u, c, e, w, ub, cb, eb, wb, more, sems):
-    cols = block_of(cb.shape[0], 256)
-    count = cb.shape[0] // cols
-    chunks = []
-    for j in range(count):
-        at = pl.ds(j * cols, cols)
-        chunks += [(c.at[at], cb.at[at]), (e.at[0, :, at], eb.at[:, at])]
-    copies = load([(w, wb), (u, ub)] + chunks[:4], sems)
-    copies[0].wait()
-    copies += load(chunks[4:] + more, sems, len(copies))
-    copies[1].wait()
-
-    def ready(j):
-        copies[2 + 2 * j].wait()
-        copies[3 + 2 * j].wait()
-
-    return ready, copies[2 + 2 * count :]
-
-
-def first_odd(u, g, c, e, w, s1, r_high, r_low, ub, gb, cb, eb, wb, sems):
+def first_top(u, g, c, h, e, w, s1, r_high, r_low, ub, gb, cb, hb, eb, wb, sems):
     @pl.when(is_odd())
     def _():
-        ready, more = load_chunks(u, c, e, w, ub, cb, eb, wb, [(g, gb)], sems)
-        grad = vertex_pass(ub, cb, eb, wb[0:1, :], r_high, r_low, ready)
-        more[0].wait()
-        s1[0], s1[1] = adagrad(ub[...], gb[...], grad)
-
-
-def first_rest(
-    u, g, c, h, e, w, r_high_in, r_low_in, u1, g1, c_out, h_out,
-    ub, gb, cb, hb, eb, wb, r_high, r_low, sems,
+        middle = s1.shape[1]
+        top, end = pl.ds(0, middle), pl.ds(middle, ub.shape[0] - middle)
+        cols = block_of(cb.shape[0], 512)
+        count = cb.shape[0] // cols
+        chunks = []
+        for j in range(count):
+            at = pl.ds(j * cols, cols)
+            chunks += [(c.at[at], cb.at[at]), (e.at[0, top, at], eb.at[top, at])]
+        copies = load(
+            [(w, wb), (u, ub)] + chunks + [(g, gb), (e.at[0, end], eb.at[end]), (h, hb)], sems
+        )
+        copies[0].wait()
+        copies[1].wait()
+        small = block_of(cb.shape[0], 256)
+
+        def ready(j):
+            if j * small % cols == 0:
+                at = 2 + 2 * (j * small // cols)
+                copies[at].wait()
+                copies[at + 1].wait()
+
+        grad = vertex_pass(ub.at[top], cb, eb.at[top], wb[0:1, :], r_high, r_low, ready)
+        copies[2 + 2 * count].wait()
+        s1[0], s1[1] = adagrad(ub[top, :], gb[top, :], grad)
+        for copy in copies[3 + 2 * count :]:
+            copy.wait()
+
+
+def first_end(u, g, c, e, w, s1, r_high, r_low):
+    @pl.when(is_odd())
+    def _():
+        rows = s1.shape[1]
+        end = pl.ds(u.shape[0] - rows, rows)
+        grad = vertex_pass(u.at[end], c, e.at[end], w[0:1, :], r_high, r_low)
+        s1[0], s1[1] = adagrad(u[end, :], g[end, :], grad)
+
+
+def first_even(
+    u, g, c, e, w, u_odd, c_odd, h_odd, rh_top, rl_top, rh_end, rl_end,
+    u1, g1, r_high, r_low, c_out, h_out, ub, gb, cb, eb, wb, sems,
 ):
     odd = is_odd()
 
     @pl.when(odd)
     def _():
+        middle, rest = rh_top.shape[0], rh_end.shape[0]
+        parts = [
+            (u_odd.at[pl.ds(0, middle)], rh_top, rl_top),
+            (u_odd.at[pl.ds(middle, rest)], rh_end, rl_end),
+        ]
+        context_pass(parts, c_odd, h_odd, c_out, h_out)
+
+    @pl.when(jnp.logical_not(odd))
+    def _():
+        cols = block_of(cb.shape[0], 256)
+        count = cb.shape[0] // cols
+        chunks = []
+        for j in range(count):
+            at = pl.ds(j * cols, cols)
+            chunks += [(c.at[at], cb.at[at]), (e.at[0, :, at], eb.at[:, at])]
+        copies = load([(w, wb), (u, ub)] + chunks + [(g, gb)], sems)
+        copies[0].wait()
+        copies[1].wait()
+
+        def ready(j):
+            copies[2 + 2 * j].wait()
+            copies[3 + 2 * j].wait()
+
+        grad = vertex_pass(ub, cb, eb, wb[0:1, :], r_high, r_low, ready)
+        copies[-1].wait()
+        u1[...], g1[...] = adagrad(ub[...], gb[...], grad)
+
+
+def first_context(u, c, h, r_high, r_low, c_out, h_out, ub, cb, hb, sems):
+    @pl.when(jnp.logical_not(is_odd()))
+    def _():
         for copy in load([(u, ub), (c, cb), (h, hb)], sems):
             copy.wait()
-        context_pass(ub, cb, hb, r_high_in, r_low_in, c_out, h_out)
-
-    @pl.when(jnp.logical_not(odd))
-    def _():
-        ready, more = load_chunks(u, c, e, w, ub, cb, eb, wb, [(g, gb), (h, hb)], sems)
-        grad = vertex_pass(ub, cb, eb, wb[0:1, :], r_high, r_low, ready)
-        more[0].wait()
-        u1[...], g1[...] = adagrad(ub[...], gb[...], grad)
-        more[1].wait()
-        context_pass(ub, cb, hb, r_high, r_low, c_out, h_out)
-
-
-def second_odd(u1, g1, c, h, e, w, u2, s2, c_out, h_out, r_high, r_low):
+        context_pass([(ub, r_high, r_low)], cb, hb, c_out, h_out)
+
+
+def second_odd(u1, g1, c, e, w, u2, s2, r_high, r_low):
     @pl.when(is_odd())
     def _():
         grad = vertex_pass(u1, c, e.at[1], w[1:2, :], r_high, r_low)
         value, moment = adagrad(u1[...], g1[...], grad)
         u2[...] = value
         s2[0], s2[1] = value, moment
-        context_pass(u1, c, h, r_high, r_low, c_out, h_out)
-
-
-def second_even(s1, c, h, e, w, after, grad_out, u2_top, u2_end, c_out, h_out, r_high, r_low):
+
+
+def second_even(
+    s1_top, s1_end, c, e, w, after, u_odd, c_odd, h_odd, rh_odd, rl_odd,
+    grad_out, u2_top, u2_end, u1, r_high, r_low, c_out, h_out,
+):
+    odd = is_odd()
+
+    @pl.when(odd)
+    def _():
+        context_pass([(u_odd, rh_odd, rl_odd)], c_odd, h_odd, c_out, h_out)
+
+    @pl.when(jnp.logical_not(odd))
+    def _():
+        middle = s1_top.shape[1]
+        u1[:middle, :] = s1_top[0]
+        u1[middle:, :] = s1_end[0]
+        grad = vertex_pass(u1, c, e.at[1], w[1:2, :], r_high, r_low)
+        grad_out[...] = grad
+        moment = jnp.concatenate([s1_top[1], s1_end[1]], axis=0)
+        value = adagrad(u1[...], moment, grad)[0]
+        half = u2_top.shape[0]
+        u2_top[...], u2_end[...] = value[:half], value[half:]
+
+
+def second_context(u, c, h, r_high, r_low, c_out, h_out):
     @pl.when(jnp.logical_not(is_odd()))
     def _():
-        grad = vertex_pass(s1.at[0], c, e.at[1], w[1:2, :], r_high, r_low)
-        grad_out[...] = grad
-        value = adagrad(s1[0], s1[1], grad)[0]
-        middle = u2_top.shape[0]
-        u2_top[...], u2_end[...] = value[:middle], value[middle:]
-        context_pass(s1.at[0], c, h, r_high, r_low, c_out, h_out)
+        context_pass([(u, r_high, r_low)], c, h, c_out, h_out)
 
 
 def third(odd, u, c, e, w, after, g2, r_high, r_low):
@@ -191,20 +243,22 @@
 
     @pl.when(odd)
     def _():
-        context_pass(u_odd, c_odd, h_odd, rh_odd, rl_odd, c_out, h_out)
+        context_pass([(u_odd, rh_odd, rl_odd)], c_odd, h_odd, c_out, h_out)
 
     @pl.when(jnp.logical_not(odd))
     def _():
-        context_pass(u_even, c_even, h_even, rh_even, rl_even, c_out, h_out)
-
-
-def last(s1, g1, g2_odd, s2, g2_even, u_out, g_out):
+        context_pass([(u_even, rh_even, rl_even)], c_even, h_even, c_out, h_out)
+
+
+def last(s1_top, s1_end, g1, g2_odd, s2, g2_even, u_out, g_out):
     odd = is_odd()
 
     @pl.when(odd)
     def _():
-        value, moment = adagrad(s1[0], s1[1], g1[...])
-        u_out[...], g_out[...] = adagrad(value, moment, g2_odd[...])
+        middle, rest = s1_top.shape[1], s1_end.shape[1]
+        for s1, at in ((s1_top, pl.ds(0, middle)), (s1_end, pl.ds(middle, rest))):
+            value, moment = adagrad(s1[0], s1[1], g1[at, :])
+            u_out[at, :], g_out[at, :] = adagrad(value, moment, g2_odd[at, :])
 
     @pl.when(jnp.logical_not(odd))
     def _():
@@ -245,27 +299,42 @@
         for x in (vertices, vertex_moments, contexts, context_moments, edge_counts, negative_weights)
     ]
 
-    s1o, rh0, rl0 = call(
-        first_odd, [HBM] * 5, [pair, half, half],
+    def stage(rows):
+        return [f32(2, rows, width)] + [jax.ShapeDtypeStruct((rows, ncols), BF16)] * 2
+
+    early = EARLY * nrows // 64 * 16
+    edges = jax.ShapeDtypeStruct((nrows, ncols), jnp.int32)
+    weights = jax.ShapeDtypeStruct(negative_weights.shape, jnp.int32)
+    s1t, rht, rlt, ub, gb, cb, hb, eb, wb = call(
+        first_top, [HBM] * 6, stage(early) + [block, block, ctx, ctx, edges, weights], [sems], hbm, "first_top",
+    )
+    s1tx = move(s1t, ring)
+    s1d, rhd, rld = call(
+        first_end, [VMEM] * 5, stage(nrows - early), [], (ub, gb, cb, eb, wb), "first_end",
+    )
+    s1dx = move(s1d, ring)
+    *s1, rhe0, rle0, c1o, h1o = call(
+        first_even, [HBM] * 5 + [VMEM] * 7, [block, block, half, half, ctx, ctx],
         [vert_buf, vert_buf, ctx_buf, edge_buf, weight_buf, sems],
-        (*hbm[:3], *hbm[4:]), "first_odd",
-    )
-    s1x = move(s1o, ring)
-    *s1, c1, h1 = call(
-        first_rest, [HBM] * 6 + [VMEM] * 2, [block, block, ctx, ctx],
-        [vert_buf, vert_buf, ctx_buf, ctx_buf, edge_buf, weight_buf, half_buf, half_buf, sems],
-        (*hbm, rh0, rl0), "first_rest",
+        (*hbm[:3], *hbm[4:], ub, cb, hb, rht, rlt, rhd, rld), "first_even",
     )
     s1i = [move(x, swap) for x in s1]
-    u2e, s2e, c2o, h2o = call(
-        second_odd, [VMEM] * 6, [block, pair, ctx, ctx], [half_buf, half_buf],
-        (*s1i, c1, h1, edge_counts, negative_weights), "second_odd",
+    c1e, h1e = call(
+        first_context, [HBM] * 3 + [VMEM] * 2, [ctx, ctx], [vert_buf, ctx_buf, ctx_buf, sems],
+        (hbm[0], hbm[2], hbm[3], rhe0, rle0), "first_context",
+    )
+    u2e, s2e, rho1, rlo1 = call(
+        second_odd, [VMEM] * 5, [block, pair, half, half], [],
+        (*s1i, c1o, edge_counts, negative_weights), "second_odd",
     )
     u2x = move(u2e, ring)
     s2h = move(s2e, swap)
-    g1, u2t, u2d, c2e, h2e = call(
-        second_even, [VMEM] * 5 + [ANY], [block, part, part, ctx, ctx], [half_buf, half_buf],
-        (s1x, c1, h1, edge_counts, negative_weights, u2e), "second_even",
+    g1, u2t, u2d, u1v, rhe1, rle1, c2o, h2o = call(
+        second_even, [VMEM] * 5 + [ANY] + [VMEM] * 5, [block, part, part, block, half, half, ctx, ctx], [],
+        (s1tx, s1dx, c1e, edge_counts, negative_weights, u2e, s1i[0], c1o, h1o, rho1, rlo1), "second_even",
+    )
+    c2e, h2e = call(
+        second_context, [VMEM] * 5, [ctx, ctx], [], (u1v, c1e, h1e, rhe1, rle1), "second_context",
     )
     g1x = move(g1, unring)
     u2ti = move(u2t, swap)
@@ -284,7 +353,7 @@
         third_context, [VMEM] * 10, [ctx, ctx], [],
         (u2i, c2o, h2o, rho, rlo, u2x, c2e, h2e, rhe, rle), "third_context",
     )
-    u3, g3 = call(last, [VMEM] * 5, [block, block], [], (s1o, g1x, g2xo, s2h, g2xe), "last")
+    u3, g3 = call(last, [VMEM] * 6, [block, block], [], (s1t, s1d, g1x, g2xo, s2h, g2xe), "last")
     return u3, g3, c3, h3
 
 

time: 47.7 us -> 46.6 us (0.977)
  waiting for transfers between devices: 19.8 us -> 16.3 us
  Pallas kernels: 14.7 us -> 17.1 us
    ppermute x10 -> x11, waiting for transfers between devices: 19.8 us -> 16.3 us  [move(): return lax.ppermute(value, 'inner', pairs)]
    pallas_call x8 -> x11, Pallas kernels: 14.7 us -> 17.1 us  [call(): pl.pallas_call(body, out_shape=outs, in_specs=in_specs, out_specs=[VMEM]...]
    ppermute x10 -> x11, starting transfers between devices: 12.2 us -> 12.2 us  [move(): return lax.ppermute(value, 'inner', pairs)]
  transfers between devices with their start and end apart: 10 -> 11, of which waited for: 7 -> 5; matrix products, arithmetic and copies ran while one was open for 0% -> 0% of each run, Pallas kernels for 28% -> 34%
where the time goes in v4:
time: 46.6 us; the launch traced here: 46.4 us
  Pallas kernels  17.1 us (37%)
  waiting for transfers between devices  16.3 us (35%)
  starting transfers between devices  12.2 us (26%)
  between operations  0.77 us (2%)
    pallas_call x11, Pallas kernels, call(): pl.pallas_call(body, out_shape=outs, in_specs=in_specs, out_specs=[VMEM]...  17.1 us
    ppermute x11, waiting for transfers between devices, move(): return lax.ppermute(value, 'inner', pairs)  16.3 us
    ppermute x11, starting transfers between devices, move(): return lax.ppermute(value, 'inner', pairs)  12.2 us
  transfers between devices with their start and end apart: 11, of which 5 were waited for; matrix products, arithmetic and copies ran while one was open for 0% of the time, Pallas kernels for 34%

profile of v4, /device:TPU:0, one launch (start us, length us, event | category | flops | bytes accessed | tf_op | source)
XLA Modules:
  0.0 46.4 jit_solution(167375293008708189)
XLA Ops:
  0.6 0.1 first_top.1
  0.8 4.0 %collective-permute-start = (f32[2,384,256]{2,1,0:T(8,128)S(1)}, f32[2,384,256]{2,1,0:T(8,128)S(1)}, u32[]{:S(2)}, u32[]{:S(2)}) collective-permute-start(f32[2,384,256]{2,1,0:T(8,128)S(1)} %get-tuple-element.49.s1_top), channel_id=1, source_target_pairs={{0,1},{1,2},{2,3},{3,4},{4,5},{5,6},{6,7},{7,8},{8,9},{9,10},{10,1... | collective-permute-start | bytes 2359304 | tf_op jit(solution)/shard_map/ppermute | solution.py:281
  4.8 0.0 slice-start
  4.8 0.0 slice-start.1
  4.8 0.0 copy-start
  4.8 4.5 %first_even.1 = (f32[512,256]{1,0:T(8,128)S(1)}, f32[512,256]{1,0:T(8,128)S(1)}, bf16[512,1024]{1,0:T(8,128)(2,1)S(1)}, bf16[512,1024]{1,0:T(8,128)(2,1)S(1)}, f...) custom-call(f32[512,256]{1,0:T(8,128)} %u.5, f32[512,256]{1,0:T(8,128)} %g.3, f32[1024,256]{1,0:T(8,128)} %c.5, ...), custom_call_target="tpu_custom_call" | custom-call | flops 1024 | bytes 1024 | tf_op jit(solution)/shard_map/first_even/pallas_call | solution.py:83
  9.3 0.1 collective-permute-start.2
  9.4 0.5 %collective-permute-start.3 = (f32[512,256]{1,0:T(8,128)S(1)}, f32[512,256]{1,0:T(8,128)S(1)}, u32[]{:S(2)}, u32[]{:S(2)}) collective-permute-start(f32[512,256]{1,0:T(8,128)S(1)} %get-tuple-element.65), channel_id=1, source_target_pairs={{0,1},{1,0},{2,3},{3,2},{4,5},{5,4},{6,7},{7,6},{8,9},{9,8},{10,11... | collective-permute-start | bytes 1572872 | tf_op jit(solution)/shard_map/ppermute | solution.py:281
  9.9 0.1 collective-permute-start.1
  10.0 1.3 %collective-permute-done.2.u1.u_odd = f32[512,256]{1,0:T(8,128)S(1)} collective-permute-done((f32[512,256]{1,0:T(8,128)S(1)}, f32[512,256]{1,0:T(8,128)S(1)}, u32[]{:S(2)}, u32[]{:S(2)}) %collective-permute-start.2) | collective-permute-done | bytes 524320 | tf_op jit(solution)/shard_map/ppermute | solution.py:281
  11.3 0.7 %collective-permute-done.3.g1 = f32[512,256]{1,0:T(8,128)S(1)} collective-permute-done((f32[512,256]{1,0:T(8,128)S(1)}, f32[512,256]{1,0:T(8,128)S(1)}, u32[]{:S(2)}, u32[]{:S(2)}) %collective-permute-start.3) | collective-permute-done | bytes 524320 | tf_op jit(solution)/shard_map/ppermute | solution.py:281
  12.1 0.0 slice-done
  12.1 0.0 slice-done.1
  12.1 0.0 copy-done
  12.1 2.7 %collective-permute-start.9 = (f32[512,256]{1,0:T(8,128)S(1)}, f32[512,256]{1,0:T(8,128)S(1)}, u32[]{:S(2)}, u32[]{:S(2)}) collective-permute-start(f32[512,256]{1,0:T(8,128)S(1)} %get-tuple-element.67.after), channel_id=1, source_target_pairs={{0,1},{1,2},{2,3},{3,4},{4,5},{5,6},{6,7},{7,8},{8,9},{9,10},{10,1... | collective-permute-start | bytes 1572872 | tf_op jit(solution)/shard_map/ppermute | solution.py:281
  14.8 0.1 collective-permute-start.8
  14.9 3.0 %first_context.1 = (f32[1024,256]{1,0:T(8,128)S(1)}, f32[1024,256]{1,0:T(8,128)S(1)}) custom-call(f32[512,256]{1,0:T(8,128)} %u.5, f32[1024,256]{1,0:T(8,128)} %c.5, f32[1024,256]{1,0:T(8,128)} %h.3, bf16[512,1024]{1,0:T(8,128)(2,1)S(1)} %get-tuple-element.61.r_high, bf16[512,1024]{1,0:T(8,128)(2,1)S(1)} %get-tuple-element.62.r_low), custom_call_target="tpu_custom_call" | custom-call | flops 1024 | bytes 1024 | tf_op jit(solution)/shard_map/first_context/pallas_call | solution.py:83
  17.9 4.4 %collective-permute-done.1.s1_end = f32[2,128,256]{2,1,0:T(8,128)S(1)} collective-permute-done((f32[2,128,256]{2,1,0:T(8,128)S(1)}, f32[2,128,256]{2,1,0:T(8,128)S(1)}, u32[]{:S(2)}, u32[]{:S(2)}) %collective-permute-start.1) | collective-permute-done | bytes 262176 | tf_op jit(solution)/shard_map/ppermute | solution.py:281
  22.3 0.0 collective-permute-done.s1_top
  22.3 2.3 %second_even.1 = (f32[512,256]{1,0:T(8,128)S(1)}, f32[256,256]{1,0:T(8,128)S(1)}, f32[256,256]{1,0:T(8,128)S(1)}, f32[512,256]{1,0:T(8,128)S(1)}, bf16[512,1024]...) custom-call(f32[2,384,256]{2,1,0:T(8,128)S(1)} %collective-permute-done.s1_t, ...), custom_call_target="tpu_custom_call" | custom-call | flops 1024 | bytes 1024 | tf_op jit(solution)/shard_map/second_even/pallas_call | solution.py:83
  24.6 0.1 collective-permute-start.6
  24.7 0.5 %collective-permute-start.5 = (f32[256,256]{1,0:T(8,128)S(1)}, f32[256,256]{1,0:T(8,128)S(1)}, u32[]{:S(2)}, u32[]{:S(2)}) collective-permute-start(f32[256,256]{1,0:T(8,128)S(1)} %get-tuple-element.72.after), channel_id=1, source_target_pairs={{0,1},{1,0},{2,3},{3,2},{4,5},{5,4},{6,7},{7,6},{8,9},{9,8},{10,11... | collective-permute-start | bytes 786440 | tf_op jit(solution)/shard_map/ppermute | solution.py:281
  25.2 0.7 %collective-permute-start.4 = (f32[512,256]{1,0:T(8,128)S(1)}, f32[512,256]{1,0:T(8,128)S(1)}, u32[]{:S(2)}, u32[]{:S(2)}) collective-permute-start(f32[512,256]{1,0:T(8,128)S(1)} %get-tuple-element.71), channel_id=1, source_target_pairs={{1,0},{2,1},{3,2},{4,3},{5,4},{6,5},{7,6},{8,7},{9,8},{10,9},{11,1... | collective-permute-start | bytes 1572872 | tf_op jit(solution)/shard_map/ppermute | solution.py:281
  25.9 1.2 %second_context.1 = (f32[1024,256]{1,0:T(8,128)S(1)}, f32[1024,256]{1,0:T(8,128)S(1)}) custom-call(f32[512,256]{1,0:T(8,128)S(1)} %get-tuple-element.77.u, f32[1024,256]{1,0:T(8,128)S(1)} %get-tuple-element.63.c, f32[1024,256]{1,0:T(8,128)S(1)} %get-tuple-element.78.h, bf16[512,1024]{1,0:T(8,128)(2,1)S(1)} %get-tuple-element.79.r_high, ...), custom_call_target="tpu_custom_call" | custom-call | flops 1024 | bytes 1024 | tf_op jit(solution)/shard_map/second_context/pallas_call | solution.py:83
  27.0 0.0 collective-permute-done.6.u_end
  27.1 0.0 collective-permute-done.5.u_top
  27.1 0.7 %collective-permute-start.7 = (f32[512,256]{1,0:T(8,128)S(1)}, f32[512,256]{1,0:T(8,128)S(1)}, u32[]{:S(2)}, u32[]{:S(2)}) collective-permute-start(f32[512,256]{1,0:T(8,128)S(1)} %get-tuple-element.75.refs_4_), channel_id=1, source_target_pairs={{0,0},{1,15},{2,2},{3,1},{4,4},{5,3},{6,6},{7,5},{8,8},{9,7},{10,1... | collective-permute-start | bytes 1572872 | tf_op jit(solution)/shard_map/ppermute | solution.py:281
  27.8 0.1 collective-permute-done.9.refs_0_.u_even
  27.9 2.3 %third_even.1 = (f32[512,256]{1,0:T(8,128)S(1)}, bf16[512,1024]{1,0:T(8,128)(2,1)S(1)}, bf16[512,1024]{1,0:T(8,128)(2,1)S(1)}) custom-call(f32[512,256]{1,0:T(8,128)S(1)} %collective-permute-done.9.refs_0_.u_even, f32[1024,256]{1,0:T(8,128)S(1)} %get-tuple-element.81.refs_1_.c_even, s32[3,512,1024]{2,1,0:T(8,128)S(1)} %bitcast.1, s32[3,1024]{1,0:T(4,128)S(1)} %copy-done, ...), custom_call_target="tpu_custom_call" | custom-call | flops 1024 | bytes 1024 | tf_op jit(solution)/shard_map/third_even/pallas_call | solution.py:83
  30.2 2.8 %collective-permute-start.10 = (f32[512,256]{1,0:T(8,128)S(1)}, f32[512,256]{1,0:T(8,128)S(1)}, u32[]{:S(2)}, u32[]{:S(2)}) collective-permute-start(f32[512,256]{1,0:T(8,128)S(1)} %get-tuple-element.82), channel_id=1, source_target_pairs={{0,14},{1,1},{2,0},{3,3},{4,2},{5,5},{6,4},{7,7},{8,6},{9,9},{10,8... | collective-permute-start | bytes 1572872 | tf_op jit(solution)/shard_map/ppermute | solution.py:281
  33.0 2.5 %third_context.1 = (f32[1024,256]{1,0:T(8,128)}, f32[1024,256]{1,0:T(8,128)}) custom-call(f32[512,256]{1,0:T(8,128)S(1)} %get-tuple-element.85.u_odd, f32[1024,256]{1,0:T(8,128)S(1)} %get-tuple-element.74.c.c_odd, f32[1024,256]{1,0:T(8,128)S(1)} %get-tuple-element.86.h_odd, bf16[512,1024]{1,0:T(8,128)(2,1)S(1)} %get-tuple-element.87.rh_odd, ...), custom_call_target="tpu_custom_call" | custom-call | flops 1024 | bytes 1024 | tf_op jit(solution)/shard_map/third_context/pallas_call | solution.py:83
  35.5 0.0 collective-permute-done.4.g1
  35.5 0.0 collective-permute-done.8.s2
  35.5 0.0 collective-permute-done.7.g2_odd
  35.5 9.8 %collective-permute-done.10.g2_even = f32[512,256]{1,0:T(8,128)S(1)} collective-permute-done((f32[512,256]{1,0:T(8,128)S(1)}, f32[512,256]{1,0:T(8,128)S(1)}, u32[]{:S(2)}, u32[]{:S(2)}) %collective-permute-start.10) | collective-permute-done | bytes 524320 | tf_op jit(solution)/shard_map/ppermute | solution.py:281
  45.3 1.1 %last.1 = (f32[512,256]{1,0:T(8,128)}, f32[512,256]{1,0:T(8,128)}) custom-call(f32[2,384,256]{2,1,0:T(8,128)S(1)} %get-tuple-element.49.s1_top, f32[2,128,256]{2,1,0:T(8,128)S(1)} %get-tuple-element.55.s1_end, f32[512,256]{1,0:T(8,128)S(1)} %collective-permute-done.4.g1, f32[512,256]{1,0:T(8,128)S(1)} %collective-permute-done.7.g2_odd, ...), custom_call_target="tpu_custom_call" | custom-call | flops 1024 | bytes 1024 | tf_op jit(solution)/shard_map/last/pallas_call | solution.py:83
  (4 shorter events, 0.1 us)
Async XLA Ops:
  0.8 21.5 %collective-permute-start = (f32[2,384,256]{2,1,0:T(8,128)S(1)}, f32[2,384,256]{2,1,0:T(8,128)S(1)}, u32[]{:S(2)}, u32[]{:S(2)}) collective-permute-start(f32[2,384,256]{2,1,0:T(8,128)S(1)} %get-tuple-element.49.s1_top), channel_id=1, source_target_pairs={{0,1},{1,2},{2,3},{3,4},{4,5},{5,6},{6,7},{7,8},{8,9},{9,10},{10,1... | collective-permute-start | bytes 2359304 | tf_op jit(solution)/shard_map/ppermute | solution.py:281
  4.8 7.2 %slice-start = ((s8[6291456]{0:T(1024)(128)(4,1)}), s8[4194304]{0:T(1024)(128)(4,1)S(1)}, s32[]{:S(2)}) async-start(s8[6291456]{0:T(1024)(128)(4,1)} %bitcast), calls=%async_computation | async-start | bytes 8388608
  4.8 7.2 %slice-start.1 = ((s8[6291456]{0:T(1024)(128)(4,1)}), s8[2097152]{0:T(1024)(128)(4,1)S(1)}, s32[]{:S(2)}) async-start(s8[6291456]{0:T(1024)(128)(4,1)} %bitcast), calls=%async_computation.1 | async-start | bytes 4194304
  4.8 7.2 %copy-start = (s32[3,1024]{1,0:T(4,128)S(1)}, s32[3,1024]{1,0:T(4,128)}, u32[]{:S(2)}) copy-start(s32[3,1024]{1,0:T(4,128)} %refs_3_.1) | copy-start | bytes 36868
  9.3 2.0 %collective-permute-start.2 = (f32[512,256]{1,0:T(8,128)S(1)}, f32[512,256]{1,0:T(8,128)S(1)}, u32[]{:S(2)}, u32[]{:S(2)}) collective-permute-start(f32[512,256]{1,0:T(8,128)S(1)} %get-tuple-element.64), channel_id=1, source_target_pairs={{0,1},{1,0},{2,3},{3,2},{4,5},{5,4},{6,7},{7,6},{8,9},{9,8},{10,11... | collective-permute-start | bytes 1572872 | tf_op jit(solution)/shard_map/ppermute | solution.py:281
  9.4 2.6 %collective-permute-start.3 = (f32[512,256]{1,0:T(8,128)S(1)}, f32[512,256]{1,0:T(8,128)S(1)}, u32[]{:S(2)}, u32[]{:S(2)}) collective-permute-start(f32[512,256]{1,0:T(8,128)S(1)} %get-tuple-element.65), channel_id=1, source_target_pairs={{0,1},{1,0},{2,3},{3,2},{4,5},{5,4},{6,7},{7,6},{8,9},{9,8},{10,11... | collective-permute-start | bytes 1572872 | tf_op jit(solution)/shard_map/ppermute | solution.py:281
  9.9 12.4 %collective-permute-start.1 = (f32[2,128,256]{2,1,0:T(8,128)S(1)}, f32[2,128,256]{2,1,0:T(8,128)S(1)}, u32[]{:S(2)}, u32[]{:S(2)}) collective-permute-start(f32[2,128,256]{2,1,0:T(8,128)S(1)} %get-tuple-element.55.s1_end), channel_id=1, source_target_pairs={{0,1},{1,2},{2,3},{3,4},{4,5},{5,6},{6,7},{7,8},{8,9},{9,10},{10,1... | collective-permute-start | bytes 786440 | tf_op jit(solution)/shard_map/ppermute | solution.py:281
  12.1 15.8 %collective-permute-start.9 = (f32[512,256]{1,0:T(8,128)S(1)}, f32[512,256]{1,0:T(8,128)S(1)}, u32[]{:S(2)}, u32[]{:S(2)}) collective-permute-start(f32[512,256]{1,0:T(8,128)S(1)} %get-tuple-element.67.after), channel_id=1, source_target_pairs={{0,1},{1,2},{2,3},{3,4},{4,5},{5,6},{6,7},{7,8},{8,9},{9,10},{10,1... | collective-permute-start | bytes 1572872 | tf_op jit(solution)/shard_map/ppermute | solution.py:281
  14.8 20.7 %collective-permute-start.8 = (f32[2,512,256]{2,1,0:T(8,128)S(1)}, f32[2,512,256]{2,1,0:T(8,128)S(1)}, u32[]{:S(2)}, u32[]{:S(2)}) collective-permute-start(f32[2,512,256]{2,1,0:T(8,128)S(1)} %get-tuple-element.76), channel_id=1, source_target_pairs={{0,1},{1,0},{2,3},{3,2},{4,5},{5,4},{6,7},{7,6},{8,9},{9,8},{10,11... | collective-permute-start | bytes 3145736 | tf_op jit(solution)/shard_map/ppermute | solution.py:281
  24.6 2.4 %collective-permute-start.6 = (f32[256,256]{1,0:T(8,128)S(1)}, f32[256,256]{1,0:T(8,128)S(1)}, u32[]{:S(2)}, u32[]{:S(2)}) collective-permute-start(f32[256,256]{1,0:T(8,128)S(1)} %get-tuple-element.73), channel_id=1, source_target_pairs={{0,1},{1,0},{2,3},{3,2},{4,5},{5,4},{6,7},{7,6},{8,9},{9,8},{10,11... | collective-permute-start | bytes 786440 | tf_op jit(solution)/shard_map/ppermute | solution.py:281
  24.7 2.4 %collective-permute-start.5 = (f32[256,256]{1,0:T(8,128)S(1)}, f32[256,256]{1,0:T(8,128)S(1)}, u32[]{:S(2)}, u32[]{:S(2)}) collective-permute-start(f32[256,256]{1,0:T(8,128)S(1)} %get-tuple-element.72.after), channel_id=1, source_target_pairs={{0,1},{1,0},{2,3},{3,2},{4,5},{5,4},{6,7},{7,6},{8,9},{9,8},{10,11... | collective-permute-start | bytes 786440 | tf_op jit(solution)/shard_map/ppermute | solution.py:281
  25.2 10.3 %collective-permute-start.4 = (f32[512,256]{1,0:T(8,128)S(1)}, f32[512,256]{1,0:T(8,128)S(1)}, u32[]{:S(2)}, u32[]{:S(2)}) collective-permute-start(f32[512,256]{1,0:T(8,128)S(1)} %get-tuple-element.71), channel_id=1, source_target_pairs={{1,0},{2,1},{3,2},{4,3},{5,4},{6,5},{7,6},{8,7},{9,8},{10,9},{11,1... | collective-permute-start | bytes 1572872 | tf_op jit(solution)/shard_map/ppermute | solution.py:281
  27.1 8.4 %collective-permute-start.7 = (f32[512,256]{1,0:T(8,128)S(1)}, f32[512,256]{1,0:T(8,128)S(1)}, u32[]{:S(2)}, u32[]{:S(2)}) collective-permute-start(f32[512,256]{1,0:T(8,128)S(1)} %get-tuple-element.75.refs_4_), channel_id=1, source_target_pairs={{0,0},{1,15},{2,2},{3,1},{4,4},{5,3},{6,6},{7,5},{8,8},{9,7},{10,1... | collective-permute-start | bytes 1572872 | tf_op jit(solution)/shard_map/ppermute | solution.py:281
  30.2 15.1 %collective-permute-start.10 = (f32[512,256]{1,0:T(8,128)S(1)}, f32[512,256]{1,0:T(8,128)S(1)}, u32[]{:S(2)}, u32[]{:S(2)}) collective-permute-start(f32[512,256]{1,0:T(8,128)S(1)} %get-tuple-element.82), channel_id=1, source_target_pairs={{0,14},{1,1},{2,0},{3,3},{4,2},{5,5},{6,4},{7,7},{8,6},{9,9},{10,8... | collective-permute-start | bytes 1572872 | tf_op jit(solution)/shard_map/ppermute | solution.py:281

commit v5 on v4

--- a/solution.py
+++ b/solution.py
@@ -234,8 +234,12 @@
     third(True, u, c, e, w, after, *refs)
 
 
-def third_even(*refs):
-    third(False, *refs)
+def third_even(u, c, e, w, g2_odd, g2, r_high, r_low):
+    @pl.when(is_odd())
+    def _():
+        g2[...] = g2_odd[...]
+
+    third(False, u, c, e, w, g2_odd, g2, r_high, r_low)
 
 
 def third_context(u_odd, c_odd, h_odd, rh_odd, rl_odd, u_even, c_even, h_even, rh_even, rl_even, c_out, h_out):
@@ -250,7 +254,7 @@
         context_pass([(u_even, rh_even, rl_even)], c_even, h_even, c_out, h_out)
 
 
-def last(s1_top, s1_end, g1, g2_odd, s2, g2_even, u_out, g_out):
+def last(s1_top, s1_end, g1, s2, g2, u_out, g_out):
     odd = is_odd()
 
     @pl.when(odd)
@@ -258,11 +262,11 @@
         middle, rest = s1_top.shape[1], s1_end.shape[1]
         for s1, at in ((s1_top, pl.ds(0, middle)), (s1_end, pl.ds(middle, rest))):
             value, moment = adagrad(s1[0], s1[1], g1[at, :])
-            u_out[at, :], g_out[at, :] = adagrad(value, moment, g2_odd[at, :])
+            u_out[at, :], g_out[at, :] = adagrad(value, moment, g2[at, :])
 
     @pl.when(jnp.logical_not(odd))
     def _():
-        u_out[...], g_out[...] = adagrad(s2[0], s2[1], g2_even[...])
+        u_out[...], g_out[...] = adagrad(s2[0], s2[1], g2[...])
 
 
 def per_device(vertices, vertex_moments, contexts, context_moments, edge_counts, negative_weights):
@@ -274,8 +278,7 @@
     ring = [(i, (i + 1) % count) for i in range(count)]
     unring = [(b, a) for a, b in ring]
     swap = [(i, i ^ 1) for i in range(count)]
-    home_odd = [(i, (i - 2) % count if i % 2 else i) for i in range(count)]
-    home_even = [(i, i if i % 2 else (i - 2) % count) for i in range(count)]
+    home = [(i, (i - 2) % count) for i in range(count)]
 
     def move(value, pairs):
         return lax.ppermute(value, "inner", pairs)
@@ -343,17 +346,16 @@
         third_odd, [VMEM] * 5 + [ANY], [block, block, half, half], [],
         (u2ti, u2di, c2o, edge_counts, negative_weights, u2t), "third_odd",
     )
-    g2xo = move(g2o, home_odd)
-    g2e, rhe, rle = call(
-        third_even, [VMEM] * 4 + [ANY], [block, half, half], [],
+    g2, rhe, rle = call(
+        third_even, [VMEM] * 5, [block, half, half], [],
         (u2x, c2e, edge_counts, negative_weights, g2o), "third_even",
     )
-    g2xe = move(g2e, home_even)
+    g2x = move(g2, home)
     c3, h3 = call(
         third_context, [VMEM] * 10, [ctx, ctx], [],
         (u2i, c2o, h2o, rho, rlo, u2x, c2e, h2e, rhe, rle), "third_context",
     )
-    u3, g3 = call(last, [VMEM] * 6, [block, block], [], (s1t, s1d, g1x, g2xo, s2h, g2xe), "last")
+    u3, g3 = call(last, [VMEM] * 5, [block, block], [], (s1t, s1d, g1x, s2h, g2x), "last")
     return u3, g3, c3, h3
 
 

time: 46.6 us -> 46.5 us (level)
  waiting for transfers between devices: 16.3 us -> 19.3 us
  starting transfers between devices: 12.2 us -> 9.26 us
    ppermute x11 -> x10, waiting for transfers between devices: 16.3 us -> 19.3 us  [move(): return lax.ppermute(value, 'inner', pairs)]
    ppermute x11 -> x10, starting transfers between devices: 12.2 us -> 9.26 us  [move(): return lax.ppermute(value, 'inner', pairs)]
  transfers between devices with their start and end apart: 11 -> 10, of which waited for: 5 -> 6; matrix products, arithmetic and copies ran while one was open for 0% -> 0% of each run, Pallas kernels for 34% -> 34%
where the time goes in v5:
time: 46.5 us; the launch traced here: 46.4 us
  waiting for transfers between devices  19.3 us (42%)
  Pallas kernels  17.1 us (37%)
  starting transfers between devices  9.26 us (20%)
  between operations  0.75 us (2%)
    ppermute x10, waiting for transfers between devices, move(): return lax.ppermute(value, 'inner', pairs)  19.3 us
    pallas_call x11, Pallas kernels, call(): pl.pallas_call(body, out_shape=outs, in_specs=in_specs, out_specs=[VMEM]...  17.1 us
    ppermute x10, starting transfers between devices, move(): return lax.ppermute(value, 'inner', pairs)  9.26 us
  transfers between devices with their start and end apart: 10, of which 6 were waited for; matrix products, arithmetic and copies ran while one was open for 0% of the time, Pallas kernels for 34%

profile of v5, /device:TPU:0, one launch (start us, length us, event | category | flops | bytes accessed | tf_op | source)
XLA Modules:
  0.0 46.4 jit_solution(6298737437550492269)
XLA Ops:
  0.6 0.1 first_top.1
  0.8 4.0 %collective-permute-start = (f32[2,384,256]{2,1,0:T(8,128)S(1)}, f32[2,384,256]{2,1,0:T(8,128)S(1)}, u32[]{:S(2)}, u32[]{:S(2)}) collective-permute-start(f32[2,384,256]{2,1,0:T(8,128)S(1)} %get-tuple-element.49.s1_top), channel_id=1, source_target_pairs={{0,1},{1,2},{2,3},{3,4},{4,5},{5,6},{6,7},{7,8},{8,9},{9,10},{10,1... | collective-permute-start | bytes 2359304 | tf_op jit(solution)/shard_map/ppermute | solution.py:284
  4.8 0.0 slice-start
  4.8 0.0 slice-start.1
  4.8 0.0 copy-start
  4.8 4.5 %first_even.1 = (f32[512,256]{1,0:T(8,128)S(1)}, f32[512,256]{1,0:T(8,128)S(1)}, bf16[512,1024]{1,0:T(8,128)(2,1)S(1)}, bf16[512,1024]{1,0:T(8,128)(2,1)S(1)}, f...) custom-call(f32[512,256]{1,0:T(8,128)} %u.5, f32[512,256]{1,0:T(8,128)} %g.3, f32[1024,256]{1,0:T(8,128)} %c.5, ...), custom_call_target="tpu_custom_call" | custom-call | flops 1024 | bytes 1024 | tf_op jit(solution)/shard_map/first_even/pallas_call | solution.py:83
  9.3 0.1 collective-permute-start.2
  9.4 0.5 %collective-permute-start.3 = (f32[512,256]{1,0:T(8,128)S(1)}, f32[512,256]{1,0:T(8,128)S(1)}, u32[]{:S(2)}, u32[]{:S(2)}) collective-permute-start(f32[512,256]{1,0:T(8,128)S(1)} %get-tuple-element.65), channel_id=1, source_target_pairs={{0,1},{1,0},{2,3},{3,2},{4,5},{5,4},{6,7},{7,6},{8,9},{9,8},{10,11... | collective-permute-start | bytes 1572872 | tf_op jit(solution)/shard_map/ppermute | solution.py:284
  9.9 0.1 collective-permute-start.1
  10.0 1.3 %collective-permute-done.2.u1.u_odd = f32[512,256]{1,0:T(8,128)S(1)} collective-permute-done((f32[512,256]{1,0:T(8,128)S(1)}, f32[512,256]{1,0:T(8,128)S(1)}, u32[]{:S(2)}, u32[]{:S(2)}) %collective-permute-start.2) | collective-permute-done | bytes 524320 | tf_op jit(solution)/shard_map/ppermute | solution.py:284
  11.3 0.7 %collective-permute-done.3.g1 = f32[512,256]{1,0:T(8,128)S(1)} collective-permute-done((f32[512,256]{1,0:T(8,128)S(1)}, f32[512,256]{1,0:T(8,128)S(1)}, u32[]{:S(2)}, u32[]{:S(2)}) %collective-permute-start.3) | collective-permute-done | bytes 524320 | tf_op jit(solution)/shard_map/ppermute | solution.py:284
  12.1 0.0 slice-done
  12.1 0.0 slice-done.1
  12.1 0.0 copy-done
  12.1 2.7 %collective-permute-start.6 = (f32[512,256]{1,0:T(8,128)S(1)}, f32[512,256]{1,0:T(8,128)S(1)}, u32[]{:S(2)}, u32[]{:S(2)}) collective-permute-start(f32[512,256]{1,0:T(8,128)S(1)} %get-tuple-element.67.after), channel_id=1, source_target_pairs={{0,1},{1,2},{2,3},{3,4},{4,5},{5,6},{6,7},{7,8},{8,9},{9,10},{10,1... | collective-permute-start | bytes 1572872 | tf_op jit(solution)/shard_map/ppermute | solution.py:284
  14.8 0.1 collective-permute-start.5
  14.9 3.0 %first_context.1 = (f32[1024,256]{1,0:T(8,128)S(1)}, f32[1024,256]{1,0:T(8,128)S(1)}) custom-call(f32[512,256]{1,0:T(8,128)} %u.5, f32[1024,256]{1,0:T(8,128)} %c.5, f32[1024,256]{1,0:T(8,128)} %h.3, bf16[512,1024]{1,0:T(8,128)(2,1)S(1)} %get-tuple-element.61.r_high, bf16[512,1024]{1,0:T(8,128)(2,1)S(1)} %get-tuple-element.62.r_low), custom_call_target="tpu_custom_call" | custom-call | flops 1024 | bytes 1024 | tf_op jit(solution)/shard_map/first_context/pallas_call | solution.py:83
  17.9 4.4 %collective-permute-done.1.s1_end = f32[2,128,256]{2,1,0:T(8,128)S(1)} collective-permute-done((f32[2,128,256]{2,1,0:T(8,128)S(1)}, f32[2,128,256]{2,1,0:T(8,128)S(1)}, u32[]{:S(2)}, u32[]{:S(2)}) %collective-permute-start.1) | collective-permute-done | bytes 262176 | tf_op jit(solution)/shard_map/ppermute | solution.py:284
  22.3 0.0 collective-permute-done.s1_top
  22.3 2.3 %second_even.1 = (f32[512,256]{1,0:T(8,128)S(1)}, f32[256,256]{1,0:T(8,128)S(1)}, f32[256,256]{1,0:T(8,128)S(1)}, f32[512,256]{1,0:T(8,128)S(1)}, bf16[512,1024]...) custom-call(f32[2,384,256]{2,1,0:T(8,128)S(1)} %collective-permute-done.s1_t, ...), custom_call_target="tpu_custom_call" | custom-call | flops 1024 | bytes 1024 | tf_op jit(solution)/shard_map/second_even/pallas_call | solution.py:83
  24.6 0.1 collective-permute-start.8
  24.7 0.5 %collective-permute-start.7 = (f32[256,256]{1,0:T(8,128)S(1)}, f32[256,256]{1,0:T(8,128)S(1)}, u32[]{:S(2)}, u32[]{:S(2)}) collective-permute-start(f32[256,256]{1,0:T(8,128)S(1)} %get-tuple-element.78.after), channel_id=1, source_target_pairs={{0,1},{1,0},{2,3},{3,2},{4,5},{5,4},{6,7},{7,6},{8,9},{9,8},{10,11... | collective-permute-start | bytes 786440 | tf_op jit(solution)/shard_map/ppermute | solution.py:284
  25.2 0.7 %collective-permute-start.4 = (f32[512,256]{1,0:T(8,128)S(1)}, f32[512,256]{1,0:T(8,128)S(1)}, u32[]{:S(2)}, u32[]{:S(2)}) collective-permute-start(f32[512,256]{1,0:T(8,128)S(1)} %get-tuple-element.71), channel_id=1, source_target_pairs={{1,0},{2,1},{3,2},{4,3},{5,4},{6,5},{7,6},{8,7},{9,8},{10,9},{11,1... | collective-permute-start | bytes 1572872 | tf_op jit(solution)/shard_map/ppermute | solution.py:284
  25.9 1.2 %second_context.1 = (f32[1024,256]{1,0:T(8,128)S(1)}, f32[1024,256]{1,0:T(8,128)S(1)}) custom-call(f32[512,256]{1,0:T(8,128)S(1)} %get-tuple-element.73.u, f32[1024,256]{1,0:T(8,128)S(1)} %get-tuple-element.63.c, f32[1024,256]{1,0:T(8,128)S(1)} %get-tuple-element.74.h, bf16[512,1024]{1,0:T(8,128)(2,1)S(1)} %get-tuple-element.75.r_high, ...), custom_call_target="tpu_custom_call" | custom-call | flops 1024 | bytes 1024 | tf_op jit(solution)/shard_map/second_context/pallas_call | solution.py:83
  27.0 0.0 collective-permute-done.8.u_end
  27.1 0.0 collective-permute-done.7.u_top
  27.1 0.8 %collective-permute-done.6.u.u_even = f32[512,256]{1,0:T(8,128)S(1)} collective-permute-done((f32[512,256]{1,0:T(8,128)S(1)}, f32[512,256]{1,0:T(8,128)S(1)}, u32[]{:S(2)}, u32[]{:S(2)}) %collective-permute-start.6) | collective-permute-done | bytes 524320 | tf_op jit(solution)/shard_map/ppermute | solution.py:284
  27.9 2.3 %third_even.1 = (f32[512,256]{1,0:T(8,128)S(1)}, bf16[512,1024]{1,0:T(8,128)(2,1)S(1)}, bf16[512,1024]{1,0:T(8,128)(2,1)S(1)}) custom-call(f32[512,256]{1,0:T(8,128)S(1)} %collective-permute-done.6.u.u_even, f32[1024,256]{1,0:T(8,128)S(1)} %get-tuple-element.77.c.c_even, s32[3,512,1024]{2,1,0:T(8,128)S(1)} %bitcast.1, s32[3,1024]{1,0:T(4,128)S(1)} %copy-done, ...), custom_call_target="tpu_custom_call" | custom-call | flops 1024 | bytes 1024 | tf_op jit(solution)/shard_map/third_even/pallas_call | solution.py:83
  30.2 0.6 %collective-permute-start.9 = (f32[512,256]{1,0:T(8,128)S(1)}, f32[512,256]{1,0:T(8,128)S(1)}, u32[]{:S(2)}, u32[]{:S(2)}) collective-permute-start(f32[512,256]{1,0:T(8,128)S(1)} %get-tuple-element.82), channel_id=1, source_target_pairs={{0,14},{1,15},{2,0},{3,1},{4,2},{5,3},{6,4},{7,5},{8,6},{9,7},{10,... | collective-permute-start | bytes 1572872 | tf_op jit(solution)/shard_map/ppermute | solution.py:284
  30.8 2.5 %third_context.1 = (f32[1024,256]{1,0:T(8,128)}, f32[1024,256]{1,0:T(8,128)}) custom-call(f32[512,256]{1,0:T(8,128)S(1)} %get-tuple-element.85.u_odd, f32[1024,256]{1,0:T(8,128)S(1)} %get-tuple-element.80.c.c_odd, f32[1024,256]{1,0:T(8,128)S(1)} %get-tuple-element.86.h_odd, bf16[512,1024]{1,0:T(8,128)(2,1)S(1)} %get-tuple-element.87.rh_odd, ...), custom_call_target="tpu_custom_call" | custom-call | flops 1024 | bytes 1024 | tf_op jit(solution)/shard_map/third_context/pallas_call | solution.py:83
  33.3 1.5 %collective-permute-done.4.g1 = f32[512,256]{1,0:T(8,128)S(1)} collective-permute-done((f32[512,256]{1,0:T(8,128)S(1)}, f32[512,256]{1,0:T(8,128)S(1)}, u32[]{:S(2)}, u32[]{:S(2)}) %collective-permute-start.4) | collective-permute-done | bytes 524320 | tf_op jit(solution)/shard_map/ppermute | solution.py:284
  34.8 0.0 collective-permute-done.5.s2
  34.8 10.5 %collective-permute-done.9.g2 = f32[512,256]{1,0:T(8,128)S(1)} collective-permute-done((f32[512,256]{1,0:T(8,128)S(1)}, f32[512,256]{1,0:T(8,128)S(1)}, u32[]{:S(2)}, u32[]{:S(2)}) %collective-permute-start.9) | collective-permute-done | bytes 524320 | tf_op jit(solution)/shard_map/ppermute | solution.py:284
  45.3 1.1 %last.1 = (f32[512,256]{1,0:T(8,128)}, f32[512,256]{1,0:T(8,128)}) custom-call(f32[2,384,256]{2,1,0:T(8,128)S(1)} %get-tuple-element.49.s1_top, f32[2,128,256]{2,1,0:T(8,128)S(1)} %get-tuple-element.55.s1_end, f32[512,256]{1,0:T(8,128)S(1)} %collective-permute-done.4.g1, f32[2,512,256]{2,1,0:T(8,128)S(1)} %collective-permute-done.5.s2, ...), custom_call_target="tpu_custom_call" | custom-call | flops 1024 | bytes 1024 | tf_op jit(solution)/shard_map/last/pallas_call | solution.py:83
  (4 shorter events, 0.1 us)
Async XLA Ops:
  0.8 21.5 %collective-permute-start = (f32[2,384,256]{2,1,0:T(8,128)S(1)}, f32[2,384,256]{2,1,0:T(8,128)S(1)}, u32[]{:S(2)}, u32[]{:S(2)}) collective-permute-start(f32[2,384,256]{2,1,0:T(8,128)S(1)} %get-tuple-element.49.s1_top), channel_id=1, source_target_pairs={{0,1},{1,2},{2,3},{3,4},{4,5},{5,6},{6,7},{7,8},{8,9},{9,10},{10,1... | collective-permute-start | bytes 2359304 | tf_op jit(solution)/shard_map/ppermute | solution.py:284
  4.8 7.2 %slice-start = ((s8[6291456]{0:T(1024)(128)(4,1)}), s8[4194304]{0:T(1024)(128)(4,1)S(1)}, s32[]{:S(2)}) async-start(s8[6291456]{0:T(1024)(128)(4,1)} %bitcast), calls=%async_computation | async-start | bytes 8388608
  4.8 7.2 %slice-start.1 = ((s8[6291456]{0:T(1024)(128)(4,1)}), s8[2097152]{0:T(1024)(128)(4,1)S(1)}, s32[]{:S(2)}) async-start(s8[6291456]{0:T(1024)(128)(4,1)} %bitcast), calls=%async_computation.1 | async-start | bytes 4194304
  4.8 7.2 %copy-start = (s32[3,1024]{1,0:T(4,128)S(1)}, s32[3,1024]{1,0:T(4,128)}, u32[]{:S(2)}) copy-start(s32[3,1024]{1,0:T(4,128)} %w.11) | copy-start | bytes 36868
  9.3 2.0 %collective-permute-start.2 = (f32[512,256]{1,0:T(8,128)S(1)}, f32[512,256]{1,0:T(8,128)S(1)}, u32[]{:S(2)}, u32[]{:S(2)}) collective-permute-start(f32[512,256]{1,0:T(8,128)S(1)} %get-tuple-element.64), channel_id=1, source_target_pairs={{0,1},{1,0},{2,3},{3,2},{4,5},{5,4},{6,7},{7,6},{8,9},{9,8},{10,11... | collective-permute-start | bytes 1572872 | tf_op jit(solution)/shard_map/ppermute | solution.py:284
  9.4 2.6 %collective-permute-start.3 = (f32[512,256]{1,0:T(8,128)S(1)}, f32[512,256]{1,0:T(8,128)S(1)}, u32[]{:S(2)}, u32[]{:S(2)}) collective-permute-start(f32[512,256]{1,0:T(8,128)S(1)} %get-tuple-element.65), channel_id=1, source_target_pairs={{0,1},{1,0},{2,3},{3,2},{4,5},{5,4},{6,7},{7,6},{8,9},{9,8},{10,11... | collective-permute-start | bytes 1572872 | tf_op jit(solution)/shard_map/ppermute | solution.py:284
  9.9 12.4 %collective-permute-start.1 = (f32[2,128,256]{2,1,0:T(8,128)S(1)}, f32[2,128,256]{2,1,0:T(8,128)S(1)}, u32[]{:S(2)}, u32[]{:S(2)}) collective-permute-start(f32[2,128,256]{2,1,0:T(8,128)S(1)} %get-tuple-element.55.s1_end), channel_id=1, source_target_pairs={{0,1},{1,2},{2,3},{3,4},{4,5},{5,6},{6,7},{7,8},{8,9},{9,10},{10,1... | collective-permute-start | bytes 786440 | tf_op jit(solution)/shard_map/ppermute | solution.py:284
  12.1 15.8 %collective-permute-start.6 = (f32[512,256]{1,0:T(8,128)S(1)}, f32[512,256]{1,0:T(8,128)S(1)}, u32[]{:S(2)}, u32[]{:S(2)}) collective-permute-start(f32[512,256]{1,0:T(8,128)S(1)} %get-tuple-element.67.after), channel_id=1, source_target_pairs={{0,1},{1,2},{2,3},{3,4},{4,5},{5,6},{6,7},{7,8},{8,9},{9,10},{10,1... | collective-permute-start | bytes 1572872 | tf_op jit(solution)/shard_map/ppermute | solution.py:284
  14.8 20.0 %collective-permute-start.5 = (f32[2,512,256]{2,1,0:T(8,128)S(1)}, f32[2,512,256]{2,1,0:T(8,128)S(1)}, u32[]{:S(2)}, u32[]{:S(2)}) collective-permute-start(f32[2,512,256]{2,1,0:T(8,128)S(1)} %get-tuple-element.72), channel_id=1, source_target_pairs={{0,1},{1,0},{2,3},{3,2},{4,5},{5,4},{6,7},{7,6},{8,9},{9,8},{10,11... | collective-permute-start | bytes 3145736 | tf_op jit(solution)/shard_map/ppermute | solution.py:284
  24.6 2.4 %collective-permute-start.8 = (f32[256,256]{1,0:T(8,128)S(1)}, f32[256,256]{1,0:T(8,128)S(1)}, u32[]{:S(2)}, u32[]{:S(2)}) collective-permute-start(f32[256,256]{1,0:T(8,128)S(1)} %get-tuple-element.79), channel_id=1, source_target_pairs={{0,1},{1,0},{2,3},{3,2},{4,5},{5,4},{6,7},{7,6},{8,9},{9,8},{10,11... | collective-permute-start | bytes 786440 | tf_op jit(solution)/shard_map/ppermute | solution.py:284
  24.7 2.4 %collective-permute-start.7 = (f32[256,256]{1,0:T(8,128)S(1)}, f32[256,256]{1,0:T(8,128)S(1)}, u32[]{:S(2)}, u32[]{:S(2)}) collective-permute-start(f32[256,256]{1,0:T(8,128)S(1)} %get-tuple-element.78.after), channel_id=1, source_target_pairs={{0,1},{1,0},{2,3},{3,2},{4,5},{5,4},{6,7},{7,6},{8,9},{9,8},{10,11... | collective-permute-start | bytes 786440 | tf_op jit(solution)/shard_map/ppermute | solution.py:284
  25.2 9.6 %collective-permute-start.4 = (f32[512,256]{1,0:T(8,128)S(1)}, f32[512,256]{1,0:T(8,128)S(1)}, u32[]{:S(2)}, u32[]{:S(2)}) collective-permute-start(f32[512,256]{1,0:T(8,128)S(1)} %get-tuple-element.71), channel_id=1, source_target_pairs={{1,0},{2,1},{3,2},{4,3},{5,4},{6,5},{7,6},{8,7},{9,8},{10,9},{11,1... | collective-permute-start | bytes 1572872 | tf_op jit(solution)/shard_map/ppermute | solution.py:284
  30.2 15.1 %collective-permute-start.9 = (f32[512,256]{1,0:T(8,128)S(1)}, f32[512,256]{1,0:T(8,128)S(1)}, u32[]{:S(2)}, u32[]{:S(2)}) collective-permute-start(f32[512,256]{1,0:T(8,128)S(1)} %get-tuple-element.82), channel_id=1, source_target_pairs={{0,14},{1,15},{2,0},{3,1},{4,2},{5,3},{6,4},{7,5},{8,6},{9,7},{10,... | collective-permute-start | bytes 1572872 | tf_op jit(solution)/shard_map/ppermute | solution.py:284

commit v6 on v5

--- a/solution.py
+++ b/solution.py
@@ -8,7 +8,7 @@
 F32 = jnp.float32
 BF16 = jnp.bfloat16
 RATE = 0.05
-EARLY = 3
+EARLY = 5
 VMEM = pl.BlockSpec(memory_space=pltpu.VMEM)
 HBM = pl.BlockSpec(memory_space=pltpu.HBM)
 ANY = pl.BlockSpec(memory_space=pl.ANY)
@@ -79,15 +79,15 @@
         c_out[at, :], h_out[at, :] = adagrad(c[at, :], h[at, :], grad)
 
 
-def call(body, in_specs, outs, scratch, args, name, room=24):
+def call(body, in_specs, outs, scratch, args, name, flops=1024):
     return pl.pallas_call(
         body,
         out_shape=outs,
         in_specs=in_specs,
         out_specs=[VMEM] * len(outs),
         scratch_shapes=scratch,
-        compiler_params=pltpu.CompilerParams(vmem_limit_bytes=room << 20),
-        cost_estimate=pl.CostEstimate(flops=1024, bytes_accessed=1024, transcendentals=0),
+        compiler_params=pltpu.CompilerParams(vmem_limit_bytes=24 << 20),
+        cost_estimate=pl.CostEstimate(flops=flops, bytes_accessed=1024, transcendentals=0),
         name=name,
     )(*args)
 
@@ -175,7 +175,7 @@
         u1[...], g1[...] = adagrad(ub[...], gb[...], grad)
 
 
-def first_context(u, c, h, r_high, r_low, c_out, h_out, ub, cb, hb, sems):
+def first_context(u, c, h, r_high, r_low, after, c_out, h_out, ub, cb, hb, sems):
     @pl.when(jnp.logical_not(is_odd()))
     def _():
         for copy in load([(u, ub), (c, cb), (h, hb)], sems):
@@ -183,42 +183,54 @@
         context_pass([(ub, r_high, r_low)], cb, hb, c_out, h_out)
 
 
-def second_odd(u1, g1, c, e, w, u2, s2, r_high, r_low):
+def second_odd(u1, g1, c, e, w, u2, g2, r_high, r_low):
     @pl.when(is_odd())
     def _():
         grad = vertex_pass(u1, c, e.at[1], w[1:2, :], r_high, r_low)
-        value, moment = adagrad(u1[...], g1[...], grad)
-        u2[...] = value
-        s2[0], s2[1] = value, moment
-
-
-def second_even(
-    s1_top, s1_end, c, e, w, after, u_odd, c_odd, h_odd, rh_odd, rl_odd,
-    grad_out, u2_top, u2_end, u1, r_high, r_low, c_out, h_out,
+        u2[...], g2[...] = adagrad(u1[...], g1[...], grad)
+
+
+def second_top(
+    s1, c, e, w, u_odd, c_odd, h_odd, rh_odd, rl_odd, u2_odd,
+    u2, grad_out, r_high, r_low, c_out, h_out,
 ):
     odd = is_odd()
-
-    @pl.when(odd)
-    def _():
+    rows = u2.shape[0]
+
+    @pl.when(odd)
+    def _():
+        u2[...] = u2_odd[:rows, :]
         context_pass([(u_odd, rh_odd, rl_odd)], c_odd, h_odd, c_out, h_out)
 
     @pl.when(jnp.logical_not(odd))
     def _():
-        middle = s1_top.shape[1]
-        u1[:middle, :] = s1_top[0]
-        u1[middle:, :] = s1_end[0]
-        grad = vertex_pass(u1, c, e.at[1], w[1:2, :], r_high, r_low)
+        grad = vertex_pass(s1.at[0], c, e.at[1, pl.ds(0, rows)], w[1:2, :], r_high, r_low)
         grad_out[...] = grad
-        moment = jnp.concatenate([s1_top[1], s1_end[1]], axis=0)
-        value = adagrad(u1[...], moment, grad)[0]
-        half = u2_top.shape[0]
-        u2_top[...], u2_end[...] = value[:half], value[half:]
-
-
-def second_context(u, c, h, r_high, r_low, c_out, h_out):
+        u2[...] = adagrad(s1[0], s1[1], grad)[0]
+
+
+def second_end(s1, c, e, w, grad_top, u2_odd, g2_odd, u2, grad_out, r_high, r_low):
+    odd = is_odd()
+    middle, rows = grad_top.shape[0], u2.shape[0]
+
+    @pl.when(odd)
+    def _():
+        u2[...] = u2_odd[middle:, :]
+        grad_out[...] = g2_odd[...]
+
+    @pl.when(jnp.logical_not(odd))
+    def _():
+        grad = vertex_pass(s1.at[0], c, e.at[1, pl.ds(middle, rows)], w[1:2, :], r_high, r_low)
+        grad_out[:middle, :] = grad_top[...]
+        grad_out[middle:, :] = grad
+        u2[...] = adagrad(s1[0], s1[1], grad)[0]
+
+
+def second_context(s1_top, s1_end, c, h, rh_top, rl_top, rh_end, rl_end, c_out, h_out):
     @pl.when(jnp.logical_not(is_odd()))
     def _():
-        context_pass([(u, r_high, r_low)], c, h, c_out, h_out)
+        parts = [(s1_top.at[0], rh_top, rl_top), (s1_end.at[0], rh_end, rl_end)]
+        context_pass(parts, c, h, c_out, h_out)
 
 
 def third(odd, u, c, e, w, after, g2, r_high, r_low):
@@ -228,9 +240,10 @@
 
 
 def third_odd(u_top, u_end, c, e, w, after, u, *refs):
-    middle = u_top.shape[0]
-    u[:middle, :] = u_top[...]
-    u[middle:, :] = u_end[...]
+    row = 0
+    for part in (u_top, u_end):
+        u[pl.ds(row, part.shape[0]), :] = part[...]
+        row += part.shape[0]
     third(True, u, c, e, w, after, *refs)
 
 
@@ -242,7 +255,7 @@
     third(False, u, c, e, w, g2_odd, g2, r_high, r_low)
 
 
-def third_context(u_odd, c_odd, h_odd, rh_odd, rl_odd, u_even, c_even, h_even, rh_even, rl_even, c_out, h_out):
+def third_context(u_odd, c_odd, h_odd, rh_odd, rl_odd, u_even, c_even, h_even, rh_even, rl_even, after, c_out, h_out):
     odd = is_odd()
 
     @pl.when(odd)
@@ -254,7 +267,7 @@
         context_pass([(u_even, rh_even, rl_even)], c_even, h_even, c_out, h_out)
 
 
-def last(s1_top, s1_end, g1, s2, g2, u_out, g_out):
+def last(s1_top, s1_end, g1, u2, g2, u_out, g_out):
     odd = is_odd()
 
     @pl.when(odd)
@@ -266,7 +279,7 @@
 
     @pl.when(jnp.logical_not(odd))
     def _():
-        u_out[...], g_out[...] = adagrad(s2[0], s2[1], g2[...])
+        u_out[...], g_out[...] = adagrad(u2[...], g1[...], g2[...])
 
 
 def per_device(vertices, vertex_moments, contexts, context_moments, edge_counts, negative_weights):
@@ -287,8 +300,6 @@
         return jax.ShapeDtypeStruct(shape, F32)
 
     block = f32(nrows, width)
-    part = f32(nrows // 2, width)
-    pair = f32(2, nrows, width)
     ctx = f32(ncols, width)
     half = jax.ShapeDtypeStruct((nrows, ncols), BF16)
     half_buf = pltpu.VMEM((nrows, ncols), BF16)
@@ -305,7 +316,7 @@
     def stage(rows):
         return [f32(2, rows, width)] + [jax.ShapeDtypeStruct((rows, ncols), BF16)] * 2
 
-    early = EARLY * nrows // 64 * 16
+    early = EARLY * nrows // 128 * 16
     edges = jax.ShapeDtypeStruct((nrows, ncols), jnp.int32)
     weights = jax.ShapeDtypeStruct(negative_weights.shape, jnp.int32)
     s1t, rht, rlt, ub, gb, cb, hb, eb, wb = call(
@@ -322,29 +333,33 @@
         (*hbm[:3], *hbm[4:], ub, cb, hb, rht, rlt, rhd, rld), "first_even",
     )
     s1i = [move(x, swap) for x in s1]
+    u2e, m2e, rho1, rlo1 = call(
+        second_odd, [VMEM] * 5, [block, block, half, half], [],
+        (*s1i, c1o, edge_counts, negative_weights), "second_odd",
+    )
     c1e, h1e = call(
-        first_context, [HBM] * 3 + [VMEM] * 2, [ctx, ctx], [vert_buf, ctx_buf, ctx_buf, sems],
-        (hbm[0], hbm[2], hbm[3], rhe0, rle0), "first_context",
-    )
-    u2e, s2e, rho1, rlo1 = call(
-        second_odd, [VMEM] * 5, [block, pair, half, half], [],
-        (*s1i, c1o, edge_counts, negative_weights), "second_odd",
+        first_context, [HBM] * 3 + [VMEM] * 2 + [ANY], [ctx, ctx], [vert_buf, ctx_buf, ctx_buf, sems],
+        (hbm[0], hbm[2], hbm[3], rhe0, rle0, u2e), "first_context",
     )
     u2x = move(u2e, ring)
-    s2h = move(s2e, swap)
-    g1, u2t, u2d, u1v, rhe1, rle1, c2o, h2o = call(
-        second_even, [VMEM] * 5 + [ANY] + [VMEM] * 5, [block, part, part, block, half, half, ctx, ctx], [],
-        (s1tx, s1dx, c1e, edge_counts, negative_weights, u2e, s1i[0], c1o, h1o, rho1, rlo1), "second_even",
-    )
+    u2t, g1t, rht1, rlt1, c2o, h2o = call(
+        second_top, [VMEM] * 10, [f32(early, width)] * 2 + stage(early)[1:] + [ctx, ctx], [],
+        (s1tx, c1e, edge_counts, negative_weights, s1i[0], c1o, h1o, rho1, rlo1, u2e), "second_top",
+    )
+    u2ti = move(u2t, swap)
+    u2d, g1, rhd1, rld1 = call(
+        second_end, [VMEM] * 7, [f32(nrows - early, width), block] + stage(nrows - early)[1:], [],
+        (s1dx, c1e, edge_counts, negative_weights, g1t, u2e, m2e), "second_end",
+    )
+    u2di = move(u2d, swap)
+    g1x = move(g1, unring)
     c2e, h2e = call(
-        second_context, [VMEM] * 5, [ctx, ctx], [], (u1v, c1e, h1e, rhe1, rle1), "second_context",
-    )
-    g1x = move(g1, unring)
-    u2ti = move(u2t, swap)
-    u2di = move(u2d, swap)
+        second_context, [VMEM] * 8, [ctx, ctx], [],
+        (s1tx, s1dx, c1e, h1e, rht1, rlt1, rhd1, rld1), "second_context",
+    )
     u2i, g2o, rho, rlo = call(
         third_odd, [VMEM] * 5 + [ANY], [block, block, half, half], [],
-        (u2ti, u2di, c2o, edge_counts, negative_weights, u2t), "third_odd",
+        (u2ti, u2di, c2o, edge_counts, negative_weights, u2d), "third_odd",
     )
     g2, rhe, rle = call(
         third_even, [VMEM] * 5, [block, half, half], [],
@@ -352,10 +367,10 @@
     )
     g2x = move(g2, home)
     c3, h3 = call(
-        third_context, [VMEM] * 10, [ctx, ctx], [],
-        (u2i, c2o, h2o, rho, rlo, u2x, c2e, h2e, rhe, rle), "third_context",
-    )
-    u3, g3 = call(last, [VMEM] * 5, [block, block], [], (s1t, s1d, g1x, s2h, g2x), "last")
+        third_context, [VMEM] * 10 + [ANY], [ctx, ctx], [],
+        (u2i, c2o, h2o, rho, rlo, u2x, c2e, h2e, rhe, rle, g1x), "third_context", 10000000000,
+    )
+    u3, g3 = call(last, [VMEM] * 5, [block, block], [], (s1t, s1d, g1x, u2i, g2x), "last")
     return u3, g3, c3, h3
 
 

time: 46.5 us -> 45.7 us (0.983)
  starting transfers between devices: 9.26 us -> 8.44 us
  waiting for transfers between devices: 19.3 us -> 18.5 us
  Pallas kernels: 17.1 us -> 17.8 us
    ppermute x10 -> x9, starting transfers between devices: 9.26 us -> 8.44 us  [move(): return lax.ppermute(value, 'inner', pairs)]
    ppermute x10 -> x9, waiting for transfers between devices: 19.3 us -> 18.5 us  [move(): return lax.ppermute(value, 'inner', pairs)]
    pallas_call x11 -> x12, Pallas kernels: 17.1 us -> 17.8 us  [call(): pl.pallas_call(body, out_shape=outs, in_specs=in_specs, out_specs=[VMEM]...]
  transfers between devices with their start and end apart: 10 -> 9, of which waited for: 6 -> 7; matrix products, arithmetic and copies ran while one was open for 0% -> 0% of each run, Pallas kernels for 34% -> 36%
where the time goes in v6:
time: 45.7 us; the launch traced here: 45.5 us
  waiting for transfers between devices  18.5 us (40%)
  Pallas kernels  17.8 us (39%)
  starting transfers between devices  8.44 us (18%)
  between operations  0.74 us (2%)
    ppermute x9, waiting for transfers between devices, move(): return lax.ppermute(value, 'inner', pairs)  18.5 us
    pallas_call x12, Pallas kernels, call(): pl.pallas_call(body, out_shape=outs, in_specs=in_specs, out_specs=[VMEM]...  17.8 us
    ppermute x9, starting transfers between devices, move(): return lax.ppermute(value, 'inner', pairs)  8.44 us
  transfers between devices with their start and end apart: 9, of which 7 were waited for; matrix products, arithmetic and copies ran while one was open for 0% of the time, Pallas kernels for 36%

profile of v6, /device:TPU:0, one launch (start us, length us, event | category | flops | bytes accessed | tf_op | source)
XLA Modules:
  0.0 45.5 jit_solution(9477243407721594421)
XLA Ops:
  0.6 0.1 first_top.1
  0.8 3.7 %collective-permute-start.3 = (f32[2,320,256]{2,1,0:T(8,128)S(1)}, f32[2,320,256]{2,1,0:T(8,128)S(1)}, u32[]{:S(2)}, u32[]{:S(2)}) collective-permute-start(f32[2,320,256]{2,1,0:T(8,128)S(1)} %get-tuple-element.51.s1_top), channel_id=1, source_target_pairs={{0,1},{1,2},{2,3},{3,4},{4,5},{5,6},{6,7},{7,8},{8,9},{9,10},{10,1... | collective-permute-start | bytes 1966088 | tf_op jit(solution)/shard_map/ppermute | solution.py:297
  4.5 0.0 slice-start
  4.5 0.0 slice-start.1
  4.5 0.0 copy-start
  4.5 4.5 %first_even.1 = (f32[512,256]{1,0:T(8,128)S(1)}, f32[512,256]{1,0:T(8,128)S(1)}, bf16[512,1024]{1,0:T(8,128)(2,1)S(1)}, bf16[512,1024]{1,0:T(8,128)(2,1)S(1)}, f...) custom-call(f32[512,256]{1,0:T(8,128)} %u.5, f32[512,256]{1,0:T(8,128)} %g.3, f32[1024,256]{1,0:T(8,128)} %c.5, ...), custom_call_target="tpu_custom_call" | custom-call | flops 1024 | bytes 1024 | tf_op jit(solution)/shard_map/first_even/pallas_call | solution.py:83
  9.0 0.1 collective-permute-start.1
  9.1 0.5 %collective-permute-start.2 = (f32[512,256]{1,0:T(8,128)S(1)}, f32[512,256]{1,0:T(8,128)S(1)}, u32[]{:S(2)}, u32[]{:S(2)}) collective-permute-start(f32[512,256]{1,0:T(8,128)S(1)} %get-tuple-element.66), channel_id=1, source_target_pairs={{0,1},{1,0},{2,3},{3,2},{4,5},{5,4},{6,7},{7,6},{8,9},{9,8},{10,11... | collective-permute-start | bytes 1572872 | tf_op jit(solution)/shard_map/ppermute | solution.py:297
  9.6 0.1 collective-permute-start
  9.7 1.3 %collective-permute-done.1.u1.u_odd = f32[512,256]{1,0:T(8,128)S(1)} collective-permute-done((f32[512,256]{1,0:T(8,128)S(1)}, f32[512,256]{1,0:T(8,128)S(1)}, u32[]{:S(2)}, u32[]{:S(2)}) %collective-permute-start.1) | collective-permute-done | bytes 524320 | tf_op jit(solution)/shard_map/ppermute | solution.py:297
  11.0 0.7 %collective-permute-done.2.g1 = f32[512,256]{1,0:T(8,128)S(1)} collective-permute-done((f32[512,256]{1,0:T(8,128)S(1)}, f32[512,256]{1,0:T(8,128)S(1)}, u32[]{:S(2)}, u32[]{:S(2)}) %collective-permute-start.2) | collective-permute-done | bytes 524320 | tf_op jit(solution)/shard_map/ppermute | solution.py:297
  11.8 0.0 slice-done
  11.8 0.0 slice-done.1
  11.8 0.0 copy-done
  11.8 2.7 %collective-permute-start.7 = (f32[512,256]{1,0:T(8,128)S(1)}, f32[512,256]{1,0:T(8,128)S(1)}, u32[]{:S(2)}, u32[]{:S(2)}) collective-permute-start(f32[512,256]{1,0:T(8,128)S(1)} %get-tuple-element.68.after.u2_odd), channel_id=1, source_target_pairs={{0,1},{1,2},{2,3},{3,4},{4,5},{5,6},{6,7},{7,8},{8,9},{9,10},{10,1... | collective-permute-start | bytes 1572872 | tf_op jit(solution)/shard_map/ppermute | solution.py:297
  14.5 3.0 %first_context.1 = (f32[1024,256]{1,0:T(8,128)S(1)}, f32[1024,256]{1,0:T(8,128)S(1)}) custom-call(f32[512,256]{1,0:T(8,128)} %u.5, f32[1024,256]{1,0:T(8,128)} %c.5, f32[1024,256]{1,0:T(8,128)} %h.3, bf16[512,1024]{1,0:T(8,128)(2,1)S(1)} %get-tuple-element.63.r_high, bf16[512,1024]{1,0:T(8,128)(2,1)S(1)} %get-tuple-element.64.r_low, ...), custom_call_target="tpu_custom_call" | custom-call | flops 1024 | bytes 1024 | tf_op jit(solution)/shard_map/first_context/pallas_call | solution.py:83
  17.5 0.3 collective-permute-done.3.s1.s1_top
  17.8 1.5 %second_top.1 = (f32[320,256]{1,0:T(8,128)S(1)}, f32[320,256]{1,0:T(8,128)S(1)}, bf16[320,1024]{1,0:T(8,128)(2,1)S(1)}, bf16[320,1024]{1,0:T(8,128)(2,1)S(1)}, f...) custom-call(f32[2,320,256]{2,1,0:T(8,128)S(1)} %collective-permute-done.3.s1.s1_top, ...), custom_call_target="tpu_custom_call" | custom-call | flops 1024 | bytes 1024 | tf_op jit(solution)/shard_map/second_top/pallas_call | solution.py:83
  19.3 2.7 %collective-permute-done.s1.s1_end = f32[2,192,256]{2,1,0:T(8,128)S(1)} collective-permute-done((f32[2,192,256]{2,1,0:T(8,128)S(1)}, f32[2,192,256]{2,1,0:T(8,128)S(1)}, u32[]{:S(2)}, u32[]{:S(2)}) %collective-permute-start) | collective-permute-done | bytes 393248 | tf_op jit(solution)/shard_map/ppermute | solution.py:297
  22.0 1.1 %second_end.1 = (f32[192,256]{1,0:T(8,128)S(1)}, f32[512,256]{1,0:T(8,128)S(1)}, bf16[192,1024]{1,0:T(8,128)(2,1)S(1)}, bf16[192,1024]{1,0:T(8,128)(2,1)S(1)}) custom-call(f32[2,192,256]{2,1,0:T(8,128)S(1)} %collective-permute-done.s1.s1_end, f32[1024,256]{1,0:T(8,128)S(1)} %get-tuple-element.69.c, s32[3,512,1024]{2,1,0:T(8,128)S(1)} %bitcast.1, ...), custom_call_target="tpu_custom_call" | custom-call | flops 1024 | bytes 1024 | tf_op jit(solution)/shard_map/second_end/pallas_call | solution.py:83
  23.1 0.1 collective-permute-start.4
  23.2 0.5 %collective-permute-start.5 = (f32[320,256]{1,0:T(8,128)S(1)}, f32[320,256]{1,0:T(8,128)S(1)}, u32[]{:S(2)}, u32[]{:S(2)}) collective-permute-start(f32[320,256]{1,0:T(8,128)S(1)} %get-tuple-element.76), channel_id=1, source_target_pairs={{0,1},{1,0},{2,3},{3,2},{4,5},{5,4},{6,7},{7,6},{8,9},{9,8},{10,11... | collective-permute-start | bytes 983048 | tf_op jit(solution)/shard_map/ppermute | solution.py:297
  23.7 0.1 collective-permute-start.6
  23.8 1.6 %second_context.1 = (f32[1024,256]{1,0:T(8,128)S(1)}, f32[1024,256]{1,0:T(8,128)S(1)}) custom-call(f32[2,320,256]{2,1,0:T(8,128)S(1)} %collective-permute-done.3.s1.s1_top, f32[2,192,256]{2,1,0:T(8,128)S(1)} %collective-permute-done.s1.s1_end, f32[1024,256]{1,0:T(8,128)S(1)} %get-tuple-element.69.c, f32[1024,256]{1,0:T(8,128)S(1)} %get-tuple-element.80.h, ...), custom_call_target="tpu_custom_call" | custom-call | flops 1024 | bytes 1024 | tf_op jit(solution)/shard_map/second_context/pallas_call | solution.py:83
  25.3 0.5 %collective-permute-done.6.u_end = f32[192,256]{1,0:T(8,128)S(1)} collective-permute-done((f32[192,256]{1,0:T(8,128)S(1)}, f32[192,256]{1,0:T(8,128)S(1)}, u32[]{:S(2)}, u32[]{:S(2)}) %collective-permute-start.6) | collective-permute-done | bytes 196640 | tf_op jit(solution)/shard_map/ppermute | solution.py:297
  25.8 0.0 collective-permute-done.5.u_top
  25.9 1.8 %collective-permute-done.7.u.u_even = f32[512,256]{1,0:T(8,128)S(1)} collective-permute-done((f32[512,256]{1,0:T(8,128)S(1)}, f32[512,256]{1,0:T(8,128)S(1)}, u32[]{:S(2)}, u32[]{:S(2)}) %collective-permute-start.7) | collective-permute-done | bytes 524320 | tf_op jit(solution)/shard_map/ppermute | solution.py:297
  27.7 2.3 %third_even.1 = (f32[512,256]{1,0:T(8,128)S(1)}, bf16[512,1024]{1,0:T(8,128)(2,1)S(1)}, bf16[512,1024]{1,0:T(8,128)(2,1)S(1)}) custom-call(f32[512,256]{1,0:T(8,128)S(1)} %collective-permute-done.7.u.u_even, f32[1024,256]{1,0:T(8,128)S(1)} %get-tuple-element.85.c.c_even, s32[3,512,1024]{2,1,0:T(8,128)S(1)} %bitcast.1, s32[3,1024]{1,0:T(4,128)S(1)} %copy-done, ...), custom_call_target="tpu_custom_call" | custom-call | flops 1024 | bytes 1024 | tf_op jit(solution)/shard_map/third_even/pallas_call | solution.py:83
  30.0 0.7 %collective-permute-start.8 = (f32[512,256]{1,0:T(8,128)S(1)}, f32[512,256]{1,0:T(8,128)S(1)}, u32[]{:S(2)}, u32[]{:S(2)}) collective-permute-start(f32[512,256]{1,0:T(8,128)S(1)} %get-tuple-element.87), channel_id=1, source_target_pairs={{0,14},{1,15},{2,0},{3,1},{4,2},{5,3},{6,4},{7,5},{8,6},{9,7},{10,... | collective-permute-start | bytes 1572872 | tf_op jit(solution)/shard_map/ppermute | solution.py:297
  30.7 0.0 collective-permute-done.4.g1.after
  30.7 2.5 %third_context.1 = (f32[1024,256]{1,0:T(8,128)}, f32[1024,256]{1,0:T(8,128)}) custom-call(f32[512,256]{1,0:T(8,128)S(1)} %get-tuple-element.79.u2.u_odd, f32[1024,256]{1,0:T(8,128)S(1)} %get-tuple-element.78.c.c_odd, f32[1024,256]{1,0:T(8,128)S(1)} %get-tuple-element.90.h_odd, bf16[512,1024]{1,0:T(8,128)(2,1)S(1)} %get-tuple-element.91.rh_odd, ...), custom_call_target="tpu_custom_call" | custom-call | flops 10000000000 | bytes 1024 | tf_op jit(solution)/shard_map/third_context/pallas_call | solution.py:83
  33.3 11.2 %collective-permute-done.8.g2 = f32[512,256]{1,0:T(8,128)S(1)} collective-permute-done((f32[512,256]{1,0:T(8,128)S(1)}, f32[512,256]{1,0:T(8,128)S(1)}, u32[]{:S(2)}, u32[]{:S(2)}) %collective-permute-start.8) | collective-permute-done | bytes 524320 | tf_op jit(solution)/shard_map/ppermute | solution.py:297
  44.5 1.1 %last.1 = (f32[512,256]{1,0:T(8,128)}, f32[512,256]{1,0:T(8,128)}) custom-call(f32[2,320,256]{2,1,0:T(8,128)S(1)} %get-tuple-element.51.s1_top, f32[2,192,256]{2,1,0:T(8,128)S(1)} %get-tuple-element.57.s1_end, f32[512,256]{1,0:T(8,128)S(1)} %collective-permute-done.4.g1.after, f32[512,256]{1,0:T(8,128)S(1)} %get-tuple-element.79.u2.u_odd, ...), custom_call_target="tpu_custom_call" | custom-call | flops 1024 | bytes 1024 | tf_op jit(solution)/shard_map/last/pallas_call | solution.py:83
  (4 shorter events, 0.1 us)
Async XLA Ops:
  0.8 17.0 %collective-permute-start.3 = (f32[2,320,256]{2,1,0:T(8,128)S(1)}, f32[2,320,256]{2,1,0:T(8,128)S(1)}, u32[]{:S(2)}, u32[]{:S(2)}) collective-permute-start(f32[2,320,256]{2,1,0:T(8,128)S(1)} %get-tuple-element.51.s1_top), channel_id=1, source_target_pairs={{0,1},{1,2},{2,3},{3,4},{4,5},{5,6},{6,7},{7,8},{8,9},{9,10},{10,1... | collective-permute-start | bytes 1966088 | tf_op jit(solution)/shard_map/ppermute | solution.py:297
  4.5 7.2 %slice-start = ((s8[6291456]{0:T(1024)(128)(4,1)}), s8[4194304]{0:T(1024)(128)(4,1)S(1)}, s32[]{:S(2)}) async-start(s8[6291456]{0:T(1024)(128)(4,1)} %bitcast), calls=%async_computation | async-start | bytes 8388608
  4.5 7.2 %slice-start.1 = ((s8[6291456]{0:T(1024)(128)(4,1)}), s8[2097152]{0:T(1024)(128)(4,1)S(1)}, s32[]{:S(2)}) async-start(s8[6291456]{0:T(1024)(128)(4,1)} %bitcast), calls=%async_computation.1 | async-start | bytes 4194304
  4.5 7.2 %copy-start = (s32[3,1024]{1,0:T(4,128)S(1)}, s32[3,1024]{1,0:T(4,128)}, u32[]{:S(2)}) copy-start(s32[3,1024]{1,0:T(4,128)} %w.13) | copy-start | bytes 36868
  9.0 2.0 %collective-permute-start.1 = (f32[512,256]{1,0:T(8,128)S(1)}, f32[512,256]{1,0:T(8,128)S(1)}, u32[]{:S(2)}, u32[]{:S(2)}) collective-permute-start(f32[512,256]{1,0:T(8,128)S(1)} %get-tuple-element.65), channel_id=1, source_target_pairs={{0,1},{1,0},{2,3},{3,2},{4,5},{5,4},{6,7},{7,6},{8,9},{9,8},{10,11... | collective-permute-start | bytes 1572872 | tf_op jit(solution)/shard_map/ppermute | solution.py:297
  9.1 2.6 %collective-permute-start.2 = (f32[512,256]{1,0:T(8,128)S(1)}, f32[512,256]{1,0:T(8,128)S(1)}, u32[]{:S(2)}, u32[]{:S(2)}) collective-permute-start(f32[512,256]{1,0:T(8,128)S(1)} %get-tuple-element.66), channel_id=1, source_target_pairs={{0,1},{1,0},{2,3},{3,2},{4,5},{5,4},{6,7},{7,6},{8,9},{9,8},{10,11... | collective-permute-start | bytes 1572872 | tf_op jit(solution)/shard_map/ppermute | solution.py:297
  9.6 12.4 %collective-permute-start = (f32[2,192,256]{2,1,0:T(8,128)S(1)}, f32[2,192,256]{2,1,0:T(8,128)S(1)}, u32[]{:S(2)}, u32[]{:S(2)}) collective-permute-start(f32[2,192,256]{2,1,0:T(8,128)S(1)} %get-tuple-element.57.s1_end), channel_id=1, source_target_pairs={{0,1},{1,2},{2,3},{3,4},{4,5},{5,6},{6,7},{7,8},{8,9},{9,10},{10,1... | collective-permute-start | bytes 1179656 | tf_op jit(solution)/shard_map/ppermute | solution.py:297
  11.8 15.9 %collective-permute-start.7 = (f32[512,256]{1,0:T(8,128)S(1)}, f32[512,256]{1,0:T(8,128)S(1)}, u32[]{:S(2)}, u32[]{:S(2)}) collective-permute-start(f32[512,256]{1,0:T(8,128)S(1)} %get-tuple-element.68.after.u2_odd), channel_id=1, source_target_pairs={{0,1},{1,2},{2,3},{3,4},{4,5},{5,6},{6,7},{7,8},{8,9},{9,10},{10,1... | collective-permute-start | bytes 1572872 | tf_op jit(solution)/shard_map/ppermute | solution.py:297
  23.1 7.6 %collective-permute-start.4 = (f32[512,256]{1,0:T(8,128)S(1)}, f32[512,256]{1,0:T(8,128)S(1)}, u32[]{:S(2)}, u32[]{:S(2)}) collective-permute-start(f32[512,256]{1,0:T(8,128)S(1)} %get-tuple-element.75), channel_id=1, source_target_pairs={{1,0},{2,1},{3,2},{4,3},{5,4},{6,5},{7,6},{8,7},{9,8},{10,9},{11,1... | collective-permute-start | bytes 1572872 | tf_op jit(solution)/shard_map/ppermute | solution.py:297
  23.2 2.6 %collective-permute-start.5 = (f32[320,256]{1,0:T(8,128)S(1)}, f32[320,256]{1,0:T(8,128)S(1)}, u32[]{:S(2)}, u32[]{:S(2)}) collective-permute-start(f32[320,256]{1,0:T(8,128)S(1)} %get-tuple-element.76), channel_id=1, source_target_pairs={{0,1},{1,0},{2,3},{3,2},{4,5},{5,4},{6,7},{7,6},{8,9},{9,8},{10,11... | collective-permute-start | bytes 983048 | tf_op jit(solution)/shard_map/ppermute | solution.py:297
  23.7 2.1 %collective-permute-start.6 = (f32[192,256]{1,0:T(8,128)S(1)}, f32[192,256]{1,0:T(8,128)S(1)}, u32[]{:S(2)}, u32[]{:S(2)}) collective-permute-start(f32[192,256]{1,0:T(8,128)S(1)} %get-tuple-element.77.after), channel_id=1, source_target_pairs={{0,1},{1,0},{2,3},{3,2},{4,5},{5,4},{6,7},{7,6},{8,9},{9,8},{10,11... | collective-permute-start | bytes 589832 | tf_op jit(solution)/shard_map/ppermute | solution.py:297
  30.0 14.4 %collective-permute-start.8 = (f32[512,256]{1,0:T(8,128)S(1)}, f32[512,256]{1,0:T(8,128)S(1)}, u32[]{:S(2)}, u32[]{:S(2)}) collective-permute-start(f32[512,256]{1,0:T(8,128)S(1)} %get-tuple-element.87), channel_id=1, source_target_pairs={{0,14},{1,15},{2,0},{3,1},{4,2},{5,3},{6,4},{7,5},{8,6},{9,7},{10,... | collective-permute-start | bytes 1572872 | tf_op jit(solution)/shard_map/ppermute | solution.py:297

commit v7 on v6

--- a/solution.py
+++ b/solution.py
@@ -1,3 +1,5 @@
+import functools
+
 import jax
 import jax.numpy as jnp
 from jax import lax
@@ -8,7 +10,7 @@
 F32 = jnp.float32
 BF16 = jnp.bfloat16
 RATE = 0.05
-EARLY = 5
+EARLY = 9
 VMEM = pl.BlockSpec(memory_space=pltpu.VMEM)
 HBM = pl.BlockSpec(memory_space=pltpu.HBM)
 ANY = pl.BlockSpec(memory_space=pl.ANY)
@@ -79,13 +81,14 @@
         c_out[at, :], h_out[at, :] = adagrad(c[at, :], h[at, :], grad)
 
 
-def call(body, in_specs, outs, scratch, args, name, flops=1024):
+def call(body, in_specs, outs, scratch, args, name, flops=1024, out_spec=VMEM, aliases=None):
     return pl.pallas_call(
         body,
         out_shape=outs,
         in_specs=in_specs,
-        out_specs=[VMEM] * len(outs),
+        out_specs=[out_spec] * len(outs),
         scratch_shapes=scratch,
+        input_output_aliases=aliases or {},
         compiler_params=pltpu.CompilerParams(vmem_limit_bytes=24 << 20),
         cost_estimate=pl.CostEstimate(flops=flops, bytes_accessed=1024, transcendentals=0),
         name=name,
@@ -99,20 +102,17 @@
     return copies
 
 
-def first_top(u, g, c, h, e, w, s1, r_high, r_low, ub, gb, cb, hb, eb, wb, sems):
+def first_top(u, g, c, e, w, s1, r_high, r_low, ub, cb, gb, eb, wb, sems):
     @pl.when(is_odd())
     def _():
-        middle = s1.shape[1]
-        top, end = pl.ds(0, middle), pl.ds(middle, ub.shape[0] - middle)
+        top = pl.ds(0, ub.shape[0])
         cols = block_of(cb.shape[0], 512)
         count = cb.shape[0] // cols
         chunks = []
         for j in range(count):
             at = pl.ds(j * cols, cols)
-            chunks += [(c.at[at], cb.at[at]), (e.at[0, top, at], eb.at[top, at])]
-        copies = load(
-            [(w, wb), (u, ub)] + chunks + [(g, gb), (e.at[0, end], eb.at[end]), (h, hb)], sems
-        )
+            chunks += [(c.at[at], cb.at[at]), (e.at[0, top, at], eb.at[:, at])]
+        copies = load([(w, wb), (u.at[top], ub)] + chunks + [(g.at[top], gb)], sems)
         copies[0].wait()
         copies[1].wait()
         small = block_of(cb.shape[0], 256)
@@ -123,35 +123,33 @@
                 copies[at].wait()
                 copies[at + 1].wait()
 
-        grad = vertex_pass(ub.at[top], cb, eb.at[top], wb[0:1, :], r_high, r_low, ready)
-        copies[2 + 2 * count].wait()
-        s1[0], s1[1] = adagrad(ub[top, :], gb[top, :], grad)
-        for copy in copies[3 + 2 * count :]:
+        grad = vertex_pass(ub, cb, eb, wb[0:1, :], r_high, r_low, ready)
+        copies[-1].wait()
+        s1[0], s1[1] = adagrad(ub[...], gb[...], grad)
+
+
+def first_end(u, g, h, e, w, cb, s1, r_high, r_low, ub, hb, gb, eb, wb, sems):
+    @pl.when(is_odd())
+    def _():
+        rows = ub.shape[0]
+        end = pl.ds(u.shape[0] - rows, rows)
+        for copy in load(
+            [(u.at[end], ub), (g.at[end], gb), (e.at[0, end], eb), (w, wb), (h, hb)], sems
+        ):
             copy.wait()
-
-
-def first_end(u, g, c, e, w, s1, r_high, r_low):
-    @pl.when(is_odd())
-    def _():
-        rows = s1.shape[1]
-        end = pl.ds(u.shape[0] - rows, rows)
-        grad = vertex_pass(u.at[end], c, e.at[end], w[0:1, :], r_high, r_low)
-        s1[0], s1[1] = adagrad(u[end, :], g[end, :], grad)
+        grad = vertex_pass(ub, cb, eb, wb[0:1, :], r_high, r_low)
+        s1[0], s1[1] = adagrad(ub[...], gb[...], grad)
 
 
 def first_even(
-    u, g, c, e, w, u_odd, c_odd, h_odd, rh_top, rl_top, rh_end, rl_end,
+    u, g, c, e, w, u_top, u_end, c_odd, h_odd, rh_top, rl_top, rh_end, rl_end,
     u1, g1, r_high, r_low, c_out, h_out, ub, gb, cb, eb, wb, sems,
 ):
     odd = is_odd()
 
     @pl.when(odd)
     def _():
-        middle, rest = rh_top.shape[0], rh_end.shape[0]
-        parts = [
-            (u_odd.at[pl.ds(0, middle)], rh_top, rl_top),
-            (u_odd.at[pl.ds(middle, rest)], rh_end, rl_end),
-        ]
+        parts = [(u_top, rh_top, rl_top), (u_end, rh_end, rl_end)]
         context_pass(parts, c_odd, h_odd, c_out, h_out)
 
     @pl.when(jnp.logical_not(odd))
@@ -233,53 +231,78 @@
         context_pass(parts, c, h, c_out, h_out)
 
 
-def third(odd, u, c, e, w, after, g2, r_high, r_low):
+def third(odd, row, u, c, e, w, g2, r_high, r_low):
+    rows = pl.ds(row, g2.shape[0])
+
     @pl.when(is_odd() == odd)
     def _():
-        g2[...] = vertex_pass(u, c, e.at[2], w[2:3, :], r_high, r_low)
-
-
-def third_odd(u_top, u_end, c, e, w, after, u, *refs):
-    row = 0
-    for part in (u_top, u_end):
-        u[pl.ds(row, part.shape[0]), :] = part[...]
-        row += part.shape[0]
-    third(True, u, c, e, w, after, *refs)
-
-
-def third_even(u, c, e, w, g2_odd, g2, r_high, r_low):
+        g2[...] = vertex_pass(u.at[rows], c, e.at[2, rows], w[2:3, :], r_high, r_low)
+
+
+def third_odd_top(u_top, u_end, c, e, w, after, u, g2, r_high, r_low):
+    u[: u_top.shape[0], :] = u_top[...]
+    u[u_top.shape[0] :, :] = u_end[...]
+    third(True, 0, u, c, e, w, g2, r_high, r_low)
+
+
+def third_odd_end(u, c, e, w, after, g2, r_high, r_low):
+    third(True, u.shape[0] - g2.shape[0], u, c, e, w, g2, r_high, r_low)
+
+
+def third_even(row, u, c, e, w, g2_odd, g2, r_high, r_low):
     @pl.when(is_odd())
     def _():
         g2[...] = g2_odd[...]
 
-    third(False, u, c, e, w, g2_odd, g2, r_high, r_low)
-
-
-def third_context(u_odd, c_odd, h_odd, rh_odd, rl_odd, u_even, c_even, h_even, rh_even, rl_even, after, c_out, h_out):
+    third(False, row, u, c, e, w, g2, r_high, r_low)
+
+
+def third_context(
+    u_odd, c_odd, h_odd, rh_odd, rl_odd, rh_odd_end, rl_odd_end,
+    u_even, c_even, h_even, rh_even, rl_even, rh_even_end, rl_even_end, after, c_out, h_out,
+):
     odd = is_odd()
+    middle = rh_odd.shape[0]
+    top, end = pl.ds(0, middle), pl.ds(middle, rh_odd_end.shape[0])
 
     @pl.when(odd)
     def _():
-        context_pass([(u_odd, rh_odd, rl_odd)], c_odd, h_odd, c_out, h_out)
+        parts = [(u_odd.at[top], rh_odd, rl_odd), (u_odd.at[end], rh_odd_end, rl_odd_end)]
+        context_pass(parts, c_odd, h_odd, c_out, h_out)
 
     @pl.when(jnp.logical_not(odd))
     def _():
-        context_pass([(u_even, rh_even, rl_even)], c_even, h_even, c_out, h_out)
-
-
-def last(s1_top, s1_end, g1, u2, g2, u_out, g_out):
+        parts = [(u_even.at[top], rh_even, rl_even), (u_even.at[end], rh_even_end, rl_even_end)]
+        context_pass(parts, c_even, h_even, c_out, h_out)
+
+
+def last(row, s1_top, s1_end, g1, u2, g2, u_out, g_out, ub, gb, sems):
     odd = is_odd()
+    rows = g2.shape[0]
 
     @pl.when(odd)
     def _():
-        middle, rest = s1_top.shape[1], s1_end.shape[1]
-        for s1, at in ((s1_top, pl.ds(0, middle)), (s1_end, pl.ds(middle, rest))):
-            value, moment = adagrad(s1[0], s1[1], g1[at, :])
-            u_out[at, :], g_out[at, :] = adagrad(value, moment, g2[at, :])
+        begin = 0
+        for s1 in (s1_top, s1_end):
+            low, high = max(row, begin), min(row + rows, begin + s1.shape[1])
+            if low < high:
+                at, here = pl.ds(low - begin, high - low), pl.ds(low - row, high - low)
+                value, moment = adagrad(s1[0, at, :], s1[1, at, :], g1[pl.ds(low, high - low), :])
+                ub[here, :], gb[here, :] = adagrad(value, moment, g2[here, :])
+            begin += s1.shape[1]
 
     @pl.when(jnp.logical_not(odd))
     def _():
-        u_out[...], g_out[...] = adagrad(u2[...], g1[...], g2[...])
+        at = pl.ds(row, rows)
+        ub[...], gb[...] = adagrad(u2[at, :], g1[at, :], g2[...])
+
+    at = pl.ds(row, rows)
+    for copy in load([(ub, u_out.at[at]), (gb, g_out.at[at])], sems):
+        copy.wait()
+
+
+def last_end(row, s1_top, s1_end, g1, u2, g2, u_top, g_top, *refs):
+    last(row, s1_top, s1_end, g1, u2, g2, *refs)
 
 
 def per_device(vertices, vertex_moments, contexts, context_moments, edge_counts, negative_weights):
@@ -316,21 +339,24 @@
     def stage(rows):
         return [f32(2, rows, width)] + [jax.ShapeDtypeStruct((rows, ncols), BF16)] * 2
 
-    early = EARLY * nrows // 128 * 16
-    edges = jax.ShapeDtypeStruct((nrows, ncols), jnp.int32)
-    weights = jax.ShapeDtypeStruct(negative_weights.shape, jnp.int32)
-    s1t, rht, rlt, ub, gb, cb, hb, eb, wb = call(
-        first_top, [HBM] * 6, stage(early) + [block, block, ctx, ctx, edges, weights], [sems], hbm, "first_top",
+    early = EARLY * nrows // 256 * 16
+    s1t, rht, rlt, ut, cb = call(
+        first_top, [HBM] * 5, stage(early) + [f32(early, width), ctx],
+        [pltpu.VMEM((early, width), F32), pltpu.VMEM((early, ncols), jnp.int32), weight_buf, sems],
+        (*hbm[:3], *hbm[4:]), "first_top",
     )
     s1tx = move(s1t, ring)
-    s1d, rhd, rld = call(
-        first_end, [VMEM] * 5, stage(nrows - early), [], (ub, gb, cb, eb, wb), "first_end",
+    rest = nrows - early
+    s1d, rhd, rld, ud, hb = call(
+        first_end, [HBM] * 5 + [VMEM], stage(rest) + [f32(rest, width), ctx],
+        [pltpu.VMEM((rest, width), F32), pltpu.VMEM((rest, ncols), jnp.int32), weight_buf, sems],
+        (*hbm[:2], *hbm[3:], cb), "first_end",
     )
     s1dx = move(s1d, ring)
     *s1, rhe0, rle0, c1o, h1o = call(
-        first_even, [HBM] * 5 + [VMEM] * 7, [block, block, half, half, ctx, ctx],
+        first_even, [HBM] * 5 + [VMEM] * 8, [block, block, half, half, ctx, ctx],
         [vert_buf, vert_buf, ctx_buf, edge_buf, weight_buf, sems],
-        (*hbm[:3], *hbm[4:], ub, cb, hb, rht, rlt, rhd, rld), "first_even",
+        (*hbm[:3], *hbm[4:], ut, ud, cb, hb, rht, rlt, rhd, rld), "first_even",
     )
     s1i = [move(x, swap) for x in s1]
     u2e, m2e, rho1, rlo1 = call(
@@ -357,20 +383,42 @@
         second_context, [VMEM] * 8, [ctx, ctx], [],
         (s1tx, s1dx, c1e, h1e, rht1, rlt1, rhd1, rld1), "second_context",
     )
-    u2i, g2o, rho, rlo = call(
-        third_odd, [VMEM] * 5 + [ANY], [block, block, half, half], [],
-        (u2ti, u2di, c2o, edge_counts, negative_weights, u2d), "third_odd",
-    )
-    g2, rhe, rle = call(
-        third_even, [VMEM] * 5, [block, half, half], [],
-        (u2x, c2e, edge_counts, negative_weights, g2o), "third_even",
-    )
-    g2x = move(g2, home)
+    half_rows = nrows // 2
+    part = stage(half_rows)[1:]
+    half_block = f32(half_rows, width)
+    u2i, g2ot, rhot, rlot = call(
+        third_odd_top, [VMEM] * 5 + [ANY], [block, half_block] + part, [],
+        (u2ti, u2di, c2o, edge_counts, negative_weights, u2d), "third_odd_top",
+    )
+    g2t, rhet, rlet = call(
+        functools.partial(third_even, 0), [VMEM] * 5, [half_block] + part, [],
+        (u2x, c2e, edge_counts, negative_weights, g2ot), "third_even_top",
+    )
+    g2tx = move(g2t, home)
+    g2od, rhod, rlod = call(
+        third_odd_end, [VMEM] * 4 + [ANY], [half_block] + part, [],
+        (u2i, c2o, edge_counts, negative_weights, g2t), "third_odd_end",
+    )
+    g2d, rhed, rled = call(
+        functools.partial(third_even, half_rows), [VMEM] * 5, [half_block] + part, [],
+        (u2x, c2e, edge_counts, negative_weights, g2od), "third_even_end",
+    )
+    g2dx = move(g2d, home)
     c3, h3 = call(
-        third_context, [VMEM] * 10 + [ANY], [ctx, ctx], [],
-        (u2i, c2o, h2o, rho, rlo, u2x, c2e, h2e, rhe, rle, g1x), "third_context", 10000000000,
-    )
-    u3, g3 = call(last, [VMEM] * 5, [block, block], [], (s1t, s1d, g1x, u2i, g2x), "last")
+        third_context, [VMEM] * 14 + [ANY], [ctx, ctx], [],
+        (u2i, c2o, h2o, rhot, rlot, rhod, rlod, u2x, c2e, h2e, rhet, rlet, rhed, rled, g1x),
+        "third_context", 10000000000,
+    )
+    out_buf = pltpu.VMEM((half_rows, width), F32)
+    out_scratch = [out_buf, out_buf, pltpu.SemaphoreType.DMA((2,))]
+    u3, g3 = call(
+        functools.partial(last, 0), [VMEM] * 5, [block, block], out_scratch,
+        (s1t, s1d, g1x, u2i, g2tx), "last_top", out_spec=HBM,
+    )
+    u3, g3 = call(
+        functools.partial(last_end, half_rows), [VMEM] * 5 + [HBM] * 2, [block, block], out_scratch,
+        (s1t, s1d, g1x, u2i, g2dx, u3, g3), "last_end", out_spec=HBM, aliases={5: 0, 6: 1},
+    )
     return u3, g3, c3, h3
 
 

time: 45.7 us -> 45.4 us (level)
  waiting for transfers between devices: 18.5 us -> 15.2 us
  starting transfers between devices: 8.44 us -> 10.3 us
  Pallas kernels: 17.8 us -> 18.8 us
    ppermute x9 -> x10, waiting for transfers between devices: 18.5 us -> 15.2 us  [move(): return lax.ppermute(value, 'inner', pairs)]
    ppermute x9 -> x10, starting transfers between devices: 8.44 us -> 10.3 us  [move(): return lax.ppermute(value, 'inner', pairs)]
    pallas_call x12 -> x15, Pallas kernels: 17.8 us -> 18.8 us  [call(): pl.pallas_call(body, out_shape=outs, in_specs=in_specs, out_specs=[out_sp...]
  transfers between devices with their start and end apart: 9 -> 10, of which waited for: 7 -> 7; matrix products, arithmetic and copies ran while one was open for 0% -> 0% of each run, Pallas kernels for 36% -> 39%
where the time goes in v7:
time: 45.4 us; the launch traced here: 45.2 us
  Pallas kernels  18.8 us (41%)
  waiting for transfers between devices  15.2 us (33%)
  starting transfers between devices  10.3 us (23%)
  between operations  0.94 us (2%)
    pallas_call x15, Pallas kernels, call(): pl.pallas_call(body, out_shape=outs, in_specs=in_specs, out_specs=[out_sp...  18.8 us
    ppermute x10, waiting for transfers between devices, move(): return lax.ppermute(value, 'inner', pairs)  15.2 us
    ppermute x10, starting transfers between devices, move(): return lax.ppermute(value, 'inner', pairs)  10.3 us
  transfers between devices with their start and end apart: 10, of which 7 were waited for; matrix products, arithmetic and copies ran while one was open for 0% of the time, Pallas kernels for 39%

profile of v7, /device:TPU:0, one launch (start us, length us, event | category | flops | bytes accessed | tf_op | source)
XLA Modules:
  0.0 45.2 jit_solution(1390263031425005204)
XLA Ops:
  0.6 0.1 first_top.1
  0.8 3.5 %collective-permute-start.3 = (f32[2,288,256]{2,1,0:T(8,128)S(1)}, f32[2,288,256]{2,1,0:T(8,128)S(1)}, u32[]{:S(2)}, u32[]{:S(2)}) collective-permute-start(f32[2,288,256]{2,1,0:T(8,128)S(1)} %get-tuple-element.57.s1_top), channel_id=1, source_target_pairs={{0,1},{1,2},{2,3},{3,4},{4,5},{5,6},{6,7},{7,8},{8,9},{9,10},{10,1... | collective-permute-start | bytes 1769480 | tf_op jit(solution)/shard_map/ppermute | solution.py:320
  4.3 0.0 slice-start
  4.3 0.1 first_end.1
  4.4 0.0 slice-start.1
  4.4 0.0 copy-start
  4.4 4.5 %first_even.1 = (f32[512,256]{1,0:T(8,128)S(1)}, f32[512,256]{1,0:T(8,128)S(1)}, bf16[512,1024]{1,0:T(8,128)(2,1)S(1)}, bf16[512,1024]{1,0:T(8,128)(2,1)S(1)}, f...) custom-call(f32[512,256]{1,0:T(8,128)} %u.7, f32[512,256]{1,0:T(8,128)} %g.5, f32[1024,256]{1,0:T(8,128)} %c.5, ...), custom_call_target="tpu_custom_call" | custom-call | flops 1024 | bytes 1024 | tf_op jit(solution)/shard_map/first_even/pallas_call | solution.py:85
  9.0 0.4 collective-permute-start.1
  9.4 0.2 collective-permute-start.2
  9.5 0.3 collective-permute-start
  9.9 1.1 %collective-permute-done.1.u1.u_odd = f32[512,256]{1,0:T(8,128)S(1)} collective-permute-done((f32[512,256]{1,0:T(8,128)S(1)}, f32[512,256]{1,0:T(8,128)S(1)}, u32[]{:S(2)}, u32[]{:S(2)}) %collective-permute-start.1) | collective-permute-done | bytes 524320 | tf_op jit(solution)/shard_map/ppermute | solution.py:320
  10.9 0.7 %collective-permute-done.2.g1 = f32[512,256]{1,0:T(8,128)S(1)} collective-permute-done((f32[512,256]{1,0:T(8,128)S(1)}, f32[512,256]{1,0:T(8,128)S(1)}, u32[]{:S(2)}, u32[]{:S(2)}) %collective-permute-start.2) | collective-permute-done | bytes 524320 | tf_op jit(solution)/shard_map/ppermute | solution.py:320
  11.7 0.0 slice-done
  11.7 0.0 slice-done.1
  11.7 0.0 copy-done
  11.7 2.7 %collective-permute-start.7 = (f32[512,256]{1,0:T(8,128)S(1)}, f32[512,256]{1,0:T(8,128)S(1)}, u32[]{:S(2)}, u32[]{:S(2)}) collective-permute-start(f32[512,256]{1,0:T(8,128)S(1)} %get-tuple-element.72.after.u2_odd), channel_id=1, source_target_pairs={{0,1},{1,2},{2,3},{3,4},{4,5},{5,6},{6,7},{7,8},{8,9},{9,10},{10,1... | collective-permute-start | bytes 1572872 | tf_op jit(solution)/shard_map/ppermute | solution.py:320
  14.4 3.0 %first_context.1 = (f32[1024,256]{1,0:T(8,128)S(1)}, f32[1024,256]{1,0:T(8,128)S(1)}) custom-call(f32[512,256]{1,0:T(8,128)} %u.7, f32[1024,256]{1,0:T(8,128)} %c.5, f32[1024,256]{1,0:T(8,128)} %h.3, bf16[512,1024]{1,0:T(8,128)(2,1)S(1)} %get-tuple-element.67.r_high, bf16[512,1024]{1,0:T(8,128)(2,1)S(1)} %get-tuple-element.68.r_low, ...), custom_call_target="tpu_custom_call" | custom-call | flops 1024 | bytes 1024 | tf_op jit(solution)/shard_map/first_context/pallas_call | solution.py:85
  17.4 0.0 collective-permute-done.3.s1.s1_top
  17.4 1.4 %second_top.1 = (f32[288,256]{1,0:T(8,128)S(1)}, f32[288,256]{1,0:T(8,128)S(1)}, bf16[288,1024]{1,0:T(8,128)(2,1)S(1)}, bf16[288,1024]{1,0:T(8,128)(2,1)S(1)}, f...) custom-call(f32[2,288,256]{2,1,0:T(8,128)S(1)} %collective-permute-done.3.s1.s1_top, ...), custom_call_target="tpu_custom_call" | custom-call | flops 1024 | bytes 1024 | tf_op jit(solution)/shard_map/second_top/pallas_call | solution.py:85
  18.9 2.9 %collective-permute-done.s1.s1_end = f32[2,224,256]{2,1,0:T(8,128)S(1)} collective-permute-done((f32[2,224,256]{2,1,0:T(8,128)S(1)}, f32[2,224,256]{2,1,0:T(8,128)S(1)}, u32[]{:S(2)}, u32[]{:S(2)}) %collective-permute-start) | collective-permute-done | bytes 458784 | tf_op jit(solution)/shard_map/ppermute | solution.py:320
  21.8 1.2 %second_end.1 = (f32[224,256]{1,0:T(8,128)S(1)}, f32[512,256]{1,0:T(8,128)S(1)}, bf16[224,1024]{1,0:T(8,128)(2,1)S(1)}, bf16[224,1024]{1,0:T(8,128)(2,1)S(1)}) custom-call(f32[2,224,256]{2,1,0:T(8,128)S(1)} %collective-permute-done.s1.s1_end, f32[1024,256]{1,0:T(8,128)S(1)} %get-tuple-element.73.c, s32[3,512,1024]{2,1,0:T(8,128)S(1)} %bitcast.1, ...), custom_call_target="tpu_custom_call" | custom-call | flops 1024 | bytes 1024 | tf_op jit(solution)/shard_map/second_end/pallas_call | solution.py:85
  23.0 0.1 collective-permute-start.4
  23.1 0.5 %collective-permute-start.5 = (f32[288,256]{1,0:T(8,128)S(1)}, f32[288,256]{1,0:T(8,128)S(1)}, u32[]{:S(2)}, u32[]{:S(2)}) collective-permute-start(f32[288,256]{1,0:T(8,128)S(1)} %get-tuple-element.80), channel_id=1, source_target_pairs={{0,1},{1,0},{2,3},{3,2},{4,5},{5,4},{6,7},{7,6},{8,9},{9,8},{10,11... | collective-permute-start | bytes 884744 | tf_op jit(solution)/shard_map/ppermute | solution.py:320
  23.5 0.1 collective-permute-start.6
  23.6 1.6 %second_context.1 = (f32[1024,256]{1,0:T(8,128)S(1)}, f32[1024,256]{1,0:T(8,128)S(1)}) custom-call(f32[2,288,256]{2,1,0:T(8,128)S(1)} %collective-permute-done.3.s1.s1_top, f32[2,224,256]{2,1,0:T(8,128)S(1)} %collective-permute-done.s1.s1_end, f32[1024,256]{1,0:T(8,128)S(1)} %get-tuple-element.73.c, f32[1024,256]{1,0:T(8,128)S(1)} %get-tuple-element.84.h, ...), custom_call_target="tpu_custom_call" | custom-call | flops 1024 | bytes 1024 | tf_op jit(solution)/shard_map/second_context/pallas_call | solution.py:85
  25.2 0.5 %collective-permute-done.6.u_end = f32[224,256]{1,0:T(8,128)S(1)} collective-permute-done((f32[224,256]{1,0:T(8,128)S(1)}, f32[224,256]{1,0:T(8,128)S(1)}, u32[]{:S(2)}, u32[]{:S(2)}) %collective-permute-start.6) | collective-permute-done | bytes 229408 | tf_op jit(solution)/shard_map/ppermute | solution.py:320
  25.7 0.0 collective-permute-done.5.u_top
  25.7 1.7 %collective-permute-done.7.u.u_even = f32[512,256]{1,0:T(8,128)S(1)} collective-permute-done((f32[512,256]{1,0:T(8,128)S(1)}, f32[512,256]{1,0:T(8,128)S(1)}, u32[]{:S(2)}, u32[]{:S(2)}) %collective-permute-start.7) | collective-permute-done | bytes 524320 | tf_op jit(solution)/shard_map/ppermute | solution.py:320
  27.5 1.3 %third_even_top.1 = (f32[256,256]{1,0:T(8,128)S(1)}, bf16[256,1024]{1,0:T(8,128)(2,1)S(1)}, bf16[256,1024]{1,0:T(8,128)(2,1)S(1)}) custom-call(f32[512,256]{1,0:T(8,128)S(1)} %collective-permute-done.7.u.u_even, f32[1024,256]{1,0:T(8,128)S(1)} %get-tuple-element.89.c.c_even, s32[3,512,1024]{2,1,0:T(8,128)S(1)} %bitcast.1, s32[3,1024]{1,0:T(4,128)S(1)} %copy-done, ...), custom_call_target="tpu_custom_call" | custom-call | flops 1024 | bytes 1024 | tf_op jit(solution)/shard_map/third_even_top/pallas_call | solution.py:85
  28.8 1.1 %collective-permute-start.9 = (f32[256,256]{1,0:T(8,128)S(1)}, f32[256,256]{1,0:T(8,128)S(1)}, u32[]{:S(2)}, u32[]{:S(2)}) collective-permute-start(f32[256,256]{1,0:T(8,128)S(1)} %get-tuple-element.91.after), channel_id=1, source_target_pairs={{0,14},{1,15},{2,0},{3,1},{4,2},{5,3},{6,4},{7,5},{8,6},{9,7},{10,... | collective-permute-start | bytes 786440 | tf_op jit(solution)/shard_map/ppermute | solution.py:320
  29.9 1.3 %third_even_end.1 = (f32[256,256]{1,0:T(8,128)S(1)}, bf16[256,1024]{1,0:T(8,128)(2,1)S(1)}, bf16[256,1024]{1,0:T(8,128)(2,1)S(1)}) custom-call(f32[512,256]{1,0:T(8,128)S(1)} %collective-permute-done.7.u.u_even, f32[1024,256]{1,0:T(8,128)S(1)} %get-tuple-element.89.c.c_even, s32[3,512,1024]{2,1,0:T(8,128)S(1)} %bitcast.1, s32[3,1024]{1,0:T(4,128)S(1)} %copy-done, ...), custom_call_target="tpu_custom_call" | custom-call | flops 1024 | bytes 1024 | tf_op jit(solution)/shard_map/third_even_end/pallas_call | solution.py:85
  31.2 1.4 %collective-permute-start.8 = (f32[256,256]{1,0:T(8,128)S(1)}, f32[256,256]{1,0:T(8,128)S(1)}, u32[]{:S(2)}, u32[]{:S(2)}) collective-permute-start(f32[256,256]{1,0:T(8,128)S(1)} %get-tuple-element.93), channel_id=1, source_target_pairs={{0,14},{1,15},{2,0},{3,1},{4,2},{5,3},{6,4},{7,5},{8,6},{9,7},{10,... | collective-permute-start | bytes 786440 | tf_op jit(solution)/shard_map/ppermute | solution.py:320
  32.6 0.0 collective-permute-done.4.g1.after
  32.6 2.4 %third_context.1 = (f32[1024,256]{1,0:T(8,128)}, f32[1024,256]{1,0:T(8,128)}) custom-call(f32[512,256]{1,0:T(8,128)S(1)} %get-tuple-element.83.u.u2.u_odd, f32[1024,256]{1,0:T(8,128)S(1)} %get-tuple-element.82.c.c_odd, f32[1024,256]{1,0:T(8,128)S(1)} %get-tuple-element.98.h_odd, bf16[256,1024]{1,0:T(8,128)(2,1)S(1)} %get-tuple-element.99.rh_odd, ...), custom_call_target="tpu_custom_call" | custom-call | flops 10000000000 | bytes 1024 | tf_op jit(solution)/shard_map/third_context/pallas_call | solution.py:85
  35.0 6.4 %collective-permute-done.9.g2 = f32[256,256]{1,0:T(8,128)S(1)} collective-permute-done((f32[256,256]{1,0:T(8,128)S(1)}, f32[256,256]{1,0:T(8,128)S(1)}, u32[]{:S(2)}, u32[]{:S(2)}) %collective-permute-start.9) | collective-permute-done | bytes 262176 | tf_op jit(solution)/shard_map/ppermute | solution.py:320
  41.4 0.9 %last_top.1 = (f32[512,256]{1,0:T(8,128)}, f32[512,256]{1,0:T(8,128)}) custom-call(f32[2,288,256]{2,1,0:T(8,128)S(1)} %get-tuple-element.57.s1_top, f32[2,224,256]{2,1,0:T(8,128)S(1)} %get-tuple-element.59.s1_end, f32[512,256]{1,0:T(8,128)S(1)} %collective-permute-done.4.g1.after, f32[512,256]{1,0:T(8,128)S(1)} %get-tuple-element.83.u.u2.u_odd, ...), custom_call_target="tpu_custom_call" | custom-call | flops 1024 | bytes 1024 | tf_op jit(solution)/shard_map/last_top/pallas_call | solution.py:85
  42.3 1.9 %collective-permute-done.8.g2 = f32[256,256]{1,0:T(8,128)S(1)} collective-permute-done((f32[256,256]{1,0:T(8,128)S(1)}, f32[256,256]{1,0:T(8,128)S(1)}, u32[]{:S(2)}, u32[]{:S(2)}) %collective-permute-start.8) | collective-permute-done | bytes 262176 | tf_op jit(solution)/shard_map/ppermute | solution.py:320
  44.2 0.9 %last_end.1 = (f32[512,256]{1,0:T(8,128)}, f32[512,256]{1,0:T(8,128)}) custom-call(f32[2,288,256]{2,1,0:T(8,128)S(1)} %get-tuple-element.57.s1_top, f32[2,224,256]{2,1,0:T(8,128)S(1)} %get-tuple-element.59.s1_end, f32[512,256]{1,0:T(8,128)S(1)} %collective-permute-done.4.g1.after, ...), custom_call_target="tpu_custom_call", output_to_operand_aliasing={{0}: (5, {}), {1}: (6, {})} | custom-call | flops 1024 | bytes 1024 | tf_op jit(solution)/shard_map/last_end/pallas_call | solution.py:85
  (4 shorter events, 0.1 us)
Async XLA Ops:
  0.8 16.7 %collective-permute-start.3 = (f32[2,288,256]{2,1,0:T(8,128)S(1)}, f32[2,288,256]{2,1,0:T(8,128)S(1)}, u32[]{:S(2)}, u32[]{:S(2)}) collective-permute-start(f32[2,288,256]{2,1,0:T(8,128)S(1)} %get-tuple-element.57.s1_top), channel_id=1, source_target_pairs={{0,1},{1,2},{2,3},{3,4},{4,5},{5,6},{6,7},{7,8},{8,9},{9,10},{10,1... | collective-permute-start | bytes 1769480 | tf_op jit(solution)/shard_map/ppermute | solution.py:320
  4.3 7.4 %slice-start = ((s8[6291456]{0:T(1024)(128)(4,1)}), s8[4194304]{0:T(1024)(128)(4,1)S(1)}, s32[]{:S(2)}) async-start(s8[6291456]{0:T(1024)(128)(4,1)} %bitcast), calls=%async_computation | async-start | bytes 8388608
  4.4 7.3 %slice-start.1 = ((s8[6291456]{0:T(1024)(128)(4,1)}), s8[2097152]{0:T(1024)(128)(4,1)S(1)}, s32[]{:S(2)}) async-start(s8[6291456]{0:T(1024)(128)(4,1)} %bitcast), calls=%async_computation.1 | async-start | bytes 4194304
  4.4 7.3 %copy-start = (s32[3,1024]{1,0:T(4,128)S(1)}, s32[3,1024]{1,0:T(4,128)}, u32[]{:S(2)}) copy-start(s32[3,1024]{1,0:T(4,128)} %w.19) | copy-start | bytes 36868
  9.0 2.0 %collective-permute-start.1 = (f32[512,256]{1,0:T(8,128)S(1)}, f32[512,256]{1,0:T(8,128)S(1)}, u32[]{:S(2)}, u32[]{:S(2)}) collective-permute-start(f32[512,256]{1,0:T(8,128)S(1)} %get-tuple-element.69), channel_id=1, source_target_pairs={{0,1},{1,0},{2,3},{3,2},{4,5},{5,4},{6,7},{7,6},{8,9},{9,8},{10,11... | collective-permute-start | bytes 1572872 | tf_op jit(solution)/shard_map/ppermute | solution.py:320
  9.4 2.3 %collective-permute-start.2 = (f32[512,256]{1,0:T(8,128)S(1)}, f32[512,256]{1,0:T(8,128)S(1)}, u32[]{:S(2)}, u32[]{:S(2)}) collective-permute-start(f32[512,256]{1,0:T(8,128)S(1)} %get-tuple-element.70), channel_id=1, source_target_pairs={{0,1},{1,0},{2,3},{3,2},{4,5},{5,4},{6,7},{7,6},{8,9},{9,8},{10,11... | collective-permute-start | bytes 1572872 | tf_op jit(solution)/shard_map/ppermute | solution.py:320
  9.5 12.2 %collective-permute-start = (f32[2,224,256]{2,1,0:T(8,128)S(1)}, f32[2,224,256]{2,1,0:T(8,128)S(1)}, u32[]{:S(2)}, u32[]{:S(2)}) collective-permute-start(f32[2,224,256]{2,1,0:T(8,128)S(1)} %get-tuple-element.59.s1_end), channel_id=1, source_target_pairs={{0,1},{1,2},{2,3},{3,4},{4,5},{5,6},{6,7},{7,8},{8,9},{9,10},{10,1... | collective-permute-start | bytes 1376264 | tf_op jit(solution)/shard_map/ppermute | solution.py:320
  11.7 15.7 %collective-permute-start.7 = (f32[512,256]{1,0:T(8,128)S(1)}, f32[512,256]{1,0:T(8,128)S(1)}, u32[]{:S(2)}, u32[]{:S(2)}) collective-permute-start(f32[512,256]{1,0:T(8,128)S(1)} %get-tuple-element.72.after.u2_odd), channel_id=1, source_target_pairs={{0,1},{1,2},{2,3},{3,4},{4,5},{5,6},{6,7},{7,8},{8,9},{9,10},{10,1... | collective-permute-start | bytes 1572872 | tf_op jit(solution)/shard_map/ppermute | solution.py:320
  23.0 9.6 %collective-permute-start.4 = (f32[512,256]{1,0:T(8,128)S(1)}, f32[512,256]{1,0:T(8,128)S(1)}, u32[]{:S(2)}, u32[]{:S(2)}) collective-permute-start(f32[512,256]{1,0:T(8,128)S(1)} %get-tuple-element.79), channel_id=1, source_target_pairs={{1,0},{2,1},{3,2},{4,3},{5,4},{6,5},{7,6},{8,7},{9,8},{10,9},{11,1... | collective-permute-start | bytes 1572872 | tf_op jit(solution)/shard_map/ppermute | solution.py:320
  23.1 2.6 %collective-permute-start.5 = (f32[288,256]{1,0:T(8,128)S(1)}, f32[288,256]{1,0:T(8,128)S(1)}, u32[]{:S(2)}, u32[]{:S(2)}) collective-permute-start(f32[288,256]{1,0:T(8,128)S(1)} %get-tuple-element.80), channel_id=1, source_target_pairs={{0,1},{1,0},{2,3},{3,2},{4,5},{5,4},{6,7},{7,6},{8,9},{9,8},{10,11... | collective-permute-start | bytes 884744 | tf_op jit(solution)/shard_map/ppermute | solution.py:320
  23.5 2.1 %collective-permute-start.6 = (f32[224,256]{1,0:T(8,128)S(1)}, f32[224,256]{1,0:T(8,128)S(1)}, u32[]{:S(2)}, u32[]{:S(2)}) collective-permute-start(f32[224,256]{1,0:T(8,128)S(1)} %get-tuple-element.81.after), channel_id=1, source_target_pairs={{0,1},{1,0},{2,3},{3,2},{4,5},{5,4},{6,7},{7,6},{8,9},{9,8},{10,11... | collective-permute-start | bytes 688136 | tf_op jit(solution)/shard_map/ppermute | solution.py:320
  28.8 12.6 %collective-permute-start.9 = (f32[256,256]{1,0:T(8,128)S(1)}, f32[256,256]{1,0:T(8,128)S(1)}, u32[]{:S(2)}, u32[]{:S(2)}) collective-permute-start(f32[256,256]{1,0:T(8,128)S(1)} %get-tuple-element.91.after), channel_id=1, source_target_pairs={{0,14},{1,15},{2,0},{3,1},{4,2},{5,3},{6,4},{7,5},{8,6},{9,7},{10,... | collective-permute-start | bytes 786440 | tf_op jit(solution)/shard_map/ppermute | solution.py:320
  31.2 13.1 %collective-permute-start.8 = (f32[256,256]{1,0:T(8,128)S(1)}, f32[256,256]{1,0:T(8,128)S(1)}, u32[]{:S(2)}, u32[]{:S(2)}) collective-permute-start(f32[256,256]{1,0:T(8,128)S(1)} %get-tuple-element.93), channel_id=1, source_target_pairs={{0,14},{1,15},{2,0},{3,1},{4,2},{5,3},{6,4},{7,5},{8,6},{9,7},{10,... | collective-permute-start | bytes 786440 | tf_op jit(solution)/shard_map/ppermute | solution.py:320

commit v8 on v7

--- a/solution.py
+++ b/solution.py
@@ -10,7 +10,8 @@
 F32 = jnp.float32
 BF16 = jnp.bfloat16
 RATE = 0.05
-EARLY = 9
+HALF = 12
+EARLY = 4
 VMEM = pl.BlockSpec(memory_space=pltpu.VMEM)
 HBM = pl.BlockSpec(memory_space=pltpu.HBM)
 ANY = pl.BlockSpec(memory_space=pl.ANY)
@@ -102,17 +103,18 @@
     return copies
 
 
-def first_top(u, g, c, e, w, s1, r_high, r_low, ub, cb, gb, eb, wb, sems):
+def first_top(u, g, c, e, w, s1, r_high, r_low, ub, gb, cb, eb, wb, sems):
     @pl.when(is_odd())
     def _():
-        top = pl.ds(0, ub.shape[0])
+        rows = s1.shape[1]
+        top, end = pl.ds(0, rows), pl.ds(rows, ub.shape[0] - rows)
         cols = block_of(cb.shape[0], 512)
         count = cb.shape[0] // cols
         chunks = []
         for j in range(count):
             at = pl.ds(j * cols, cols)
-            chunks += [(c.at[at], cb.at[at]), (e.at[0, top, at], eb.at[:, at])]
-        copies = load([(w, wb), (u.at[top], ub)] + chunks + [(g.at[top], gb)], sems)
+            chunks += [(c.at[at], cb.at[at]), (e.at[0, top, at], eb.at[top, at])]
+        copies = load([(w, wb), (u, ub)] + chunks + [(g, gb), (e.at[0, end], eb.at[end])], sems)
         copies[0].wait()
         copies[1].wait()
         small = block_of(cb.shape[0], 256)
@@ -123,65 +125,67 @@
                 copies[at].wait()
                 copies[at + 1].wait()
 
-        grad = vertex_pass(ub, cb, eb, wb[0:1, :], r_high, r_low, ready)
+        grad = vertex_pass(ub.at[top], cb, eb.at[top], wb[0:1, :], r_high, r_low, ready)
+        copies[-2].wait()
+        s1[0], s1[1] = adagrad(ub[top, :], gb[top, :], grad)
         copies[-1].wait()
-        s1[0], s1[1] = adagrad(ub[...], gb[...], grad)
-
-
-def first_end(u, g, h, e, w, cb, s1, r_high, r_low, ub, hb, gb, eb, wb, sems):
-    @pl.when(is_odd())
-    def _():
-        rows = ub.shape[0]
-        end = pl.ds(u.shape[0] - rows, rows)
-        for copy in load(
-            [(u.at[end], ub), (g.at[end], gb), (e.at[0, end], eb), (w, wb), (h, hb)], sems
-        ):
+
+
+def first_end(
+    u, g, c, h, e, w, u_odd, g_odd, c_odd, e_odd, w_odd,
+    s1, r_high, r_low, hb, ub, gb, cb, eb, wb, sems,
+):
+    odd = is_odd()
+
+    @pl.when(odd)
+    def _():
+        rows = s1.shape[1]
+        end = pl.ds(u_odd.shape[0] - rows, rows)
+        (copy,) = load([(h, hb)], sems)
+        grad = vertex_pass(u_odd.at[end], c_odd, e_odd.at[end], w_odd[0:1, :], r_high, r_low)
+        s1[0], s1[1] = adagrad(u_odd[end, :], g_odd[end, :], grad)
+        copy.wait()
+
+    @pl.when(jnp.logical_not(odd))
+    def _():
+        for copy in load([(w, wb), (u, ub), (c, cb), (e.at[0], eb), (g, gb)], sems):
             copy.wait()
-        grad = vertex_pass(ub, cb, eb, wb[0:1, :], r_high, r_low)
-        s1[0], s1[1] = adagrad(ub[...], gb[...], grad)
 
 
 def first_even(
-    u, g, c, e, w, u_top, u_end, c_odd, h_odd, rh_top, rl_top, rh_end, rl_end,
-    u1, g1, r_high, r_low, c_out, h_out, ub, gb, cb, eb, wb, sems,
+    u, g, c, e, w, u_odd, c_odd, h_odd, rh_top, rl_top, rh_end, rl_end,
+    u1, g1, r_high, r_low, c_out, h_out,
 ):
     odd = is_odd()
 
     @pl.when(odd)
     def _():
-        parts = [(u_top, rh_top, rl_top), (u_end, rh_end, rl_end)]
+        middle, rest = rh_top.shape[0], rh_end.shape[0]
+        parts = [
+            (u_odd.at[pl.ds(0, middle)], rh_top, rl_top),
+            (u_odd.at[pl.ds(middle, rest)], rh_end, rl_end),
+        ]
         context_pass(parts, c_odd, h_odd, c_out, h_out)
 
     @pl.when(jnp.logical_not(odd))
     def _():
-        cols = block_of(cb.shape[0], 256)
-        count = cb.shape[0] // cols
-        chunks = []
-        for j in range(count):
-            at = pl.ds(j * cols, cols)
-            chunks += [(c.at[at], cb.at[at]), (e.at[0, :, at], eb.at[:, at])]
-        copies = load([(w, wb), (u, ub)] + chunks + [(g, gb)], sems)
-        copies[0].wait()
-        copies[1].wait()
-
-        def ready(j):
-            copies[2 + 2 * j].wait()
-            copies[3 + 2 * j].wait()
-
-        grad = vertex_pass(ub, cb, eb, wb[0:1, :], r_high, r_low, ready)
-        copies[-1].wait()
-        u1[...], g1[...] = adagrad(ub[...], gb[...], grad)
-
-
-def first_context(u, c, h, r_high, r_low, after, c_out, h_out, ub, cb, hb, sems):
+        grad = vertex_pass(u, c, e, w[0:1, :], r_high, r_low)
+        u1[...], g1[...] = adagrad(u[...], g[...], grad)
+
+
+def first_context(h, u, c, r_high, r_low, after, c_out, h_out, hb, sems):
     @pl.when(jnp.logical_not(is_odd()))
     def _():
-        for copy in load([(u, ub), (c, cb), (h, hb)], sems):
+        for copy in load([(h, hb)], sems):
             copy.wait()
-        context_pass([(ub, r_high, r_low)], cb, hb, c_out, h_out)
-
-
-def second_odd(u1, g1, c, e, w, u2, g2, r_high, r_low):
+        context_pass([(u, r_high, r_low)], c, hb, c_out, h_out)
+
+
+def gate(arrived, out):
+    out[...] = jnp.zeros_like(out)
+
+
+def second_odd(u1, g1, c, e, w, after, u2, g2, r_high, r_low):
     @pl.when(is_odd())
     def _():
         grad = vertex_pass(u1, c, e.at[1], w[1:2, :], r_high, r_low)
@@ -325,11 +329,8 @@
     block = f32(nrows, width)
     ctx = f32(ncols, width)
     half = jax.ShapeDtypeStruct((nrows, ncols), BF16)
-    half_buf = pltpu.VMEM((nrows, ncols), BF16)
     vert_buf = pltpu.VMEM((nrows, width), F32)
     ctx_buf = pltpu.VMEM((ncols, width), F32)
-    edge_buf = pltpu.VMEM((nrows, ncols), jnp.int32)
-    weight_buf = pltpu.VMEM(negative_weights.shape, jnp.int32)
     sems = pltpu.SemaphoreType.DMA((4 + 2 * (ncols // block_of(ncols, 256)),))
     hbm = [
         pltpu.with_memory_space_constraint(x, pltpu.HBM)
@@ -340,32 +341,31 @@
         return [f32(2, rows, width)] + [jax.ShapeDtypeStruct((rows, ncols), BF16)] * 2
 
     early = EARLY * nrows // 256 * 16
-    s1t, rht, rlt, ut, cb = call(
-        first_top, [HBM] * 5, stage(early) + [f32(early, width), ctx],
-        [pltpu.VMEM((early, width), F32), pltpu.VMEM((early, ncols), jnp.int32), weight_buf, sems],
-        (*hbm[:3], *hbm[4:]), "first_top",
+    edges = jax.ShapeDtypeStruct((nrows, ncols), jnp.int32)
+    weights = jax.ShapeDtypeStruct(negative_weights.shape, jnp.int32)
+    operands = [block, block, ctx, edges, weights]
+    s1t, rht, rlt, *odds = call(
+        first_top, [HBM] * 5, stage(early) + operands, [sems], (*hbm[:3], *hbm[4:]), "first_top",
     )
     s1tx = move(s1t, ring)
     rest = nrows - early
-    s1d, rhd, rld, ud, hb = call(
-        first_end, [HBM] * 5 + [VMEM], stage(rest) + [f32(rest, width), ctx],
-        [pltpu.VMEM((rest, width), F32), pltpu.VMEM((rest, ncols), jnp.int32), weight_buf, sems],
-        (*hbm[:2], *hbm[3:], cb), "first_end",
+    s1d, rhd, rld, hb, *evens = call(
+        first_end, [HBM] * 6 + [VMEM] * 5, stage(rest) + [ctx] + operands, [sems], (*hbm, *odds), "first_end",
     )
     s1dx = move(s1d, ring)
     *s1, rhe0, rle0, c1o, h1o = call(
-        first_even, [HBM] * 5 + [VMEM] * 8, [block, block, half, half, ctx, ctx],
-        [vert_buf, vert_buf, ctx_buf, edge_buf, weight_buf, sems],
-        (*hbm[:3], *hbm[4:], ut, ud, cb, hb, rht, rlt, rhd, rld), "first_even",
+        first_even, [VMEM] * 12, [block, block, half, half, ctx, ctx], [],
+        (*evens, odds[0], odds[2], hb, rht, rlt, rhd, rld), "first_even",
     )
     s1i = [move(x, swap) for x in s1]
+    (gated,) = call(gate, [ANY], [f32(8, 128)], [], (s1tx,), "gate", 7000000000)
     u2e, m2e, rho1, rlo1 = call(
-        second_odd, [VMEM] * 5, [block, block, half, half], [],
-        (*s1i, c1o, edge_counts, negative_weights), "second_odd",
+        second_odd, [VMEM] * 5 + [ANY], [block, block, half, half], [],
+        (*s1i, c1o, edge_counts, negative_weights, gated), "second_odd",
     )
     c1e, h1e = call(
-        first_context, [HBM] * 3 + [VMEM] * 2 + [ANY], [ctx, ctx], [vert_buf, ctx_buf, ctx_buf, sems],
-        (hbm[0], hbm[2], hbm[3], rhe0, rle0, u2e), "first_context",
+        first_context, [HBM] + [VMEM] * 4 + [ANY], [ctx, ctx], [ctx_buf, sems],
+        (hbm[3], evens[0], evens[2], rhe0, rle0, u2e), "first_context",
     )
     u2x = move(u2e, ring)
     u2t, g1t, rht1, rlt1, c2o, h2o = call(
@@ -383,9 +383,11 @@
         second_context, [VMEM] * 8, [ctx, ctx], [],
         (s1tx, s1dx, c1e, h1e, rht1, rlt1, rhd1, rld1), "second_context",
     )
-    half_rows = nrows // 2
+    half_rows = HALF * nrows // 256 * 16
     part = stage(half_rows)[1:]
     half_block = f32(half_rows, width)
+    end_part = stage(nrows - half_rows)[1:]
+    end_block = f32(nrows - half_rows, width)
     u2i, g2ot, rhot, rlot = call(
         third_odd_top, [VMEM] * 5 + [ANY], [block, half_block] + part, [],
         (u2ti, u2di, c2o, edge_counts, negative_weights, u2d), "third_odd_top",
@@ -396,11 +398,11 @@
     )
     g2tx = move(g2t, home)
     g2od, rhod, rlod = call(
-        third_odd_end, [VMEM] * 4 + [ANY], [half_block] + part, [],
+        third_odd_end, [VMEM] * 4 + [ANY], [end_block] + end_part, [],
         (u2i, c2o, edge_counts, negative_weights, g2t), "third_odd_end",
     )
     g2d, rhed, rled = call(
-        functools.partial(third_even, half_rows), [VMEM] * 5, [half_block] + part, [],
+        functools.partial(third_even, half_rows), [VMEM] * 5, [end_block] + end_part, [],
         (u2x, c2e, edge_counts, negative_weights, g2od), "third_even_end",
     )
     g2dx = move(g2d, home)
@@ -409,14 +411,16 @@
         (u2i, c2o, h2o, rhot, rlot, rhod, rlod, u2x, c2e, h2e, rhet, rlet, rhed, rled, g1x),
         "third_context", 10000000000,
     )
-    out_buf = pltpu.VMEM((half_rows, width), F32)
-    out_scratch = [out_buf, out_buf, pltpu.SemaphoreType.DMA((2,))]
+
+    def out_scratch(rows):
+        return [pltpu.VMEM((rows, width), F32)] * 2 + [pltpu.SemaphoreType.DMA((2,))]
+
     u3, g3 = call(
-        functools.partial(last, 0), [VMEM] * 5, [block, block], out_scratch,
+        functools.partial(last, 0), [VMEM] * 5, [block, block], out_scratch(half_rows),
         (s1t, s1d, g1x, u2i, g2tx), "last_top", out_spec=HBM,
     )
     u3, g3 = call(
-        functools.partial(last_end, half_rows), [VMEM] * 5 + [HBM] * 2, [block, block], out_scratch,
+        functools.partial(last_end, half_rows), [VMEM] * 5 + [HBM] * 2, [block, block], out_scratch(nrows - half_rows),
         (s1t, s1d, g1x, u2i, g2dx, u3, g3), "last_end", out_spec=HBM, aliases={5: 0, 6: 1},
     )
     return u3, g3, c3, h3

time: 45.4 us -> 45 us (level)
  waiting for transfers between devices: 15.2 us -> 13.4 us
  starting transfers between devices: 10.3 us -> 11 us
  Pallas kernels: 18.8 us -> 19.4 us
    ppermute x10, waiting for transfers between devices: 15.2 us -> 13.4 us  [move(): return lax.ppermute(value, 'inner', pairs)]
    pallas_call x15 -> x16, Pallas kernels: 18.8 us -> 19.4 us  [call(): pl.pallas_call(body, out_shape=outs, in_specs=in_specs, out_specs=[out_sp...]
    ppermute x10, starting transfers between devices: 10.3 us -> 11 us  [move(): return lax.ppermute(value, 'inner', pairs)]
  transfers between devices with their start and end apart: 10 -> 10, of which waited for: 7 -> 6; matrix products, arithmetic and copies ran while one was open for 0% -> 0% of each run, Pallas kernels for 39% -> 41%
where the time goes in v8:
time: 45 us; the launch traced here: 44.8 us
  Pallas kernels  19.4 us (43%)
  waiting for transfers between devices  13.4 us (30%)
  starting transfers between devices  11 us (24%)
  between operations  0.94 us (2%)
    pallas_call x16, Pallas kernels, call(): pl.pallas_call(body, out_shape=outs, in_specs=in_specs, out_specs=[out_sp...  19.4 us
    ppermute x10, waiting for transfers between devices, move(): return lax.ppermute(value, 'inner', pairs)  13.4 us
    ppermute x10, starting transfers between devices, move(): return lax.ppermute(value, 'inner', pairs)  11 us
  transfers between devices with their start and end apart: 10, of which 6 were waited for; matrix products, arithmetic and copies ran while one was open for 0% of the time, Pallas kernels for 41%

profile of v8, /device:TPU:0, one launch (start us, length us, event | category | flops | bytes accessed | tf_op | source)
XLA Modules:
  0.0 44.8 jit_solution(1064071878679502465)
XLA Ops:
  0.6 0.1 first_top.1
  0.8 3.1 %collective-permute-start.3 = (f32[2,128,256]{2,1,0:T(8,128)S(1)}, f32[2,128,256]{2,1,0:T(8,128)S(1)}, u32[]{:S(2)}, u32[]{:S(2)}) collective-permute-start(f32[2,128,256]{2,1,0:T(8,128)S(1)} %get-tuple-element.64.s1_top), channel_id=1, source_target_pairs={{0,1},{1,2},{2,3},{3,4},{4,5},{5,6},{6,7},{7,8},{8,9},{9,10},{10,1... | collective-permute-start | bytes 786440 | tf_op jit(solution)/shard_map/ppermute | solution.py:324
  3.8 2.3 %first_end.1 = (f32[2,384,256]{2,1,0:T(8,128)S(1)}, bf16[384,1024]{1,0:T(8,128)(2,1)S(1)}, bf16[384,1024]{1,0:T(8,128)(2,1)S(1)}, f32[1024,256]{1,0:T(8,128)S(1)...) custom-call(f32[512,256]{1,0:T(8,128)} %u.3, ...), custom_call_target="tpu_custom_call" | custom-call | flops 1024 | bytes 1024 | tf_op jit(solution)/shard_map/first_end/pallas_call | solution.py:86
  6.1 0.7 %collective-permute-start = (f32[2,384,256]{2,1,0:T(8,128)S(1)}, f32[2,384,256]{2,1,0:T(8,128)S(1)}, u32[]{:S(2)}, u32[]{:S(2)}) collective-permute-start(f32[2,384,256]{2,1,0:T(8,128)S(1)} %get-tuple-element.70.s1_end), channel_id=1, source_target_pairs={{0,1},{1,2},{2,3},{3,4},{4,5},{5,6},{6,7},{7,8},{8,9},{9,10},{10,1... | collective-permute-start | bytes 2359304 | tf_op jit(solution)/shard_map/ppermute | solution.py:324
  6.8 0.0 slice-start
  6.8 2.3 %first_even.1 = (f32[512,256]{1,0:T(8,128)S(1)}, f32[512,256]{1,0:T(8,128)S(1)}, bf16[512,1024]{1,0:T(8,128)(2,1)S(1)}, bf16[512,1024]{1,0:T(8,128)(2,1)S(1)}, f...) custom-call(f32[512,256]{1,0:T(8,128)S(1)} %get-tuple-element.71.u, f32[512,256]{1,0:T(8,128)S(1)} %get-tuple-element.73.g, ...), custom_call_target="tpu_custom_call" | custom-call | flops 1024 | bytes 1024 | tf_op jit(solution)/shard_map/first_even/pallas_call | solution.py:86
  9.1 1.1 %collective-permute-start.1 = (f32[512,256]{1,0:T(8,128)S(1)}, f32[512,256]{1,0:T(8,128)S(1)}, u32[]{:S(2)}, u32[]{:S(2)}) collective-permute-start(f32[512,256]{1,0:T(8,128)S(1)} %get-tuple-element.83), channel_id=1, source_target_pairs={{0,1},{1,0},{2,3},{3,2},{4,5},{5,4},{6,7},{7,6},{8,9},{9,8},{10,11... | collective-permute-start | bytes 1572872 | tf_op jit(solution)/shard_map/ppermute | solution.py:324
  10.2 0.0 slice-start.1
  10.2 0.0 copy-start
  10.2 0.1 collective-permute-start.2
  10.3 2.6 %collective-permute-done.3.arrived.s1.s1_top = f32[2,128,256]{2,1,0:T(8,128)S(1)} collective-permute-done((f32[2,128,256]{2,1,0:T(8,128)S(1)}, f32[2,128,256]{2,1,0:T(8,128)S(1)}, u32[]{:S(2)}, u32[]{:S(2)}) %collective-permute-start.3) | collective-permute-done | bytes 262176 | tf_op jit(solution)/shard_map/ppermute | solution.py:324
  12.9 0.0 collective-permute-done.1.u1.u_odd
  12.9 0.0 collective-permute-done.2.g1
  12.9 0.0 slice-done
  12.9 0.0 slice-done.1
  12.9 0.0 copy-done
  13.0 2.3 %collective-permute-start.7 = (f32[512,256]{1,0:T(8,128)S(1)}, f32[512,256]{1,0:T(8,128)S(1)}, u32[]{:S(2)}, u32[]{:S(2)}) collective-permute-start(f32[512,256]{1,0:T(8,128)S(1)} %get-tuple-element.86.after.u2_odd), channel_id=1, source_target_pairs={{0,1},{1,2},{2,3},{3,4},{4,5},{5,6},{6,7},{7,8},{8,9},{9,10},{10,1... | collective-permute-start | bytes 1572872 | tf_op jit(solution)/shard_map/ppermute | solution.py:324
  15.3 2.5 %first_context.1 = (f32[1024,256]{1,0:T(8,128)S(1)}, f32[1024,256]{1,0:T(8,128)S(1)}) custom-call(f32[1024,256]{1,0:T(8,128)} %h.3, f32[512,256]{1,0:T(8,128)S(1)} %get-tuple-element.71.u, f32[1024,256]{1,0:T(8,128)S(1)} %get-tuple-element.72.c, bf16[512,1024]{1,0:T(8,128)(2,1)S(1)} %get-tuple-element.81.r_high, ...), custom_call_target="tpu_custom_call" | custom-call | flops 1024 | bytes 1024 | tf_op jit(solution)/shard_map/first_context/pallas_call | solution.py:86
  17.8 1.2 %second_top.1 = (f32[128,256]{1,0:T(8,128)S(1)}, f32[128,256]{1,0:T(8,128)S(1)}, bf16[128,1024]{1,0:T(8,128)(2,1)S(1)}, bf16[128,1024]{1,0:T(8,128)(2,1)S(1)}, f...) custom-call(f32[2,128,256]{2,1,0:T(8,128)S(1)} %collective-permute-done.3.arrived.s1.s1_top, ...), custom_call_target="tpu_custom_call" | custom-call | flops 1024 | bytes 1024 | tf_op jit(solution)/shard_map/second_top/pallas_call | solution.py:86
  19.1 2.3 %collective-permute-done.s1.s1_end = f32[2,384,256]{2,1,0:T(8,128)S(1)} collective-permute-done((f32[2,384,256]{2,1,0:T(8,128)S(1)}, f32[2,384,256]{2,1,0:T(8,128)S(1)}, u32[]{:S(2)}, u32[]{:S(2)}) %collective-permute-start) | collective-permute-done | bytes 786464 | tf_op jit(solution)/shard_map/ppermute | solution.py:324
  21.4 1.8 %second_end.1 = (f32[384,256]{1,0:T(8,128)S(1)}, f32[512,256]{1,0:T(8,128)S(1)}, bf16[384,1024]{1,0:T(8,128)(2,1)S(1)}, bf16[384,1024]{1,0:T(8,128)(2,1)S(1)}) custom-call(f32[2,384,256]{2,1,0:T(8,128)S(1)} %collective-permute-done.s1.s1_end, f32[1024,256]{1,0:T(8,128)S(1)} %get-tuple-element.87.c, s32[3,512,1024]{2,1,0:T(8,128)S(1)} %bitcast.1, ...), custom_call_target="tpu_custom_call" | custom-call | flops 1024 | bytes 1024 | tf_op jit(solution)/shard_map/second_end/pallas_call | solution.py:86
  23.2 0.1 collective-permute-start.4
  23.3 0.5 %collective-permute-start.6 = (f32[384,256]{1,0:T(8,128)S(1)}, f32[384,256]{1,0:T(8,128)S(1)}, u32[]{:S(2)}, u32[]{:S(2)}) collective-permute-start(f32[384,256]{1,0:T(8,128)S(1)} %get-tuple-element.95.after), channel_id=1, source_target_pairs={{0,1},{1,0},{2,3},{3,2},{4,5},{5,4},{6,7},{7,6},{8,9},{9,8},{10,11... | collective-permute-start | bytes 1179656 | tf_op jit(solution)/shard_map/ppermute | solution.py:324
  23.8 0.1 collective-permute-start.5
  23.9 1.5 %second_context.1 = (f32[1024,256]{1,0:T(8,128)S(1)}, f32[1024,256]{1,0:T(8,128)S(1)}) custom-call(f32[2,128,256]{2,1,0:T(8,128)S(1)} %collective-permute-done.3.arrived.s1.s1_top, f32[2,384,256]{2,1,0:T(8,128)S(1)} %collective-permute-done.s1.s1_end, f32[1024,256]{1,0:T(8,128)S(1)} %get-tuple-element.87.c, f32[1024,256]{1,0:T(8,128)S(1)} %get-tuple-element.98.h, ...), custom_call_target="tpu_custom_call" | custom-call | flops 1024 | bytes 1024 | tf_op jit(solution)/shard_map/second_context/pallas_call | solution.py:86
  25.4 0.6 %collective-permute-done.5.u_top = f32[128,256]{1,0:T(8,128)S(1)} collective-permute-done((f32[128,256]{1,0:T(8,128)S(1)}, f32[128,256]{1,0:T(8,128)S(1)}, u32[]{:S(2)}, u32[]{:S(2)}) %collective-permute-start.5) | collective-permute-done | bytes 131104 | tf_op jit(solution)/shard_map/ppermute | solution.py:324
  25.9 0.0 collective-permute-done.6.u_end
  26.0 1.2 %collective-permute-done.7.u.u_even = f32[512,256]{1,0:T(8,128)S(1)} collective-permute-done((f32[512,256]{1,0:T(8,128)S(1)}, f32[512,256]{1,0:T(8,128)S(1)}, u32[]{:S(2)}, u32[]{:S(2)}) %collective-permute-start.7) | collective-permute-done | bytes 524320 | tf_op jit(solution)/shard_map/ppermute | solution.py:324
  27.1 1.8 %third_even_top.1 = (f32[384,256]{1,0:T(8,128)S(1)}, bf16[384,1024]{1,0:T(8,128)(2,1)S(1)}, bf16[384,1024]{1,0:T(8,128)(2,1)S(1)}) custom-call(f32[512,256]{1,0:T(8,128)S(1)} %collective-permute-done.7.u.u_even, f32[1024,256]{1,0:T(8,128)S(1)} %get-tuple-element.103.c.c_even, s32[3,512,1024]{2,1,0:T(8,128)S(1)} %bitcast.1, s32[3,1024]{1,0:T(4,128)S(1)} %copy-done, ...), custom_call_target="tpu_custom_call" | custom-call | flops 1024 | bytes 1024 | tf_op jit(solution)/shard_map/third_even_top/pallas_call | solution.py:86
  28.9 1.5 %collective-permute-start.9 = (f32[384,256]{1,0:T(8,128)S(1)}, f32[384,256]{1,0:T(8,128)S(1)}, u32[]{:S(2)}, u32[]{:S(2)}) collective-permute-start(f32[384,256]{1,0:T(8,128)S(1)} %get-tuple-element.105.after), channel_id=1, source_target_pairs={{0,14},{1,15},{2,0},{3,1},{4,2},{5,3},{6,4},{7,5},{8,6},{9,7},{10,... | collective-permute-start | bytes 1179656 | tf_op jit(solution)/shard_map/ppermute | solution.py:324
  30.4 1.2 %third_even_end.1 = (f32[128,256]{1,0:T(8,128)S(1)}, bf16[128,1024]{1,0:T(8,128)(2,1)S(1)}, bf16[128,1024]{1,0:T(8,128)(2,1)S(1)}) custom-call(f32[512,256]{1,0:T(8,128)S(1)} %collective-permute-done.7.u.u_even, f32[1024,256]{1,0:T(8,128)S(1)} %get-tuple-element.103.c.c_even, s32[3,512,1024]{2,1,0:T(8,128)S(1)} %bitcast.1, s32[3,1024]{1,0:T(4,128)S(1)} %copy-done, ...), custom_call_target="tpu_custom_call" | custom-call | flops 1024 | bytes 1024 | tf_op jit(solution)/shard_map/third_even_end/pallas_call | solution.py:86
  31.7 1.5 %collective-permute-start.8 = (f32[128,256]{1,0:T(8,128)S(1)}, f32[128,256]{1,0:T(8,128)S(1)}, u32[]{:S(2)}, u32[]{:S(2)}) collective-permute-start(f32[128,256]{1,0:T(8,128)S(1)} %get-tuple-element.107), channel_id=1, source_target_pairs={{0,14},{1,15},{2,0},{3,1},{4,2},{5,3},{6,4},{7,5},{8,6},{9,7},{10,... | collective-permute-start | bytes 393224 | tf_op jit(solution)/shard_map/ppermute | solution.py:324
  33.2 0.0 collective-permute-done.4.g1.after
  33.2 2.9 %third_context.1 = (f32[1024,256]{1,0:T(8,128)}, f32[1024,256]{1,0:T(8,128)}) custom-call(f32[512,256]{1,0:T(8,128)S(1)} %get-tuple-element.97.u.u2.u_odd, f32[1024,256]{1,0:T(8,128)S(1)} %get-tuple-element.96.c.c_odd, f32[1024,256]{1,0:T(8,128)S(1)} %get-tuple-element.112.h_odd, bf16[384,1024]{1,0:T(8,128)(2,1)S(1)} %get-tuple-element.113.rh_odd, ...), custom_call_target="tpu_custom_call" | custom-call | flops 10000000000 | bytes 1024 | tf_op jit(solution)/shard_map/third_context/pallas_call | solution.py:86
  36.1 6.4 %collective-permute-done.9.g2 = f32[384,256]{1,0:T(8,128)S(1)} collective-permute-done((f32[384,256]{1,0:T(8,128)S(1)}, f32[384,256]{1,0:T(8,128)S(1)}, u32[]{:S(2)}, u32[]{:S(2)}) %collective-permute-start.9) | collective-permute-done | bytes 393248 | tf_op jit(solution)/shard_map/ppermute | solution.py:324
  42.5 1.0 %last_top.1 = (f32[512,256]{1,0:T(8,128)}, f32[512,256]{1,0:T(8,128)}) custom-call(f32[2,128,256]{2,1,0:T(8,128)S(1)} %get-tuple-element.64.s1_top, f32[2,384,256]{2,1,0:T(8,128)S(1)} %get-tuple-element.70.s1_end, f32[512,256]{1,0:T(8,128)S(1)} %collective-permute-done.4.g1.after, f32[512,256]{1,0:T(8,128)S(1)} %get-tuple-element.97.u.u2.u_odd, ...), custom_call_target="tpu_custom_call" | custom-call | flops 1024 | bytes 1024 | tf_op jit(solution)/shard_map/last_top/pallas_call | solution.py:86
  43.5 0.4 collective-permute-done.8.g2
  43.9 0.7 %last_end.1 = (f32[512,256]{1,0:T(8,128)}, f32[512,256]{1,0:T(8,128)}) custom-call(f32[2,128,256]{2,1,0:T(8,128)S(1)} %get-tuple-element.64.s1_top, f32[2,384,256]{2,1,0:T(8,128)S(1)} %get-tuple-element.70.s1_end, f32[512,256]{1,0:T(8,128)S(1)} %collective-permute-done.4.g1.after, ...), custom_call_target="tpu_custom_call", output_to_operand_aliasing={{0}: (5, {}), {1}: (6, {})} | custom-call | flops 1024 | bytes 1024 | tf_op jit(solution)/shard_map/last_end/pallas_call | solution.py:86
  (5 shorter events, 0.1 us)
Async XLA Ops:
  0.8 12.1 %collective-permute-start.3 = (f32[2,128,256]{2,1,0:T(8,128)S(1)}, f32[2,128,256]{2,1,0:T(8,128)S(1)}, u32[]{:S(2)}, u32[]{:S(2)}) collective-permute-start(f32[2,128,256]{2,1,0:T(8,128)S(1)} %get-tuple-element.64.s1_top), channel_id=1, source_target_pairs={{0,1},{1,2},{2,3},{3,4},{4,5},{5,6},{6,7},{7,8},{8,9},{9,10},{10,1... | collective-permute-start | bytes 786440 | tf_op jit(solution)/shard_map/ppermute | solution.py:324
  6.1 15.3 %collective-permute-start = (f32[2,384,256]{2,1,0:T(8,128)S(1)}, f32[2,384,256]{2,1,0:T(8,128)S(1)}, u32[]{:S(2)}, u32[]{:S(2)}) collective-permute-start(f32[2,384,256]{2,1,0:T(8,128)S(1)} %get-tuple-element.70.s1_end), channel_id=1, source_target_pairs={{0,1},{1,2},{2,3},{3,4},{4,5},{5,6},{6,7},{7,8},{8,9},{9,10},{10,1... | collective-permute-start | bytes 2359304 | tf_op jit(solution)/shard_map/ppermute | solution.py:324
  6.8 6.1 %slice-start = ((s8[6291456]{0:T(1024)(128)(4,1)}), s8[4194304]{0:T(1024)(128)(4,1)S(1)}, s32[]{:S(2)}) async-start(s8[6291456]{0:T(1024)(128)(4,1)} %bitcast), calls=%async_computation | async-start | bytes 8388608
  9.1 3.8 %collective-permute-start.1 = (f32[512,256]{1,0:T(8,128)S(1)}, f32[512,256]{1,0:T(8,128)S(1)}, u32[]{:S(2)}, u32[]{:S(2)}) collective-permute-start(f32[512,256]{1,0:T(8,128)S(1)} %get-tuple-element.83), channel_id=1, source_target_pairs={{0,1},{1,0},{2,3},{3,2},{4,5},{5,4},{6,7},{7,6},{8,9},{9,8},{10,11... | collective-permute-start | bytes 1572872 | tf_op jit(solution)/shard_map/ppermute | solution.py:324
  10.2 2.7 %slice-start.1 = ((s8[6291456]{0:T(1024)(128)(4,1)}), s8[2097152]{0:T(1024)(128)(4,1)S(1)}, s32[]{:S(2)}) async-start(s8[6291456]{0:T(1024)(128)(4,1)} %bitcast), calls=%async_computation.1 | async-start | bytes 4194304
  10.2 2.7 %copy-start = (s32[3,1024]{1,0:T(4,128)S(1)}, s32[3,1024]{1,0:T(4,128)}, u32[]{:S(2)}) copy-start(s32[3,1024]{1,0:T(4,128)} %w.17) | copy-start | bytes 36868
  10.2 2.7 %collective-permute-start.2 = (f32[512,256]{1,0:T(8,128)S(1)}, f32[512,256]{1,0:T(8,128)S(1)}, u32[]{:S(2)}, u32[]{:S(2)}) collective-permute-start(f32[512,256]{1,0:T(8,128)S(1)} %get-tuple-element.84), channel_id=1, source_target_pairs={{0,1},{1,0},{2,3},{3,2},{4,5},{5,4},{6,7},{7,6},{8,9},{9,8},{10,11... | collective-permute-start | bytes 1572872 | tf_op jit(solution)/shard_map/ppermute | solution.py:324
  13.0 14.2 %collective-permute-start.7 = (f32[512,256]{1,0:T(8,128)S(1)}, f32[512,256]{1,0:T(8,128)S(1)}, u32[]{:S(2)}, u32[]{:S(2)}) collective-permute-start(f32[512,256]{1,0:T(8,128)S(1)} %get-tuple-element.86.after.u2_odd), channel_id=1, source_target_pairs={{0,1},{1,2},{2,3},{3,4},{4,5},{5,6},{6,7},{7,8},{8,9},{9,10},{10,1... | collective-permute-start | bytes 1572872 | tf_op jit(solution)/shard_map/ppermute | solution.py:324
  23.2 10.0 %collective-permute-start.4 = (f32[512,256]{1,0:T(8,128)S(1)}, f32[512,256]{1,0:T(8,128)S(1)}, u32[]{:S(2)}, u32[]{:S(2)}) collective-permute-start(f32[512,256]{1,0:T(8,128)S(1)} %get-tuple-element.93), channel_id=1, source_target_pairs={{1,0},{2,1},{3,2},{4,3},{5,4},{6,5},{7,6},{8,7},{9,8},{10,9},{11,1... | collective-permute-start | bytes 1572872 | tf_op jit(solution)/shard_map/ppermute | solution.py:324
  23.3 2.6 %collective-permute-start.6 = (f32[384,256]{1,0:T(8,128)S(1)}, f32[384,256]{1,0:T(8,128)S(1)}, u32[]{:S(2)}, u32[]{:S(2)}) collective-permute-start(f32[384,256]{1,0:T(8,128)S(1)} %get-tuple-element.95.after), channel_id=1, source_target_pairs={{0,1},{1,0},{2,3},{3,2},{4,5},{5,4},{6,7},{7,6},{8,9},{9,8},{10,11... | collective-permute-start | bytes 1179656 | tf_op jit(solution)/shard_map/ppermute | solution.py:324
  23.8 2.1 %collective-permute-start.5 = (f32[128,256]{1,0:T(8,128)S(1)}, f32[128,256]{1,0:T(8,128)S(1)}, u32[]{:S(2)}, u32[]{:S(2)}) collective-permute-start(f32[128,256]{1,0:T(8,128)S(1)} %get-tuple-element.94), channel_id=1, source_target_pairs={{0,1},{1,0},{2,3},{3,2},{4,5},{5,4},{6,7},{7,6},{8,9},{9,8},{10,11... | collective-permute-start | bytes 393224 | tf_op jit(solution)/shard_map/ppermute | solution.py:324
  28.9 13.5 %collective-permute-start.9 = (f32[384,256]{1,0:T(8,128)S(1)}, f32[384,256]{1,0:T(8,128)S(1)}, u32[]{:S(2)}, u32[]{:S(2)}) collective-permute-start(f32[384,256]{1,0:T(8,128)S(1)} %get-tuple-element.105.after), channel_id=1, source_target_pairs={{0,14},{1,15},{2,0},{3,1},{4,2},{5,3},{6,4},{7,5},{8,6},{9,7},{10,... | collective-permute-start | bytes 1179656 | tf_op jit(solution)/shard_map/ppermute | solution.py:324
  31.7 12.2 %collective-permute-start.8 = (f32[128,256]{1,0:T(8,128)S(1)}, f32[128,256]{1,0:T(8,128)S(1)}, u32[]{:S(2)}, u32[]{:S(2)}) collective-permute-start(f32[128,256]{1,0:T(8,128)S(1)} %get-tuple-element.107), channel_id=1, source_target_pairs={{0,14},{1,15},{2,0},{3,1},{4,2},{5,3},{6,4},{7,5},{8,6},{9,7},{10,... | collective-permute-start | bytes 393224 | tf_op jit(solution)/shard_map/ppermute | solution.py:324

commit v9 on v8

--- a/solution.py
+++ b/solution.py
@@ -10,6 +10,7 @@
 F32 = jnp.float32
 BF16 = jnp.bfloat16
 RATE = 0.05
+DETOUR = 3
 HALF = 12
 EARLY = 4
 VMEM = pl.BlockSpec(memory_space=pltpu.VMEM)
@@ -193,38 +194,40 @@
 
 
 def second_top(
-    s1, c, e, w, u_odd, c_odd, h_odd, rh_odd, rl_odd, u2_odd,
+    s1, c, e, w, u_odd, c_odd, h_odd, rh_odd, rl_odd, u2_odd, g2_odd,
     u2, grad_out, r_high, r_low, c_out, h_out,
 ):
     odd = is_odd()
-    rows = u2.shape[0]
-
-    @pl.when(odd)
-    def _():
-        u2[...] = u2_odd[:rows, :]
+    rows = grad_out.shape[0]
+
+    @pl.when(odd)
+    def _():
+        u2[:rows, :] = u2_odd[:rows, :]
+        u2[rows:, :] = g2_odd[: u2.shape[0] - rows, :]
         context_pass([(u_odd, rh_odd, rl_odd)], c_odd, h_odd, c_out, h_out)
 
     @pl.when(jnp.logical_not(odd))
     def _():
         grad = vertex_pass(s1.at[0], c, e.at[1, pl.ds(0, rows)], w[1:2, :], r_high, r_low)
         grad_out[...] = grad
-        u2[...] = adagrad(s1[0], s1[1], grad)[0]
-
-
-def second_end(s1, c, e, w, grad_top, u2_odd, g2_odd, u2, grad_out, r_high, r_low):
-    odd = is_odd()
-    middle, rows = grad_top.shape[0], u2.shape[0]
+        u2[:rows, :] = adagrad(s1[0], s1[1], grad)[0]
+
+
+def second_end(s1, c, e, w, grad_top, u2_odd, g2_odd, u2, grad_a, grad_b, r_high, r_low, buf):
+    odd = is_odd()
+    middle, rows, first = grad_top.shape[0], s1.shape[1], grad_b.shape[0]
 
     @pl.when(odd)
     def _():
         u2[...] = u2_odd[middle:, :]
-        grad_out[...] = g2_odd[...]
+        grad_a[...] = g2_odd[first:, :]
 
     @pl.when(jnp.logical_not(odd))
     def _():
         grad = vertex_pass(s1.at[0], c, e.at[1, pl.ds(middle, rows)], w[1:2, :], r_high, r_low)
-        grad_out[:middle, :] = grad_top[...]
-        grad_out[middle:, :] = grad
+        buf[:middle, :] = grad_top[...]
+        buf[middle:, :] = grad
+        grad_a[...], grad_b[...] = buf[first:, :], buf[:first, :]
         u2[...] = adagrad(s1[0], s1[1], grad)[0]
 
 
@@ -244,8 +247,9 @@
 
 
 def third_odd_top(u_top, u_end, c, e, w, after, u, g2, r_high, r_low):
-    u[: u_top.shape[0], :] = u_top[...]
-    u[u_top.shape[0] :, :] = u_end[...]
+    middle = u.shape[0] - u_end.shape[0]
+    u[:middle, :] = u_top[:middle, :]
+    u[middle:, :] = u_end[...]
     third(True, 0, u, c, e, w, g2, r_high, r_low)
 
 
@@ -259,6 +263,11 @@
         g2[...] = g2_odd[...]
 
     third(False, row, u, c, e, w, g2, r_high, r_low)
+
+
+def third_even_end(row, u, c, e, w, g2_odd, g1, g2, r_high, r_low, g1_out):
+    g1_out[...] = g1[...]
+    third_even(row, u, c, e, w, g2_odd, g2, r_high, r_low)
 
 
 def third_context(
@@ -291,21 +300,42 @@
             low, high = max(row, begin), min(row + rows, begin + s1.shape[1])
             if low < high:
                 at, here = pl.ds(low - begin, high - low), pl.ds(low - row, high - low)
-                value, moment = adagrad(s1[0, at, :], s1[1, at, :], g1[pl.ds(low, high - low), :])
+                value, moment = adagrad(s1[0, at, :], s1[1, at, :], g1[here, :])
                 ub[here, :], gb[here, :] = adagrad(value, moment, g2[here, :])
             begin += s1.shape[1]
 
     @pl.when(jnp.logical_not(odd))
     def _():
-        at = pl.ds(row, rows)
-        ub[...], gb[...] = adagrad(u2[at, :], g1[at, :], g2[...])
+        ub[...], gb[...] = adagrad(u2[pl.ds(row, rows), :], g1[...], g2[...])
 
     at = pl.ds(row, rows)
     for copy in load([(ub, u_out.at[at]), (gb, g_out.at[at])], sems):
         copy.wait()
 
 
-def last_end(row, s1_top, s1_end, g1, u2, g2, u_top, g_top, *refs):
+def last_top(s1_top, s1_end, g1_a, g1_b, g1_over, swapped, u2, g2, u_out, g_out, buf, *scratch):
+    first, rows = g1_b.shape[0], g2.shape[0]
+    place = lax.axis_index("inner")
+    odd = is_odd()
+
+    @pl.when(jnp.logical_and(odd, place != 1))
+    def _():
+        buf[:first, :] = g1_b[...]
+
+    @pl.when(place == 1)
+    def _():
+        buf[:first, :] = g1_over[...]
+
+    @pl.when(jnp.logical_not(odd))
+    def _():
+        buf[:first, :] = swapped[swapped.shape[0] - first :, :]
+
+    buf[first:, :] = g1_a[: rows - first, :]
+    last(0, s1_top, s1_end, buf, u2, g2, u_out, g_out, *scratch)
+
+
+def last_end(row, s1_top, s1_end, g1_a, u2, g2, u_top, g_top, *refs):
+    g1 = g1_a.at[pl.ds(g1_a.shape[0] - g2.shape[0], g2.shape[0])]
     last(row, s1_top, s1_end, g1, u2, g2, *refs)
 
 
@@ -313,12 +343,15 @@
     nrows, width = vertices.shape
     ncols = contexts.shape[0]
     count = lax.axis_size("inner")
-    assert count % 2 == 0 and edge_counts.shape[0] == 3
+    assert count % 2 == 0 and count > 5 and edge_counts.shape[0] == 3
 
     ring = [(i, (i + 1) % count) for i in range(count)]
     unring = [(b, a) for a, b in ring]
     swap = [(i, i ^ 1) for i in range(count)]
     home = [(i, (i - 2) % count) for i in range(count)]
+
+    def change(pairs, targets):
+        return [(a, targets.get(a, b)) for a, b in pairs]
 
     def move(value, pairs):
         return lax.ppermute(value, "inner", pairs)
@@ -368,17 +401,20 @@
         (hbm[3], evens[0], evens[2], rhe0, rle0, u2e), "first_context",
     )
     u2x = move(u2e, ring)
+    detour = DETOUR * nrows // 256 * 16
     u2t, g1t, rht1, rlt1, c2o, h2o = call(
-        second_top, [VMEM] * 10, [f32(early, width)] * 2 + stage(early)[1:] + [ctx, ctx], [],
-        (s1tx, c1e, edge_counts, negative_weights, s1i[0], c1o, h1o, rho1, rlo1, u2e), "second_top",
+        second_top, [VMEM] * 11, [f32(early + detour, width), f32(early, width)] + stage(early)[1:] + [ctx, ctx], [],
+        (s1tx, c1e, edge_counts, negative_weights, s1i[0], c1o, h1o, rho1, rlo1, u2e, m2e), "second_top",
     )
     u2ti = move(u2t, swap)
-    u2d, g1, rhd1, rld1 = call(
-        second_end, [VMEM] * 7, [f32(nrows - early, width), block] + stage(nrows - early)[1:], [],
-        (s1dx, c1e, edge_counts, negative_weights, g1t, u2e, m2e), "second_end",
+    u2d, g1a, g1b, rhd1, rld1 = call(
+        second_end, [VMEM] * 7,
+        [f32(rest, width), f32(nrows - detour, width), f32(detour, width)] + stage(rest)[1:], [vert_buf],
+        (s1dx, c1e, edge_counts, negative_weights, g1t, u2e, m2e), "second_end", 10000000000,
     )
     u2di = move(u2d, swap)
-    g1x = move(g1, unring)
+    g1ax = move(g1a, unring)
+    g1bx = move(g1b, change(unring, {2: 4, 5: 1}))
     c2e, h2e = call(
         second_context, [VMEM] * 8, [ctx, ctx], [],
         (s1tx, s1dx, c1e, h1e, rht1, rlt1, rhd1, rld1), "second_context",
@@ -401,14 +437,15 @@
         third_odd_end, [VMEM] * 4 + [ANY], [end_block] + end_part, [],
         (u2i, c2o, edge_counts, negative_weights, g2t), "third_odd_end",
     )
-    g2d, rhed, rled = call(
-        functools.partial(third_even, half_rows), [VMEM] * 5, [end_block] + end_part, [],
-        (u2x, c2e, edge_counts, negative_weights, g2od), "third_even_end",
+    g2d, rhed, rled, g1r = call(
+        functools.partial(third_even_end, half_rows), [VMEM] * 6, [end_block] + end_part + [f32(detour, width)], [],
+        (u2x, c2e, edge_counts, negative_weights, g2od, g1bx), "third_even_end", 1024,
     )
     g2dx = move(g2d, home)
+    g1rx = move(g1r, [(4, 1)])
     c3, h3 = call(
         third_context, [VMEM] * 14 + [ANY], [ctx, ctx], [],
-        (u2i, c2o, h2o, rhot, rlot, rhod, rlod, u2x, c2e, h2e, rhet, rlet, rhed, rled, g1x),
+        (u2i, c2o, h2o, rhot, rlot, rhod, rlod, u2x, c2e, h2e, rhet, rlet, rhed, rled, g1ax),
         "third_context", 10000000000,
     )
 
@@ -416,12 +453,13 @@
         return [pltpu.VMEM((rows, width), F32)] * 2 + [pltpu.SemaphoreType.DMA((2,))]
 
     u3, g3 = call(
-        functools.partial(last, 0), [VMEM] * 5, [block, block], out_scratch(half_rows),
-        (s1t, s1d, g1x, u2i, g2tx), "last_top", out_spec=HBM,
+        last_top, [VMEM] * 8, [block, block],
+        [pltpu.VMEM((half_rows, width), F32)] + out_scratch(half_rows),
+        (s1t, s1d, g1ax, g1bx, g1rx, u2ti, u2i, g2tx), "last_top", out_spec=HBM,
     )
     u3, g3 = call(
         functools.partial(last_end, half_rows), [VMEM] * 5 + [HBM] * 2, [block, block], out_scratch(nrows - half_rows),
-        (s1t, s1d, g1x, u2i, g2dx, u3, g3), "last_end", out_spec=HBM, aliases={5: 0, 6: 1},
+        (s1t, s1d, g1ax, u2i, g2dx, u3, g3), "last_end", out_spec=HBM, aliases={5: 0, 6: 1},
     )
     return u3, g3, c3, h3
 

time: 45 us -> 44 us (0.978)
  waiting for transfers between devices: 13.4 us -> 6.84 us
  starting transfers between devices: 11 us -> 16.4 us
    ppermute x10 -> x12, waiting for transfers between devices: 13.4 us -> 6.84 us  [move(): return lax.ppermute(value, 'inner', pairs)]
    ppermute x10 -> x12, starting transfers between devices: 11 us -> 16.4 us  [move(): return lax.ppermute(value, 'inner', pairs)]
  transfers between devices with their start and end apart: 10 -> 12, of which waited for: 6 -> 4; matrix products, arithmetic and copies ran while one was open for 0% -> 0% of each run, Pallas kernels for 41% -> 43%
where the time goes in v9:
time: 44 us; the launch traced here: 43.7 us
  Pallas kernels  19.5 us (44%)
  starting transfers between devices  16.4 us (37%)
  waiting for transfers between devices  6.84 us (16%)
  between operations  0.97 us (2%)
    pallas_call x16, Pallas kernels, call(): pl.pallas_call(body, out_shape=outs, in_specs=in_specs, out_specs=[out_sp...  19.5 us
    ppermute x12, starting transfers between devices, move(): return lax.ppermute(value, 'inner', pairs)  16.4 us
    ppermute x12, waiting for transfers between devices, move(): return lax.ppermute(value, 'inner', pairs)  6.84 us
  transfers between devices with their start and end apart: 12, of which 4 were waited for; matrix products, arithmetic and copies ran while one was open for 0% of the time, Pallas kernels for 43%

profile of v9, /device:TPU:0, one launch (start us, length us, event | category | flops | bytes accessed | tf_op | source)
XLA Modules:
  0.0 43.7 jit_solution(13289837184851217773)
XLA Ops:
  0.6 0.1 first_top.1
  0.8 3.1 %collective-permute-start.3 = (f32[2,128,256]{2,1,0:T(8,128)S(1)}, f32[2,128,256]{2,1,0:T(8,128)S(1)}, u32[]{:S(2)}, u32[]{:S(2)}) collective-permute-start(f32[2,128,256]{2,1,0:T(8,128)S(1)} %get-tuple-element.66.s1_top), channel_id=1, source_target_pairs={{0,1},{1,2},{2,3},{3,4},{4,5},{5,6},{6,7},{7,8},{8,9},{9,10},{10,1... | collective-permute-start | bytes 786440 | tf_op jit(solution)/shard_map/ppermute | solution.py:357
  3.8 2.3 %first_end.1 = (f32[2,384,256]{2,1,0:T(8,128)S(1)}, bf16[384,1024]{1,0:T(8,128)(2,1)S(1)}, bf16[384,1024]{1,0:T(8,128)(2,1)S(1)}, f32[1024,256]{1,0:T(8,128)S(1)...) custom-call(f32[512,256]{1,0:T(8,128)} %u.3, ...), custom_call_target="tpu_custom_call" | custom-call | flops 1024 | bytes 1024 | tf_op jit(solution)/shard_map/first_end/pallas_call | solution.py:87
  6.1 0.7 %collective-permute-start = (f32[2,384,256]{2,1,0:T(8,128)S(1)}, f32[2,384,256]{2,1,0:T(8,128)S(1)}, u32[]{:S(2)}, u32[]{:S(2)}) collective-permute-start(f32[2,384,256]{2,1,0:T(8,128)S(1)} %get-tuple-element.72.s1_end), channel_id=1, source_target_pairs={{0,1},{1,2},{2,3},{3,4},{4,5},{5,6},{6,7},{7,8},{8,9},{9,10},{10,1... | collective-permute-start | bytes 2359304 | tf_op jit(solution)/shard_map/ppermute | solution.py:357
  6.8 0.0 slice-start
  6.8 2.3 %first_even.1 = (f32[512,256]{1,0:T(8,128)S(1)}, f32[512,256]{1,0:T(8,128)S(1)}, bf16[512,1024]{1,0:T(8,128)(2,1)S(1)}, bf16[512,1024]{1,0:T(8,128)(2,1)S(1)}, f...) custom-call(f32[512,256]{1,0:T(8,128)S(1)} %get-tuple-element.73.u, f32[512,256]{1,0:T(8,128)S(1)} %get-tuple-element.75.g, ...), custom_call_target="tpu_custom_call" | custom-call | flops 1024 | bytes 1024 | tf_op jit(solution)/shard_map/first_even/pallas_call | solution.py:87
  9.1 1.1 %collective-permute-start.1 = (f32[512,256]{1,0:T(8,128)S(1)}, f32[512,256]{1,0:T(8,128)S(1)}, u32[]{:S(2)}, u32[]{:S(2)}) collective-permute-start(f32[512,256]{1,0:T(8,128)S(1)} %get-tuple-element.85), channel_id=1, source_target_pairs={{0,1},{1,0},{2,3},{3,2},{4,5},{5,4},{6,7},{7,6},{8,9},{9,8},{10,11... | collective-permute-start | bytes 1572872 | tf_op jit(solution)/shard_map/ppermute | solution.py:357
  10.2 0.0 slice-start.1
  10.2 0.0 copy-start
  10.2 0.1 collective-permute-start.2
  10.3 2.6 %collective-permute-done.3.arrived.s1.s1_top = f32[2,128,256]{2,1,0:T(8,128)S(1)} collective-permute-done((f32[2,128,256]{2,1,0:T(8,128)S(1)}, f32[2,128,256]{2,1,0:T(8,128)S(1)}, u32[]{:S(2)}, u32[]{:S(2)}) %collective-permute-start.3) | collective-permute-done | bytes 262176 | tf_op jit(solution)/shard_map/ppermute | solution.py:357
  12.9 0.0 collective-permute-done.1.u1.u_odd
  12.9 0.0 collective-permute-done.2.g1
  12.9 0.0 slice-done
  12.9 0.0 slice-done.1
  12.9 0.0 copy-done
  13.0 2.3 %collective-permute-start.7 = (f32[512,256]{1,0:T(8,128)S(1)}, f32[512,256]{1,0:T(8,128)S(1)}, u32[]{:S(2)}, u32[]{:S(2)}) collective-permute-start(f32[512,256]{1,0:T(8,128)S(1)} %get-tuple-element.88.after.u2_odd), channel_id=1, source_target_pairs={{0,1},{1,2},{2,3},{3,4},{4,5},{5,6},{6,7},{7,8},{8,9},{9,10},{10,1... | collective-permute-start | bytes 1572872 | tf_op jit(solution)/shard_map/ppermute | solution.py:357
  15.3 2.5 %first_context.1 = (f32[1024,256]{1,0:T(8,128)S(1)}, f32[1024,256]{1,0:T(8,128)S(1)}) custom-call(f32[1024,256]{1,0:T(8,128)} %h.3, f32[512,256]{1,0:T(8,128)S(1)} %get-tuple-element.73.u, f32[1024,256]{1,0:T(8,128)S(1)} %get-tuple-element.74.c, bf16[512,1024]{1,0:T(8,128)(2,1)S(1)} %get-tuple-element.83.r_high, ...), custom_call_target="tpu_custom_call" | custom-call | flops 1024 | bytes 1024 | tf_op jit(solution)/shard_map/first_context/pallas_call | solution.py:87
  17.8 1.2 %second_top.1 = (f32[224,256]{1,0:T(8,128)S(1)}, f32[128,256]{1,0:T(8,128)S(1)}, bf16[128,1024]{1,0:T(8,128)(2,1)S(1)}, bf16[128,1024]{1,0:T(8,128)(2,1)S(1)}, f...) custom-call(f32[2,128,256]{2,1,0:T(8,128)S(1)} %collective-permute-done.3.arrived.s1.s1_top, ...), custom_call_target="tpu_custom_call" | custom-call | flops 1024 | bytes 1024 | tf_op jit(solution)/shard_map/second_top/pallas_call | solution.py:87
  19.1 2.4 %collective-permute-done.s1.s1_end = f32[2,384,256]{2,1,0:T(8,128)S(1)} collective-permute-done((f32[2,384,256]{2,1,0:T(8,128)S(1)}, f32[2,384,256]{2,1,0:T(8,128)S(1)}, u32[]{:S(2)}, u32[]{:S(2)}) %collective-permute-start) | collective-permute-done | bytes 786464 | tf_op jit(solution)/shard_map/ppermute | solution.py:357
  21.4 1.8 %second_end.1 = (f32[384,256]{1,0:T(8,128)S(1)}, f32[416,256]{1,0:T(8,128)S(1)}, f32[96,256]{1,0:T(8,128)S(1)}, bf16[384,1024]{1,0:T(8,128)(2,1)S(1)}, bf16[384,1024]{1,0:T(8,128)(2,1)S(1)}) custom-call(f32[2,384,256]{2,1,0:T(8,128)S(1)} %collective-permute-done.s1.s1_end, f32[1024,256]{1,0:T(8,128)S(1)} %get-tuple-element.89.c, ...), custom_call_target="tpu_custom_call" | custom-call | flops 10000000000 | bytes 1024 | tf_op jit(solution)/shard_map/second_end/pallas_call | solution.py:87
  23.2 0.1 collective-permute-start.4
  23.3 0.5 %collective-permute-start.6 = (f32[384,256]{1,0:T(8,128)S(1)}, f32[384,256]{1,0:T(8,128)S(1)}, u32[]{:S(2)}, u32[]{:S(2)}) collective-permute-start(f32[384,256]{1,0:T(8,128)S(1)} %get-tuple-element.97.after), channel_id=1, source_target_pairs={{0,1},{1,0},{2,3},{3,2},{4,5},{5,4},{6,7},{7,6},{8,9},{9,8},{10,11... | collective-permute-start | bytes 1179656 | tf_op jit(solution)/shard_map/ppermute | solution.py:357
  23.8 0.1 collective-permute-start.5
  23.9 2.3 %collective-permute-start.8 = (f32[96,256]{1,0:T(8,128)S(1)}, f32[96,256]{1,0:T(8,128)S(1)}, u32[]{:S(2)}, u32[]{:S(2)}) collective-permute-start(f32[96,256]{1,0:T(8,128)S(1)} %get-tuple-element.109), channel_id=1, source_target_pairs={{1,0},{2,4},{3,2},{4,3},{5,1},{6,5},{7,6},{8,7},{9,8},{10,9},{11,1... | collective-permute-start | bytes 294920 | tf_op jit(solution)/shard_map/ppermute | solution.py:357
  26.2 1.5 %second_context.1 = (f32[1024,256]{1,0:T(8,128)S(1)}, f32[1024,256]{1,0:T(8,128)S(1)}) custom-call(f32[2,128,256]{2,1,0:T(8,128)S(1)} %collective-permute-done.3.arrived.s1.s1_top, f32[2,384,256]{2,1,0:T(8,128)S(1)} %collective-permute-done.s1.s1_end, f32[1024,256]{1,0:T(8,128)S(1)} %get-tuple-element.89.c, f32[1024,256]{1,0:T(8,128)S(1)} %get-tuple-element.100.h, ...), custom_call_target="tpu_custom_call" | custom-call | flops 1024 | bytes 1024 | tf_op jit(solution)/shard_map/second_context/pallas_call | solution.py:87
  27.7 0.0 collective-permute-done.5.u_top.swapped
  27.7 0.0 collective-permute-done.6.u_end
  27.8 0.0 collective-permute-done.7.u.u_even
  27.8 1.8 %third_even_top.1 = (f32[384,256]{1,0:T(8,128)S(1)}, bf16[384,1024]{1,0:T(8,128)(2,1)S(1)}, bf16[384,1024]{1,0:T(8,128)(2,1)S(1)}) custom-call(f32[512,256]{1,0:T(8,128)S(1)} %collective-permute-done.7.u.u_even, f32[1024,256]{1,0:T(8,128)S(1)} %get-tuple-element.105.c.c_even, s32[3,512,1024]{2,1,0:T(8,128)S(1)} %bitcast.1, s32[3,1024]{1,0:T(4,128)S(1)} %copy-done, ...), custom_call_target="tpu_custom_call" | custom-call | flops 1024 | bytes 1024 | tf_op jit(solution)/shard_map/third_even_top/pallas_call | solution.py:87
  29.6 0.8 %collective-permute-start.11 = (f32[384,256]{1,0:T(8,128)S(1)}, f32[384,256]{1,0:T(8,128)S(1)}, u32[]{:S(2)}, u32[]{:S(2)}) collective-permute-start(f32[384,256]{1,0:T(8,128)S(1)} %get-tuple-element.107.after), channel_id=1, source_target_pairs={{0,14},{1,15},{2,0},{3,1},{4,2},{5,3},{6,4},{7,5},{8,6},{9,7},{10,... | collective-permute-start | bytes 1179656 | tf_op jit(solution)/shard_map/ppermute | solution.py:357
  30.4 0.0 collective-permute-done.8.g1.g1_b
  30.4 1.2 %third_even_end.1 = (f32[128,256]{1,0:T(8,128)S(1)}, bf16[128,1024]{1,0:T(8,128)(2,1)S(1)}, bf16[128,1024]{1,0:T(8,128)(2,1)S(1)}, f32[96,256]{1,0:T(8,128)S(1)}) custom-call(f32[512,256]{1,0:T(8,128)S(1)} %collective-permute-done.7.u.u_even, f32[1024,256]{1,0:T(8,128)S(1)} %get-tuple-element.105.c.c_even, s32[3,512,1024]{2,1,0:T(8,128)S(1)} %bitcast.1, ...), custom_call_target="tpu_custom_call" | custom-call | flops 1024 | bytes 1024 | tf_op jit(solution)/shard_map/third_even_end/pallas_call | solution.py:87
  31.7 0.7 %collective-permute-start.10 = (f32[96,256]{1,0:T(8,128)S(1)}, f32[96,256]{1,0:T(8,128)S(1)}, u32[]{:S(2)}, u32[]{:S(2)}) collective-permute-start(f32[96,256]{1,0:T(8,128)S(1)} %get-tuple-element.111), channel_id=1, source_target_pairs={{4,1},{20,17}} | collective-permute-start | bytes 294920 | tf_op jit(solution)/shard_map/ppermute | solution.py:357
  32.4 4.7 %collective-permute-start.9 = (f32[128,256]{1,0:T(8,128)S(1)}, f32[128,256]{1,0:T(8,128)S(1)}, u32[]{:S(2)}, u32[]{:S(2)}) collective-permute-start(f32[128,256]{1,0:T(8,128)S(1)} %get-tuple-element.110), channel_id=1, source_target_pairs={{0,14},{1,15},{2,0},{3,1},{4,2},{5,3},{6,4},{7,5},{8,6},{9,7},{10,... | collective-permute-start | bytes 393224 | tf_op jit(solution)/shard_map/ppermute | solution.py:357
  37.0 0.0 collective-permute-done.4.g1_a.after
  37.0 2.9 %third_context.1 = (f32[1024,256]{1,0:T(8,128)}, f32[1024,256]{1,0:T(8,128)}) custom-call(f32[512,256]{1,0:T(8,128)S(1)} %get-tuple-element.99.u.u2.u_odd, f32[1024,256]{1,0:T(8,128)S(1)} %get-tuple-element.98.c.c_odd, f32[1024,256]{1,0:T(8,128)S(1)} %get-tuple-element.116.h_odd, bf16[384,1024]{1,0:T(8,128)(2,1)S(1)} %get-tuple-element.117.rh_odd, ...), custom_call_target="tpu_custom_call" | custom-call | flops 10000000000 | bytes 1024 | tf_op jit(solution)/shard_map/third_context/pallas_call | solution.py:87
  39.9 0.0 collective-permute-done.10.g1_over
  39.9 1.5 %collective-permute-done.11.g2 = f32[384,256]{1,0:T(8,128)S(1)} collective-permute-done((f32[384,256]{1,0:T(8,128)S(1)}, f32[384,256]{1,0:T(8,128)S(1)}, u32[]{:S(2)}, u32[]{:S(2)}) %collective-permute-start.11) | collective-permute-done | bytes 393248 | tf_op jit(solution)/shard_map/ppermute | solution.py:357
  41.4 1.0 %last_top.1 = (f32[512,256]{1,0:T(8,128)}, f32[512,256]{1,0:T(8,128)}) custom-call(f32[2,128,256]{2,1,0:T(8,128)S(1)} %get-tuple-element.66.s1_top, f32[2,384,256]{2,1,0:T(8,128)S(1)} %get-tuple-element.72.s1_end, f32[416,256]{1,0:T(8,128)S(1)} %collective-permute-done.4.g1_a.after, f32[96,256]{1,0:T(8,128)S(1)} %collective-permute-done.8.g1.g1_b, ...), custom_call_target="tpu_custom_call" | custom-call | flops 1024 | bytes 1024 | tf_op jit(solution)/shard_map/last_top/pallas_call | solution.py:87
  42.4 0.4 collective-permute-done.9.g2
  42.8 0.7 %last_end.1 = (f32[512,256]{1,0:T(8,128)}, f32[512,256]{1,0:T(8,128)}) custom-call(f32[2,128,256]{2,1,0:T(8,128)S(1)} %get-tuple-element.66.s1_top, f32[2,384,256]{2,1,0:T(8,128)S(1)} %get-tuple-element.72.s1_end, f32[416,256]{1,0:T(8,128)S(1)} %collective-permute-done.4.g1_a.after, ...), custom_call_target="tpu_custom_call", output_to_operand_aliasing={{0}: (5, {}), {1}: (6, {})} | custom-call | flops 1024 | bytes 1024 | tf_op jit(solution)/shard_map/last_end/pallas_call | solution.py:87
  (5 shorter events, 0.1 us)
Async XLA Ops:
  0.8 12.1 %collective-permute-start.3 = (f32[2,128,256]{2,1,0:T(8,128)S(1)}, f32[2,128,256]{2,1,0:T(8,128)S(1)}, u32[]{:S(2)}, u32[]{:S(2)}) collective-permute-start(f32[2,128,256]{2,1,0:T(8,128)S(1)} %get-tuple-element.66.s1_top), channel_id=1, source_target_pairs={{0,1},{1,2},{2,3},{3,4},{4,5},{5,6},{6,7},{7,8},{8,9},{9,10},{10,1... | collective-permute-start | bytes 786440 | tf_op jit(solution)/shard_map/ppermute | solution.py:357
  6.1 15.3 %collective-permute-start = (f32[2,384,256]{2,1,0:T(8,128)S(1)}, f32[2,384,256]{2,1,0:T(8,128)S(1)}, u32[]{:S(2)}, u32[]{:S(2)}) collective-permute-start(f32[2,384,256]{2,1,0:T(8,128)S(1)} %get-tuple-element.72.s1_end), channel_id=1, source_target_pairs={{0,1},{1,2},{2,3},{3,4},{4,5},{5,6},{6,7},{7,8},{8,9},{9,10},{10,1... | collective-permute-start | bytes 2359304 | tf_op jit(solution)/shard_map/ppermute | solution.py:357
  6.8 6.1 %slice-start = ((s8[6291456]{0:T(1024)(128)(4,1)}), s8[4194304]{0:T(1024)(128)(4,1)S(1)}, s32[]{:S(2)}) async-start(s8[6291456]{0:T(1024)(128)(4,1)} %bitcast), calls=%async_computation | async-start | bytes 8388608
  9.1 3.8 %collective-permute-start.1 = (f32[512,256]{1,0:T(8,128)S(1)}, f32[512,256]{1,0:T(8,128)S(1)}, u32[]{:S(2)}, u32[]{:S(2)}) collective-permute-start(f32[512,256]{1,0:T(8,128)S(1)} %get-tuple-element.85), channel_id=1, source_target_pairs={{0,1},{1,0},{2,3},{3,2},{4,5},{5,4},{6,7},{7,6},{8,9},{9,8},{10,11... | collective-permute-start | bytes 1572872 | tf_op jit(solution)/shard_map/ppermute | solution.py:357
  10.2 2.7 %slice-start.1 = ((s8[6291456]{0:T(1024)(128)(4,1)}), s8[2097152]{0:T(1024)(128)(4,1)S(1)}, s32[]{:S(2)}) async-start(s8[6291456]{0:T(1024)(128)(4,1)} %bitcast), calls=%async_computation.1 | async-start | bytes 4194304
  10.2 2.7 %copy-start = (s32[3,1024]{1,0:T(4,128)S(1)}, s32[3,1024]{1,0:T(4,128)}, u32[]{:S(2)}) copy-start(s32[3,1024]{1,0:T(4,128)} %w.17) | copy-start | bytes 36868
  10.2 2.7 %collective-permute-start.2 = (f32[512,256]{1,0:T(8,128)S(1)}, f32[512,256]{1,0:T(8,128)S(1)}, u32[]{:S(2)}, u32[]{:S(2)}) collective-permute-start(f32[512,256]{1,0:T(8,128)S(1)} %get-tuple-element.86), channel_id=1, source_target_pairs={{0,1},{1,0},{2,3},{3,2},{4,5},{5,4},{6,7},{7,6},{8,9},{9,8},{10,11... | collective-permute-start | bytes 1572872 | tf_op jit(solution)/shard_map/ppermute | solution.py:357
  13.0 14.8 %collective-permute-start.7 = (f32[512,256]{1,0:T(8,128)S(1)}, f32[512,256]{1,0:T(8,128)S(1)}, u32[]{:S(2)}, u32[]{:S(2)}) collective-permute-start(f32[512,256]{1,0:T(8,128)S(1)} %get-tuple-element.88.after.u2_odd), channel_id=1, source_target_pairs={{0,1},{1,2},{2,3},{3,4},{4,5},{5,6},{6,7},{7,8},{8,9},{9,10},{10,1... | collective-permute-start | bytes 1572872 | tf_op jit(solution)/shard_map/ppermute | solution.py:357
  23.2 13.8 %collective-permute-start.4 = (f32[416,256]{1,0:T(8,128)S(1)}, f32[416,256]{1,0:T(8,128)S(1)}, u32[]{:S(2)}, u32[]{:S(2)}) collective-permute-start(f32[416,256]{1,0:T(8,128)S(1)} %get-tuple-element.95), channel_id=1, source_target_pairs={{1,0},{2,1},{3,2},{4,3},{5,4},{6,5},{7,6},{8,7},{9,8},{10,9},{11,1... | collective-permute-start | bytes 1277960 | tf_op jit(solution)/shard_map/ppermute | solution.py:357
  23.3 4.4 %collective-permute-start.6 = (f32[384,256]{1,0:T(8,128)S(1)}, f32[384,256]{1,0:T(8,128)S(1)}, u32[]{:S(2)}, u32[]{:S(2)}) collective-permute-start(f32[384,256]{1,0:T(8,128)S(1)} %get-tuple-element.97.after), channel_id=1, source_target_pairs={{0,1},{1,0},{2,3},{3,2},{4,5},{5,4},{6,7},{7,6},{8,9},{9,8},{10,11... | collective-permute-start | bytes 1179656 | tf_op jit(solution)/shard_map/ppermute | solution.py:357
  23.8 3.9 %collective-permute-start.5 = (f32[224,256]{1,0:T(8,128)S(1)}, f32[224,256]{1,0:T(8,128)S(1)}, u32[]{:S(2)}, u32[]{:S(2)}) collective-permute-start(f32[224,256]{1,0:T(8,128)S(1)} %get-tuple-element.96), channel_id=1, source_target_pairs={{0,1},{1,0},{2,3},{3,2},{4,5},{5,4},{6,7},{7,6},{8,9},{9,8},{10,11... | collective-permute-start | bytes 688136 | tf_op jit(solution)/shard_map/ppermute | solution.py:357
  23.9 6.6 %collective-permute-start.8 = (f32[96,256]{1,0:T(8,128)S(1)}, f32[96,256]{1,0:T(8,128)S(1)}, u32[]{:S(2)}, u32[]{:S(2)}) collective-permute-start(f32[96,256]{1,0:T(8,128)S(1)} %get-tuple-element.109), channel_id=1, source_target_pairs={{1,0},{2,4},{3,2},{4,3},{5,1},{6,5},{7,6},{8,7},{9,8},{10,9},{11,1... | collective-permute-start | bytes 294920 | tf_op jit(solution)/shard_map/ppermute | solution.py:357
  29.6 11.8 %collective-permute-start.11 = (f32[384,256]{1,0:T(8,128)S(1)}, f32[384,256]{1,0:T(8,128)S(1)}, u32[]{:S(2)}, u32[]{:S(2)}) collective-permute-start(f32[384,256]{1,0:T(8,128)S(1)} %get-tuple-element.107.after), channel_id=1, source_target_pairs={{0,14},{1,15},{2,0},{3,1},{4,2},{5,3},{6,4},{7,5},{8,6},{9,7},{10,... | collective-permute-start | bytes 1179656 | tf_op jit(solution)/shard_map/ppermute | solution.py:357
  31.7 8.3 %collective-permute-start.10 = (f32[96,256]{1,0:T(8,128)S(1)}, f32[96,256]{1,0:T(8,128)S(1)}, u32[]{:S(2)}, u32[]{:S(2)}) collective-permute-start(f32[96,256]{1,0:T(8,128)S(1)} %get-tuple-element.111), channel_id=1, source_target_pairs={{4,1},{20,17}} | collective-permute-start | bytes 294920 | tf_op jit(solution)/shard_map/ppermute | solution.py:357
  32.4 10.5 %collective-permute-start.9 = (f32[128,256]{1,0:T(8,128)S(1)}, f32[128,256]{1,0:T(8,128)S(1)}, u32[]{:S(2)}, u32[]{:S(2)}) collective-permute-start(f32[128,256]{1,0:T(8,128)S(1)} %get-tuple-element.110), channel_id=1, source_target_pairs={{0,14},{1,15},{2,0},{3,1},{4,2},{5,3},{6,4},{7,5},{8,6},{9,7},{10,... | collective-permute-start | bytes 393224 | tf_op jit(solution)/shard_map/ppermute | solution.py:357

commit v10 on v9

--- a/solution.py
+++ b/solution.py
@@ -10,9 +10,9 @@
 F32 = jnp.float32
 BF16 = jnp.bfloat16
 RATE = 0.05
-DETOUR = 3
+DETOUR = 4
 HALF = 12
-EARLY = 4
+EARLY = 5
 VMEM = pl.BlockSpec(memory_space=pltpu.VMEM)
 HBM = pl.BlockSpec(memory_space=pltpu.HBM)
 ANY = pl.BlockSpec(memory_space=pl.ANY)
@@ -182,7 +182,8 @@
         context_pass([(u, r_high, r_low)], c, hb, c_out, h_out)
 
 
-def gate(arrived, out):
+def gate(*refs):
+    out = refs[-1]
     out[...] = jnp.zeros_like(out)
 
 
@@ -203,7 +204,7 @@
     @pl.when(odd)
     def _():
         u2[:rows, :] = u2_odd[:rows, :]
-        u2[rows:, :] = g2_odd[: u2.shape[0] - rows, :]
+        u2[rows:, :] = g2_odd[g2_odd.shape[0] + rows - u2.shape[0] :, :]
         context_pass([(u_odd, rh_odd, rl_odd)], c_odd, h_odd, c_out, h_out)
 
     @pl.when(jnp.logical_not(odd))
@@ -215,19 +216,19 @@
 
 def second_end(s1, c, e, w, grad_top, u2_odd, g2_odd, u2, grad_a, grad_b, r_high, r_low, buf):
     odd = is_odd()
-    middle, rows, first = grad_top.shape[0], s1.shape[1], grad_b.shape[0]
+    middle, direct = grad_top.shape[0], grad_a.shape[0]
 
     @pl.when(odd)
     def _():
         u2[...] = u2_odd[middle:, :]
-        grad_a[...] = g2_odd[first:, :]
-
-    @pl.when(jnp.logical_not(odd))
-    def _():
-        grad = vertex_pass(s1.at[0], c, e.at[1, pl.ds(middle, rows)], w[1:2, :], r_high, r_low)
+        grad_a[...] = g2_odd[:direct, :]
+
+    @pl.when(jnp.logical_not(odd))
+    def _():
+        grad = vertex_pass(s1.at[0], c, e.at[1, pl.ds(middle, s1.shape[1])], w[1:2, :], r_high, r_low)
         buf[:middle, :] = grad_top[...]
         buf[middle:, :] = grad
-        grad_a[...], grad_b[...] = buf[first:, :], buf[:first, :]
+        grad_a[...], grad_b[...] = buf[:direct, :], buf[direct:, :]
         u2[...] = adagrad(s1[0], s1[1], grad)[0]
 
 
@@ -306,37 +307,37 @@
 
     @pl.when(jnp.logical_not(odd))
     def _():
-        ub[...], gb[...] = adagrad(u2[pl.ds(row, rows), :], g1[...], g2[...])
+        ub[...], gb[...] = adagrad(u2[pl.ds(row, rows), :], g1[:rows, :], g2[...])
 
     at = pl.ds(row, rows)
     for copy in load([(ub, u_out.at[at]), (gb, g_out.at[at])], sems):
         copy.wait()
 
 
-def last_top(s1_top, s1_end, g1_a, g1_b, g1_over, swapped, u2, g2, u_out, g_out, buf, *scratch):
-    first, rows = g1_b.shape[0], g2.shape[0]
+def last_top(s1_top, s1_end, g1, u2, g2, u_out, g_out, done, *scratch):
+    last(0, s1_top, s1_end, g1, u2, g2, u_out, g_out, *scratch)
+
+
+def last_end(row, s1_top, s1_end, g1_a, g1_b, g1_over, swapped, u2, g2, after, u_top, g_top, u_out, g_out, buf, *scratch):
+    rows, detour = g2.shape[0], g1_b.shape[0]
     place = lax.axis_index("inner")
     odd = is_odd()
 
     @pl.when(jnp.logical_and(odd, place != 1))
     def _():
-        buf[:first, :] = g1_b[...]
+        buf[rows - detour :, :] = g1_b[...]
 
     @pl.when(place == 1)
     def _():
-        buf[:first, :] = g1_over[...]
-
-    @pl.when(jnp.logical_not(odd))
-    def _():
-        buf[:first, :] = swapped[swapped.shape[0] - first :, :]
-
-    buf[first:, :] = g1_a[: rows - first, :]
-    last(0, s1_top, s1_end, buf, u2, g2, u_out, g_out, *scratch)
-
-
-def last_end(row, s1_top, s1_end, g1_a, u2, g2, u_top, g_top, *refs):
-    g1 = g1_a.at[pl.ds(g1_a.shape[0] - g2.shape[0], g2.shape[0])]
-    last(row, s1_top, s1_end, g1, u2, g2, *refs)
+        buf[rows - detour :, :] = g1_over[...]
+
+    @pl.when(jnp.logical_not(odd))
+    def _():
+        buf[rows - detour :, :] = swapped[swapped.shape[0] - detour :, :]
+
+    if rows > detour:
+        buf[: rows - detour, :] = g1_a[row:, :]
+    last(row, s1_top, s1_end, buf, u2, g2, u_out, g_out, *scratch)
 
 
 def per_device(vertices, vertex_moments, contexts, context_moments, edge_counts, negative_weights):
@@ -452,14 +453,15 @@
     def out_scratch(rows):
         return [pltpu.VMEM((rows, width), F32)] * 2 + [pltpu.SemaphoreType.DMA((2,))]
 
+    u3, g3, done = call(
+        last_top, [VMEM] * 5, [block, block, f32(8, 128)], out_scratch(half_rows), (s1t, s1d, g1ax, u2i, g2tx), "last_top",
+        out_spec=HBM,
+    )
+    (arrived,) = call(gate, [ANY] * 2, [f32(8, 128)], [], (g1rx, done), "gate_last", 10000000000)
     u3, g3 = call(
-        last_top, [VMEM] * 8, [block, block],
-        [pltpu.VMEM((half_rows, width), F32)] + out_scratch(half_rows),
-        (s1t, s1d, g1ax, g1bx, g1rx, u2ti, u2i, g2tx), "last_top", out_spec=HBM,
-    )
-    u3, g3 = call(
-        functools.partial(last_end, half_rows), [VMEM] * 5 + [HBM] * 2, [block, block], out_scratch(nrows - half_rows),
-        (s1t, s1d, g1ax, u2i, g2dx, u3, g3), "last_end", out_spec=HBM, aliases={5: 0, 6: 1},
+        functools.partial(last_end, half_rows), [VMEM] * 8 + [ANY] + [HBM] * 2, [block, block],
+        [pltpu.VMEM((nrows - half_rows, width), F32)] + out_scratch(nrows - half_rows),
+        (s1t, s1d, g1ax, g1bx, g1rx, u2ti, u2i, g2dx, arrived, u3, g3), "last_end", out_spec=HBM, aliases={9: 0, 10: 1},
     )
     return u3, g3, c3, h3
 

time: 44 us -> 43.7 us (level)
  starting transfers between devices: 16.4 us -> 14.8 us
  waiting for transfers between devices: 6.84 us -> 8.21 us
    ppermute x12, starting transfers between devices: 16.4 us -> 14.8 us  [move(): return lax.ppermute(value, 'inner', pairs)]
    ppermute x12, waiting for transfers between devices: 6.84 us -> 8.21 us  [move(): return lax.ppermute(value, 'inner', pairs)]
    pallas_call x16 -> x17, Pallas kernels: 19.5 us -> 19.4 us  [call(): pl.pallas_call(body, out_shape=outs, in_specs=in_specs, out_specs=[out_sp...]
where the time goes in v10:
time: 43.7 us; the launch traced here: 43.4 us
  Pallas kernels  19.4 us (44%)
  starting transfers between devices  14.8 us (34%)
  waiting for transfers between devices  8.21 us (19%)
  between operations  1 us (2%)
    pallas_call x17, Pallas kernels, call(): pl.pallas_call(body, out_shape=outs, in_specs=in_specs, out_specs=[out_sp...  19.4 us
    ppermute x12, starting transfers between devices, move(): return lax.ppermute(value, 'inner', pairs)  14.8 us
    ppermute x12, waiting for transfers between devices, move(): return lax.ppermute(value, 'inner', pairs)  8.21 us
  transfers between devices with their start and end apart: 12, of which 4 were waited for; matrix products, arithmetic and copies ran while one was open for 0% of the time, Pallas kernels for 43%

profile of v10, /device:TPU:0, one launch (start us, length us, event | category | flops | bytes accessed | tf_op | source)
XLA Modules:
  0.0 43.4 jit_solution(13476565263238626211)
XLA Ops:
  0.6 0.1 first_top.1
  0.8 3.2 %collective-permute-start.3 = (f32[2,160,256]{2,1,0:T(8,128)S(1)}, f32[2,160,256]{2,1,0:T(8,128)S(1)}, u32[]{:S(2)}, u32[]{:S(2)}) collective-permute-start(f32[2,160,256]{2,1,0:T(8,128)S(1)} %get-tuple-element.67.s1_top), channel_id=1, source_target_pairs={{0,1},{1,2},{2,3},{3,4},{4,5},{5,6},{6,7},{7,8},{8,9},{9,10},{10,1... | collective-permute-start | bytes 983048 | tf_op jit(solution)/shard_map/ppermute | solution.py:358
  4.0 2.3 %first_end.1 = (f32[2,352,256]{2,1,0:T(8,128)S(1)}, bf16[352,1024]{1,0:T(8,128)(2,1)S(1)}, bf16[352,1024]{1,0:T(8,128)(2,1)S(1)}, f32[1024,256]{1,0:T(8,128)S(1)...) custom-call(f32[512,256]{1,0:T(8,128)} %u.3, ...), custom_call_target="tpu_custom_call" | custom-call | flops 1024 | bytes 1024 | tf_op jit(solution)/shard_map/first_end/pallas_call | solution.py:87
  6.3 0.1 collective-permute-start
  6.3 0.0 slice-start
  6.3 2.3 %first_even.1 = (f32[512,256]{1,0:T(8,128)S(1)}, f32[512,256]{1,0:T(8,128)S(1)}, bf16[512,1024]{1,0:T(8,128)(2,1)S(1)}, bf16[512,1024]{1,0:T(8,128)(2,1)S(1)}, f...) custom-call(f32[512,256]{1,0:T(8,128)S(1)} %get-tuple-element.74.u, f32[512,256]{1,0:T(8,128)S(1)} %get-tuple-element.76.g, ...), custom_call_target="tpu_custom_call" | custom-call | flops 1024 | bytes 1024 | tf_op jit(solution)/shard_map/first_even/pallas_call | solution.py:87
  8.7 1.7 %collective-permute-start.1 = (f32[512,256]{1,0:T(8,128)S(1)}, f32[512,256]{1,0:T(8,128)S(1)}, u32[]{:S(2)}, u32[]{:S(2)}) collective-permute-start(f32[512,256]{1,0:T(8,128)S(1)} %get-tuple-element.86), channel_id=1, source_target_pairs={{0,1},{1,0},{2,3},{3,2},{4,5},{5,4},{6,7},{7,6},{8,9},{9,8},{10,11... | collective-permute-start | bytes 1572872 | tf_op jit(solution)/shard_map/ppermute | solution.py:358
  10.4 0.0 slice-start.1
  10.4 0.0 copy-start
  10.4 0.1 collective-permute-start.2
  10.5 3.3 %collective-permute-done.3.refs_0_.s1.s1_top = f32[2,160,256]{2,1,0:T(8,128)S(1)} collective-permute-done((f32[2,160,256]{2,1,0:T(8,128)S(1)}, f32[2,160,256]{2,1,0:T(8,128)S(1)}, u32[]{:S(2)}, u32[]{:S(2)}) %collective-permute-start.3) | collective-permute-done | bytes 327712 | tf_op jit(solution)/shard_map/ppermute | solution.py:358
  13.7 0.0 collective-permute-done.1.u1.u_odd
  13.7 0.0 collective-permute-done.2.g1
  13.7 0.0 slice-done
  13.8 0.0 slice-done.1
  13.8 0.0 copy-done
  13.8 1.7 %collective-permute-start.6 = (f32[512,256]{1,0:T(8,128)S(1)}, f32[512,256]{1,0:T(8,128)S(1)}, u32[]{:S(2)}, u32[]{:S(2)}) collective-permute-start(f32[512,256]{1,0:T(8,128)S(1)} %get-tuple-element.89.after.u2_odd), channel_id=1, source_target_pairs={{0,1},{1,2},{2,3},{3,4},{4,5},{5,6},{6,7},{7,8},{8,9},{9,10},{10,1... | collective-permute-start | bytes 1572872 | tf_op jit(solution)/shard_map/ppermute | solution.py:358
  15.5 2.5 %first_context.1 = (f32[1024,256]{1,0:T(8,128)S(1)}, f32[1024,256]{1,0:T(8,128)S(1)}) custom-call(f32[1024,256]{1,0:T(8,128)} %h.3, f32[512,256]{1,0:T(8,128)S(1)} %get-tuple-element.74.u, f32[1024,256]{1,0:T(8,128)S(1)} %get-tuple-element.75.c, bf16[512,1024]{1,0:T(8,128)(2,1)S(1)} %get-tuple-element.84.r_high, ...), custom_call_target="tpu_custom_call" | custom-call | flops 1024 | bytes 1024 | tf_op jit(solution)/shard_map/first_context/pallas_call | solution.py:87
  18.0 1.2 %second_top.1 = (f32[288,256]{1,0:T(8,128)S(1)}, f32[160,256]{1,0:T(8,128)S(1)}, bf16[160,1024]{1,0:T(8,128)(2,1)S(1)}, bf16[160,1024]{1,0:T(8,128)(2,1)S(1)}, f...) custom-call(f32[2,160,256]{2,1,0:T(8,128)S(1)} %collective-permute-done.3.refs_0_.s1.s1_top, ...), custom_call_target="tpu_custom_call" | custom-call | flops 1024 | bytes 1024 | tf_op jit(solution)/shard_map/second_top/pallas_call | solution.py:87
  19.2 2.2 %collective-permute-done.s1.s1_end = f32[2,352,256]{2,1,0:T(8,128)S(1)} collective-permute-done((f32[2,352,256]{2,1,0:T(8,128)S(1)}, f32[2,352,256]{2,1,0:T(8,128)S(1)}, u32[]{:S(2)}, u32[]{:S(2)}) %collective-permute-start) | collective-permute-done | bytes 720928 | tf_op jit(solution)/shard_map/ppermute | solution.py:358
  21.5 1.7 %second_end.1 = (f32[352,256]{1,0:T(8,128)S(1)}, f32[384,256]{1,0:T(8,128)S(1)}, f32[128,256]{1,0:T(8,128)S(1)}, bf16[352,1024]{1,0:T(8,128)(2,1)S(1)}, bf16[352,1024]{1,0:T(8,128)(2,1)S(1)}) custom-call(f32[2,352,256]{2,1,0:T(8,128)S(1)} %collective-permute-done.s1.s1_end, f32[1024,256]{1,0:T(8,128)S(1)} %get-tuple-element.90.c, ...), custom_call_target="tpu_custom_call" | custom-call | flops 10000000000 | bytes 1024 | tf_op jit(solution)/shard_map/second_end/pallas_call | solution.py:87
  23.1 0.1 collective-permute-start.4
  23.2 0.5 %collective-permute-start.8 = (f32[352,256]{1,0:T(8,128)S(1)}, f32[352,256]{1,0:T(8,128)S(1)}, u32[]{:S(2)}, u32[]{:S(2)}) collective-permute-start(f32[352,256]{1,0:T(8,128)S(1)} %get-tuple-element.105.after), channel_id=1, source_target_pairs={{0,1},{1,0},{2,3},{3,2},{4,5},{5,4},{6,7},{7,6},{8,9},{9,8},{10,11... | collective-permute-start | bytes 1081352 | tf_op jit(solution)/shard_map/ppermute | solution.py:358
  23.7 0.1 collective-permute-start.7
  23.8 1.9 %collective-permute-start.5 = (f32[128,256]{1,0:T(8,128)S(1)}, f32[128,256]{1,0:T(8,128)S(1)}, u32[]{:S(2)}, u32[]{:S(2)}) collective-permute-start(f32[128,256]{1,0:T(8,128)S(1)} %get-tuple-element.97), channel_id=1, source_target_pairs={{1,0},{2,4},{3,2},{4,3},{5,1},{6,5},{7,6},{8,7},{9,8},{10,9},{11,1... | collective-permute-start | bytes 393224 | tf_op jit(solution)/shard_map/ppermute | solution.py:358
  25.7 1.5 %second_context.1 = (f32[1024,256]{1,0:T(8,128)S(1)}, f32[1024,256]{1,0:T(8,128)S(1)}) custom-call(f32[2,160,256]{2,1,0:T(8,128)S(1)} %collective-permute-done.3.refs_0_.s1.s1_top, f32[2,352,256]{2,1,0:T(8,128)S(1)} %collective-permute-done.s1.s1_end, f32[1024,256]{1,0:T(8,128)S(1)} %get-tuple-element.90.c, f32[1024,256]{1,0:T(8,128)S(1)} %get-tuple-element.98.h, ...), custom_call_target="tpu_custom_call" | custom-call | flops 1024 | bytes 1024 | tf_op jit(solution)/shard_map/second_context/pallas_call | solution.py:87
  27.2 0.0 collective-permute-done.7.u_top.swapped
  27.2 0.0 collective-permute-done.8.u_end
  27.3 0.0 collective-permute-done.6.u.u_even
  27.3 1.8 %third_even_top.1 = (f32[384,256]{1,0:T(8,128)S(1)}, bf16[384,1024]{1,0:T(8,128)(2,1)S(1)}, bf16[384,1024]{1,0:T(8,128)(2,1)S(1)}) custom-call(f32[512,256]{1,0:T(8,128)S(1)} %collective-permute-done.6.u.u_even, f32[1024,256]{1,0:T(8,128)S(1)} %get-tuple-element.103.c.c_even, s32[3,512,1024]{2,1,0:T(8,128)S(1)} %bitcast.1, s32[3,1024]{1,0:T(4,128)S(1)} %copy-done, ...), custom_call_target="tpu_custom_call" | custom-call | flops 1024 | bytes 1024 | tf_op jit(solution)/shard_map/third_even_top/pallas_call | solution.py:87
  29.1 1.2 %collective-permute-start.11 = (f32[384,256]{1,0:T(8,128)S(1)}, f32[384,256]{1,0:T(8,128)S(1)}, u32[]{:S(2)}, u32[]{:S(2)}) collective-permute-start(f32[384,256]{1,0:T(8,128)S(1)} %get-tuple-element.109.after), channel_id=1, source_target_pairs={{0,14},{1,15},{2,0},{3,1},{4,2},{5,3},{6,4},{7,5},{8,6},{9,7},{10,... | collective-permute-start | bytes 1179656 | tf_op jit(solution)/shard_map/ppermute | solution.py:358
  30.4 0.0 collective-permute-done.5.g1.g1_b
  30.4 1.2 %third_even_end.1 = (f32[128,256]{1,0:T(8,128)S(1)}, bf16[128,1024]{1,0:T(8,128)(2,1)S(1)}, bf16[128,1024]{1,0:T(8,128)(2,1)S(1)}, f32[128,256]{1,0:T(8,128)S(1)}) custom-call(f32[512,256]{1,0:T(8,128)S(1)} %collective-permute-done.6.u.u_even, f32[1024,256]{1,0:T(8,128)S(1)} %get-tuple-element.103.c.c_even, s32[3,512,1024]{2,1,0:T(8,128)S(1)} %bitcast.1, ...), custom_call_target="tpu_custom_call" | custom-call | flops 1024 | bytes 1024 | tf_op jit(solution)/shard_map/third_even_end/pallas_call | solution.py:87
  31.6 0.7 %collective-permute-start.9 = (f32[128,256]{1,0:T(8,128)S(1)}, f32[128,256]{1,0:T(8,128)S(1)}, u32[]{:S(2)}, u32[]{:S(2)}) collective-permute-start(f32[128,256]{1,0:T(8,128)S(1)} %get-tuple-element.111), channel_id=1, source_target_pairs={{4,1},{20,17}} | collective-permute-start | bytes 393224 | tf_op jit(solution)/shard_map/ppermute | solution.py:358
  32.3 3.6 %collective-permute-start.10 = (f32[128,256]{1,0:T(8,128)S(1)}, f32[128,256]{1,0:T(8,128)S(1)}, u32[]{:S(2)}, u32[]{:S(2)}) collective-permute-start(f32[128,256]{1,0:T(8,128)S(1)} %get-tuple-element.112), channel_id=1, source_target_pairs={{0,14},{1,15},{2,0},{3,1},{4,2},{5,3},{6,4},{7,5},{8,6},{9,7},{10,... | collective-permute-start | bytes 393224 | tf_op jit(solution)/shard_map/ppermute | solution.py:358
  35.9 0.0 collective-permute-done.4.g1.g1_a.after
  35.9 2.9 %third_context.1 = (f32[1024,256]{1,0:T(8,128)}, f32[1024,256]{1,0:T(8,128)}) custom-call(f32[512,256]{1,0:T(8,128)S(1)} %get-tuple-element.107.u.u2.u_odd, f32[1024,256]{1,0:T(8,128)S(1)} %get-tuple-element.106.c.c_odd, f32[1024,256]{1,0:T(8,128)S(1)} %get-tuple-element.118.h_odd, bf16[384,1024]{1,0:T(8,128)(2,1)S(1)} %get-tuple-element.119.rh_odd, ...), custom_call_target="tpu_custom_call" | custom-call | flops 10000000000 | bytes 1024 | tf_op jit(solution)/shard_map/third_context/pallas_call | solution.py:87
  38.8 2.3 %collective-permute-done.11.g2 = f32[384,256]{1,0:T(8,128)S(1)} collective-permute-done((f32[384,256]{1,0:T(8,128)S(1)}, f32[384,256]{1,0:T(8,128)S(1)}, u32[]{:S(2)}, u32[]{:S(2)}) %collective-permute-start.11) | collective-permute-done | bytes 393248 | tf_op jit(solution)/shard_map/ppermute | solution.py:358
  41.1 1.0 %last_top.1 = (f32[512,256]{1,0:T(8,128)}, f32[512,256]{1,0:T(8,128)}, f32[8,128]{1,0:T(8,128)S(1)}) custom-call(f32[2,160,256]{2,1,0:T(8,128)S(1)} %get-tuple-element.67.s1_top, f32[2,352,256]{2,1,0:T(8,128)S(1)} %get-tuple-element.73.s1_end, f32[384,256]{1,0:T(8,128)S(1)} %collective-permute-done.4.g1.g1_a.after, ...), custom_call_target="tpu_custom_call" | custom-call | flops 1024 | bytes 1024 | tf_op jit(solution)/shard_map/last_top/pallas_call | solution.py:87
  42.1 0.0 collective-permute-done.9.refs_0_.g1_over
  42.1 0.4 collective-permute-done.10.g2
  42.5 0.8 %last_end.1 = (f32[512,256]{1,0:T(8,128)}, f32[512,256]{1,0:T(8,128)}) custom-call(f32[2,160,256]{2,1,0:T(8,128)S(1)} %get-tuple-element.67.s1_top, f32[2,352,256]{2,1,0:T(8,128)S(1)} %get-tuple-element.73.s1_end, f32[384,256]{1,0:T(8,128)S(1)} %collective-permute-done.4.g1.g1_a.after, ...), custom_call_target="tpu_custom_call", output_to_operand_aliasing={{0}: (9, {}), {1}: (10, {})} | custom-call | flops 1024 | bytes 1024 | tf_op jit(solution)/shard_map/last_end/pallas_call | solution.py:87
  (6 shorter events, 0.1 us)
Async XLA Ops:
  0.8 13.0 %collective-permute-start.3 = (f32[2,160,256]{2,1,0:T(8,128)S(1)}, f32[2,160,256]{2,1,0:T(8,128)S(1)}, u32[]{:S(2)}, u32[]{:S(2)}) collective-permute-start(f32[2,160,256]{2,1,0:T(8,128)S(1)} %get-tuple-element.67.s1_top), channel_id=1, source_target_pairs={{0,1},{1,2},{2,3},{3,4},{4,5},{5,6},{6,7},{7,8},{8,9},{9,10},{10,1... | collective-permute-start | bytes 983048 | tf_op jit(solution)/shard_map/ppermute | solution.py:358
  6.3 15.2 %collective-permute-start = (f32[2,352,256]{2,1,0:T(8,128)S(1)}, f32[2,352,256]{2,1,0:T(8,128)S(1)}, u32[]{:S(2)}, u32[]{:S(2)}) collective-permute-start(f32[2,352,256]{2,1,0:T(8,128)S(1)} %get-tuple-element.73.s1_end), channel_id=1, source_target_pairs={{0,1},{1,2},{2,3},{3,4},{4,5},{5,6},{6,7},{7,8},{8,9},{9,10},{10,1... | collective-permute-start | bytes 2162696 | tf_op jit(solution)/shard_map/ppermute | solution.py:358
  6.3 7.4 %slice-start = ((s8[6291456]{0:T(1024)(128)(4,1)}), s8[4194304]{0:T(1024)(128)(4,1)S(1)}, s32[]{:S(2)}) async-start(s8[6291456]{0:T(1024)(128)(4,1)} %bitcast), calls=%async_computation | async-start | bytes 8388608
  8.7 5.1 %collective-permute-start.1 = (f32[512,256]{1,0:T(8,128)S(1)}, f32[512,256]{1,0:T(8,128)S(1)}, u32[]{:S(2)}, u32[]{:S(2)}) collective-permute-start(f32[512,256]{1,0:T(8,128)S(1)} %get-tuple-element.86), channel_id=1, source_target_pairs={{0,1},{1,0},{2,3},{3,2},{4,5},{5,4},{6,7},{7,6},{8,9},{9,8},{10,11... | collective-permute-start | bytes 1572872 | tf_op jit(solution)/shard_map/ppermute | solution.py:358
  10.4 3.4 %slice-start.1 = ((s8[6291456]{0:T(1024)(128)(4,1)}), s8[2097152]{0:T(1024)(128)(4,1)S(1)}, s32[]{:S(2)}) async-start(s8[6291456]{0:T(1024)(128)(4,1)} %bitcast), calls=%async_computation.1 | async-start | bytes 4194304
  10.4 3.4 %copy-start = (s32[3,1024]{1,0:T(4,128)S(1)}, s32[3,1024]{1,0:T(4,128)}, u32[]{:S(2)}) copy-start(s32[3,1024]{1,0:T(4,128)} %w.17) | copy-start | bytes 36868
  10.4 3.4 %collective-permute-start.2 = (f32[512,256]{1,0:T(8,128)S(1)}, f32[512,256]{1,0:T(8,128)S(1)}, u32[]{:S(2)}, u32[]{:S(2)}) collective-permute-start(f32[512,256]{1,0:T(8,128)S(1)} %get-tuple-element.87), channel_id=1, source_target_pairs={{0,1},{1,0},{2,3},{3,2},{4,5},{5,4},{6,7},{7,6},{8,9},{9,8},{10,11... | collective-permute-start | bytes 1572872 | tf_op jit(solution)/shard_map/ppermute | solution.py:358
  13.8 13.5 %collective-permute-start.6 = (f32[512,256]{1,0:T(8,128)S(1)}, f32[512,256]{1,0:T(8,128)S(1)}, u32[]{:S(2)}, u32[]{:S(2)}) collective-permute-start(f32[512,256]{1,0:T(8,128)S(1)} %get-tuple-element.89.after.u2_odd), channel_id=1, source_target_pairs={{0,1},{1,2},{2,3},{3,4},{4,5},{5,6},{6,7},{7,8},{8,9},{9,10},{10,1... | collective-permute-start | bytes 1572872 | tf_op jit(solution)/shard_map/ppermute | solution.py:358
  23.1 12.8 %collective-permute-start.4 = (f32[384,256]{1,0:T(8,128)S(1)}, f32[384,256]{1,0:T(8,128)S(1)}, u32[]{:S(2)}, u32[]{:S(2)}) collective-permute-start(f32[384,256]{1,0:T(8,128)S(1)} %get-tuple-element.96), channel_id=1, source_target_pairs={{1,0},{2,1},{3,2},{4,3},{5,4},{6,5},{7,6},{8,7},{9,8},{10,9},{11,1... | collective-permute-start | bytes 1179656 | tf_op jit(solution)/shard_map/ppermute | solution.py:358
  23.2 4.0 %collective-permute-start.8 = (f32[352,256]{1,0:T(8,128)S(1)}, f32[352,256]{1,0:T(8,128)S(1)}, u32[]{:S(2)}, u32[]{:S(2)}) collective-permute-start(f32[352,256]{1,0:T(8,128)S(1)} %get-tuple-element.105.after), channel_id=1, source_target_pairs={{0,1},{1,0},{2,3},{3,2},{4,5},{5,4},{6,7},{7,6},{8,9},{9,8},{10,11... | collective-permute-start | bytes 1081352 | tf_op jit(solution)/shard_map/ppermute | solution.py:358
  23.7 3.5 %collective-permute-start.7 = (f32[288,256]{1,0:T(8,128)S(1)}, f32[288,256]{1,0:T(8,128)S(1)}, u32[]{:S(2)}, u32[]{:S(2)}) collective-permute-start(f32[288,256]{1,0:T(8,128)S(1)} %get-tuple-element.104), channel_id=1, source_target_pairs={{0,1},{1,0},{2,3},{3,2},{4,5},{5,4},{6,7},{7,6},{8,9},{9,8},{10,11... | collective-permute-start | bytes 884744 | tf_op jit(solution)/shard_map/ppermute | solution.py:358
  23.8 6.6 %collective-permute-start.5 = (f32[128,256]{1,0:T(8,128)S(1)}, f32[128,256]{1,0:T(8,128)S(1)}, u32[]{:S(2)}, u32[]{:S(2)}) collective-permute-start(f32[128,256]{1,0:T(8,128)S(1)} %get-tuple-element.97), channel_id=1, source_target_pairs={{1,0},{2,4},{3,2},{4,3},{5,1},{6,5},{7,6},{8,7},{9,8},{10,9},{11,1... | collective-permute-start | bytes 393224 | tf_op jit(solution)/shard_map/ppermute | solution.py:358
  29.1 12.0 %collective-permute-start.11 = (f32[384,256]{1,0:T(8,128)S(1)}, f32[384,256]{1,0:T(8,128)S(1)}, u32[]{:S(2)}, u32[]{:S(2)}) collective-permute-start(f32[384,256]{1,0:T(8,128)S(1)} %get-tuple-element.109.after), channel_id=1, source_target_pairs={{0,14},{1,15},{2,0},{3,1},{4,2},{5,3},{6,4},{7,5},{8,6},{9,7},{10,... | collective-permute-start | bytes 1179656 | tf_op jit(solution)/shard_map/ppermute | solution.py:358
  31.6 10.5 %collective-permute-start.9 = (f32[128,256]{1,0:T(8,128)S(1)}, f32[128,256]{1,0:T(8,128)S(1)}, u32[]{:S(2)}, u32[]{:S(2)}) collective-permute-start(f32[128,256]{1,0:T(8,128)S(1)} %get-tuple-element.111), channel_id=1, source_target_pairs={{4,1},{20,17}} | collective-permute-start | bytes 393224 | tf_op jit(solution)/shard_map/ppermute | solution.py:358
  32.3 10.2 %collective-permute-start.10 = (f32[128,256]{1,0:T(8,128)S(1)}, f32[128,256]{1,0:T(8,128)S(1)}, u32[]{:S(2)}, u32[]{:S(2)}) collective-permute-start(f32[128,256]{1,0:T(8,128)S(1)} %get-tuple-element.112), channel_id=1, source_target_pairs={{0,14},{1,15},{2,0},{3,1},{4,2},{5,3},{6,4},{7,5},{8,6},{9,7},{10,... | collective-permute-start | bytes 393224 | tf_op jit(solution)/shard_map/ppermute | solution.py:358

commit v11 on v10

--- a/solution.py
+++ b/solution.py
@@ -10,9 +10,9 @@
 F32 = jnp.float32
 BF16 = jnp.bfloat16
 RATE = 0.05
-DETOUR = 4
+DETOUR = 8
 HALF = 12
-EARLY = 5
+EARLY = 6
 VMEM = pl.BlockSpec(memory_space=pltpu.VMEM)
 HBM = pl.BlockSpec(memory_space=pltpu.HBM)
 ANY = pl.BlockSpec(memory_space=pl.ANY)
@@ -293,6 +293,8 @@
 def last(row, s1_top, s1_end, g1, u2, g2, u_out, g_out, ub, gb, sems):
     odd = is_odd()
     rows = g2.shape[0]
+    at = pl.ds(row, rows)
+    copies = [pltpu.make_async_copy(gb, g_out.at[at], sems.at[0]), pltpu.make_async_copy(ub, u_out.at[at], sems.at[1])]
 
     @pl.when(odd)
     def _():
@@ -300,17 +302,21 @@
         for s1 in (s1_top, s1_end):
             low, high = max(row, begin), min(row + rows, begin + s1.shape[1])
             if low < high:
-                at, here = pl.ds(low - begin, high - low), pl.ds(low - row, high - low)
-                value, moment = adagrad(s1[0, at, :], s1[1, at, :], g1[here, :])
-                ub[here, :], gb[here, :] = adagrad(value, moment, g2[here, :])
+                there, here = pl.ds(low - begin, high - low), pl.ds(low - row, high - low)
+                value, moment = adagrad(s1[0, there, :], s1[1, there, :], g1[here, :])
+                gb[here, :] = moment + g2[here, :] * g2[here, :]
+                ub[here, :] = value
             begin += s1.shape[1]
 
     @pl.when(jnp.logical_not(odd))
     def _():
-        ub[...], gb[...] = adagrad(u2[pl.ds(row, rows), :], g1[:rows, :], g2[...])
-
-    at = pl.ds(row, rows)
-    for copy in load([(ub, u_out.at[at]), (gb, g_out.at[at])], sems):
+        gb[...] = g1[:rows, :] + g2[...] * g2[...]
+        ub[...] = u2[at, :]
+
+    copies[0].start()
+    ub[...] = ub[...] - RATE * g2[...] * lax.rsqrt(gb[...])
+    copies[1].start()
+    for copy in copies:
         copy.wait()
 
 
@@ -392,7 +398,7 @@
         (*evens, odds[0], odds[2], hb, rht, rlt, rhd, rld), "first_even",
     )
     s1i = [move(x, swap) for x in s1]
-    (gated,) = call(gate, [ANY], [f32(8, 128)], [], (s1tx,), "gate", 7000000000)
+    (gated,) = call(gate, [ANY], [f32(8, 128)], [], (s1tx,), "gate", 6000000000)
     u2e, m2e, rho1, rlo1 = call(
         second_odd, [VMEM] * 5 + [ANY], [block, block, half, half], [],
         (*s1i, c1o, edge_counts, negative_weights, gated), "second_odd",
@@ -402,7 +408,7 @@
         (hbm[3], evens[0], evens[2], rhe0, rle0, u2e), "first_context",
     )
     u2x = move(u2e, ring)
-    detour = DETOUR * nrows // 256 * 16
+    detour = DETOUR * nrows // 512 * 16
     u2t, g1t, rht1, rlt1, c2o, h2o = call(
         second_top, [VMEM] * 11, [f32(early + detour, width), f32(early, width)] + stage(early)[1:] + [ctx, ctx], [],
         (s1tx, c1e, edge_counts, negative_weights, s1i[0], c1o, h1o, rho1, rlo1, u2e, m2e), "second_top",

time: 43.7 us -> 43.6 us (level)
  waiting for transfers between devices: 8.21 us -> 9.69 us
  starting transfers between devices: 14.8 us -> 13.6 us
    ppermute x12, waiting for transfers between devices: 8.21 us -> 9.69 us  [move(): return lax.ppermute(value, 'inner', pairs)]
    ppermute x12, starting transfers between devices: 14.8 us -> 13.6 us  [move(): return lax.ppermute(value, 'inner', pairs)]
  transfers between devices with their start and end apart: 12 -> 12, of which waited for: 4 -> 4; matrix products, arithmetic and copies ran while one was open for 0% -> 0% of each run, Pallas kernels for 43% -> 42%
where the time goes in v11:
time: 43.6 us; the launch traced here: 43.4 us
  Pallas kernels  19.1 us (44%)
  starting transfers between devices  13.6 us (31%)
  waiting for transfers between devices  9.69 us (22%)
  between operations  0.99 us (2%)
    pallas_call x17, Pallas kernels, call(): pl.pallas_call(body, out_shape=outs, in_specs=in_specs, out_specs=[out_sp...  19.1 us
    ppermute x12, starting transfers between devices, move(): return lax.ppermute(value, 'inner', pairs)  13.6 us
    ppermute x12, waiting for transfers between devices, move(): return lax.ppermute(value, 'inner', pairs)  9.69 us
  transfers between devices with their start and end apart: 12, of which 4 were waited for; matrix products, arithmetic and copies ran while one was open for 0% of the time, Pallas kernels for 42%

profile of v11, /device:TPU:0, one launch (start us, length us, event | category | flops | bytes accessed | tf_op | source)
XLA Modules:
  0.0 43.4 jit_solution(10005440061299842854)
XLA Ops:
  0.6 0.1 first_top.1
  0.8 3.2 %collective-permute-start.3 = (f32[2,192,256]{2,1,0:T(8,128)S(1)}, f32[2,192,256]{2,1,0:T(8,128)S(1)}, u32[]{:S(2)}, u32[]{:S(2)}) collective-permute-start(f32[2,192,256]{2,1,0:T(8,128)S(1)} %get-tuple-element.67.s1_top), channel_id=1, source_target_pairs={{0,1},{1,2},{2,3},{3,4},{4,5},{5,6},{6,7},{7,8},{8,9},{9,10},{10,1... | collective-permute-start | bytes 1179656 | tf_op jit(solution)/shard_map/ppermute | solution.py:364
  3.9 2.3 %first_end.1 = (f32[2,320,256]{2,1,0:T(8,128)S(1)}, bf16[320,1024]{1,0:T(8,128)(2,1)S(1)}, bf16[320,1024]{1,0:T(8,128)(2,1)S(1)}, f32[1024,256]{1,0:T(8,128)S(1)...) custom-call(f32[512,256]{1,0:T(8,128)} %u.3, ...), custom_call_target="tpu_custom_call" | custom-call | flops 1024 | bytes 1024 | tf_op jit(solution)/shard_map/first_end/pallas_call | solution.py:87
  6.2 0.4 collective-permute-start
  6.6 0.0 slice-start
  6.6 2.3 %first_even.1 = (f32[512,256]{1,0:T(8,128)S(1)}, f32[512,256]{1,0:T(8,128)S(1)}, bf16[512,1024]{1,0:T(8,128)(2,1)S(1)}, bf16[512,1024]{1,0:T(8,128)(2,1)S(1)}, f...) custom-call(f32[512,256]{1,0:T(8,128)S(1)} %get-tuple-element.74.u, f32[512,256]{1,0:T(8,128)S(1)} %get-tuple-element.76.g, ...), custom_call_target="tpu_custom_call" | custom-call | flops 1024 | bytes 1024 | tf_op jit(solution)/shard_map/first_even/pallas_call | solution.py:87
  8.9 1.4 %collective-permute-start.1 = (f32[512,256]{1,0:T(8,128)S(1)}, f32[512,256]{1,0:T(8,128)S(1)}, u32[]{:S(2)}, u32[]{:S(2)}) collective-permute-start(f32[512,256]{1,0:T(8,128)S(1)} %get-tuple-element.86), channel_id=1, source_target_pairs={{0,1},{1,0},{2,3},{3,2},{4,5},{5,4},{6,7},{7,6},{8,9},{9,8},{10,11... | collective-permute-start | bytes 1572872 | tf_op jit(solution)/shard_map/ppermute | solution.py:364
  10.3 0.0 slice-start.1
  10.3 0.0 copy-start
  10.3 0.1 collective-permute-start.2
  10.4 4.0 %collective-permute-done.3.refs_0_.s1.s1_top = f32[2,192,256]{2,1,0:T(8,128)S(1)} collective-permute-done((f32[2,192,256]{2,1,0:T(8,128)S(1)}, f32[2,192,256]{2,1,0:T(8,128)S(1)}, u32[]{:S(2)}, u32[]{:S(2)}) %collective-permute-start.3) | collective-permute-done | bytes 393248 | tf_op jit(solution)/shard_map/ppermute | solution.py:364
  14.4 0.0 collective-permute-done.1.u1.u_odd
  14.4 0.0 collective-permute-done.2.g1
  14.4 0.0 slice-done
  14.4 0.0 slice-done.1
  14.4 0.0 copy-done
  14.5 0.9 %collective-permute-start.6 = (f32[512,256]{1,0:T(8,128)S(1)}, f32[512,256]{1,0:T(8,128)S(1)}, u32[]{:S(2)}, u32[]{:S(2)}) collective-permute-start(f32[512,256]{1,0:T(8,128)S(1)} %get-tuple-element.89.after.u2_odd), channel_id=1, source_target_pairs={{0,1},{1,2},{2,3},{3,4},{4,5},{5,6},{6,7},{7,8},{8,9},{9,10},{10,1... | collective-permute-start | bytes 1572872 | tf_op jit(solution)/shard_map/ppermute | solution.py:364
  15.4 2.5 %first_context.1 = (f32[1024,256]{1,0:T(8,128)S(1)}, f32[1024,256]{1,0:T(8,128)S(1)}) custom-call(f32[1024,256]{1,0:T(8,128)} %h.3, f32[512,256]{1,0:T(8,128)S(1)} %get-tuple-element.74.u, f32[1024,256]{1,0:T(8,128)S(1)} %get-tuple-element.75.c, bf16[512,1024]{1,0:T(8,128)(2,1)S(1)} %get-tuple-element.84.r_high, ...), custom_call_target="tpu_custom_call" | custom-call | flops 1024 | bytes 1024 | tf_op jit(solution)/shard_map/first_context/pallas_call | solution.py:87
  17.9 1.2 %second_top.1 = (f32[320,256]{1,0:T(8,128)S(1)}, f32[192,256]{1,0:T(8,128)S(1)}, bf16[192,1024]{1,0:T(8,128)(2,1)S(1)}, bf16[192,1024]{1,0:T(8,128)(2,1)S(1)}, f...) custom-call(f32[2,192,256]{2,1,0:T(8,128)S(1)} %collective-permute-done.3.refs_0_.s1.s1_top, ...), custom_call_target="tpu_custom_call" | custom-call | flops 1024 | bytes 1024 | tf_op jit(solution)/shard_map/second_top/pallas_call | solution.py:87
  19.1 2.3 %collective-permute-done.s1.s1_end = f32[2,320,256]{2,1,0:T(8,128)S(1)} collective-permute-done((f32[2,320,256]{2,1,0:T(8,128)S(1)}, f32[2,320,256]{2,1,0:T(8,128)S(1)}, u32[]{:S(2)}, u32[]{:S(2)}) %collective-permute-start) | collective-permute-done | bytes 655392 | tf_op jit(solution)/shard_map/ppermute | solution.py:364
  21.4 1.5 %second_end.1 = (f32[320,256]{1,0:T(8,128)S(1)}, f32[384,256]{1,0:T(8,128)S(1)}, f32[128,256]{1,0:T(8,128)S(1)}, bf16[320,1024]{1,0:T(8,128)(2,1)S(1)}, bf16[320,1024]{1,0:T(8,128)(2,1)S(1)}) custom-call(f32[2,320,256]{2,1,0:T(8,128)S(1)} %collective-permute-done.s1.s1_end, f32[1024,256]{1,0:T(8,128)S(1)} %get-tuple-element.90.c, ...), custom_call_target="tpu_custom_call" | custom-call | flops 10000000000 | bytes 1024 | tf_op jit(solution)/shard_map/second_end/pallas_call | solution.py:87
  23.0 0.1 collective-permute-start.4
  23.0 0.5 %collective-permute-start.7 = (f32[320,256]{1,0:T(8,128)S(1)}, f32[320,256]{1,0:T(8,128)S(1)}, u32[]{:S(2)}, u32[]{:S(2)}) collective-permute-start(f32[320,256]{1,0:T(8,128)S(1)} %get-tuple-element.104), channel_id=1, source_target_pairs={{0,1},{1,0},{2,3},{3,2},{4,5},{5,4},{6,7},{7,6},{8,9},{9,8},{10,11... | collective-permute-start | bytes 983048 | tf_op jit(solution)/shard_map/ppermute | solution.py:364
  23.5 0.1 collective-permute-start.8
  23.6 2.1 %collective-permute-start.5 = (f32[128,256]{1,0:T(8,128)S(1)}, f32[128,256]{1,0:T(8,128)S(1)}, u32[]{:S(2)}, u32[]{:S(2)}) collective-permute-start(f32[128,256]{1,0:T(8,128)S(1)} %get-tuple-element.97), channel_id=1, source_target_pairs={{1,0},{2,4},{3,2},{4,3},{5,1},{6,5},{7,6},{8,7},{9,8},{10,9},{11,1... | collective-permute-start | bytes 393224 | tf_op jit(solution)/shard_map/ppermute | solution.py:364
  25.7 1.5 %second_context.1 = (f32[1024,256]{1,0:T(8,128)S(1)}, f32[1024,256]{1,0:T(8,128)S(1)}) custom-call(f32[2,192,256]{2,1,0:T(8,128)S(1)} %collective-permute-done.3.refs_0_.s1.s1_top, f32[2,320,256]{2,1,0:T(8,128)S(1)} %collective-permute-done.s1.s1_end, f32[1024,256]{1,0:T(8,128)S(1)} %get-tuple-element.90.c, f32[1024,256]{1,0:T(8,128)S(1)} %get-tuple-element.98.h, ...), custom_call_target="tpu_custom_call" | custom-call | flops 1024 | bytes 1024 | tf_op jit(solution)/shard_map/second_context/pallas_call | solution.py:87
  27.2 0.0 collective-permute-done.7.u_top.swapped
  27.2 0.0 collective-permute-done.8.u_end
  27.3 0.0 collective-permute-done.6.u.u_even
  27.3 1.8 %third_even_top.1 = (f32[384,256]{1,0:T(8,128)S(1)}, bf16[384,1024]{1,0:T(8,128)(2,1)S(1)}, bf16[384,1024]{1,0:T(8,128)(2,1)S(1)}) custom-call(f32[512,256]{1,0:T(8,128)S(1)} %collective-permute-done.6.u.u_even, f32[1024,256]{1,0:T(8,128)S(1)} %get-tuple-element.103.c.c_even, s32[3,512,1024]{2,1,0:T(8,128)S(1)} %bitcast.1, s32[3,1024]{1,0:T(4,128)S(1)} %copy-done, ...), custom_call_target="tpu_custom_call" | custom-call | flops 1024 | bytes 1024 | tf_op jit(solution)/shard_map/third_even_top/pallas_call | solution.py:87
  29.1 1.0 %collective-permute-start.11 = (f32[384,256]{1,0:T(8,128)S(1)}, f32[384,256]{1,0:T(8,128)S(1)}, u32[]{:S(2)}, u32[]{:S(2)}) collective-permute-start(f32[384,256]{1,0:T(8,128)S(1)} %get-tuple-element.109.after), channel_id=1, source_target_pairs={{0,14},{1,15},{2,0},{3,1},{4,2},{5,3},{6,4},{7,5},{8,6},{9,7},{10,... | collective-permute-start | bytes 1179656 | tf_op jit(solution)/shard_map/ppermute | solution.py:364
  30.1 0.0 collective-permute-done.5.g1.g1_b
  30.1 1.2 %third_even_end.1 = (f32[128,256]{1,0:T(8,128)S(1)}, bf16[128,1024]{1,0:T(8,128)(2,1)S(1)}, bf16[128,1024]{1,0:T(8,128)(2,1)S(1)}, f32[128,256]{1,0:T(8,128)S(1)}) custom-call(f32[512,256]{1,0:T(8,128)S(1)} %collective-permute-done.6.u.u_even, f32[1024,256]{1,0:T(8,128)S(1)} %get-tuple-element.103.c.c_even, s32[3,512,1024]{2,1,0:T(8,128)S(1)} %bitcast.1, ...), custom_call_target="tpu_custom_call" | custom-call | flops 1024 | bytes 1024 | tf_op jit(solution)/shard_map/third_even_end/pallas_call | solution.py:87
  31.3 0.7 %collective-permute-start.9 = (f32[128,256]{1,0:T(8,128)S(1)}, f32[128,256]{1,0:T(8,128)S(1)}, u32[]{:S(2)}, u32[]{:S(2)}) collective-permute-start(f32[128,256]{1,0:T(8,128)S(1)} %get-tuple-element.111), channel_id=1, source_target_pairs={{4,1},{20,17}} | collective-permute-start | bytes 393224 | tf_op jit(solution)/shard_map/ppermute | solution.py:364
  32.0 3.2 %collective-permute-start.10 = (f32[128,256]{1,0:T(8,128)S(1)}, f32[128,256]{1,0:T(8,128)S(1)}, u32[]{:S(2)}, u32[]{:S(2)}) collective-permute-start(f32[128,256]{1,0:T(8,128)S(1)} %get-tuple-element.112), channel_id=1, source_target_pairs={{0,14},{1,15},{2,0},{3,1},{4,2},{5,3},{6,4},{7,5},{8,6},{9,7},{10,... | collective-permute-start | bytes 393224 | tf_op jit(solution)/shard_map/ppermute | solution.py:364
  35.2 0.0 collective-permute-done.4.g1.g1_a.after
  35.2 2.9 %third_context.1 = (f32[1024,256]{1,0:T(8,128)}, f32[1024,256]{1,0:T(8,128)}) custom-call(f32[512,256]{1,0:T(8,128)S(1)} %get-tuple-element.107.u.u2.u_odd, f32[1024,256]{1,0:T(8,128)S(1)} %get-tuple-element.106.c.c_odd, f32[1024,256]{1,0:T(8,128)S(1)} %get-tuple-element.118.h_odd, bf16[384,1024]{1,0:T(8,128)(2,1)S(1)} %get-tuple-element.119.rh_odd, ...), custom_call_target="tpu_custom_call" | custom-call | flops 10000000000 | bytes 1024 | tf_op jit(solution)/shard_map/third_context/pallas_call | solution.py:87
  38.1 3.0 %collective-permute-done.11.g2 = f32[384,256]{1,0:T(8,128)S(1)} collective-permute-done((f32[384,256]{1,0:T(8,128)S(1)}, f32[384,256]{1,0:T(8,128)S(1)}, u32[]{:S(2)}, u32[]{:S(2)}) %collective-permute-start.11) | collective-permute-done | bytes 393248 | tf_op jit(solution)/shard_map/ppermute | solution.py:364
  41.1 1.0 %last_top.1 = (f32[512,256]{1,0:T(8,128)}, f32[512,256]{1,0:T(8,128)}, f32[8,128]{1,0:T(8,128)S(1)}) custom-call(f32[2,192,256]{2,1,0:T(8,128)S(1)} %get-tuple-element.67.s1_top, f32[2,320,256]{2,1,0:T(8,128)S(1)} %get-tuple-element.73.s1_end, f32[384,256]{1,0:T(8,128)S(1)} %collective-permute-done.4.g1.g1_a.after, ...), custom_call_target="tpu_custom_call" | custom-call | flops 1024 | bytes 1024 | tf_op jit(solution)/shard_map/last_top/pallas_call | solution.py:87
  42.0 0.0 collective-permute-done.9.refs_0_.g1_over
  42.1 0.4 collective-permute-done.10.g2
  42.5 0.8 %last_end.1 = (f32[512,256]{1,0:T(8,128)}, f32[512,256]{1,0:T(8,128)}) custom-call(f32[2,192,256]{2,1,0:T(8,128)S(1)} %get-tuple-element.67.s1_top, f32[2,320,256]{2,1,0:T(8,128)S(1)} %get-tuple-element.73.s1_end, f32[384,256]{1,0:T(8,128)S(1)} %collective-permute-done.4.g1.g1_a.after, ...), custom_call_target="tpu_custom_call", output_to_operand_aliasing={{0}: (9, {}), {1}: (10, {})} | custom-call | flops 1024 | bytes 1024 | tf_op jit(solution)/shard_map/last_end/pallas_call | solution.py:87
  (6 shorter events, 0.1 us)
Async XLA Ops:
  0.8 13.6 %collective-permute-start.3 = (f32[2,192,256]{2,1,0:T(8,128)S(1)}, f32[2,192,256]{2,1,0:T(8,128)S(1)}, u32[]{:S(2)}, u32[]{:S(2)}) collective-permute-start(f32[2,192,256]{2,1,0:T(8,128)S(1)} %get-tuple-element.67.s1_top), channel_id=1, source_target_pairs={{0,1},{1,2},{2,3},{3,4},{4,5},{5,6},{6,7},{7,8},{8,9},{9,10},{10,1... | collective-permute-start | bytes 1179656 | tf_op jit(solution)/shard_map/ppermute | solution.py:364
  6.2 15.2 %collective-permute-start = (f32[2,320,256]{2,1,0:T(8,128)S(1)}, f32[2,320,256]{2,1,0:T(8,128)S(1)}, u32[]{:S(2)}, u32[]{:S(2)}) collective-permute-start(f32[2,320,256]{2,1,0:T(8,128)S(1)} %get-tuple-element.73.s1_end), channel_id=1, source_target_pairs={{0,1},{1,2},{2,3},{3,4},{4,5},{5,6},{6,7},{7,8},{8,9},{9,10},{10,1... | collective-permute-start | bytes 1966088 | tf_op jit(solution)/shard_map/ppermute | solution.py:364
  6.6 7.8 %slice-start = ((s8[6291456]{0:T(1024)(128)(4,1)}), s8[4194304]{0:T(1024)(128)(4,1)S(1)}, s32[]{:S(2)}) async-start(s8[6291456]{0:T(1024)(128)(4,1)} %bitcast), calls=%async_computation | async-start | bytes 8388608
  8.9 5.5 %collective-permute-start.1 = (f32[512,256]{1,0:T(8,128)S(1)}, f32[512,256]{1,0:T(8,128)S(1)}, u32[]{:S(2)}, u32[]{:S(2)}) collective-permute-start(f32[512,256]{1,0:T(8,128)S(1)} %get-tuple-element.86), channel_id=1, source_target_pairs={{0,1},{1,0},{2,3},{3,2},{4,5},{5,4},{6,7},{7,6},{8,9},{9,8},{10,11... | collective-permute-start | bytes 1572872 | tf_op jit(solution)/shard_map/ppermute | solution.py:364
  10.3 4.1 %slice-start.1 = ((s8[6291456]{0:T(1024)(128)(4,1)}), s8[2097152]{0:T(1024)(128)(4,1)S(1)}, s32[]{:S(2)}) async-start(s8[6291456]{0:T(1024)(128)(4,1)} %bitcast), calls=%async_computation.1 | async-start | bytes 4194304
  10.3 4.1 %copy-start = (s32[3,1024]{1,0:T(4,128)S(1)}, s32[3,1024]{1,0:T(4,128)}, u32[]{:S(2)}) copy-start(s32[3,1024]{1,0:T(4,128)} %w.17) | copy-start | bytes 36868
  10.3 4.1 %collective-permute-start.2 = (f32[512,256]{1,0:T(8,128)S(1)}, f32[512,256]{1,0:T(8,128)S(1)}, u32[]{:S(2)}, u32[]{:S(2)}) collective-permute-start(f32[512,256]{1,0:T(8,128)S(1)} %get-tuple-element.87), channel_id=1, source_target_pairs={{0,1},{1,0},{2,3},{3,2},{4,5},{5,4},{6,7},{7,6},{8,9},{9,8},{10,11... | collective-permute-start | bytes 1572872 | tf_op jit(solution)/shard_map/ppermute | solution.py:364
  14.5 12.8 %collective-permute-start.6 = (f32[512,256]{1,0:T(8,128)S(1)}, f32[512,256]{1,0:T(8,128)S(1)}, u32[]{:S(2)}, u32[]{:S(2)}) collective-permute-start(f32[512,256]{1,0:T(8,128)S(1)} %get-tuple-element.89.after.u2_odd), channel_id=1, source_target_pairs={{0,1},{1,2},{2,3},{3,4},{4,5},{5,6},{6,7},{7,8},{8,9},{9,10},{10,1... | collective-permute-start | bytes 1572872 | tf_op jit(solution)/shard_map/ppermute | solution.py:364
  23.0 12.3 %collective-permute-start.4 = (f32[384,256]{1,0:T(8,128)S(1)}, f32[384,256]{1,0:T(8,128)S(1)}, u32[]{:S(2)}, u32[]{:S(2)}) collective-permute-start(f32[384,256]{1,0:T(8,128)S(1)} %get-tuple-element.96), channel_id=1, source_target_pairs={{1,0},{2,1},{3,2},{4,3},{5,4},{6,5},{7,6},{8,7},{9,8},{10,9},{11,1... | collective-permute-start | bytes 1179656 | tf_op jit(solution)/shard_map/ppermute | solution.py:364
  23.0 4.2 %collective-permute-start.7 = (f32[320,256]{1,0:T(8,128)S(1)}, f32[320,256]{1,0:T(8,128)S(1)}, u32[]{:S(2)}, u32[]{:S(2)}) collective-permute-start(f32[320,256]{1,0:T(8,128)S(1)} %get-tuple-element.104), channel_id=1, source_target_pairs={{0,1},{1,0},{2,3},{3,2},{4,5},{5,4},{6,7},{7,6},{8,9},{9,8},{10,11... | collective-permute-start | bytes 983048 | tf_op jit(solution)/shard_map/ppermute | solution.py:364
  23.5 3.7 %collective-permute-start.8 = (f32[320,256]{1,0:T(8,128)S(1)}, f32[320,256]{1,0:T(8,128)S(1)}, u32[]{:S(2)}, u32[]{:S(2)}) collective-permute-start(f32[320,256]{1,0:T(8,128)S(1)} %get-tuple-element.105.after), channel_id=1, source_target_pairs={{0,1},{1,0},{2,3},{3,2},{4,5},{5,4},{6,7},{7,6},{8,9},{9,8},{10,11... | collective-permute-start | bytes 983048 | tf_op jit(solution)/shard_map/ppermute | solution.py:364
  23.6 6.5 %collective-permute-start.5 = (f32[128,256]{1,0:T(8,128)S(1)}, f32[128,256]{1,0:T(8,128)S(1)}, u32[]{:S(2)}, u32[]{:S(2)}) collective-permute-start(f32[128,256]{1,0:T(8,128)S(1)} %get-tuple-element.97), channel_id=1, source_target_pairs={{1,0},{2,4},{3,2},{4,3},{5,1},{6,5},{7,6},{8,7},{9,8},{10,9},{11,1... | collective-permute-start | bytes 393224 | tf_op jit(solution)/shard_map/ppermute | solution.py:364
  29.1 11.9 %collective-permute-start.11 = (f32[384,256]{1,0:T(8,128)S(1)}, f32[384,256]{1,0:T(8,128)S(1)}, u32[]{:S(2)}, u32[]{:S(2)}) collective-permute-start(f32[384,256]{1,0:T(8,128)S(1)} %get-tuple-element.109.after), channel_id=1, source_target_pairs={{0,14},{1,15},{2,0},{3,1},{4,2},{5,3},{6,4},{7,5},{8,6},{9,7},{10,... | collective-permute-start | bytes 1179656 | tf_op jit(solution)/shard_map/ppermute | solution.py:364
  31.3 10.7 %collective-permute-start.9 = (f32[128,256]{1,0:T(8,128)S(1)}, f32[128,256]{1,0:T(8,128)S(1)}, u32[]{:S(2)}, u32[]{:S(2)}) collective-permute-start(f32[128,256]{1,0:T(8,128)S(1)} %get-tuple-element.111), channel_id=1, source_target_pairs={{4,1},{20,17}} | collective-permute-start | bytes 393224 | tf_op jit(solution)/shard_map/ppermute | solution.py:364
  32.0 10.5 %collective-permute-start.10 = (f32[128,256]{1,0:T(8,128)S(1)}, f32[128,256]{1,0:T(8,128)S(1)}, u32[]{:S(2)}, u32[]{:S(2)}) collective-permute-start(f32[128,256]{1,0:T(8,128)S(1)} %get-tuple-element.112), channel_id=1, source_target_pairs={{0,14},{1,15},{2,0},{3,1},{4,2},{5,3},{6,4},{7,5},{8,6},{9,7},{10,... | collective-permute-start | bytes 393224 | tf_op jit(solution)/shard_map/ppermute | solution.py:364

commit v12 on v11

--- a/solution.py
+++ b/solution.py
@@ -10,6 +10,7 @@
 F32 = jnp.float32
 BF16 = jnp.bfloat16
 RATE = 0.05
+STACKED = 256
 DETOUR = 8
 HALF = 12
 EARLY = 6
@@ -29,6 +30,10 @@
             x, y, (((dim_a,), (dim_b,)), ((), ())), preferred_element_type=F32
         )
 
+    rows = a[0].shape[0]
+    if dim_a == 1 and rows <= STACKED:
+        both = one(jnp.concatenate(a, axis=0), b[0])
+        return both[:rows] + (both[rows:] + one(a[0], b[1]))
     return one(a[0], b[0]) + (one(a[1], b[0]) + one(a[0], b[1]))
 
 

time: 43.6 us -> 43.6 us (level)
    pallas_call x17, Pallas kernels: 19.1 us -> 18.7 us  [call(): pl.pallas_call(body, out_shape=outs, in_specs=in_specs, out_specs=[out_sp...]
  transfers between devices with their start and end apart: 12 -> 12, of which waited for: 4 -> 4; matrix products, arithmetic and copies ran while one was open for 0% -> 0% of each run, Pallas kernels for 42% -> 41%
where the time goes in v12:
time: 43.6 us; the launch traced here: 43.3 us
  Pallas kernels  18.7 us (43%)
  starting transfers between devices  13.6 us (31%)
  waiting for transfers between devices  10 us (23%)
  between operations  0.99 us (2%)
    pallas_call x17, Pallas kernels, call(): pl.pallas_call(body, out_shape=outs, in_specs=in_specs, out_specs=[out_sp...  18.7 us
    ppermute x12, starting transfers between devices, move(): return lax.ppermute(value, 'inner', pairs)  13.6 us
    ppermute x12, waiting for transfers between devices, move(): return lax.ppermute(value, 'inner', pairs)  10 us
  transfers between devices with their start and end apart: 12, of which 4 were waited for; matrix products, arithmetic and copies ran while one was open for 0% of the time, Pallas kernels for 41%

profile of v12, /device:TPU:0, one launch (start us, length us, event | category | flops | bytes accessed | tf_op | source)
XLA Modules:
  0.0 43.3 jit_solution(7142981751766558799)
XLA Ops:
  0.6 0.1 first_top.1
  0.8 3.1 %collective-permute-start.3 = (f32[2,192,256]{2,1,0:T(8,128)S(1)}, f32[2,192,256]{2,1,0:T(8,128)S(1)}, u32[]{:S(2)}, u32[]{:S(2)}) collective-permute-start(f32[2,192,256]{2,1,0:T(8,128)S(1)} %get-tuple-element.67.s1_top), channel_id=1, source_target_pairs={{0,1},{1,2},{2,3},{3,4},{4,5},{5,6},{6,7},{7,8},{8,9},{9,10},{10,1... | collective-permute-start | bytes 1179656 | tf_op jit(solution)/shard_map/ppermute | solution.py:369
  3.9 2.3 %first_end.1 = (f32[2,320,256]{2,1,0:T(8,128)S(1)}, bf16[320,1024]{1,0:T(8,128)(2,1)S(1)}, bf16[320,1024]{1,0:T(8,128)(2,1)S(1)}, f32[1024,256]{1,0:T(8,128)S(1)...) custom-call(f32[512,256]{1,0:T(8,128)} %u.3, ...), custom_call_target="tpu_custom_call" | custom-call | flops 1024 | bytes 1024 | tf_op jit(solution)/shard_map/first_end/pallas_call | solution.py:92
  6.2 0.4 collective-permute-start
  6.5 0.0 slice-start
  6.5 2.3 %first_even.1 = (f32[512,256]{1,0:T(8,128)S(1)}, f32[512,256]{1,0:T(8,128)S(1)}, bf16[512,1024]{1,0:T(8,128)(2,1)S(1)}, bf16[512,1024]{1,0:T(8,128)(2,1)S(1)}, f...) custom-call(f32[512,256]{1,0:T(8,128)S(1)} %get-tuple-element.74.u, f32[512,256]{1,0:T(8,128)S(1)} %get-tuple-element.76.g, ...), custom_call_target="tpu_custom_call" | custom-call | flops 1024 | bytes 1024 | tf_op jit(solution)/shard_map/first_even/pallas_call | solution.py:92
  8.9 1.4 %collective-permute-start.1 = (f32[512,256]{1,0:T(8,128)S(1)}, f32[512,256]{1,0:T(8,128)S(1)}, u32[]{:S(2)}, u32[]{:S(2)}) collective-permute-start(f32[512,256]{1,0:T(8,128)S(1)} %get-tuple-element.86), channel_id=1, source_target_pairs={{0,1},{1,0},{2,3},{3,2},{4,5},{5,4},{6,7},{7,6},{8,9},{9,8},{10,11... | collective-permute-start | bytes 1572872 | tf_op jit(solution)/shard_map/ppermute | solution.py:369
  10.3 0.0 slice-start.1
  10.3 0.0 copy-start
  10.3 0.1 collective-permute-start.2
  10.4 4.0 %collective-permute-done.3.refs_0_.s1.s1_top = f32[2,192,256]{2,1,0:T(8,128)S(1)} collective-permute-done((f32[2,192,256]{2,1,0:T(8,128)S(1)}, f32[2,192,256]{2,1,0:T(8,128)S(1)}, u32[]{:S(2)}, u32[]{:S(2)}) %collective-permute-start.3) | collective-permute-done | bytes 393248 | tf_op jit(solution)/shard_map/ppermute | solution.py:369
  14.3 0.0 collective-permute-done.1.u1.u_odd
  14.3 0.0 collective-permute-done.2.g1
  14.4 0.0 slice-done
  14.4 0.0 slice-done.1
  14.4 0.0 copy-done
  14.4 0.9 %collective-permute-start.6 = (f32[512,256]{1,0:T(8,128)S(1)}, f32[512,256]{1,0:T(8,128)S(1)}, u32[]{:S(2)}, u32[]{:S(2)}) collective-permute-start(f32[512,256]{1,0:T(8,128)S(1)} %get-tuple-element.89.after.u2_odd), channel_id=1, source_target_pairs={{0,1},{1,2},{2,3},{3,4},{4,5},{5,6},{6,7},{7,8},{8,9},{9,10},{10,1... | collective-permute-start | bytes 1572872 | tf_op jit(solution)/shard_map/ppermute | solution.py:369
  15.4 2.5 %first_context.1 = (f32[1024,256]{1,0:T(8,128)S(1)}, f32[1024,256]{1,0:T(8,128)S(1)}) custom-call(f32[1024,256]{1,0:T(8,128)} %h.3, f32[512,256]{1,0:T(8,128)S(1)} %get-tuple-element.74.u, f32[1024,256]{1,0:T(8,128)S(1)} %get-tuple-element.75.c, bf16[512,1024]{1,0:T(8,128)(2,1)S(1)} %get-tuple-element.84.r_high, ...), custom_call_target="tpu_custom_call" | custom-call | flops 1024 | bytes 1024 | tf_op jit(solution)/shard_map/first_context/pallas_call | solution.py:92
  17.9 1.1 %second_top.1 = (f32[320,256]{1,0:T(8,128)S(1)}, f32[192,256]{1,0:T(8,128)S(1)}, bf16[192,1024]{1,0:T(8,128)(2,1)S(1)}, bf16[192,1024]{1,0:T(8,128)(2,1)S(1)}, f...) custom-call(f32[2,192,256]{2,1,0:T(8,128)S(1)} %collective-permute-done.3.refs_0_.s1.s1_top, ...), custom_call_target="tpu_custom_call" | custom-call | flops 1024 | bytes 1024 | tf_op jit(solution)/shard_map/second_top/pallas_call | solution.py:92
  19.0 2.4 %collective-permute-done.s1.s1_end = f32[2,320,256]{2,1,0:T(8,128)S(1)} collective-permute-done((f32[2,320,256]{2,1,0:T(8,128)S(1)}, f32[2,320,256]{2,1,0:T(8,128)S(1)}, u32[]{:S(2)}, u32[]{:S(2)}) %collective-permute-start) | collective-permute-done | bytes 655392 | tf_op jit(solution)/shard_map/ppermute | solution.py:369
  21.4 1.5 %second_end.1 = (f32[320,256]{1,0:T(8,128)S(1)}, f32[384,256]{1,0:T(8,128)S(1)}, f32[128,256]{1,0:T(8,128)S(1)}, bf16[320,1024]{1,0:T(8,128)(2,1)S(1)}, bf16[320,1024]{1,0:T(8,128)(2,1)S(1)}) custom-call(f32[2,320,256]{2,1,0:T(8,128)S(1)} %collective-permute-done.s1.s1_end, f32[1024,256]{1,0:T(8,128)S(1)} %get-tuple-element.90.c, ...), custom_call_target="tpu_custom_call" | custom-call | flops 10000000000 | bytes 1024 | tf_op jit(solution)/shard_map/second_end/pallas_call | solution.py:92
  22.9 0.1 collective-permute-start.4
  23.0 0.5 %collective-permute-start.7 = (f32[320,256]{1,0:T(8,128)S(1)}, f32[320,256]{1,0:T(8,128)S(1)}, u32[]{:S(2)}, u32[]{:S(2)}) collective-permute-start(f32[320,256]{1,0:T(8,128)S(1)} %get-tuple-element.104), channel_id=1, source_target_pairs={{0,1},{1,0},{2,3},{3,2},{4,5},{5,4},{6,7},{7,6},{8,9},{9,8},{10,11... | collective-permute-start | bytes 983048 | tf_op jit(solution)/shard_map/ppermute | solution.py:369
  23.5 0.1 collective-permute-start.8
  23.6 2.0 %collective-permute-start.5 = (f32[128,256]{1,0:T(8,128)S(1)}, f32[128,256]{1,0:T(8,128)S(1)}, u32[]{:S(2)}, u32[]{:S(2)}) collective-permute-start(f32[128,256]{1,0:T(8,128)S(1)} %get-tuple-element.97), channel_id=1, source_target_pairs={{1,0},{2,4},{3,2},{4,3},{5,1},{6,5},{7,6},{8,7},{9,8},{10,9},{11,1... | collective-permute-start | bytes 393224 | tf_op jit(solution)/shard_map/ppermute | solution.py:369
  25.6 1.5 %second_context.1 = (f32[1024,256]{1,0:T(8,128)S(1)}, f32[1024,256]{1,0:T(8,128)S(1)}) custom-call(f32[2,192,256]{2,1,0:T(8,128)S(1)} %collective-permute-done.3.refs_0_.s1.s1_top, f32[2,320,256]{2,1,0:T(8,128)S(1)} %collective-permute-done.s1.s1_end, f32[1024,256]{1,0:T(8,128)S(1)} %get-tuple-element.90.c, f32[1024,256]{1,0:T(8,128)S(1)} %get-tuple-element.98.h, ...), custom_call_target="tpu_custom_call" | custom-call | flops 1024 | bytes 1024 | tf_op jit(solution)/shard_map/second_context/pallas_call | solution.py:92
  27.1 0.0 collective-permute-done.7.u_top.swapped
  27.1 0.0 collective-permute-done.8.u_end
  27.2 0.0 collective-permute-done.6.u.u_even
  27.2 1.8 %third_even_top.1 = (f32[384,256]{1,0:T(8,128)S(1)}, bf16[384,1024]{1,0:T(8,128)(2,1)S(1)}, bf16[384,1024]{1,0:T(8,128)(2,1)S(1)}) custom-call(f32[512,256]{1,0:T(8,128)S(1)} %collective-permute-done.6.u.u_even, f32[1024,256]{1,0:T(8,128)S(1)} %get-tuple-element.103.c.c_even, s32[3,512,1024]{2,1,0:T(8,128)S(1)} %bitcast.1, s32[3,1024]{1,0:T(4,128)S(1)} %copy-done, ...), custom_call_target="tpu_custom_call" | custom-call | flops 1024 | bytes 1024 | tf_op jit(solution)/shard_map/third_even_top/pallas_call | solution.py:92
  29.0 1.0 %collective-permute-start.11 = (f32[384,256]{1,0:T(8,128)S(1)}, f32[384,256]{1,0:T(8,128)S(1)}, u32[]{:S(2)}, u32[]{:S(2)}) collective-permute-start(f32[384,256]{1,0:T(8,128)S(1)} %get-tuple-element.109.after), channel_id=1, source_target_pairs={{0,14},{1,15},{2,0},{3,1},{4,2},{5,3},{6,4},{7,5},{8,6},{9,7},{10,... | collective-permute-start | bytes 1179656 | tf_op jit(solution)/shard_map/ppermute | solution.py:369
  30.0 0.0 collective-permute-done.5.g1.g1_b
  30.0 0.9 %third_even_end.1 = (f32[128,256]{1,0:T(8,128)S(1)}, bf16[128,1024]{1,0:T(8,128)(2,1)S(1)}, bf16[128,1024]{1,0:T(8,128)(2,1)S(1)}, f32[128,256]{1,0:T(8,128)S(1)}) custom-call(f32[512,256]{1,0:T(8,128)S(1)} %collective-permute-done.6.u.u_even, f32[1024,256]{1,0:T(8,128)S(1)} %get-tuple-element.103.c.c_even, s32[3,512,1024]{2,1,0:T(8,128)S(1)} %bitcast.1, ...), custom_call_target="tpu_custom_call" | custom-call | flops 1024 | bytes 1024 | tf_op jit(solution)/shard_map/third_even_end/pallas_call | solution.py:92
  30.8 0.7 %collective-permute-start.9 = (f32[128,256]{1,0:T(8,128)S(1)}, f32[128,256]{1,0:T(8,128)S(1)}, u32[]{:S(2)}, u32[]{:S(2)}) collective-permute-start(f32[128,256]{1,0:T(8,128)S(1)} %get-tuple-element.111), channel_id=1, source_target_pairs={{4,1},{20,17}} | collective-permute-start | bytes 393224 | tf_op jit(solution)/shard_map/ppermute | solution.py:369
  31.5 3.4 %collective-permute-start.10 = (f32[128,256]{1,0:T(8,128)S(1)}, f32[128,256]{1,0:T(8,128)S(1)}, u32[]{:S(2)}, u32[]{:S(2)}) collective-permute-start(f32[128,256]{1,0:T(8,128)S(1)} %get-tuple-element.112), channel_id=1, source_target_pairs={{0,14},{1,15},{2,0},{3,1},{4,2},{5,3},{6,4},{7,5},{8,6},{9,7},{10,... | collective-permute-start | bytes 393224 | tf_op jit(solution)/shard_map/ppermute | solution.py:369
  34.9 0.0 collective-permute-done.4.g1.g1_a.after
  34.9 2.9 %third_context.1 = (f32[1024,256]{1,0:T(8,128)}, f32[1024,256]{1,0:T(8,128)}) custom-call(f32[512,256]{1,0:T(8,128)S(1)} %get-tuple-element.107.u.u2.u_odd, f32[1024,256]{1,0:T(8,128)S(1)} %get-tuple-element.106.c.c_odd, f32[1024,256]{1,0:T(8,128)S(1)} %get-tuple-element.118.h_odd, bf16[384,1024]{1,0:T(8,128)(2,1)S(1)} %get-tuple-element.119.rh_odd, ...), custom_call_target="tpu_custom_call" | custom-call | flops 10000000000 | bytes 1024 | tf_op jit(solution)/shard_map/third_context/pallas_call | solution.py:92
  37.8 3.2 %collective-permute-done.11.g2 = f32[384,256]{1,0:T(8,128)S(1)} collective-permute-done((f32[384,256]{1,0:T(8,128)S(1)}, f32[384,256]{1,0:T(8,128)S(1)}, u32[]{:S(2)}, u32[]{:S(2)}) %collective-permute-start.11) | collective-permute-done | bytes 393248 | tf_op jit(solution)/shard_map/ppermute | solution.py:369
  41.0 1.0 %last_top.1 = (f32[512,256]{1,0:T(8,128)}, f32[512,256]{1,0:T(8,128)}, f32[8,128]{1,0:T(8,128)S(1)}) custom-call(f32[2,192,256]{2,1,0:T(8,128)S(1)} %get-tuple-element.67.s1_top, f32[2,320,256]{2,1,0:T(8,128)S(1)} %get-tuple-element.73.s1_end, f32[384,256]{1,0:T(8,128)S(1)} %collective-permute-done.4.g1.g1_a.after, ...), custom_call_target="tpu_custom_call" | custom-call | flops 1024 | bytes 1024 | tf_op jit(solution)/shard_map/last_top/pallas_call | solution.py:92
  42.0 0.0 collective-permute-done.9.refs_0_.g1_over
  42.0 0.4 collective-permute-done.10.g2
  42.4 0.8 %last_end.1 = (f32[512,256]{1,0:T(8,128)}, f32[512,256]{1,0:T(8,128)}) custom-call(f32[2,192,256]{2,1,0:T(8,128)S(1)} %get-tuple-element.67.s1_top, f32[2,320,256]{2,1,0:T(8,128)S(1)} %get-tuple-element.73.s1_end, f32[384,256]{1,0:T(8,128)S(1)} %collective-permute-done.4.g1.g1_a.after, ...), custom_call_target="tpu_custom_call", output_to_operand_aliasing={{0}: (9, {}), {1}: (10, {})} | custom-call | flops 1024 | bytes 1024 | tf_op jit(solution)/shard_map/last_end/pallas_call | solution.py:92
  (6 shorter events, 0.1 us)
Async XLA Ops:
  0.8 13.6 %collective-permute-start.3 = (f32[2,192,256]{2,1,0:T(8,128)S(1)}, f32[2,192,256]{2,1,0:T(8,128)S(1)}, u32[]{:S(2)}, u32[]{:S(2)}) collective-permute-start(f32[2,192,256]{2,1,0:T(8,128)S(1)} %get-tuple-element.67.s1_top), channel_id=1, source_target_pairs={{0,1},{1,2},{2,3},{3,4},{4,5},{5,6},{6,7},{7,8},{8,9},{9,10},{10,1... | collective-permute-start | bytes 1179656 | tf_op jit(solution)/shard_map/ppermute | solution.py:369
  6.2 15.2 %collective-permute-start = (f32[2,320,256]{2,1,0:T(8,128)S(1)}, f32[2,320,256]{2,1,0:T(8,128)S(1)}, u32[]{:S(2)}, u32[]{:S(2)}) collective-permute-start(f32[2,320,256]{2,1,0:T(8,128)S(1)} %get-tuple-element.73.s1_end), channel_id=1, source_target_pairs={{0,1},{1,2},{2,3},{3,4},{4,5},{5,6},{6,7},{7,8},{8,9},{9,10},{10,1... | collective-permute-start | bytes 1966088 | tf_op jit(solution)/shard_map/ppermute | solution.py:369
  6.5 7.8 %slice-start = ((s8[6291456]{0:T(1024)(128)(4,1)}), s8[4194304]{0:T(1024)(128)(4,1)S(1)}, s32[]{:S(2)}) async-start(s8[6291456]{0:T(1024)(128)(4,1)} %bitcast), calls=%async_computation | async-start | bytes 8388608
  8.9 5.5 %collective-permute-start.1 = (f32[512,256]{1,0:T(8,128)S(1)}, f32[512,256]{1,0:T(8,128)S(1)}, u32[]{:S(2)}, u32[]{:S(2)}) collective-permute-start(f32[512,256]{1,0:T(8,128)S(1)} %get-tuple-element.86), channel_id=1, source_target_pairs={{0,1},{1,0},{2,3},{3,2},{4,5},{5,4},{6,7},{7,6},{8,9},{9,8},{10,11... | collective-permute-start | bytes 1572872 | tf_op jit(solution)/shard_map/ppermute | solution.py:369
  10.3 4.1 %slice-start.1 = ((s8[6291456]{0:T(1024)(128)(4,1)}), s8[2097152]{0:T(1024)(128)(4,1)S(1)}, s32[]{:S(2)}) async-start(s8[6291456]{0:T(1024)(128)(4,1)} %bitcast), calls=%async_computation.1 | async-start | bytes 4194304
  10.3 4.1 %copy-start = (s32[3,1024]{1,0:T(4,128)S(1)}, s32[3,1024]{1,0:T(4,128)}, u32[]{:S(2)}) copy-start(s32[3,1024]{1,0:T(4,128)} %w.17) | copy-start | bytes 36868
  10.3 4.1 %collective-permute-start.2 = (f32[512,256]{1,0:T(8,128)S(1)}, f32[512,256]{1,0:T(8,128)S(1)}, u32[]{:S(2)}, u32[]{:S(2)}) collective-permute-start(f32[512,256]{1,0:T(8,128)S(1)} %get-tuple-element.87), channel_id=1, source_target_pairs={{0,1},{1,0},{2,3},{3,2},{4,5},{5,4},{6,7},{7,6},{8,9},{9,8},{10,11... | collective-permute-start | bytes 1572872 | tf_op jit(solution)/shard_map/ppermute | solution.py:369
  14.4 12.8 %collective-permute-start.6 = (f32[512,256]{1,0:T(8,128)S(1)}, f32[512,256]{1,0:T(8,128)S(1)}, u32[]{:S(2)}, u32[]{:S(2)}) collective-permute-start(f32[512,256]{1,0:T(8,128)S(1)} %get-tuple-element.89.after.u2_odd), channel_id=1, source_target_pairs={{0,1},{1,2},{2,3},{3,4},{4,5},{5,6},{6,7},{7,8},{8,9},{9,10},{10,1... | collective-permute-start | bytes 1572872 | tf_op jit(solution)/shard_map/ppermute | solution.py:369
  22.9 12.0 %collective-permute-start.4 = (f32[384,256]{1,0:T(8,128)S(1)}, f32[384,256]{1,0:T(8,128)S(1)}, u32[]{:S(2)}, u32[]{:S(2)}) collective-permute-start(f32[384,256]{1,0:T(8,128)S(1)} %get-tuple-element.96), channel_id=1, source_target_pairs={{1,0},{2,1},{3,2},{4,3},{5,4},{6,5},{7,6},{8,7},{9,8},{10,9},{11,1... | collective-permute-start | bytes 1179656 | tf_op jit(solution)/shard_map/ppermute | solution.py:369
  23.0 4.1 %collective-permute-start.7 = (f32[320,256]{1,0:T(8,128)S(1)}, f32[320,256]{1,0:T(8,128)S(1)}, u32[]{:S(2)}, u32[]{:S(2)}) collective-permute-start(f32[320,256]{1,0:T(8,128)S(1)} %get-tuple-element.104), channel_id=1, source_target_pairs={{0,1},{1,0},{2,3},{3,2},{4,5},{5,4},{6,7},{7,6},{8,9},{9,8},{10,11... | collective-permute-start | bytes 983048 | tf_op jit(solution)/shard_map/ppermute | solution.py:369
  23.5 3.6 %collective-permute-start.8 = (f32[320,256]{1,0:T(8,128)S(1)}, f32[320,256]{1,0:T(8,128)S(1)}, u32[]{:S(2)}, u32[]{:S(2)}) collective-permute-start(f32[320,256]{1,0:T(8,128)S(1)} %get-tuple-element.105.after), channel_id=1, source_target_pairs={{0,1},{1,0},{2,3},{3,2},{4,5},{5,4},{6,7},{7,6},{8,9},{9,8},{10,11... | collective-permute-start | bytes 983048 | tf_op jit(solution)/shard_map/ppermute | solution.py:369
  23.6 6.4 %collective-permute-start.5 = (f32[128,256]{1,0:T(8,128)S(1)}, f32[128,256]{1,0:T(8,128)S(1)}, u32[]{:S(2)}, u32[]{:S(2)}) collective-permute-start(f32[128,256]{1,0:T(8,128)S(1)} %get-tuple-element.97), channel_id=1, source_target_pairs={{1,0},{2,4},{3,2},{4,3},{5,1},{6,5},{7,6},{8,7},{9,8},{10,9},{11,1... | collective-permute-start | bytes 393224 | tf_op jit(solution)/shard_map/ppermute | solution.py:369
  29.0 12.0 %collective-permute-start.11 = (f32[384,256]{1,0:T(8,128)S(1)}, f32[384,256]{1,0:T(8,128)S(1)}, u32[]{:S(2)}, u32[]{:S(2)}) collective-permute-start(f32[384,256]{1,0:T(8,128)S(1)} %get-tuple-element.109.after), channel_id=1, source_target_pairs={{0,14},{1,15},{2,0},{3,1},{4,2},{5,3},{6,4},{7,5},{8,6},{9,7},{10,... | collective-permute-start | bytes 1179656 | tf_op jit(solution)/shard_map/ppermute | solution.py:369
  30.8 11.2 %collective-permute-start.9 = (f32[128,256]{1,0:T(8,128)S(1)}, f32[128,256]{1,0:T(8,128)S(1)}, u32[]{:S(2)}, u32[]{:S(2)}) collective-permute-start(f32[128,256]{1,0:T(8,128)S(1)} %get-tuple-element.111), channel_id=1, source_target_pairs={{4,1},{20,17}} | collective-permute-start | bytes 393224 | tf_op jit(solution)/shard_map/ppermute | solution.py:369
  31.5 10.9 %collective-permute-start.10 = (f32[128,256]{1,0:T(8,128)S(1)}, f32[128,256]{1,0:T(8,128)S(1)}, u32[]{:S(2)}, u32[]{:S(2)}) collective-permute-start(f32[128,256]{1,0:T(8,128)S(1)} %get-tuple-element.112), channel_id=1, source_target_pairs={{0,14},{1,15},{2,0},{3,1},{4,2},{5,3},{6,4},{7,5},{8,6},{9,7},{10,... | collective-permute-start | bytes 393224 | tf_op jit(solution)/shard_map/ppermute | solution.py:369

commit v13 on v12

--- a/solution.py
+++ b/solution.py
@@ -10,7 +10,7 @@
 F32 = jnp.float32
 BF16 = jnp.bfloat16
 RATE = 0.05
-STACKED = 256
+STACKED = 384
 DETOUR = 8
 HALF = 12
 EARLY = 6

time: 43.6 us -> 43.6 us (level)
  no operation moved by 1% of the time
where the time goes in v13:
time: 43.6 us; the launch traced here: 43.3 us
  Pallas kernels  18.7 us (43%)
  starting transfers between devices  13.6 us (31%)
  waiting for transfers between devices  10 us (23%)
  between operations  0.99 us (2%)
    pallas_call x17, Pallas kernels, call(): pl.pallas_call(body, out_shape=outs, in_specs=in_specs, out_specs=[out_sp...  18.7 us
    ppermute x12, starting transfers between devices, move(): return lax.ppermute(value, 'inner', pairs)  13.6 us
    ppermute x12, waiting for transfers between devices, move(): return lax.ppermute(value, 'inner', pairs)  10 us
  transfers between devices with their start and end apart: 12, of which 4 were waited for; matrix products, arithmetic and copies ran while one was open for 0% of the time, Pallas kernels for 41%

profile of v13, /device:TPU:0, one launch (start us, length us, event | category | flops | bytes accessed | tf_op | source)
XLA Modules:
  0.0 43.3 jit_solution(14497188503455900001)
XLA Ops:
  0.6 0.1 first_top.1
  0.8 3.1 %collective-permute-start.3 = (f32[2,192,256]{2,1,0:T(8,128)S(1)}, f32[2,192,256]{2,1,0:T(8,128)S(1)}, u32[]{:S(2)}, u32[]{:S(2)}) collective-permute-start(f32[2,192,256]{2,1,0:T(8,128)S(1)} %get-tuple-element.67.s1_top), channel_id=1, source_target_pairs={{0,1},{1,2},{2,3},{3,4},{4,5},{5,6},{6,7},{7,8},{8,9},{9,10},{10,1... | collective-permute-start | bytes 1179656 | tf_op jit(solution)/shard_map/ppermute | solution.py:369
  3.9 2.3 %first_end.1 = (f32[2,320,256]{2,1,0:T(8,128)S(1)}, bf16[320,1024]{1,0:T(8,128)(2,1)S(1)}, bf16[320,1024]{1,0:T(8,128)(2,1)S(1)}, f32[1024,256]{1,0:T(8,128)S(1)...) custom-call(f32[512,256]{1,0:T(8,128)} %u.3, ...), custom_call_target="tpu_custom_call" | custom-call | flops 1024 | bytes 1024 | tf_op jit(solution)/shard_map/first_end/pallas_call | solution.py:92
  6.2 0.4 collective-permute-start
  6.6 0.0 slice-start
  6.6 2.3 %first_even.1 = (f32[512,256]{1,0:T(8,128)S(1)}, f32[512,256]{1,0:T(8,128)S(1)}, bf16[512,1024]{1,0:T(8,128)(2,1)S(1)}, bf16[512,1024]{1,0:T(8,128)(2,1)S(1)}, f...) custom-call(f32[512,256]{1,0:T(8,128)S(1)} %get-tuple-element.74.u, f32[512,256]{1,0:T(8,128)S(1)} %get-tuple-element.76.g, ...), custom_call_target="tpu_custom_call" | custom-call | flops 1024 | bytes 1024 | tf_op jit(solution)/shard_map/first_even/pallas_call | solution.py:92
  8.9 1.4 %collective-permute-start.1 = (f32[512,256]{1,0:T(8,128)S(1)}, f32[512,256]{1,0:T(8,128)S(1)}, u32[]{:S(2)}, u32[]{:S(2)}) collective-permute-start(f32[512,256]{1,0:T(8,128)S(1)} %get-tuple-element.86), channel_id=1, source_target_pairs={{0,1},{1,0},{2,3},{3,2},{4,5},{5,4},{6,7},{7,6},{8,9},{9,8},{10,11... | collective-permute-start | bytes 1572872 | tf_op jit(solution)/shard_map/ppermute | solution.py:369
  10.3 0.0 slice-start.1
  10.3 0.0 copy-start
  10.3 0.1 collective-permute-start.2
  10.4 4.0 %collective-permute-done.3.refs_0_.s1.s1_top = f32[2,192,256]{2,1,0:T(8,128)S(1)} collective-permute-done((f32[2,192,256]{2,1,0:T(8,128)S(1)}, f32[2,192,256]{2,1,0:T(8,128)S(1)}, u32[]{:S(2)}, u32[]{:S(2)}) %collective-permute-start.3) | collective-permute-done | bytes 393248 | tf_op jit(solution)/shard_map/ppermute | solution.py:369
  14.3 0.0 collective-permute-done.1.u1.u_odd
  14.3 0.0 collective-permute-done.2.g1
  14.4 0.0 slice-done
  14.4 0.0 slice-done.1
  14.4 0.0 copy-done
  14.4 0.9 %collective-permute-start.6 = (f32[512,256]{1,0:T(8,128)S(1)}, f32[512,256]{1,0:T(8,128)S(1)}, u32[]{:S(2)}, u32[]{:S(2)}) collective-permute-start(f32[512,256]{1,0:T(8,128)S(1)} %get-tuple-element.89.after.u2_odd), channel_id=1, source_target_pairs={{0,1},{1,2},{2,3},{3,4},{4,5},{5,6},{6,7},{7,8},{8,9},{9,10},{10,1... | collective-permute-start | bytes 1572872 | tf_op jit(solution)/shard_map/ppermute | solution.py:369
  15.4 2.5 %first_context.1 = (f32[1024,256]{1,0:T(8,128)S(1)}, f32[1024,256]{1,0:T(8,128)S(1)}) custom-call(f32[1024,256]{1,0:T(8,128)} %h.3, f32[512,256]{1,0:T(8,128)S(1)} %get-tuple-element.74.u, f32[1024,256]{1,0:T(8,128)S(1)} %get-tuple-element.75.c, bf16[512,1024]{1,0:T(8,128)(2,1)S(1)} %get-tuple-element.84.r_high, ...), custom_call_target="tpu_custom_call" | custom-call | flops 1024 | bytes 1024 | tf_op jit(solution)/shard_map/first_context/pallas_call | solution.py:92
  17.9 1.1 %second_top.1 = (f32[320,256]{1,0:T(8,128)S(1)}, f32[192,256]{1,0:T(8,128)S(1)}, bf16[192,1024]{1,0:T(8,128)(2,1)S(1)}, bf16[192,1024]{1,0:T(8,128)(2,1)S(1)}, f...) custom-call(f32[2,192,256]{2,1,0:T(8,128)S(1)} %collective-permute-done.3.refs_0_.s1.s1_top, ...), custom_call_target="tpu_custom_call" | custom-call | flops 1024 | bytes 1024 | tf_op jit(solution)/shard_map/second_top/pallas_call | solution.py:92
  19.0 2.4 %collective-permute-done.s1.s1_end = f32[2,320,256]{2,1,0:T(8,128)S(1)} collective-permute-done((f32[2,320,256]{2,1,0:T(8,128)S(1)}, f32[2,320,256]{2,1,0:T(8,128)S(1)}, u32[]{:S(2)}, u32[]{:S(2)}) %collective-permute-start) | collective-permute-done | bytes 655392 | tf_op jit(solution)/shard_map/ppermute | solution.py:369
  21.4 1.6 %second_end.1 = (f32[320,256]{1,0:T(8,128)S(1)}, f32[384,256]{1,0:T(8,128)S(1)}, f32[128,256]{1,0:T(8,128)S(1)}, bf16[320,1024]{1,0:T(8,128)(2,1)S(1)}, bf16[320,1024]{1,0:T(8,128)(2,1)S(1)}) custom-call(f32[2,320,256]{2,1,0:T(8,128)S(1)} %collective-permute-done.s1.s1_end, f32[1024,256]{1,0:T(8,128)S(1)} %get-tuple-element.90.c, ...), custom_call_target="tpu_custom_call" | custom-call | flops 10000000000 | bytes 1024 | tf_op jit(solution)/shard_map/second_end/pallas_call | solution.py:92
  22.9 0.1 collective-permute-start.4
  23.0 0.5 %collective-permute-start.7 = (f32[320,256]{1,0:T(8,128)S(1)}, f32[320,256]{1,0:T(8,128)S(1)}, u32[]{:S(2)}, u32[]{:S(2)}) collective-permute-start(f32[320,256]{1,0:T(8,128)S(1)} %get-tuple-element.104), channel_id=1, source_target_pairs={{0,1},{1,0},{2,3},{3,2},{4,5},{5,4},{6,7},{7,6},{8,9},{9,8},{10,11... | collective-permute-start | bytes 983048 | tf_op jit(solution)/shard_map/ppermute | solution.py:369
  23.5 0.1 collective-permute-start.8
  23.6 2.0 %collective-permute-start.5 = (f32[128,256]{1,0:T(8,128)S(1)}, f32[128,256]{1,0:T(8,128)S(1)}, u32[]{:S(2)}, u32[]{:S(2)}) collective-permute-start(f32[128,256]{1,0:T(8,128)S(1)} %get-tuple-element.97), channel_id=1, source_target_pairs={{1,0},{2,4},{3,2},{4,3},{5,1},{6,5},{7,6},{8,7},{9,8},{10,9},{11,1... | collective-permute-start | bytes 393224 | tf_op jit(solution)/shard_map/ppermute | solution.py:369
  25.6 1.5 %second_context.1 = (f32[1024,256]{1,0:T(8,128)S(1)}, f32[1024,256]{1,0:T(8,128)S(1)}) custom-call(f32[2,192,256]{2,1,0:T(8,128)S(1)} %collective-permute-done.3.refs_0_.s1.s1_top, f32[2,320,256]{2,1,0:T(8,128)S(1)} %collective-permute-done.s1.s1_end, f32[1024,256]{1,0:T(8,128)S(1)} %get-tuple-element.90.c, f32[1024,256]{1,0:T(8,128)S(1)} %get-tuple-element.98.h, ...), custom_call_target="tpu_custom_call" | custom-call | flops 1024 | bytes 1024 | tf_op jit(solution)/shard_map/second_context/pallas_call | solution.py:92
  27.1 0.0 collective-permute-done.7.u_top.swapped
  27.1 0.0 collective-permute-done.8.u_end
  27.2 0.0 collective-permute-done.6.u.u_even
  27.2 1.8 %third_even_top.1 = (f32[384,256]{1,0:T(8,128)S(1)}, bf16[384,1024]{1,0:T(8,128)(2,1)S(1)}, bf16[384,1024]{1,0:T(8,128)(2,1)S(1)}) custom-call(f32[512,256]{1,0:T(8,128)S(1)} %collective-permute-done.6.u.u_even, f32[1024,256]{1,0:T(8,128)S(1)} %get-tuple-element.103.c.c_even, s32[3,512,1024]{2,1,0:T(8,128)S(1)} %bitcast.1, s32[3,1024]{1,0:T(4,128)S(1)} %copy-done, ...), custom_call_target="tpu_custom_call" | custom-call | flops 1024 | bytes 1024 | tf_op jit(solution)/shard_map/third_even_top/pallas_call | solution.py:92
  29.0 0.9 %collective-permute-start.11 = (f32[384,256]{1,0:T(8,128)S(1)}, f32[384,256]{1,0:T(8,128)S(1)}, u32[]{:S(2)}, u32[]{:S(2)}) collective-permute-start(f32[384,256]{1,0:T(8,128)S(1)} %get-tuple-element.109.after), channel_id=1, source_target_pairs={{0,14},{1,15},{2,0},{3,1},{4,2},{5,3},{6,4},{7,5},{8,6},{9,7},{10,... | collective-permute-start | bytes 1179656 | tf_op jit(solution)/shard_map/ppermute | solution.py:369
  30.0 0.0 collective-permute-done.5.g1.g1_b
  30.0 0.9 %third_even_end.1 = (f32[128,256]{1,0:T(8,128)S(1)}, bf16[128,1024]{1,0:T(8,128)(2,1)S(1)}, bf16[128,1024]{1,0:T(8,128)(2,1)S(1)}, f32[128,256]{1,0:T(8,128)S(1)}) custom-call(f32[512,256]{1,0:T(8,128)S(1)} %collective-permute-done.6.u.u_even, f32[1024,256]{1,0:T(8,128)S(1)} %get-tuple-element.103.c.c_even, s32[3,512,1024]{2,1,0:T(8,128)S(1)} %bitcast.1, ...), custom_call_target="tpu_custom_call" | custom-call | flops 1024 | bytes 1024 | tf_op jit(solution)/shard_map/third_even_end/pallas_call | solution.py:92
  30.8 0.7 %collective-permute-start.9 = (f32[128,256]{1,0:T(8,128)S(1)}, f32[128,256]{1,0:T(8,128)S(1)}, u32[]{:S(2)}, u32[]{:S(2)}) collective-permute-start(f32[128,256]{1,0:T(8,128)S(1)} %get-tuple-element.111), channel_id=1, source_target_pairs={{4,1},{20,17}} | collective-permute-start | bytes 393224 | tf_op jit(solution)/shard_map/ppermute | solution.py:369
  31.5 3.4 %collective-permute-start.10 = (f32[128,256]{1,0:T(8,128)S(1)}, f32[128,256]{1,0:T(8,128)S(1)}, u32[]{:S(2)}, u32[]{:S(2)}) collective-permute-start(f32[128,256]{1,0:T(8,128)S(1)} %get-tuple-element.112), channel_id=1, source_target_pairs={{0,14},{1,15},{2,0},{3,1},{4,2},{5,3},{6,4},{7,5},{8,6},{9,7},{10,... | collective-permute-start | bytes 393224 | tf_op jit(solution)/shard_map/ppermute | solution.py:369
  34.9 0.0 collective-permute-done.4.g1.g1_a.after
  34.9 2.9 %third_context.1 = (f32[1024,256]{1,0:T(8,128)}, f32[1024,256]{1,0:T(8,128)}) custom-call(f32[512,256]{1,0:T(8,128)S(1)} %get-tuple-element.107.u.u2.u_odd, f32[1024,256]{1,0:T(8,128)S(1)} %get-tuple-element.106.c.c_odd, f32[1024,256]{1,0:T(8,128)S(1)} %get-tuple-element.118.h_odd, bf16[384,1024]{1,0:T(8,128)(2,1)S(1)} %get-tuple-element.119.rh_odd, ...), custom_call_target="tpu_custom_call" | custom-call | flops 10000000000 | bytes 1024 | tf_op jit(solution)/shard_map/third_context/pallas_call | solution.py:92
  37.8 3.3 %collective-permute-done.11.g2 = f32[384,256]{1,0:T(8,128)S(1)} collective-permute-done((f32[384,256]{1,0:T(8,128)S(1)}, f32[384,256]{1,0:T(8,128)S(1)}, u32[]{:S(2)}, u32[]{:S(2)}) %collective-permute-start.11) | collective-permute-done | bytes 393248 | tf_op jit(solution)/shard_map/ppermute | solution.py:369
  41.0 1.0 %last_top.1 = (f32[512,256]{1,0:T(8,128)}, f32[512,256]{1,0:T(8,128)}, f32[8,128]{1,0:T(8,128)S(1)}) custom-call(f32[2,192,256]{2,1,0:T(8,128)S(1)} %get-tuple-element.67.s1_top, f32[2,320,256]{2,1,0:T(8,128)S(1)} %get-tuple-element.73.s1_end, f32[384,256]{1,0:T(8,128)S(1)} %collective-permute-done.4.g1.g1_a.after, ...), custom_call_target="tpu_custom_call" | custom-call | flops 1024 | bytes 1024 | tf_op jit(solution)/shard_map/last_top/pallas_call | solution.py:92
  42.0 0.0 collective-permute-done.9.refs_0_.g1_over
  42.0 0.4 collective-permute-done.10.g2
  42.4 0.8 %last_end.1 = (f32[512,256]{1,0:T(8,128)}, f32[512,256]{1,0:T(8,128)}) custom-call(f32[2,192,256]{2,1,0:T(8,128)S(1)} %get-tuple-element.67.s1_top, f32[2,320,256]{2,1,0:T(8,128)S(1)} %get-tuple-element.73.s1_end, f32[384,256]{1,0:T(8,128)S(1)} %collective-permute-done.4.g1.g1_a.after, ...), custom_call_target="tpu_custom_call", output_to_operand_aliasing={{0}: (9, {}), {1}: (10, {})} | custom-call | flops 1024 | bytes 1024 | tf_op jit(solution)/shard_map/last_end/pallas_call | solution.py:92
  (6 shorter events, 0.1 us)
Async XLA Ops:
  0.8 13.6 %collective-permute-start.3 = (f32[2,192,256]{2,1,0:T(8,128)S(1)}, f32[2,192,256]{2,1,0:T(8,128)S(1)}, u32[]{:S(2)}, u32[]{:S(2)}) collective-permute-start(f32[2,192,256]{2,1,0:T(8,128)S(1)} %get-tuple-element.67.s1_top), channel_id=1, source_target_pairs={{0,1},{1,2},{2,3},{3,4},{4,5},{5,6},{6,7},{7,8},{8,9},{9,10},{10,1... | collective-permute-start | bytes 1179656 | tf_op jit(solution)/shard_map/ppermute | solution.py:369
  6.2 15.2 %collective-permute-start = (f32[2,320,256]{2,1,0:T(8,128)S(1)}, f32[2,320,256]{2,1,0:T(8,128)S(1)}, u32[]{:S(2)}, u32[]{:S(2)}) collective-permute-start(f32[2,320,256]{2,1,0:T(8,128)S(1)} %get-tuple-element.73.s1_end), channel_id=1, source_target_pairs={{0,1},{1,2},{2,3},{3,4},{4,5},{5,6},{6,7},{7,8},{8,9},{9,10},{10,1... | collective-permute-start | bytes 1966088 | tf_op jit(solution)/shard_map/ppermute | solution.py:369
  6.6 7.8 %slice-start = ((s8[6291456]{0:T(1024)(128)(4,1)}), s8[4194304]{0:T(1024)(128)(4,1)S(1)}, s32[]{:S(2)}) async-start(s8[6291456]{0:T(1024)(128)(4,1)} %bitcast), calls=%async_computation | async-start | bytes 8388608
  8.9 5.5 %collective-permute-start.1 = (f32[512,256]{1,0:T(8,128)S(1)}, f32[512,256]{1,0:T(8,128)S(1)}, u32[]{:S(2)}, u32[]{:S(2)}) collective-permute-start(f32[512,256]{1,0:T(8,128)S(1)} %get-tuple-element.86), channel_id=1, source_target_pairs={{0,1},{1,0},{2,3},{3,2},{4,5},{5,4},{6,7},{7,6},{8,9},{9,8},{10,11... | collective-permute-start | bytes 1572872 | tf_op jit(solution)/shard_map/ppermute | solution.py:369
  10.3 4.1 %slice-start.1 = ((s8[6291456]{0:T(1024)(128)(4,1)}), s8[2097152]{0:T(1024)(128)(4,1)S(1)}, s32[]{:S(2)}) async-start(s8[6291456]{0:T(1024)(128)(4,1)} %bitcast), calls=%async_computation.1 | async-start | bytes 4194304
  10.3 4.1 %copy-start = (s32[3,1024]{1,0:T(4,128)S(1)}, s32[3,1024]{1,0:T(4,128)}, u32[]{:S(2)}) copy-start(s32[3,1024]{1,0:T(4,128)} %w.17) | copy-start | bytes 36868
  10.3 4.1 %collective-permute-start.2 = (f32[512,256]{1,0:T(8,128)S(1)}, f32[512,256]{1,0:T(8,128)S(1)}, u32[]{:S(2)}, u32[]{:S(2)}) collective-permute-start(f32[512,256]{1,0:T(8,128)S(1)} %get-tuple-element.87), channel_id=1, source_target_pairs={{0,1},{1,0},{2,3},{3,2},{4,5},{5,4},{6,7},{7,6},{8,9},{9,8},{10,11... | collective-permute-start | bytes 1572872 | tf_op jit(solution)/shard_map/ppermute | solution.py:369
  14.4 12.8 %collective-permute-start.6 = (f32[512,256]{1,0:T(8,128)S(1)}, f32[512,256]{1,0:T(8,128)S(1)}, u32[]{:S(2)}, u32[]{:S(2)}) collective-permute-start(f32[512,256]{1,0:T(8,128)S(1)} %get-tuple-element.89.after.u2_odd), channel_id=1, source_target_pairs={{0,1},{1,2},{2,3},{3,4},{4,5},{5,6},{6,7},{7,8},{8,9},{9,10},{10,1... | collective-permute-start | bytes 1572872 | tf_op jit(solution)/shard_map/ppermute | solution.py:369
  22.9 12.0 %collective-permute-start.4 = (f32[384,256]{1,0:T(8,128)S(1)}, f32[384,256]{1,0:T(8,128)S(1)}, u32[]{:S(2)}, u32[]{:S(2)}) collective-permute-start(f32[384,256]{1,0:T(8,128)S(1)} %get-tuple-element.96), channel_id=1, source_target_pairs={{1,0},{2,1},{3,2},{4,3},{5,4},{6,5},{7,6},{8,7},{9,8},{10,9},{11,1... | collective-permute-start | bytes 1179656 | tf_op jit(solution)/shard_map/ppermute | solution.py:369
  23.0 4.1 %collective-permute-start.7 = (f32[320,256]{1,0:T(8,128)S(1)}, f32[320,256]{1,0:T(8,128)S(1)}, u32[]{:S(2)}, u32[]{:S(2)}) collective-permute-start(f32[320,256]{1,0:T(8,128)S(1)} %get-tuple-element.104), channel_id=1, source_target_pairs={{0,1},{1,0},{2,3},{3,2},{4,5},{5,4},{6,7},{7,6},{8,9},{9,8},{10,11... | collective-permute-start | bytes 983048 | tf_op jit(solution)/shard_map/ppermute | solution.py:369
  23.5 3.7 %collective-permute-start.8 = (f32[320,256]{1,0:T(8,128)S(1)}, f32[320,256]{1,0:T(8,128)S(1)}, u32[]{:S(2)}, u32[]{:S(2)}) collective-permute-start(f32[320,256]{1,0:T(8,128)S(1)} %get-tuple-element.105.after), channel_id=1, source_target_pairs={{0,1},{1,0},{2,3},{3,2},{4,5},{5,4},{6,7},{7,6},{8,9},{9,8},{10,11... | collective-permute-start | bytes 983048 | tf_op jit(solution)/shard_map/ppermute | solution.py:369
  23.6 6.4 %collective-permute-start.5 = (f32[128,256]{1,0:T(8,128)S(1)}, f32[128,256]{1,0:T(8,128)S(1)}, u32[]{:S(2)}, u32[]{:S(2)}) collective-permute-start(f32[128,256]{1,0:T(8,128)S(1)} %get-tuple-element.97), channel_id=1, source_target_pairs={{1,0},{2,4},{3,2},{4,3},{5,1},{6,5},{7,6},{8,7},{9,8},{10,9},{11,1... | collective-permute-start | bytes 393224 | tf_op jit(solution)/shard_map/ppermute | solution.py:369
  29.0 12.0 %collective-permute-start.11 = (f32[384,256]{1,0:T(8,128)S(1)}, f32[384,256]{1,0:T(8,128)S(1)}, u32[]{:S(2)}, u32[]{:S(2)}) collective-permute-start(f32[384,256]{1,0:T(8,128)S(1)} %get-tuple-element.109.after), channel_id=1, source_target_pairs={{0,14},{1,15},{2,0},{3,1},{4,2},{5,3},{6,4},{7,5},{8,6},{9,7},{10,... | collective-permute-start | bytes 1179656 | tf_op jit(solution)/shard_map/ppermute | solution.py:369
  30.8 11.1 %collective-permute-start.9 = (f32[128,256]{1,0:T(8,128)S(1)}, f32[128,256]{1,0:T(8,128)S(1)}, u32[]{:S(2)}, u32[]{:S(2)}) collective-permute-start(f32[128,256]{1,0:T(8,128)S(1)} %get-tuple-element.111), channel_id=1, source_target_pairs={{4,1},{20,17}} | collective-permute-start | bytes 393224 | tf_op jit(solution)/shard_map/ppermute | solution.py:369
  31.5 10.9 %collective-permute-start.10 = (f32[128,256]{1,0:T(8,128)S(1)}, f32[128,256]{1,0:T(8,128)S(1)}, u32[]{:S(2)}, u32[]{:S(2)}) collective-permute-start(f32[128,256]{1,0:T(8,128)S(1)} %get-tuple-element.112), channel_id=1, source_target_pairs={{0,14},{1,15},{2,0},{3,1},{4,2},{5,3},{6,4},{7,5},{8,6},{9,7},{10,... | collective-permute-start | bytes 393224 | tf_op jit(solution)/shard_map/ppermute | solution.py:369
